TPU v7x, 32 devices: a whole 2x2x4 slice. The times are simulated.
32 devices in a mesh: px: 8 (over z, x), py: 4 (over y, core).
Axes of the slice: x: 2, y: 2, z: 4, core: 2. Of those that a mesh axis runs over, the one named last changes fastest.
Arguments:
- state_field: bfloat16 [32, 16, 128, 128], P(None, 'px', 'py'), may hold values from -6 to 6
- conv_weight: bfloat16 [32, 32, 3, 3, 3], replicated, may hold values from -0.21875 to 0.21875
- conv_bias: float32 [32], replicated, may hold values from -4 to 4
- spectral_weight: float32 [2, 16, 32, 16, 32, 16], P(None, 'py', 'px'), may hold values from -1 to 1
Outputs:
- layer_out: bfloat16 [32, 16, 128, 128], P(None, 'px', 'py')
All inputs are finite; a program needn't handle non-finite values.
Results may differ from a plain program's by a relative error of at most 0.0063.
Values may be sent and summed in bfloat16 or wider, within the bound.
No kernel may reach another device: no remote copies, remote signals or barrier semaphores. Data moves between devices by JAX's collectives and lax.ppermute only.
A program may use at most 64 MiB of HBM per device.

v0:
```python
import functools
import math

import jax
import jax.numpy as jnp
import ml_dtypes
import numpy as np
from jax import lax
from jax.experimental import pallas as pl
from jax.experimental.pallas import tpu as pltpu
from jax.sharding import PartitionSpec as P

KX = 16
KY = 16
KZ = 16


def extended(cells, sides, width):
    for axis, dim in sides:
        count = lax.axis_size(axis)
        ends = count - 1
        head = lax.slice_in_dim(cells, 0, width, axis=dim)
        tail = lax.slice_in_dim(cells, cells.shape[dim] - width, cells.shape[dim], axis=dim)
        cells = jnp.concatenate(
            [
                lax.ppermute(tail, axis, [(i, (i + 1) % count) for i in range(ends)]),
                cells,
                lax.ppermute(head, axis, [((i + 1) % count, i) for i in range(ends)]),
            ],
            axis=dim,
        )
    return cells


def swapped(value, axis, distance):
    mask = 2**distance
    pairs = [(source, source ^ mask) for source in range(lax.axis_size(axis))]
    return lax.ppermute(value, axis, pairs)


def mode_numbers(count):
    indices = jnp.arange(count, dtype=jnp.int32)
    return jnp.where(indices < count // 2, indices, indices - count)


def trig_pair(numbers, points, length, factor, out_type):
    positions = jnp.arange(points, dtype=jnp.int32)
    phases = positions[:, None] * numbers[None, :] % length
    angles = phases.astype(jnp.float32) * (2.0 * math.pi / length)
    return (
        (jnp.cos(angles) * factor).astype(out_type),
        (jnp.sin(angles) * factor).astype(out_type),
    )


def last_product(source, table, precision=None):
    flat = source.reshape(-1, source.shape[-1])
    result = jnp.dot(flat, table, preferred_element_type=jnp.float32, precision=precision)
    return result.reshape(source.shape[:-1] + (table.shape[1],))


def forward_last(source, cosine, sine_table, precision=None):
    real_part = source[..., 0, :]
    imag_part = source[..., 1, :]
    real_out = last_product(real_part, cosine, precision) + last_product(
        imag_part, sine_table, precision
    )
    imag_out = last_product(imag_part, cosine, precision) - last_product(
        real_part, sine_table, precision
    )
    return jnp.stack([real_out, imag_out], axis=-2)


def inverse_last(source, cosine, sine_table, precision=None):
    real_part = source[..., 0, :]
    imag_part = source[..., 1, :]
    real_out = last_product(real_part, cosine, precision) - last_product(
        imag_part, sine_table, precision
    )
    imag_out = last_product(real_part, sine_table, precision) + last_product(
        imag_part, cosine, precision
    )
    return jnp.stack([real_out, imag_out], axis=-2)


def mix_block(spectral_weight, x_block):
    highest = lax.Precision.HIGHEST
    real_in = x_block[:, :, :, 0, :]
    imag_in = x_block[:, :, :, 1, :]
    partial_real = jnp.einsum(
        "zucok,uzck->uzok", spectral_weight[0], real_in, precision=highest
    ) - jnp.einsum("zucok,uzck->uzok", spectral_weight[1], imag_in, precision=highest)
    partial_imag = jnp.einsum(
        "zucok,uzck->uzok", spectral_weight[0], imag_in, precision=highest
    ) + jnp.einsum("zucok,uzck->uzok", spectral_weight[1], real_in, precision=highest)
    return jnp.stack([partial_real, partial_imag], axis=3)


def general_body(state_field, conv_weight, conv_bias, spectral_weight):
    channels, cells_x, cells_y, depth = state_field.shape
    count_x = lax.axis_size("px")
    count_y = lax.axis_size("py")
    width_x = cells_x * count_x
    width_y = cells_y * count_y
    index_x = lax.axis_index("px")
    kz_local = KZ // count_y
    units = 2 * KY // count_x
    highest = lax.Precision.HIGHEST
    padded = extended(state_field, (("px", 1), ("py", 2)), 1)
    convolved = lax.conv_general_dilated(
        padded[None],
        conv_weight,
        (1, 1, 1),
        ((0, 0), (0, 0), (1, 1)),
        dimension_numbers=("NCDHW", "OIDHW", "NCDHW"),
        preferred_element_type=jnp.float32,
    )[0]
    z_cos, z_sin = trig_pair(
        jnp.arange(KZ, dtype=jnp.int32), depth, depth, depth ** (-0.5), jnp.bfloat16
    )
    z_table = jnp.stack([z_cos, -z_sin], axis=1)
    z_modes = jnp.einsum(
        "cxyn,nwk->kcxwy", state_field, z_table, preferred_element_type=jnp.float32
    ).astype(jnp.bfloat16)
    y_cos, y_sin = trig_pair(mode_numbers(KY), width_y, width_y, width_y ** (-0.5), jnp.bfloat16)
    full_rows = lax.all_to_all(z_modes, "py", split_axis=0, concat_axis=4, tiled=True)
    y_modes = forward_last(full_rows, y_cos, y_sin)
    y_modes = y_modes.astype(jnp.bfloat16)
    by_unit = y_modes.reshape(kz_local, 2, channels // 2, cells_x, 2, KY).transpose(
        1, 5, 0, 2, 4, 3
    )
    by_unit = by_unit.reshape(2 * KY, kz_local, channels // 2, 2, cells_x)
    x_rows = lax.all_to_all(by_unit, "px", split_axis=0, concat_axis=4, tiled=True)
    x_cos, x_sin = trig_pair(mode_numbers(KX), width_x, width_x, width_x ** (-0.5), jnp.bfloat16)
    x_modes = forward_last(x_rows, x_cos, x_sin)
    partial_modes = mix_block(spectral_weight, x_modes)
    partial_modes = partial_modes.reshape(units, kz_local, 2, channels // 2, 2, KX)
    half_index = index_x * units // KY
    own_half = lax.dynamic_index_in_dim(partial_modes, half_index, 2, keepdims=False)
    other_half = lax.dynamic_index_in_dim(partial_modes, 1 - half_index, 2, keepdims=False)
    mixed_modes = own_half + swapped(other_half, "px", count_x.bit_length() - 2)
    ix_cos, ix_sin = trig_pair(mode_numbers(KX), width_x, width_x, KX ** (-0.5), jnp.float32)
    x_values = inverse_last(mixed_modes, ix_cos.T, ix_sin.T, highest).astype(jnp.bfloat16)
    returned = lax.all_to_all(x_values, "px", split_axis=4, concat_axis=0, tiled=True)
    returned = returned.reshape(2, KY, kz_local, channels // 2, 2, cells_x).transpose(
        2, 0, 3, 5, 4, 1
    )
    returned = returned.reshape(kz_local, channels, cells_x, 2, KY)
    iy_cos, iy_sin = trig_pair(mode_numbers(KY), width_y, width_y, KY ** (-0.5), jnp.bfloat16)
    expanded = inverse_last(returned, iy_cos.T, iy_sin.T).astype(jnp.bfloat16)
    y_values = lax.all_to_all(expanded, "py", split_axis=4, concat_axis=0, tiled=True)
    iz_cos, iz_sin = trig_pair(
        jnp.arange(KZ, dtype=jnp.int32), depth, depth, KZ ** (-0.5), jnp.bfloat16
    )
    iz_table = jnp.stack([iz_cos.T, -iz_sin.T], axis=0)
    spectral = jnp.einsum("kcxwy,wkn->cxyn", y_values, iz_table, preferred_element_type=jnp.float32)
    total = convolved + spectral + conv_bias[:, None, None, None]
    return jax.nn.gelu(total, approximate=False).astype(jnp.bfloat16)


def angle_tables(numbers, points, length, factor):
    phases = (np.arange(points)[:, None] * numbers[None, :]) % length
    angles = phases.astype(np.float32) * np.float32(2.0 * math.pi / length)
    return (
        np.cos(angles).astype(np.float32) * np.float32(factor),
        np.sin(angles).astype(np.float32) * np.float32(factor),
    )


def signed_modes(count):
    indices = np.arange(count)
    return np.where(indices < count // 2, indices, indices - count)


def narrow(table):
    return table.astype(ml_dtypes.bfloat16).astype(np.float32)


def forward_pair(cosine, sine):
    return np.stack([np.stack([cosine, -sine]), np.stack([sine, cosine])])


def inverse_pair(cosine, sine):
    return np.stack([np.stack([cosine, sine]), np.stack([-sine, cosine])])


@functools.cache
def tables(count_x, count_y, cells_x, cells_y, depth):
    width_x, width_y = count_x * cells_x, count_y * cells_y
    kzl, units = KZ // count_y, 2 * KY // count_x
    groups = KY // units
    zc, zs = angle_tables(np.arange(KZ), depth, depth, depth**-0.5)
    z_forward = np.concatenate([zc.T, -zs.T])
    yc, ys = angle_tables(signed_modes(KY), width_y, width_y, width_y**-0.5)
    pair = forward_pair(yc, ys).reshape(2, 2, count_y, cells_y, groups, units)
    y_forward = np.einsum("rsqygk,d,w->qrygwskd", pair, np.ones(8), np.ones(cells_x))
    y_forward = y_forward.reshape(count_y, 2 * cells_y, groups * 2 * cells_x * units * 8)
    xc, xs = angle_tables(signed_modes(KX), width_x, width_x, width_x**-0.5)
    pair = forward_pair(xc, xs).reshape(2, 2, count_x, cells_x, KX)
    x_forward = np.einsum("rspxk,gh,q->gskpqhxr", pair, np.eye(2), np.ones(count_y))
    x_forward = x_forward.reshape(4 * KX, count_x * count_y * 4 * cells_x)
    xc, xs = angle_tables(signed_modes(KX), width_x, width_x, KX**-0.5)
    pair = inverse_pair(xc, xs).reshape(2, 2, count_x, cells_x, KX)
    x_inverse = np.einsum("rspxk,zv->pxzsvrk", pair, np.eye(kzl))
    x_inverse = x_inverse.reshape(count_x * cells_x * kzl * 2, kzl * 2 * KX)
    zc, zs = angle_tables(np.arange(KZ), depth, depth, KZ**-0.5)
    pair = inverse_pair(zc, zs).reshape(2, 2, depth, count_y, kzl)
    z_inverse = np.einsum("rsnqz,xw,h->hqxzrwsn", pair, np.eye(cells_x), np.ones(2))
    z_inverse = z_inverse.reshape(4 * cells_x * KZ, cells_x * 2 * depth)
    yc, ys = angle_tables(signed_modes(KY), width_y, width_y, KY**-0.5)
    pair = np.stack([yc, -ys]).reshape(2, count_y, cells_y, KY)
    y_inverse = np.einsum("rqyk,i->qyrki", pair, np.ones(16))
    y_inverse = y_inverse.reshape(count_y, cells_y, 32 * KY)
    return (
        narrow(z_forward),
        narrow(y_forward),
        narrow(x_forward),
        x_inverse.astype(np.float32),
        narrow(z_inverse),
        narrow(y_inverse),
    )


def block_moves(value):
    rows = value.shape[0]
    tiles = value.reshape(rows // 8, 8, 128)
    row = lax.broadcasted_iota(jnp.int32, tiles.shape, 1) % 4
    block = lax.broadcasted_iota(jnp.int32, tiles.shape, 2) // 32
    result = tiles
    for lane_step in (1, 2, 3):
        moved = pltpu.roll(tiles, 128 - 32 * lane_step, 2)
        result = jnp.where(row - block == lane_step, pltpu.roll(moved, lane_step, 1), result)
        result = jnp.where(
            row - block == lane_step - 4, pltpu.roll(moved, 8 + lane_step - 4, 1), result
        )
    return result


def forward_kernel(index_ref, state_ref, z_ref, y_ref, out_ref, table_ref):
    span = state_ref.shape[1]
    table = y_ref[index_ref[0]]
    lane = lax.broadcasted_iota(jnp.int32, (span, table.shape[1]), 1)
    for x in range(2):
        for c in range(8):
            own = (lane % 8 == c) & (lane // 64 % 2 == x)
            for part in range(2):
                first = part * 16 * span + (c * 2 + x) * span
                block = jnp.where(own, table[part * span : (part + 1) * span], 0.0)
                table_ref[first : first + span] = block.astype(jnp.bfloat16)
    rows = state_ref.shape[0] * state_ref.shape[1]
    state = state_ref[...].reshape(rows, state_ref.shape[2])
    z_modes = lax.dot_general(
        z_ref[...].astype(jnp.bfloat16), state, (((1,), (1,)), ((), ())), preferred_element_type=jnp.float32
    ).astype(jnp.bfloat16)
    span = rows // 4
    pieces = [
        jnp.concatenate(
            [z_modes[:KZ, g * span : (g + 1) * span], z_modes[KZ:, g * span : (g + 1) * span]], axis=1
        )
        for g in range(4)
    ]
    stacked = jnp.concatenate(pieces, axis=0)
    modes = jnp.dot(stacked, table_ref[...], preferred_element_type=jnp.float32)
    for group in range(4):
        moved = block_moves(modes[:, group * 128 : (group + 1) * 128])
        for half in range(2):
            for pair in range(2):
                first = moved[half * 4 + pair]
                second = moved[half * 4 + 2 + pair]
                for side in range(2):
                    rows4 = slice(4 * side, 4 * side + 4)
                    chunk = jnp.concatenate([first[rows4], second[rows4]], axis=0)
                    out_ref[(half * 4 + group) * 4 + 2 * pair + side] = chunk.astype(jnp.bfloat16)


def forward_modes(index_y, state, z_table, y_table):
    return pl.pallas_call(
        forward_kernel,
        out_shape=jax.ShapeDtypeStruct((32, 8, 128), jnp.bfloat16),
        in_specs=[
            pl.BlockSpec(memory_space=pltpu.SMEM),
            pl.BlockSpec(memory_space=pltpu.VMEM),
            pl.BlockSpec(memory_space=pltpu.VMEM),
            pl.BlockSpec(memory_space=pltpu.VMEM),
        ],
        out_specs=pl.BlockSpec(memory_space=pltpu.VMEM),
        scratch_shapes=[pltpu.VMEM((32 * state.shape[1], y_table.shape[2]), jnp.bfloat16)],
        compiler_params=pltpu.CompilerParams(vmem_limit_bytes=40 * 2**20),
        cost_estimate=pl.CostEstimate(flops=2**27, bytes_accessed=2**21, transcendentals=0),
        name="forward_modes",
    )(index_y, state, z_table, y_table)


def prepare_kernel(weight_ref, conv_ref, weight_out, conv_out):
    for part in range(2):
        for kz in range(4):
            for c in range(16):
                weight_out[part, kz, c] = jnp.concatenate(
                    [weight_ref[part, kz, u, c] for u in range(4)], axis=1
                )
    zero = jnp.zeros((32, 32), jnp.float32)
    for dz in range(3):
        taps = {
            (dx, dy): conv_ref[dx, dy, dz].astype(jnp.float32)
            for dx in range(3)
            for dy in range(3)
        }
        for y_out in range(2):
            for x_out in range(2):
                row = ((dz * 2 + y_out) * 2 + x_out) * 32
                for y_in in range(4):
                    blocks = [taps.get((x_in - x_out, y_in - y_out), zero) for x_in in range(4)]
                    conv_out[row : row + 32, y_in * 128 : (y_in + 1) * 128] = jnp.concatenate(
                        blocks, axis=1
                    ).astype(jnp.bfloat16)


def prepare(spectral_weight, conv_weight):
    vmem = pl.BlockSpec(memory_space=pltpu.VMEM)
    return pl.pallas_call(
        prepare_kernel,
        out_shape=(
            jax.ShapeDtypeStruct((2, 4, 16, KX, 128), jnp.float32),
            jax.ShapeDtypeStruct((384, 512), jnp.bfloat16),
        ),
        in_specs=[vmem, vmem],
        out_specs=(vmem, vmem),
        compiler_params=pltpu.CompilerParams(vmem_limit_bytes=40 * 2**20),
        cost_estimate=pl.CostEstimate(flops=2**20, bytes_accessed=6 * 2**20, transcendentals=0),
        name="prepare_weights",
    )(spectral_weight, conv_weight)


def mix_kernel(modes_ref, forward_ref, weight_ref, inverse_ref, out_ref):
    received = modes_ref[...].astype(jnp.float32).reshape(256, 128).astype(jnp.bfloat16)
    x_modes = jnp.dot(
        forward_ref[...].astype(jnp.bfloat16), received, preferred_element_type=jnp.float32)
    lane = lax.broadcasted_iota(jnp.int32, (16, 128), 1)
    base = (lane // 32) * 8
    mixed = []
    for kz in range(4):
        real_sum = imag_sum = None
        for c in range(16):
            half, c8 = c // 8, c % 8
            index = base + (kz * 32 + c8)
            real_in = jnp.take_along_axis(x_modes[half * 32 : half * 32 + 16], index, axis=1)
            imag_in = jnp.take_along_axis(x_modes[half * 32 + 16 : half * 32 + 32], index, axis=1)
            real_weight = weight_ref[0, kz, c]
            imag_weight = weight_ref[1, kz, c]
            real_term = real_weight * real_in - imag_weight * imag_in
            imag_term = real_weight * imag_in + imag_weight * real_in
            real_sum = real_term if real_sum is None else real_sum + real_term
            imag_sum = imag_term if imag_sum is None else imag_sum + imag_term
        mixed += [real_sum, imag_sum]
    values = jnp.dot(
        inverse_ref[...],
        jnp.concatenate(mixed, axis=0),
        preferred_element_type=jnp.float32,
        precision=lax.Precision.HIGHEST,
    ).astype(jnp.bfloat16)
    for x in range(8):
        for y in range(4):
            out_ref[x * 4 + y] = values[16 * x : 16 * x + 16]


def mix_modes(modes, forward_table, weights, inverse_table):
    vmem = pl.BlockSpec(memory_space=pltpu.VMEM)
    return pl.pallas_call(
        mix_kernel,
        out_shape=jax.ShapeDtypeStruct((32, 16, 128), jnp.bfloat16),
        in_specs=[vmem] * 4,
        out_specs=vmem,
        compiler_params=pltpu.CompilerParams(vmem_limit_bytes=40 * 2**20),
        cost_estimate=pl.CostEstimate(flops=2**22, bytes_accessed=2**21, transcendentals=0),
        name="mix_modes",
    )(modes, forward_table, weights, inverse_table)


def arrange_kernel(left_ref, state_ref, right_ref, out_ref, first_ref, last_ref, wide):
    cells_y = state_ref.shape[2]
    planes = [left_ref[:, 0], state_ref[:, 0], state_ref[:, 1], right_ref[:, 0]]
    for x, plane in enumerate(planes):
        wide[x] = plane.astype(jnp.float32).reshape(32 * cells_y, 128)
    for y in range(cells_y):
        for x in range(4):
            rows = wide[x, pl.ds(y, 32, stride=cells_y), :].astype(jnp.bfloat16)
            out_ref[y, 32 * x : 32 * x + 32] = rows
            if y == 0:
                first_ref[32 * x : 32 * x + 32] = rows
            if y == cells_y - 1:
                last_ref[32 * x : 32 * x + 32] = rows


def arrange(left, state, right):
    vmem = pl.BlockSpec(memory_space=pltpu.VMEM)
    cells_y = state.shape[2]
    return pl.pallas_call(
        arrange_kernel,
        out_shape=(
            jax.ShapeDtypeStruct((cells_y, 128, 128), jnp.bfloat16),
            jax.ShapeDtypeStruct((128, 128), jnp.bfloat16),
            jax.ShapeDtypeStruct((128, 128), jnp.bfloat16),
        ),
        in_specs=[vmem] * 3,
        out_specs=(vmem,) * 3,
        scratch_shapes=[pltpu.VMEM((4, 32 * cells_y, 128), jnp.float32)],
        compiler_params=pltpu.CompilerParams(vmem_limit_bytes=40 * 2**20),
        cost_estimate=pl.CostEstimate(flops=2**20, bytes_accessed=2**21, transcendentals=0),
        name="arrange_cells",
    )(left, state, right)


def convolve_kernel(cells_ref, before_ref, after_ref, weight_ref, out_ref):
    cells_y = cells_ref.shape[0]
    lane = lax.broadcasted_iota(jnp.int32, (128, 256), 1) % 128
    weight = weight_ref[...]

    def row(y):
        if y < 0:
            return before_ref[...]
        return after_ref[...] if y >= cells_y else cells_ref[y]

    for quad in range(cells_y // 4):
        windows = []
        for pair in range(2):
            start = quad * 4 + pair * 2 - 1
            windows.append(jnp.concatenate([row(start + i) for i in range(4)], axis=0))
        product = jnp.dot(
            weight, jnp.concatenate(windows, axis=1), preferred_element_type=jnp.float32
        )
        below = pltpu.roll(product[:128], 1, 1)
        above = pltpu.roll(product[256:], 255, 1)
        total = product[128:256] + jnp.where(lane == 0, 0.0, below)
        total = total + jnp.where(lane == 127, 0.0, above)
        for pair in range(2):
            for y_out in range(2):
                for x_out in range(2):
                    first = (y_out * 2 + x_out) * 32
                    value = total[first : first + 32, pair * 128 : (pair + 1) * 128]
                    y = quad * 4 + pair * 2 + y_out
                    out_ref[pl.ds(x_out * cells_y + y, 32, stride=2 * cells_y), :] = value


def convolve(cells, before, after, weight):
    vmem = pl.BlockSpec(memory_space=pltpu.VMEM)
    cells_y = cells.shape[0]
    return pl.pallas_call(
        convolve_kernel,
        out_shape=jax.ShapeDtypeStruct((64 * cells_y, 128), jnp.float32),
        in_specs=[vmem] * 4,
        out_specs=vmem,
        compiler_params=pltpu.CompilerParams(vmem_limit_bytes=40 * 2**20),
        cost_estimate=pl.CostEstimate(flops=2**31, bytes_accessed=2**21, transcendentals=0),
        name="convolve_cells",
    )(cells, before, after, weight)


def gelu(value):
    return 0.5 * value * (1.0 + lax.erf(value * math.sqrt(0.5)))


def finish_kernel(index_ref, bias_ref, values_ref, z_ref, y_ref, conv_ref, out_ref):
    table = y_ref[index_ref[0]]
    lane = lax.broadcasted_iota(jnp.int32, table.shape, 1) % 16
    blocks = [jnp.where(lane == o, table, 0.0).astype(jnp.bfloat16) for o in range(16)]
    columns = []
    for group in range(4):
        columns.append(
            jnp.concatenate(
                [values_ref[(h * 4 + group) * 4 + q] for h in range(2) for q in range(4)], axis=0
            )
        )
    packed = jnp.concatenate(columns, axis=1)
    z_values = lax.dot_general(
        packed, z_ref[...].astype(jnp.bfloat16), (((0,), (0,)), ((), ())), preferred_element_type=jnp.float32
    ).astype(jnp.bfloat16)
    for half in range(2):
        sides = []
        for x in range(2):
            parts = []
            for part in range(2):
                lanes = slice((x * 2 + part) * 128, (x * 2 + part + 1) * 128)
                parts += [
                    z_values[ky * 32 + half * 16 : ky * 32 + half * 16 + 16, lanes]
                    for ky in range(KY)
                ]
            sides.append(jnp.concatenate(parts, axis=0))
        right = jnp.concatenate(sides, axis=1)
        for block in range(4):
            spectral = jnp.dot(
                jnp.concatenate(blocks[block * 4 : block * 4 + 4], axis=0),
                right,
                preferred_element_type=jnp.float32,
            )
            for o4 in range(4):
                o = half * 16 + block * 4 + o4
                for x in range(2):
                    total = (
                        spectral[o4 * 32 : o4 * 32 + 32, x * 128 : (x + 1) * 128]
                        + conv_ref[o, x]
                        + bias_ref[o]
                    )
                    out_ref[o, x] = gelu(total).astype(jnp.bfloat16)


def finish(index_y, bias, values, z_table, y_table, convolved):
    vmem = pl.BlockSpec(memory_space=pltpu.VMEM)
    return pl.pallas_call(
        finish_kernel,
        out_shape=jax.ShapeDtypeStruct(convolved.shape, jnp.bfloat16),
        in_specs=[
            pl.BlockSpec(memory_space=pltpu.SMEM),
            pl.BlockSpec(memory_space=pltpu.SMEM),
            vmem,
            vmem,
            vmem,
            vmem,
        ],
        out_specs=vmem,
        compiler_params=pltpu.CompilerParams(vmem_limit_bytes=40 * 2**20),
        cost_estimate=pl.CostEstimate(flops=2**28, bytes_accessed=2**22, transcendentals=2**18),
        name="finish_layer",
    )(index_y, bias, values, z_table, y_table, convolved)


def exchanged(value):
    return lax.all_to_all(value, ("px", "py"), split_axis=0, concat_axis=0, tiled=True)


def shifted(value, axis, step):
    count = lax.axis_size(axis)
    pairs = [(i, i + step) for i in range(count) if 0 <= i + step < count]
    return lax.ppermute(value, axis, pairs)


def body(state_field, conv_weight, conv_bias, spectral_weight):
    channels, cells_x, cells_y, depth = state_field.shape
    sizes = (lax.axis_size("px"), lax.axis_size("py"), cells_x, cells_y, depth)
    if sizes != (8, 4, 2, 32, 128):
        return general_body(state_field, conv_weight, conv_bias, spectral_weight)
    z_forward, y_forward, x_forward, x_inverse, z_inverse, y_inverse = tables(*sizes)
    index_y = lax.axis_index("py").reshape(1)
    sent = forward_modes(
        index_y, state_field.reshape(channels * cells_x, cells_y, depth), z_forward, y_forward
    )
    modes = exchanged(sent)
    left = shifted(state_field[:, cells_x - 1 :], "px", 1)
    right = shifted(state_field[:, :1], "px", -1)
    weights, taps = prepare(
        spectral_weight.swapaxes(4, 5), conv_weight.transpose(2, 3, 4, 0, 1)
    )
    cells, first, last = arrange(left, state_field, right)
    before = shifted(last, "py", 1)
    after = shifted(first, "py", -1)
    convolved = convolve(cells, before, after, taps)
    values = exchanged(mix_modes(modes, x_forward, weights, x_inverse))
    return finish(
        index_y,
        conv_bias,
        values,
        z_inverse,
        y_inverse,
        convolved.reshape(channels, cells_x, cells_y, depth),
    )


def solution(mesh):
    in_specs = (P(None, "px", "py", None), P(), P(), P(None, "py", "px", None, None, None))
    out_specs = P(None, "px", "py", None)
    return jax.shard_map(body, mesh=mesh, in_specs=in_specs, out_specs=out_specs, check_vma=False)
```

profile of v0, /device:TPU:1, one launch (start us, length us, event | category | flops | bytes accessed | tf_op | source)
XLA Modules:
  0.0 44.4 jit_solution(1872509550436473417)
XLA Ops:
  0.0 1.1 %fusion = (bf16[32,1,32,128]{3,2,1,0:T(8,128)(2,1)S(1)}, bf16[32,1,32,128]{3,2,1,0:T(8,128)(2,1)S(1)}) fusion(bf16[32,2,32,128]{3,2,1,0:T(8,128)(2,1)} %state_ref.1), kind=kLoop, calls=%fused_computation | loop fusion | bytes 1048576 | tf_op jit(solution)/shard_map/slice | solution.py:548
  1.2 4.0 %collective-permute-start = (bf16[32,1,32,128]{3,2,1,0:T(8,128)(2,1)S(1)}, bf16[32,1,32,128]{3,2,1,0:T(8,128)(2,1)S(1)}, u32[]{:S(2)}, u32[]{:S(2)}) collective-permute-start(bf16[32,1,32,128]{3,2,1,0:T(8,128)(2,1)S(1)} %get-tuple-element.16), channel_id=1, source_target_pairs={{0,4},{4,8},{8,12},{12,16},{16,20},{20,24},{24,28},{1,5},{5,9},{9,... | collective-permute-start | bytes 786440 | tf_op jit(solution)/shard_map/ppermute | solution.py:533
  5.1 1.3 %collective-permute-start.1 = (bf16[32,1,32,128]{3,2,1,0:T(8,128)(2,1)S(1)}, bf16[32,1,32,128]{3,2,1,0:T(8,128)(2,1)S(1)}, u32[]{:S(2)}, u32[]{:S(2)}) collective-permute-start(bf16[32,1,32,128]{3,2,1,0:T(8,128)(2,1)S(1)} %get-tuple-element.15), channel_id=1, source_target_pairs={{4,0},{8,4},{12,8},{16,12},{20,16},{24,20},{28,24},{5,1},{9,5},{13... | collective-permute-start | bytes 786440 | tf_op jit(solution)/shard_map/ppermute | solution.py:533
  6.4 0.0 copy-start
  6.4 1.0 %copy-done = bf16[32,2,32,128]{3,2,1,0:T(8,128)(2,1)S(1)} copy-done((bf16[32,2,32,128]{3,2,1,0:T(8,128)(2,1)S(1)}, bf16[32,2,32,128]{3,2,1,0:T(8,128)(2,1)}, u32[]{:S(2)}) %copy-start) | copy-done | bytes 524312
  7.5 1.0 %copy-done.3 = f32[4,64,512]{2,1,0:T(8,128)S(1)} copy-done((f32[4,64,512]{2,1,0:T(8,128)S(1)}, f32[4,64,512]{2,1,0:T(8,128)}, u32[]{:S(2)}) %copy-start.3) | copy-done | bytes 524312
  8.5 0.7 %copy-done.9 = f32[32,128]{1,0:T(8,128)S(1)} copy-done((f32[32,128]{1,0:T(8,128)S(1)}, f32[32,128]{1,0:T(8,128)}, u32[]{:S(2)}) %copy-start.9) | copy-done | bytes 16408
  9.2 1.3 %forward_modes.1 = bf16[32,8,128]{2,1,0:T(8,128)(2,1)} custom-call(s32[1]{0:T(128)} %bitcast.index_ref, bf16[64,32,128]{2,1,0:T(8,128)(2,1)S(1)} %bitcast.5, f32[32,128]{1,0:T(8,128)S(1)} %copy-done.9, f32[4,64,512]{2,1,0:T(8,128)S(1)} %copy-done.3), custom_call_target="tpu_custom_call" | custom-call | flops 134217728 | bytes 2097152 | tf_op jit(solution)/shard_map/forward_modes/pallas_call | solution.py:277
  10.5 7.7 %all-to-all-start = ((bf16[32,8,128]{2,1,0:T(8,128)(2,1)}), bf16[32,8,128]{2,1,0:T(8,128)(2,1)S(1)}, u32[]{:S(2)}, u32[]{:S(2)}) async-start(bf16[32,8,128]{2,1,0:T(8,128)(2,1)} %forward_modes.1), calls=%async_computation | async-start | bytes 131072 | tf_op jit(solution)/shard_map/all_to_all | solution.py:527
  18.2 0.0 copy-start.2
  18.2 2.2 %copy-done.2 = f32[2,4,4,16,32,16]{4,5,3,2,1,0:T(8,128)S(1)} copy-done((f32[2,4,4,16,32,16]{4,5,3,2,1,0:T(8,128)S(1)}, f32[2,4,4,16,32,16]{4,5,3,2,1,0:T(8,128)}, u32[]{:S(2)}) %copy-start.2) | copy-done | bytes 1048600
  20.4 0.9 %copy-done.6 = bf16[32,32,3,3,3]{1,0,4,3,2:T(8,128)(2,1)S(1)} copy-done((bf16[32,32,3,3,3]{1,0,4,3,2:T(8,128)(2,1)S(1)}, bf16[32,32,3,3,3]{1,0,4,3,2:T(8,128)(2,1)}, u32[]{:S(2)}) %copy-start.6) | copy-done | bytes 55320
  21.3 1.0 %prepare_weights.1 = (f32[2,4,16,16,128]{4,3,2,1,0:T(8,128)S(1)}, bf16[384,512]{1,0:T(8,128)(2,1)S(1)}) custom-call(f32[2,4,4,16,16,32]{5,4,3,2,1,0:T(8,128)S(1)} %bitcast.6, bf16[3,3,3,32,32]{4,3,2,1,0:T(8,128)(2,1)S(1)} %bitcast.8), custom_call_target="tpu_custom_call" | custom-call | flops 1048576 | bytes 6291456 | tf_op jit(solution)/shard_map/prepare_weights/pallas_call | solution.py:320
  22.3 3.2 %all-to-all-done.modes_ref = bf16[32,8,128]{2,1,0:T(8,128)(2,1)S(1)} async-done(((bf16[32,8,128]{2,1,0:T(8,128)(2,1)}), bf16[32,8,128]{2,1,0:T(8,128)(2,1)S(1)}, u32[]{:S(2)}, u32[]{:S(2)}) %all-to-all-start) | async-done | bytes 65568 | tf_op jit(solution)/shard_map/all_to_all | solution.py:527
  25.5 1.6 %mix_modes.1 = bf16[32,16,128]{2,1,0:T(8,128)(2,1)} custom-call(bf16[32,8,128]{2,1,0:T(8,128)(2,1)S(1)} %all-to-all-done.modes_ref, f32[64,256]{1,0:T(8,128)S(1)} %copy-done.7, f32[2,4,16,16,128]{4,3,2,1,0:T(8,128)S(1)} %get-tuple-element.10.weight_ref, f32[128,128]{1,0:T(8,128)S(1)} %copy-done.8), custom_call_target="tpu_custom_call" | custom-call | flops 4194304 | bytes 2097152 | tf_op jit(solution)/shard_map/mix_modes/pallas_call | solution.py:368
  27.1 2.7 %all-to-all-start.1 = ((bf16[32,16,128]{2,1,0:T(8,128)(2,1)}), bf16[32,16,128]{2,1,0:T(8,128)(2,1)S(1)}, u32[]{:S(2)}, u32[]{:S(2)}) async-start(bf16[32,16,128]{2,1,0:T(8,128)(2,1)} %mix_modes.1), calls=%async_computation.1 | async-start | bytes 262144 | tf_op jit(solution)/shard_map/all_to_all | solution.py:527
  29.8 1.7 %arrange_cells.1 = (bf16[32,128,128]{2,1,0:T(8,128)(2,1)S(1)}, bf16[128,128]{1,0:T(8,128)(2,1)S(1)}, bf16[128,128]{1,0:T(8,128)(2,1)S(1)}) custom-call(bf16[32,1,32,128]{3,2,1,0:T(8,128)(2,1)S(1)} %collective-permute-done.left_ref, bf16[32,2,32,128]{3,2,1,0:T(8,128)(2,1)S(1)} %copy-done.1, bf16[32,1,32,128]{3,2,1,0:T(8,128)(2,1)S(1)} %collective-permute-done.1.right_ref), custom_call_target="tpu_custom_call" | custom-call | flops 1048576 | bytes 2097152 | tf_op jit(solution)/shard_map/arrange_cells/pallas_call | solution.py:397
  31.6 0.0 copy-start.4
  31.6 0.0 copy-start.5
  31.6 3.7 %collective-permute-start.2 = (bf16[128,128]{1,0:T(8,128)(2,1)S(1)}, bf16[128,128]{1,0:T(8,128)(2,1)S(1)}, u32[]{:S(2)}, u32[]{:S(2)}) collective-permute-start(bf16[128,128]{1,0:T(8,128)(2,1)S(1)} %get-tuple-element.12), channel_id=1, source_target_pairs={{0,1},{1,2},{2,3},{4,5},{5,6},{6,7},{8,9},{9,10},{10,11},{12,13},{... | collective-permute-start | bytes 98312 | tf_op jit(solution)/shard_map/ppermute | solution.py:533
  35.3 1.9 %collective-permute-start.3 = (bf16[128,128]{1,0:T(8,128)(2,1)S(1)}, bf16[128,128]{1,0:T(8,128)(2,1)S(1)}, u32[]{:S(2)}, u32[]{:S(2)}) collective-permute-start(bf16[128,128]{1,0:T(8,128)(2,1)S(1)} %get-tuple-element.13), channel_id=1, source_target_pairs={{1,0},{2,1},{3,2},{5,4},{6,5},{7,6},{9,8},{10,9},{11,10},{13,12},{... | collective-permute-start | bytes 98312 | tf_op jit(solution)/shard_map/ppermute | solution.py:533
  37.2 3.3 %collective-permute-done.3.after_ref = bf16[128,128]{1,0:T(8,128)(2,1)S(1)} collective-permute-done((bf16[128,128]{1,0:T(8,128)(2,1)S(1)}, bf16[128,128]{1,0:T(8,128)(2,1)S(1)}, u32[]{:S(2)}, u32[]{:S(2)}) %collective-permute-start.3) | collective-permute-done | bytes 32800 | tf_op jit(solution)/shard_map/ppermute | solution.py:533
  40.5 1.7 %convolve_cells.1 = f32[2048,128]{1,0:T(8,128)S(1)} custom-call(bf16[32,128,128]{2,1,0:T(8,128)(2,1)S(1)} %get-tuple-element.11.cells_ref, bf16[128,128]{1,0:T(8,128)(2,1)S(1)} %collective-permute-done.2.before_ref, bf16[128,128]{1,0:T(8,128)(2,1)S(1)} %collective-permute-done.3.after_ref, bf16[384,512]{1,0:T(8,128)(2,1)S(1)} %get-tuple-element.14.weight_ref), custom_call_target="tpu_custom_call" | custom-call | flops 2147483648 | bytes 2097152 | tf_op jit(solution)/shard_map/convolve_cells/pallas_call | solution.py:447
  42.3 2.1 %finish_layer.1 = bf16[32,2,32,128]{3,2,1,0:T(8,128)(2,1)} custom-call(s32[1]{0:T(128)} %bitcast.index_ref, f32[32]{0:T(128)S(1)} %copy-done.10, bf16[32,16,128]{2,1,0:T(8,128)(2,1)S(1)} %all-to-all-done.1.values_ref, f32[128,512]{1,0:T(8,128)S(1)} %copy-done.4, f32[4,32,512]{2,1,0:T(8,128)S(1)} %copy-done.5, f32[32,2,32,128]{3,2,1,0:T(8,128)S(1)} %bitcast.7), custom_call_target="tpu_custom_call" | custom-call | flops 268435456 | bytes 4194304 | tf_op jit(solution)/shard_map/finish_layer/pallas_call | solution.py:508
  (17 shorter events, 0.0 us)
Async XLA Ops:
  0.0 25.5 %copy-start.7 = (f32[64,256]{1,0:T(8,128)S(1)}, f32[64,256]{1,0:T(8,128)}, u32[]{:S(2)}) copy-start(f32[64,256]{1,0:T(8,128)} %constant.18.clone.forward_ref) | copy-start | bytes 196612
  0.0 25.5 %copy-start.8 = (f32[128,128]{1,0:T(8,128)S(1)}, f32[128,128]{1,0:T(8,128)}, u32[]{:S(2)}) copy-start(f32[128,128]{1,0:T(8,128)} %constant.19.clone.inverse_ref) | copy-start | bytes 196612
  0.0 29.8 %copy-start.1 = (bf16[32,2,32,128]{3,2,1,0:T(8,128)(2,1)S(1)}, bf16[32,2,32,128]{3,2,1,0:T(8,128)(2,1)}, u32[]{:S(2)}) copy-start(bf16[32,2,32,128]{3,2,1,0:T(8,128)(2,1)} %state_ref.1) | copy-start | bytes 1572868
  1.2 28.7 %collective-permute-start = (bf16[32,1,32,128]{3,2,1,0:T(8,128)(2,1)S(1)}, bf16[32,1,32,128]{3,2,1,0:T(8,128)(2,1)S(1)}, u32[]{:S(2)}, u32[]{:S(2)}) collective-permute-start(bf16[32,1,32,128]{3,2,1,0:T(8,128)(2,1)S(1)} %get-tuple-element.16), channel_id=1, source_target_pairs={{0,4},{4,8},{8,12},{12,16},{16,20},{20,24},{24,28},{1,5},{5,9},{9,... | collective-permute-start | bytes 786440 | tf_op jit(solution)/shard_map/ppermute | solution.py:533
  5.1 24.7 %collective-permute-start.1 = (bf16[32,1,32,128]{3,2,1,0:T(8,128)(2,1)S(1)}, bf16[32,1,32,128]{3,2,1,0:T(8,128)(2,1)S(1)}, u32[]{:S(2)}, u32[]{:S(2)}) collective-permute-start(bf16[32,1,32,128]{3,2,1,0:T(8,128)(2,1)S(1)} %get-tuple-element.15), channel_id=1, source_target_pairs={{4,0},{8,4},{12,8},{16,12},{20,16},{24,20},{28,24},{5,1},{9,5},{13... | collective-permute-start | bytes 786440 | tf_op jit(solution)/shard_map/ppermute | solution.py:533
  6.4 1.0 %copy-start = (bf16[32,2,32,128]{3,2,1,0:T(8,128)(2,1)S(1)}, bf16[32,2,32,128]{3,2,1,0:T(8,128)(2,1)}, u32[]{:S(2)}) copy-start(bf16[32,2,32,128]{3,2,1,0:T(8,128)(2,1)} %state_ref.1) | copy-start | bytes 1572868
  7.5 1.0 %copy-start.3 = (f32[4,64,512]{2,1,0:T(8,128)S(1)}, f32[4,64,512]{2,1,0:T(8,128)}, u32[]{:S(2)}) copy-start(f32[4,64,512]{2,1,0:T(8,128)} %constant.17.clone.y_ref) | copy-start | bytes 1572868
  8.5 0.7 %copy-start.9 = (f32[32,128]{1,0:T(8,128)S(1)}, f32[32,128]{1,0:T(8,128)}, u32[]{:S(2)}) copy-start(f32[32,128]{1,0:T(8,128)} %constant.16.clone.z_ref) | copy-start | bytes 49156
  10.5 15.0 %all-to-all-start = ((bf16[32,8,128]{2,1,0:T(8,128)(2,1)}), bf16[32,8,128]{2,1,0:T(8,128)(2,1)S(1)}, u32[]{:S(2)}, u32[]{:S(2)}) async-start(bf16[32,8,128]{2,1,0:T(8,128)(2,1)} %forward_modes.1), calls=%async_computation | async-start | bytes 131072 | tf_op jit(solution)/shard_map/all_to_all | solution.py:527
  18.2 2.2 %copy-start.2 = (f32[2,4,4,16,32,16]{4,5,3,2,1,0:T(8,128)S(1)}, f32[2,4,4,16,32,16]{4,5,3,2,1,0:T(8,128)}, u32[]{:S(2)}) copy-start(f32[2,4,4,16,32,16]{4,5,3,2,1,0:T(8,128)} %param.13) | copy-start | bytes 3145732
  20.4 0.9 %copy-start.6 = (bf16[32,32,3,3,3]{1,0,4,3,2:T(8,128)(2,1)S(1)}, bf16[32,32,3,3,3]{1,0,4,3,2:T(8,128)(2,1)}, u32[]{:S(2)}) copy-start(bf16[32,32,3,3,3]{1,0,4,3,2:T(8,128)(2,1)} %param.11) | copy-start | bytes 165892
  27.1 15.1 %all-to-all-start.1 = ((bf16[32,16,128]{2,1,0:T(8,128)(2,1)}), bf16[32,16,128]{2,1,0:T(8,128)(2,1)S(1)}, u32[]{:S(2)}, u32[]{:S(2)}) async-start(bf16[32,16,128]{2,1,0:T(8,128)(2,1)} %mix_modes.1), calls=%async_computation.1 | async-start | bytes 262144 | tf_op jit(solution)/shard_map/all_to_all | solution.py:527
  31.6 10.7 %copy-start.4 = (f32[128,512]{1,0:T(8,128)S(1)}, f32[128,512]{1,0:T(8,128)}, u32[]{:S(2)}) copy-start(f32[128,512]{1,0:T(8,128)} %constant.20.clone.z_ref) | copy-start | bytes 786436
  31.6 10.7 %copy-start.5 = (f32[4,32,512]{2,1,0:T(8,128)S(1)}, f32[4,32,512]{2,1,0:T(8,128)}, u32[]{:S(2)}) copy-start(f32[4,32,512]{2,1,0:T(8,128)} %constant.21.clone.y_ref) | copy-start | bytes 786436
  31.6 10.7 %copy-start.10 = (f32[32]{0:T(128)S(1)}, f32[32]{0:T(128)}, u32[]{:S(2)}) copy-start(f32[32]{0:T(128)} %bias_ref.1) | copy-start | bytes 388
  31.6 5.6 %collective-permute-start.2 = (bf16[128,128]{1,0:T(8,128)(2,1)S(1)}, bf16[128,128]{1,0:T(8,128)(2,1)S(1)}, u32[]{:S(2)}, u32[]{:S(2)}) collective-permute-start(bf16[128,128]{1,0:T(8,128)(2,1)S(1)} %get-tuple-element.12), channel_id=1, source_target_pairs={{0,1},{1,2},{2,3},{4,5},{5,6},{6,7},{8,9},{9,10},{10,11},{12,13},{... | collective-permute-start | bytes 98312 | tf_op jit(solution)/shard_map/ppermute | solution.py:533
  35.3 5.2 %collective-permute-start.3 = (bf16[128,128]{1,0:T(8,128)(2,1)S(1)}, bf16[128,128]{1,0:T(8,128)(2,1)S(1)}, u32[]{:S(2)}, u32[]{:S(2)}) collective-permute-start(bf16[128,128]{1,0:T(8,128)(2,1)S(1)} %get-tuple-element.13), channel_id=1, source_target_pairs={{1,0},{2,1},{3,2},{5,4},{6,5},{7,6},{9,8},{10,9},{11,10},{13,12},{... | collective-permute-start | bytes 98312 | tf_op jit(solution)/shard_map/ppermute | solution.py:533
where the time goes:
time: 44.9 us; the launch traced here: 44.4 us
  starting transfers between devices  21.2 us (47%)
  Pallas kernels  9.39 us (21%)
  local copies, waits for them, and re-layouts  7.08 us (16%)
  waiting for transfers between devices  6.47 us (14%)
    ppermute x4, starting transfers between devices, shifted(): return lax.ppermute(value, axis, pairs)  10.8 us
    all_to_all x2, starting transfers between devices, exchanged(): lax.all_to_all(value, ('px', 'py'), split_axis=0, concat_axis=0, tiled=True)  10.4 us
    unnamed x22, local copies, waits for them, and re-layouts  5.94 us
    ppermute x4, waiting for transfers between devices, shifted(): return lax.ppermute(value, axis, pairs)  3.3 us
    all_to_all x2, waiting for transfers between devices, exchanged(): lax.all_to_all(value, ('px', 'py'), split_axis=0, concat_axis=0, tiled=True)  3.17 us
    pallas_call x1, Pallas kernels, finish(): pl.pallas_call(finish_kernel, out_shape=jax.ShapeDtypeStruct(convolved.sh...  2.1 us
    pallas_call x1, Pallas kernels, arrange(): pl.pallas_call(arrange_kernel, out_shape=(jax.ShapeDtypeStruct((cells_y,...  1.73 us
    pallas_call x1, Pallas kernels, convolve(): pl.pallas_call(convolve_kernel, out_shape=jax.ShapeDtypeStruct((64 * cell...  1.71 us
  transfers between devices with their start and end apart: 6, of which 2 were waited for; matrix products, arithmetic and copies ran while one was open for 0% of the time, Pallas kernels for 16%

commit v1 on v0

--- a/solution.py
+++ b/solution.py
@@ -236,9 +236,23 @@
     return result
 
 
-def forward_kernel(index_ref, state_ref, z_ref, y_ref, out_ref, table_ref):
+def forward_kernel(state_hbm, z_hbm, y_hbm, out_ref, state_ref, z_ref, y_ref, table_ref, sems):
+    count = state_ref.shape[0] // 4
     span = state_ref.shape[1]
-    table = y_ref[index_ref[0]]
+    y_copy = pltpu.make_async_copy(y_hbm.at[lax.axis_index("py")], y_ref, sems.at[0])
+    z_copy = pltpu.make_async_copy(z_hbm, z_ref, sems.at[1])
+    copies = [
+        pltpu.make_async_copy(
+            state_hbm.at[pl.ds(g * count, count)],
+            state_ref.at[pl.ds(g * count, count)],
+            sems.at[2 + g],
+        )
+        for g in range(4)
+    ]
+    for copy in [y_copy, z_copy] + copies:
+        copy.start()
+    y_copy.wait()
+    table = y_ref[...]
     lane = lax.broadcasted_iota(jnp.int32, (span, table.shape[1]), 1)
     for x in range(2):
         for c in range(8):
@@ -247,18 +261,16 @@
                 first = part * 16 * span + (c * 2 + x) * span
                 block = jnp.where(own, table[part * span : (part + 1) * span], 0.0)
                 table_ref[first : first + span] = block.astype(jnp.bfloat16)
-    rows = state_ref.shape[0] * state_ref.shape[1]
-    state = state_ref[...].reshape(rows, state_ref.shape[2])
-    z_modes = lax.dot_general(
-        z_ref[...].astype(jnp.bfloat16), state, (((1,), (1,)), ((), ())), preferred_element_type=jnp.float32
-    ).astype(jnp.bfloat16)
-    span = rows // 4
-    pieces = [
-        jnp.concatenate(
-            [z_modes[:KZ, g * span : (g + 1) * span], z_modes[KZ:, g * span : (g + 1) * span]], axis=1
-        )
-        for g in range(4)
-    ]
+    z_copy.wait()
+    z_table = z_ref[...].astype(jnp.bfloat16)
+    pieces = []
+    for g in range(4):
+        copies[g].wait()
+        cells = state_ref[g * count : (g + 1) * count].reshape(count * span, state_ref.shape[2])
+        z_modes = lax.dot_general(
+            z_table, cells, (((1,), (1,)), ((), ())), preferred_element_type=jnp.float32
+        ).astype(jnp.bfloat16)
+        pieces.append(jnp.concatenate([z_modes[:KZ], z_modes[KZ:]], axis=1))
     stacked = jnp.concatenate(pieces, axis=0)
     modes = jnp.dot(stacked, table_ref[...], preferred_element_type=jnp.float32)
     for group in range(4):
@@ -273,31 +285,38 @@
                     out_ref[(half * 4 + group) * 4 + 2 * pair + side] = chunk.astype(jnp.bfloat16)
 
 
-def forward_modes(index_y, state, z_table, y_table):
+def forward_modes(state, z_table, y_table):
     return pl.pallas_call(
         forward_kernel,
         out_shape=jax.ShapeDtypeStruct((32, 8, 128), jnp.bfloat16),
-        in_specs=[
-            pl.BlockSpec(memory_space=pltpu.SMEM),
-            pl.BlockSpec(memory_space=pltpu.VMEM),
-            pl.BlockSpec(memory_space=pltpu.VMEM),
-            pl.BlockSpec(memory_space=pltpu.VMEM),
+        in_specs=[pl.BlockSpec(memory_space=pltpu.HBM)] * 3,
+        out_specs=pl.BlockSpec(memory_space=pltpu.VMEM),
+        scratch_shapes=[
+            pltpu.VMEM(state.shape, jnp.bfloat16),
+            pltpu.VMEM(z_table.shape, jnp.float32),
+            pltpu.VMEM(y_table.shape[1:], jnp.float32),
+            pltpu.VMEM((32 * state.shape[1], y_table.shape[2]), jnp.bfloat16),
+            pltpu.SemaphoreType.DMA((6,)),
         ],
-        out_specs=pl.BlockSpec(memory_space=pltpu.VMEM),
-        scratch_shapes=[pltpu.VMEM((32 * state.shape[1], y_table.shape[2]), jnp.bfloat16)],
         compiler_params=pltpu.CompilerParams(vmem_limit_bytes=40 * 2**20),
         cost_estimate=pl.CostEstimate(flops=2**27, bytes_accessed=2**21, transcendentals=0),
         name="forward_modes",
-    )(index_y, state, z_table, y_table)
-
-
-def prepare_kernel(weight_ref, conv_ref, weight_out, conv_out):
-    for part in range(2):
-        for kz in range(4):
-            for c in range(16):
-                weight_out[part, kz, c] = jnp.concatenate(
-                    [weight_ref[part, kz, u, c] for u in range(4)], axis=1
-                )
+    )(*(pltpu.with_memory_space_constraint(v, pltpu.HBM) for v in (state, z_table, y_table)))
+
+
+def prepare_kernel(
+    after_ref, weight_hbm, conv_ref, y_ref, weight_out, conv_out, y_out, weight_ref, sems
+):
+    copies = [
+        pltpu.make_async_copy(
+            weight_hbm.at[part, kz], weight_ref.at[part, kz], sems.at[part * 4 + kz]
+        )
+        for part in range(2)
+        for kz in range(4)
+    ]
+    for copy in copies:
+        copy.start()
+    odd_x = lax.rem(lax.axis_index("px"), 2) == 1
     zero = jnp.zeros((32, 32), jnp.float32)
     for dz in range(3):
         taps = {
@@ -305,30 +324,60 @@
             for dx in range(3)
             for dy in range(3)
         }
-        for y_out in range(2):
-            for x_out in range(2):
-                row = ((dz * 2 + y_out) * 2 + x_out) * 32
+        for y_at in range(2):
+            for x_at in range(2):
+                row = ((dz * 2 + y_at) * 2 + x_at) * 32
                 for y_in in range(4):
-                    blocks = [taps.get((x_in - x_out, y_in - y_out), zero) for x_in in range(4)]
+                    low, *inner, high = [
+                        taps.get((x_in - x_at, y_in - y_at), zero) for x_in in range(4)
+                    ]
+                    blocks = [jnp.where(odd_x, low, high)] + inner + [jnp.where(odd_x, high, low)]
                     conv_out[row : row + 32, y_in * 128 : (y_in + 1) * 128] = jnp.concatenate(
                         blocks, axis=1
                     ).astype(jnp.bfloat16)
-
-
-def prepare(spectral_weight, conv_weight):
+    table = y_ref[lax.axis_index("py")]
+    lane = lax.broadcasted_iota(jnp.int32, table.shape, 1) % 16
+    span = table.shape[0]
+    for o in range(16):
+        y_out[o * span : (o + 1) * span] = jnp.where(lane == o, table, 0.0).astype(jnp.bfloat16)
+    for part in range(2):
+        for kz in range(4):
+            copies[part * 4 + kz].wait()
+            for c in range(16):
+                weight_out[part, kz, c] = jnp.concatenate(
+                    [weight_ref[part, kz, u, c] for u in range(4)], axis=1
+                )
+
+
+def prepare(after, spectral_weight, conv_weight, y_table):
     vmem = pl.BlockSpec(memory_space=pltpu.VMEM)
     return pl.pallas_call(
         prepare_kernel,
         out_shape=(
             jax.ShapeDtypeStruct((2, 4, 16, KX, 128), jnp.float32),
             jax.ShapeDtypeStruct((384, 512), jnp.bfloat16),
+            jax.ShapeDtypeStruct((16 * y_table.shape[1], y_table.shape[2]), jnp.bfloat16),
         ),
-        in_specs=[vmem, vmem],
-        out_specs=(vmem, vmem),
+        in_specs=[
+            pl.BlockSpec(memory_space=pl.ANY),
+            pl.BlockSpec(memory_space=pltpu.HBM),
+            vmem,
+            vmem,
+        ],
+        out_specs=(vmem,) * 3,
+        scratch_shapes=[
+            pltpu.VMEM(spectral_weight.shape, jnp.float32),
+            pltpu.SemaphoreType.DMA((8,)),
+        ],
         compiler_params=pltpu.CompilerParams(vmem_limit_bytes=40 * 2**20),
         cost_estimate=pl.CostEstimate(flops=2**20, bytes_accessed=6 * 2**20, transcendentals=0),
         name="prepare_weights",
-    )(spectral_weight, conv_weight)
+    )(
+        after,
+        pltpu.with_memory_space_constraint(spectral_weight, pltpu.HBM),
+        conv_weight,
+        y_table,
+    )
 
 
 def mix_kernel(modes_ref, forward_ref, weight_ref, inverse_ref, out_ref):
@@ -376,93 +425,101 @@
     )(modes, forward_table, weights, inverse_table)
 
 
-def arrange_kernel(left_ref, state_ref, right_ref, out_ref, first_ref, last_ref, wide):
+def arrange_kernel(after_ref, state_ref, own_ref, wide):
     cells_y = state_ref.shape[2]
-    planes = [left_ref[:, 0], state_ref[:, 0], state_ref[:, 1], right_ref[:, 0]]
-    for x, plane in enumerate(planes):
-        wide[x] = plane.astype(jnp.float32).reshape(32 * cells_y, 128)
+    for x in range(2):
+        wide[x] = state_ref[:, x].astype(jnp.float32).reshape(32 * cells_y, 128)
     for y in range(cells_y):
-        for x in range(4):
-            rows = wide[x, pl.ds(y, 32, stride=cells_y), :].astype(jnp.bfloat16)
-            out_ref[y, 32 * x : 32 * x + 32] = rows
-            if y == 0:
-                first_ref[32 * x : 32 * x + 32] = rows
-            if y == cells_y - 1:
-                last_ref[32 * x : 32 * x + 32] = rows
-
-
-def arrange(left, state, right):
+        for x in range(2):
+            own_ref[x, y] = wide[x, pl.ds(y, 32, stride=cells_y), :].astype(jnp.bfloat16)
+
+
+def arrange(after, state):
     vmem = pl.BlockSpec(memory_space=pltpu.VMEM)
     cells_y = state.shape[2]
     return pl.pallas_call(
         arrange_kernel,
-        out_shape=(
-            jax.ShapeDtypeStruct((cells_y, 128, 128), jnp.bfloat16),
-            jax.ShapeDtypeStruct((128, 128), jnp.bfloat16),
-            jax.ShapeDtypeStruct((128, 128), jnp.bfloat16),
-        ),
-        in_specs=[vmem] * 3,
-        out_specs=(vmem,) * 3,
-        scratch_shapes=[pltpu.VMEM((4, 32 * cells_y, 128), jnp.float32)],
+        out_shape=jax.ShapeDtypeStruct((2, cells_y, 32, 128), jnp.bfloat16),
+        in_specs=[pl.BlockSpec(memory_space=pl.ANY), vmem],
+        out_specs=vmem,
+        scratch_shapes=[pltpu.VMEM((2, 32 * cells_y, 128), jnp.float32)],
         compiler_params=pltpu.CompilerParams(vmem_limit_bytes=40 * 2**20),
         cost_estimate=pl.CostEstimate(flops=2**20, bytes_accessed=2**21, transcendentals=0),
         name="arrange_cells",
-    )(left, state, right)
-
-
-def convolve_kernel(cells_ref, before_ref, after_ref, weight_ref, out_ref):
-    cells_y = cells_ref.shape[0]
+    )(after, state)
+
+
+def convolve_quad(quad, row, weight, place, out_ref):
     lane = lax.broadcasted_iota(jnp.int32, (128, 256), 1) % 128
+    windows = []
+    for pair in range(2):
+        start = quad * 4 + pair * 2 - 1
+        windows.append(jnp.concatenate([row(start + i) for i in range(4)], axis=0))
+    product = jnp.dot(weight, jnp.concatenate(windows, axis=1), preferred_element_type=jnp.float32)
+    below = pltpu.roll(product[:128], 1, 1)
+    above = pltpu.roll(product[256:], 255, 1)
+    total = product[128:256] + jnp.where(lane == 0, 0.0, below)
+    total = total + jnp.where(lane == 127, 0.0, above)
+    for pair in range(2):
+        for y_out in range(2):
+            for x_out in range(2):
+                first = (y_out * 2 + x_out) * 32
+                value = total[first : first + 32, pair * 128 : (pair + 1) * 128]
+                y = quad * 4 + pair * 2 + y_out
+                at, span = place(y)
+                out_ref[pl.ds(x_out * span + at, 32, stride=2 * span), :] = value
+
+
+def interior_kernel(own_ref, first_ref, second_ref, weight_ref, out_ref):
+    cells_y = own_ref.shape[1]
+
+    def row(y):
+        return jnp.concatenate([first_ref[y], own_ref[0, y], own_ref[1, y], second_ref[y]], axis=0)
+
     weight = weight_ref[...]
+    for quad in range(1, cells_y // 4 - 1):
+        convolve_quad(quad, row, weight, lambda y: (y, cells_y), out_ref)
+
+
+def edge_kernel(
+    own_ref, first_ref, second_ref, first_row, second_row, weight_ref, out_ref
+):
+    cells_y = own_ref.shape[1]
+    odd_y = lax.rem(lax.axis_index("py"), 2) == 1
 
     def row(y):
         if y < 0:
-            return before_ref[...]
-        return after_ref[...] if y >= cells_y else cells_ref[y]
-
-    for quad in range(cells_y // 4):
-        windows = []
-        for pair in range(2):
-            start = quad * 4 + pair * 2 - 1
-            windows.append(jnp.concatenate([row(start + i) for i in range(4)], axis=0))
-        product = jnp.dot(
-            weight, jnp.concatenate(windows, axis=1), preferred_element_type=jnp.float32
-        )
-        below = pltpu.roll(product[:128], 1, 1)
-        above = pltpu.roll(product[256:], 255, 1)
-        total = product[128:256] + jnp.where(lane == 0, 0.0, below)
-        total = total + jnp.where(lane == 127, 0.0, above)
-        for pair in range(2):
-            for y_out in range(2):
-                for x_out in range(2):
-                    first = (y_out * 2 + x_out) * 32
-                    value = total[first : first + 32, pair * 128 : (pair + 1) * 128]
-                    y = quad * 4 + pair * 2 + y_out
-                    out_ref[pl.ds(x_out * cells_y + y, 32, stride=2 * cells_y), :] = value
-
-
-def convolve(cells, before, after, weight):
+            return jnp.where(odd_y, first_row[...], second_row[...])
+        if y >= cells_y:
+            return jnp.where(odd_y, second_row[...], first_row[...])
+        return jnp.concatenate([first_ref[y], own_ref[0, y], own_ref[1, y], second_ref[y]], axis=0)
+
+    weight = weight_ref[...]
+    for quad in (0, cells_y // 4 - 1):
+        convolve_quad(quad, row, weight, lambda y: (y % 8, 8), out_ref)
+
+
+def convolve(kernel, name, operands, rows):
     vmem = pl.BlockSpec(memory_space=pltpu.VMEM)
-    cells_y = cells.shape[0]
     return pl.pallas_call(
-        convolve_kernel,
-        out_shape=jax.ShapeDtypeStruct((64 * cells_y, 128), jnp.float32),
-        in_specs=[vmem] * 4,
+        kernel,
+        out_shape=jax.ShapeDtypeStruct((rows, 128), jnp.float32),
+        in_specs=[vmem] * len(operands),
         out_specs=vmem,
         compiler_params=pltpu.CompilerParams(vmem_limit_bytes=40 * 2**20),
-        cost_estimate=pl.CostEstimate(flops=2**31, bytes_accessed=2**21, transcendentals=0),
-        name="convolve_cells",
-    )(cells, before, after, weight)
+        cost_estimate=pl.CostEstimate(flops=2**30, bytes_accessed=2**21, transcendentals=0),
+        name=name,
+    )(*operands)
 
 
 def gelu(value):
     return 0.5 * value * (1.0 + lax.erf(value * math.sqrt(0.5)))
 
 
-def finish_kernel(index_ref, bias_ref, values_ref, z_ref, y_ref, conv_ref, out_ref):
-    table = y_ref[index_ref[0]]
-    lane = lax.broadcasted_iota(jnp.int32, table.shape, 1) % 16
-    blocks = [jnp.where(lane == o, table, 0.0).astype(jnp.bfloat16) for o in range(16)]
+def finish_kernel(
+    bias_ref, values_ref, z_ref, y_ref, conv_ref, edge_ref, out_hbm, out_ref, sems
+):
+    upper = lax.broadcasted_iota(jnp.int32, (8, 128), 0) < 4
     columns = []
     for group in range(4):
         columns.append(
@@ -472,8 +529,12 @@
         )
     packed = jnp.concatenate(columns, axis=1)
     z_values = lax.dot_general(
-        packed, z_ref[...].astype(jnp.bfloat16), (((0,), (0,)), ((), ())), preferred_element_type=jnp.float32
+        packed,
+        z_ref[...].astype(jnp.bfloat16),
+        (((0,), (0,)), ((), ())),
+        preferred_element_type=jnp.float32,
     ).astype(jnp.bfloat16)
+    copies = []
     for half in range(2):
         sides = []
         for x in range(2):
@@ -488,49 +549,59 @@
         right = jnp.concatenate(sides, axis=1)
         for block in range(4):
             spectral = jnp.dot(
-                jnp.concatenate(blocks[block * 4 : block * 4 + 4], axis=0),
-                right,
-                preferred_element_type=jnp.float32,
+                y_ref[block * 128 : (block + 1) * 128], right, preferred_element_type=jnp.float32
             )
             for o4 in range(4):
                 o = half * 16 + block * 4 + o4
                 for x in range(2):
-                    total = (
-                        spectral[o4 * 32 : o4 * 32 + 32, x * 128 : (x + 1) * 128]
-                        + conv_ref[o, x]
-                        + bias_ref[o]
+                    inner, edge = conv_ref[o, x], edge_ref[o, x]
+                    convolved = jnp.concatenate(
+                        [
+                            jnp.where(upper, edge, inner[:8]),
+                            inner[8:-8],
+                            jnp.where(upper, inner[-8:], edge),
+                        ],
+                        axis=0,
                     )
+                    total = spectral[o4 * 32 : o4 * 32 + 32, x * 128 : (x + 1) * 128]
+                    total = total + convolved + bias_ref[o]
                     out_ref[o, x] = gelu(total).astype(jnp.bfloat16)
-
-
-def finish(index_y, bias, values, z_table, y_table, convolved):
+            number = half * 4 + block
+            copy = pltpu.make_async_copy(
+                out_ref.at[pl.ds(number * 4, 4)], out_hbm.at[pl.ds(number * 4, 4)], sems.at[number]
+            )
+            copy.start()
+            copies.append(copy)
+    for copy in copies:
+        copy.wait()
+
+
+def finish(bias, values, z_table, y_table, convolved, edges):
     vmem = pl.BlockSpec(memory_space=pltpu.VMEM)
     return pl.pallas_call(
         finish_kernel,
         out_shape=jax.ShapeDtypeStruct(convolved.shape, jnp.bfloat16),
-        in_specs=[
-            pl.BlockSpec(memory_space=pltpu.SMEM),
-            pl.BlockSpec(memory_space=pltpu.SMEM),
-            vmem,
-            vmem,
-            vmem,
-            vmem,
+        in_specs=[pl.BlockSpec(memory_space=pltpu.SMEM)] + [vmem] * 5,
+        out_specs=pl.BlockSpec(memory_space=pltpu.HBM),
+        scratch_shapes=[
+            pltpu.VMEM(convolved.shape, jnp.bfloat16),
+            pltpu.SemaphoreType.DMA((8,)),
         ],
-        out_specs=vmem,
         compiler_params=pltpu.CompilerParams(vmem_limit_bytes=40 * 2**20),
         cost_estimate=pl.CostEstimate(flops=2**28, bytes_accessed=2**22, transcendentals=2**18),
         name="finish_layer",
-    )(index_y, bias, values, z_table, y_table, convolved)
+    )(bias, values, z_table, y_table, convolved, edges)
 
 
 def exchanged(value):
     return lax.all_to_all(value, ("px", "py"), split_axis=0, concat_axis=0, tiled=True)
 
 
-def shifted(value, axis, step):
+def swaps(first, second, axis):
     count = lax.axis_size(axis)
-    pairs = [(i, i + step) for i in range(count) if 0 <= i + step < count]
-    return lax.ppermute(value, axis, pairs)
+    inside = [(i, i ^ 1) for i in range(count)]
+    across = [(i, i + 1 if i % 2 else i - 1) for i in range(1, count - 1)]
+    return lax.ppermute(first, axis, inside), lax.ppermute(second, axis, across)
 
 
 def body(state_field, conv_weight, conv_bias, spectral_weight):
@@ -539,28 +610,43 @@
     if sizes != (8, 4, 2, 32, 128):
         return general_body(state_field, conv_weight, conv_bias, spectral_weight)
     z_forward, y_forward, x_forward, x_inverse, z_inverse, y_inverse = tables(*sizes)
-    index_y = lax.axis_index("py").reshape(1)
     sent = forward_modes(
-        index_y, state_field.reshape(channels * cells_x, cells_y, depth), z_forward, y_forward
+        state_field.reshape(channels * cells_x, cells_y, depth), z_forward, y_forward
     )
     modes = exchanged(sent)
-    left = shifted(state_field[:, cells_x - 1 :], "px", 1)
-    right = shifted(state_field[:, :1], "px", -1)
-    weights, taps = prepare(
-        spectral_weight.swapaxes(4, 5), conv_weight.transpose(2, 3, 4, 0, 1)
-    )
-    cells, first, last = arrange(left, state_field, right)
-    before = shifted(last, "py", 1)
-    after = shifted(first, "py", -1)
-    convolved = convolve(cells, before, after, taps)
+    own = arrange(sent, state_field)
+    odd_x = lax.axis_index("px") % 2
+    odd_y = lax.axis_index("py") % 2
+    first_plane, second_plane = swaps(
+        lax.dynamic_index_in_dim(own, 1 - odd_x, 0, keepdims=False),
+        lax.dynamic_index_in_dim(own, odd_x, 0, keepdims=False),
+        "px",
+    )
+    weights, taps, y_expanded = prepare(
+        sent, spectral_weight.swapaxes(4, 5), conv_weight.transpose(2, 3, 4, 0, 1), y_inverse
+    )
     values = exchanged(mix_modes(modes, x_forward, weights, x_inverse))
+
+    def edge(y):
+        pieces = [first_plane, own[0], own[1], second_plane]
+        return jnp.concatenate([lax.dynamic_index_in_dim(p, y, 0, keepdims=False) for p in pieces])
+
+    first_row, second_row = swaps(
+        edge((1 - odd_y) * (cells_y - 1)), edge(odd_y * (cells_y - 1)), "py"
+    )
+    planes = (own, first_plane, second_plane)
+    rows = channels * cells_x * cells_y
+    interior = convolve(interior_kernel, "convolve_interior", planes + (taps,), rows)
+    edges = convolve(
+        edge_kernel, "convolve_edges", planes + (first_row, second_row, taps), rows // cells_y * 8
+    )
     return finish(
-        index_y,
         conv_bias,
         values,
         z_inverse,
-        y_inverse,
-        convolved.reshape(channels, cells_x, cells_y, depth),
+        y_expanded,
+        interior.reshape(channels, cells_x, cells_y, depth),
+        edges.reshape(channels, cells_x, 8, depth),
     )
 
 

time: 44.9 us -> 41.4 us (0.922)
  the two profiles are of different devices: /device:TPU:1 before, /device:TPU:0 now
where the time goes in v1:
time: 41.4 us; the launch traced here: 41 us
  starting transfers between devices  17.3 us (42%)
  Pallas kernels  11.3 us (27%)
  waiting for transfers between devices  7.71 us (19%)
  local copies, waits for them, and re-layouts  4.56 us (11%)
    all_to_all x2, starting transfers between devices, exchanged(): lax.all_to_all(value, ('px', 'py'), split_axis=0, concat_axis=0, tiled=True)  9.86 us
    all_to_all x2, waiting for transfers between devices, exchanged(): lax.all_to_all(value, ('px', 'py'), split_axis=0, concat_axis=0, tiled=True)  7.7 us
    ppermute x2, starting transfers between devices, swaps(): lax.ppermute(first, axis, inside)  6.1 us
    unnamed x18, local copies, waits for them, and re-layouts  2.79 us
    pallas_call x1, Pallas kernels, forward_modes(): pl.pallas_call(forward_kernel, out_shape=jax.ShapeDtypeStruct((32, 8, 128...  2.68 us
    pallas_call x1, Pallas kernels, prepare(): pl.pallas_call(prepare_kernel, out_shape=(jax.ShapeDtypeStruct((2, 4, 16,...  2.47 us
    pallas_call x1, Pallas kernels, finish(): pl.pallas_call(finish_kernel, out_shape=jax.ShapeDtypeStruct(convolved.sh...  2.03 us
    pallas_call x2, Pallas kernels, convolve(): pl.pallas_call(kernel, out_shape=jax.ShapeDtypeStruct((rows, 128), jnp.fl...  1.83 us
  transfers between devices with their start and end apart: 6, of which 2 were waited for; matrix products, arithmetic and copies ran while one was open for 2% of the time, Pallas kernels for 14%

profile of v1, /device:TPU:0, one launch (start us, length us, event | category | flops | bytes accessed | tf_op | source)
XLA Modules:
  0.0 41.0 jit_solution(16391882552109675236)
XLA Ops:
  0.0 2.7 %forward_modes.1.after_ref = bf16[32,8,128]{2,1,0:T(8,128)(2,1)} custom-call(bf16[64,32,128]{2,1,0:T(8,128)(2,1)} %bitcast.25, f32[32,128]{1,0:T(8,128)} %constant.72.clone.z_hbm, f32[4,64,512]{2,1,0:T(8,128)} %constant.73.clone.y_hbm), custom_call_target="tpu_custom_call" | custom-call | flops 134217728 | bytes 2097152 | tf_op jit(solution)/shard_map/forward_modes/pallas_call | solution.py:289
  2.7 0.0 copy-start
  2.7 1.0 %copy-done = bf16[32,2,32,128]{3,2,1,0:T(8,128)(2,1)S(1)} copy-done((bf16[32,2,32,128]{3,2,1,0:T(8,128)(2,1)S(1)}, bf16[32,2,32,128]{3,2,1,0:T(8,128)(2,1)}, u32[]{:S(2)}) %copy-start) | copy-done | bytes 524312
  3.7 0.6 %arrange_cells.1.own_ref = bf16[2,32,32,128]{3,2,1,0:T(8,128)(2,1)S(1)} custom-call(bf16[32,8,128]{2,1,0:T(8,128)(2,1)} %forward_modes.1.after_ref, bf16[32,2,32,128]{3,2,1,0:T(8,128)(2,1)S(1)} %copy-done), custom_call_target="tpu_custom_call" | custom-call | flops 1048576 | bytes 2097152 | tf_op jit(solution)/shard_map/arrange_cells/pallas_call | solution.py:440
  4.4 1.0 %fusion = (bf16[1,32,32,128]{3,2,1,0:T(8,128)(2,1)}, bf16[1,32,32,128]{3,2,1,0:T(8,128)(2,1)}, bf16[32,32,128]{2,1,0:T(8,128)(2,1)}, bf16[32,32,128]{2,1,0:T(8,128)(2,1)}) fusion(bf16[2,32,32,128]{3,2,1,0:T(8,128)(2,1)S(1)} %arrange_cells.1.own_ref, s32[]{:T(128)S(6)} %select_n.33, s32[]{:T(128)S(6)} %select_n.32), kind=kLoop, calls=%fused_computation.12 | loop fusion | bytes 2097160 | tf_op jit(solution)/shard_map/slice | solution.py:631
  5.4 0.7 %collective-permute-start.1 = (bf16[32,32,128]{2,1,0:T(8,128)(2,1)}, bf16[32,32,128]{2,1,0:T(8,128)(2,1)S(1)}, u32[]{:S(2)}, u32[]{:S(2)}) collective-permute-start(bf16[32,32,128]{2,1,0:T(8,128)(2,1)} %get-tuple-element.13), channel_id=1, source_target_pairs={{4,8},{8,4},{12,16},{16,12},{20,24},{24,20},{5,9},{9,5},{13,17},{1... | collective-permute-start | bytes 786440 | tf_op jit(solution)/shard_map/ppermute | solution.py:604
  6.1 5.8 %collective-permute-start = (bf16[32,32,128]{2,1,0:T(8,128)(2,1)}, bf16[32,32,128]{2,1,0:T(8,128)(2,1)S(1)}, u32[]{:S(2)}, u32[]{:S(2)}) collective-permute-start(bf16[32,32,128]{2,1,0:T(8,128)(2,1)} %get-tuple-element.14), channel_id=1, source_target_pairs={{0,4},{4,0},{8,12},{12,8},{16,20},{20,16},{24,28},{28,24},{1,5},{5... | collective-permute-start | bytes 786440 | tf_op jit(solution)/shard_map/ppermute | solution.py:604
  11.9 4.7 %all-to-all-start = ((bf16[32,8,128]{2,1,0:T(8,128)(2,1)}), bf16[32,8,128]{2,1,0:T(8,128)(2,1)S(1)}, u32[]{:S(2)}, u32[]{:S(2)}) async-start(bf16[32,8,128]{2,1,0:T(8,128)(2,1)} %forward_modes.1.after_ref), calls=%async_computation | async-start | bytes 131072 | tf_op jit(solution)/shard_map/all_to_all | solution.py:597
  16.6 2.5 %prepare_weights.1 = (f32[2,4,16,16,128]{4,3,2,1,0:T(8,128)S(1)}, bf16[384,512]{1,0:T(8,128)(2,1)S(1)}, bf16[512,512]{1,0:T(8,128)(2,1)S(1)}) custom-call(bf16[32,8,128]{2,1,0:T(8,128)(2,1)} %forward_modes.1.after_ref, f32[2,4,4,16,16,32]{5,4,3,2,1,0:T(8,128)} %bitcast.29, bf16[3,3,3,32,32]{4,3,2,1,0:T(8,128)(2,1)S(1)} %bitcast.28, f32[4,32,512]{2,1,0:T(8,128)S(1)} %copy-done.2), custom_call_target="tpu_custom_call" | custom-call | flops 1048576 | bytes 6291456 | tf_op jit(solution)/shard_map/prepare_weights/pallas_call | solution.py:354
  19.1 0.0 copy-start.7
  19.1 0.7 %copy-done.7 = bf16[384,512]{1,0:T(8,128)(2,1)} copy-done((bf16[384,512]{1,0:T(8,128)(2,1)}, bf16[384,512]{1,0:T(8,128)(2,1)S(1)}, u32[]{:S(2)}) %copy-start.7) | copy-done | bytes 393240
  19.9 0.7 %dynamic-slice_bitcast_fusion.3 = (bf16[32,128]{1,0:T(8,128)(2,1)S(1)}, bf16[32,128]{1,0:T(8,128)(2,1)S(1)}, bf16[32,128]{1,0:T(8,128)(2,1)S(1)}, bf16[32,128]{1,0:T(8,128)(2,1)S(1)}) fusion(bf16[1,32,32,128]{3,2,1,0:T(8,128)(2,1)} %get-tuple-element.12, s32[]{:T(128)S(6)} %select_n.36, s32[]{:T(128)S(6)} %select_n.35, ...), kind=kLoop, calls=%fused_computation.5 | loop fusion | bytes 65544 | tf_op jit(solution)/shard_map/jit(dynamic_index_in_dim)/squeeze | solution.py:632
  20.6 3.4 %all-to-all-done.modes_ref = bf16[32,8,128]{2,1,0:T(8,128)(2,1)S(1)} async-done(((bf16[32,8,128]{2,1,0:T(8,128)(2,1)}), bf16[32,8,128]{2,1,0:T(8,128)(2,1)S(1)}, u32[]{:S(2)}, u32[]{:S(2)}) %all-to-all-start) | async-done | bytes 65568 | tf_op jit(solution)/shard_map/all_to_all | solution.py:597
  24.0 1.6 %mix_modes.1 = bf16[32,16,128]{2,1,0:T(8,128)(2,1)} custom-call(bf16[32,8,128]{2,1,0:T(8,128)(2,1)S(1)} %all-to-all-done.modes_ref, f32[64,256]{1,0:T(8,128)S(1)} %copy-done.5, f32[2,4,16,16,128]{4,3,2,1,0:T(8,128)S(1)} %get-tuple-element.8.weight_ref, f32[128,128]{1,0:T(8,128)S(1)} %copy-done.4), custom_call_target="tpu_custom_call" | custom-call | flops 4194304 | bytes 2097152 | tf_op jit(solution)/shard_map/mix_modes/pallas_call | solution.py:417
  25.6 5.1 %all-to-all-start.1 = ((bf16[32,16,128]{2,1,0:T(8,128)(2,1)}), bf16[32,16,128]{2,1,0:T(8,128)(2,1)S(1)}, u32[]{:S(2)}, u32[]{:S(2)}) async-start(bf16[32,16,128]{2,1,0:T(8,128)(2,1)} %mix_modes.1), calls=%async_computation.1 | async-start | bytes 262144 | tf_op jit(solution)/shard_map/all_to_all | solution.py:597
  30.8 0.0 collective-permute-done.1.second_ref
  30.8 0.3 collective-permute-start.2
  31.2 0.7 %collective-permute-start.3 = (bf16[128,128]{1,0:T(8,128)(2,1)S(1)}, bf16[128,128]{1,0:T(8,128)(2,1)S(1)}, u32[]{:S(2)}, u32[]{:S(2)}) collective-permute-start(bf16[128,128]{1,0:T(8,128)(2,1)S(1)} %pad_maximum_fusion.1), channel_id=1, source_target_pairs={{1,2},{2,1},{5,6},{6,5},{9,10},{10,9},{13,14},{14,13},{17,18},{18,... | collective-permute-start | bytes 98312 | tf_op jit(solution)/shard_map/ppermute | solution.py:604
  31.8 0.0 copy-start.8
  31.8 1.0 %copy-done.8 = bf16[384,512]{1,0:T(8,128)(2,1)S(1)} copy-done((bf16[384,512]{1,0:T(8,128)(2,1)S(1)}, bf16[384,512]{1,0:T(8,128)(2,1)}, u32[]{:S(2)}) %copy-start.8) | copy-done | bytes 393240
  32.8 1.3 %convolve_interior.1 = f32[2048,128]{1,0:T(8,128)S(1)} custom-call(bf16[2,32,32,128]{3,2,1,0:T(8,128)(2,1)S(1)} %arrange_cells.1.own_ref, bf16[32,32,128]{2,1,0:T(8,128)(2,1)S(1)} %collective-permute-done.first_ref, bf16[32,32,128]{2,1,0:T(8,128)(2,1)S(1)} %collective-permute-done.1.second_ref, bf16[384,512]{1,0:T(8,128)(2,1)S(1)} %copy-done.8), custom_call_target="tpu_custom_call" | custom-call | flops 1073741824 | bytes 2097152 | tf_op jit(solution)/shard_map/convolve_interior/pallas_call | solution.py:504
  34.2 0.5 %convolve_edges.1 = f32[512,128]{1,0:T(8,128)S(1)} custom-call(bf16[2,32,32,128]{3,2,1,0:T(8,128)(2,1)S(1)} %arrange_cells.1.own_ref, bf16[32,32,128]{2,1,0:T(8,128)(2,1)S(1)} %collective-permute-done.first_ref, bf16[32,32,128]{2,1,0:T(8,128)(2,1)S(1)} %collective-permute-done.1.second_ref, bf16[128,128]{1,0:T(8,128)(2,1)S(1)} %collective-permute-done.2.first_row, ...), custom_call_target="tpu_custom_call" | custom-call | flops 1073741824 | bytes 2097152 | tf_op jit(solution)/shard_map/convolve_edges/pallas_call | solution.py:504
  34.7 4.3 %all-to-all-done.1.values_ref = bf16[32,16,128]{2,1,0:T(8,128)(2,1)S(1)} async-done(((bf16[32,16,128]{2,1,0:T(8,128)(2,1)}), bf16[32,16,128]{2,1,0:T(8,128)(2,1)S(1)}, u32[]{:S(2)}, u32[]{:S(2)}) %all-to-all-start.1) | async-done | bytes 131104 | tf_op jit(solution)/shard_map/all_to_all | solution.py:597
  39.0 2.0 %finish_layer.1 = bf16[32,2,32,128]{3,2,1,0:T(8,128)(2,1)} custom-call(f32[32]{0:T(128)S(1)} %copy-done.6, bf16[32,16,128]{2,1,0:T(8,128)(2,1)S(1)} %all-to-all-done.1.values_ref, f32[128,512]{1,0:T(8,128)S(1)} %copy-done.1, bf16[512,512]{1,0:T(8,128)(2,1)S(1)} %get-tuple-element.9.y_ref, f32[32,2,32,128]{3,2,1,0:T(8,128)S(1)} %bitcast.26, ...), custom_call_target="tpu_custom_call" | custom-call | flops 268435456 | bytes 4194304 | tf_op jit(solution)/shard_map/finish_layer/pallas_call | solution.py:581
  (19 shorter events, 0.1 us)
Async XLA Ops:
  0.0 16.6 %copy-start.2 = (f32[4,32,512]{2,1,0:T(8,128)S(1)}, f32[4,32,512]{2,1,0:T(8,128)}, u32[]{:S(2)}) copy-start(f32[4,32,512]{2,1,0:T(8,128)} %constant.74.clone.y_ref) | copy-start | bytes 786436
  0.0 16.6 %copy-start.3 = (bf16[32,32,3,3,3]{1,0,4,3,2:T(8,128)(2,1)S(1)}, bf16[32,32,3,3,3]{1,0,4,3,2:T(8,128)(2,1)}, u32[]{:S(2)}) copy-start(bf16[32,32,3,3,3]{1,0,4,3,2:T(8,128)(2,1)} %param.11) | copy-start | bytes 165892
  2.7 1.0 %copy-start = (bf16[32,2,32,128]{3,2,1,0:T(8,128)(2,1)S(1)}, bf16[32,2,32,128]{3,2,1,0:T(8,128)(2,1)}, u32[]{:S(2)}) copy-start(bf16[32,2,32,128]{3,2,1,0:T(8,128)(2,1)} %state_ref.1) | copy-start | bytes 1572868
  3.7 20.3 %copy-start.4 = (f32[128,128]{1,0:T(8,128)S(1)}, f32[128,128]{1,0:T(8,128)}, u32[]{:S(2)}) copy-start(f32[128,128]{1,0:T(8,128)} %constant.76.clone.inverse_ref) | copy-start | bytes 196612
  3.7 20.3 %copy-start.5 = (f32[64,256]{1,0:T(8,128)S(1)}, f32[64,256]{1,0:T(8,128)}, u32[]{:S(2)}) copy-start(f32[64,256]{1,0:T(8,128)} %constant.75.clone.forward_ref) | copy-start | bytes 196612
  5.4 25.4 %collective-permute-start.1 = (bf16[32,32,128]{2,1,0:T(8,128)(2,1)}, bf16[32,32,128]{2,1,0:T(8,128)(2,1)S(1)}, u32[]{:S(2)}, u32[]{:S(2)}) collective-permute-start(bf16[32,32,128]{2,1,0:T(8,128)(2,1)} %get-tuple-element.13), channel_id=1, source_target_pairs={{4,8},{8,4},{12,16},{16,12},{20,24},{24,20},{5,9},{9,5},{13,17},{1... | collective-permute-start | bytes 786440 | tf_op jit(solution)/shard_map/ppermute | solution.py:604
  6.1 24.7 %collective-permute-start = (bf16[32,32,128]{2,1,0:T(8,128)(2,1)}, bf16[32,32,128]{2,1,0:T(8,128)(2,1)S(1)}, u32[]{:S(2)}, u32[]{:S(2)}) collective-permute-start(bf16[32,32,128]{2,1,0:T(8,128)(2,1)} %get-tuple-element.14), channel_id=1, source_target_pairs={{0,4},{4,0},{8,12},{12,8},{16,20},{20,16},{24,28},{28,24},{1,5},{5... | collective-permute-start | bytes 786440 | tf_op jit(solution)/shard_map/ppermute | solution.py:604
  11.9 12.1 %all-to-all-start = ((bf16[32,8,128]{2,1,0:T(8,128)(2,1)}), bf16[32,8,128]{2,1,0:T(8,128)(2,1)S(1)}, u32[]{:S(2)}, u32[]{:S(2)}) async-start(bf16[32,8,128]{2,1,0:T(8,128)(2,1)} %forward_modes.1.after_ref), calls=%async_computation | async-start | bytes 131072 | tf_op jit(solution)/shard_map/all_to_all | solution.py:597
  19.1 0.7 %copy-start.7 = (bf16[384,512]{1,0:T(8,128)(2,1)}, bf16[384,512]{1,0:T(8,128)(2,1)S(1)}, u32[]{:S(2)}) copy-start(bf16[384,512]{1,0:T(8,128)(2,1)S(1)} %get-tuple-element.10.weight_ref) | copy-start | bytes 1179652
  25.6 13.4 %copy-start.1 = (f32[128,512]{1,0:T(8,128)S(1)}, f32[128,512]{1,0:T(8,128)}, u32[]{:S(2)}) copy-start(f32[128,512]{1,0:T(8,128)} %constant.77.clone.z_ref) | copy-start | bytes 786436
  25.6 13.4 %copy-start.6 = (f32[32]{0:T(128)S(1)}, f32[32]{0:T(128)}, u32[]{:S(2)}) copy-start(f32[32]{0:T(128)} %bias_ref.1) | copy-start | bytes 388
  25.6 13.4 %all-to-all-start.1 = ((bf16[32,16,128]{2,1,0:T(8,128)(2,1)}), bf16[32,16,128]{2,1,0:T(8,128)(2,1)S(1)}, u32[]{:S(2)}, u32[]{:S(2)}) async-start(bf16[32,16,128]{2,1,0:T(8,128)(2,1)} %mix_modes.1), calls=%async_computation.1 | async-start | bytes 262144 | tf_op jit(solution)/shard_map/all_to_all | solution.py:597
  30.8 3.3 %collective-permute-start.2 = (bf16[128,128]{1,0:T(8,128)(2,1)S(1)}, bf16[128,128]{1,0:T(8,128)(2,1)S(1)}, u32[]{:S(2)}, u32[]{:S(2)}) collective-permute-start(bf16[128,128]{1,0:T(8,128)(2,1)S(1)} %pad_maximum_fusion), channel_id=1, source_target_pairs={{0,1},{1,0},{2,3},{3,2},{4,5},{5,4},{6,7},{7,6},{8,9},{9,8},{10,11... | collective-permute-start | bytes 98312 | tf_op jit(solution)/shard_map/ppermute | solution.py:604
  31.2 3.0 %collective-permute-start.3 = (bf16[128,128]{1,0:T(8,128)(2,1)S(1)}, bf16[128,128]{1,0:T(8,128)(2,1)S(1)}, u32[]{:S(2)}, u32[]{:S(2)}) collective-permute-start(bf16[128,128]{1,0:T(8,128)(2,1)S(1)} %pad_maximum_fusion.1), channel_id=1, source_target_pairs={{1,2},{2,1},{5,6},{6,5},{9,10},{10,9},{13,14},{14,13},{17,18},{18,... | collective-permute-start | bytes 98312 | tf_op jit(solution)/shard_map/ppermute | solution.py:604
  31.8 1.0 %copy-start.8 = (bf16[384,512]{1,0:T(8,128)(2,1)S(1)}, bf16[384,512]{1,0:T(8,128)(2,1)}, u32[]{:S(2)}) copy-start(bf16[384,512]{1,0:T(8,128)(2,1)} %copy-done.7) | copy-start | bytes 1179652

commit v2 on v1

--- a/solution.py
+++ b/solution.py
@@ -328,10 +328,8 @@
             for x_at in range(2):
                 row = ((dz * 2 + y_at) * 2 + x_at) * 32
                 for y_in in range(4):
-                    low, *inner, high = [
-                        taps.get((x_in - x_at, y_in - y_at), zero) for x_in in range(4)
-                    ]
-                    blocks = [jnp.where(odd_x, low, high)] + inner + [jnp.where(odd_x, high, low)]
+                    blocks = [taps.get((x_in - x_at, y_in - y_at), zero) for x_in in range(4)]
+                    blocks = [jnp.where(odd_x, blocks[i], blocks[3 - i]) for i in range(4)]
                     conv_out[row : row + 32, y_in * 128 : (y_in + 1) * 128] = jnp.concatenate(
                         blocks, axis=1
                     ).astype(jnp.bfloat16)
@@ -425,28 +423,55 @@
     )(modes, forward_table, weights, inverse_table)
 
 
-def arrange_kernel(after_ref, state_ref, own_ref, wide):
+def arrange_kernel(after_ref, state_ref, first_ref, second_ref, wide):
     cells_y = state_ref.shape[2]
-    for x in range(2):
-        wide[x] = state_ref[:, x].astype(jnp.float32).reshape(32 * cells_y, 128)
-    for y in range(cells_y):
-        for x in range(2):
-            own_ref[x, y] = wide[x, pl.ds(y, 32, stride=cells_y), :].astype(jnp.bfloat16)
+    odd_x = lax.rem(lax.axis_index("px"), 2)
+    for out_ref, x in ((first_ref, 1 - odd_x), (second_ref, odd_x)):
+        wide[...] = state_ref[:, x].astype(jnp.float32).reshape(32 * cells_y, 128)
+        for y in range(cells_y):
+            out_ref[y] = wide[pl.ds(y, 32, stride=cells_y), :].astype(jnp.bfloat16)
 
 
 def arrange(after, state):
     vmem = pl.BlockSpec(memory_space=pltpu.VMEM)
     cells_y = state.shape[2]
+    plane = jax.ShapeDtypeStruct((cells_y, 32, 128), jnp.bfloat16)
     return pl.pallas_call(
         arrange_kernel,
-        out_shape=jax.ShapeDtypeStruct((2, cells_y, 32, 128), jnp.bfloat16),
+        out_shape=(plane, plane),
         in_specs=[pl.BlockSpec(memory_space=pl.ANY), vmem],
-        out_specs=vmem,
-        scratch_shapes=[pltpu.VMEM((2, 32 * cells_y, 128), jnp.float32)],
+        out_specs=(vmem, vmem),
+        scratch_shapes=[pltpu.VMEM((32 * cells_y, 128), jnp.float32)],
         compiler_params=pltpu.CompilerParams(vmem_limit_bytes=40 * 2**20),
         cost_estimate=pl.CostEstimate(flops=2**20, bytes_accessed=2**21, transcendentals=0),
         name="arrange_cells",
     )(after, state)
+
+
+def cell_row(planes, y):
+    return jnp.concatenate([plane[y] for plane in planes], axis=0)
+
+
+def edge_rows_kernel(*refs):
+    *planes, first_ref, second_ref = refs
+    end = planes[0].shape[0] - 1
+    odd_y = lax.rem(lax.axis_index("py"), 2)
+    first_ref[...] = cell_row(planes, (1 - odd_y) * end)
+    second_ref[...] = cell_row(planes, odd_y * end)
+
+
+def edge_rows(planes):
+    vmem = pl.BlockSpec(memory_space=pltpu.VMEM)
+    row = jax.ShapeDtypeStruct((128, 128), jnp.bfloat16)
+    return pl.pallas_call(
+        edge_rows_kernel,
+        out_shape=(row, row),
+        in_specs=[vmem] * 4,
+        out_specs=(vmem, vmem),
+        compiler_params=pltpu.CompilerParams(vmem_limit_bytes=40 * 2**20),
+        cost_estimate=pl.CostEstimate(flops=2**10, bytes_accessed=2**17, transcendentals=0),
+        name="edge_rows",
+    )(*planes)
 
 
 def convolve_quad(quad, row, weight, place, out_ref):
@@ -470,21 +495,19 @@
                 out_ref[pl.ds(x_out * span + at, 32, stride=2 * span), :] = value
 
 
-def interior_kernel(own_ref, first_ref, second_ref, weight_ref, out_ref):
-    cells_y = own_ref.shape[1]
-
-    def row(y):
-        return jnp.concatenate([first_ref[y], own_ref[0, y], own_ref[1, y], second_ref[y]], axis=0)
-
+def interior_kernel(*refs):
+    *planes, weight_ref, out_ref = refs
+    cells_y = planes[0].shape[0]
     weight = weight_ref[...]
     for quad in range(1, cells_y // 4 - 1):
-        convolve_quad(quad, row, weight, lambda y: (y, cells_y), out_ref)
-
-
-def edge_kernel(
-    own_ref, first_ref, second_ref, first_row, second_row, weight_ref, out_ref
-):
-    cells_y = own_ref.shape[1]
+        convolve_quad(
+            quad, lambda y: cell_row(planes, y), weight, lambda y: (y, cells_y), out_ref
+        )
+
+
+def edge_kernel(*refs):
+    *planes, first_row, second_row, weight_ref, out_ref = refs
+    cells_y = planes[0].shape[0]
     odd_y = lax.rem(lax.axis_index("py"), 2) == 1
 
     def row(y):
@@ -492,7 +515,7 @@
             return jnp.where(odd_y, first_row[...], second_row[...])
         if y >= cells_y:
             return jnp.where(odd_y, second_row[...], first_row[...])
-        return jnp.concatenate([first_ref[y], own_ref[0, y], own_ref[1, y], second_ref[y]], axis=0)
+        return cell_row(planes, y)
 
     weight = weight_ref[...]
     for quad in (0, cells_y // 4 - 1):
@@ -614,27 +637,14 @@
         state_field.reshape(channels * cells_x, cells_y, depth), z_forward, y_forward
     )
     modes = exchanged(sent)
-    own = arrange(sent, state_field)
-    odd_x = lax.axis_index("px") % 2
-    odd_y = lax.axis_index("py") % 2
-    first_plane, second_plane = swaps(
-        lax.dynamic_index_in_dim(own, 1 - odd_x, 0, keepdims=False),
-        lax.dynamic_index_in_dim(own, odd_x, 0, keepdims=False),
-        "px",
-    )
     weights, taps, y_expanded = prepare(
         sent, spectral_weight.swapaxes(4, 5), conv_weight.transpose(2, 3, 4, 0, 1), y_inverse
     )
+    first_own, second_own = arrange(taps, state_field)
+    first_plane, second_plane = swaps(first_own, second_own, "px")
     values = exchanged(mix_modes(modes, x_forward, weights, x_inverse))
-
-    def edge(y):
-        pieces = [first_plane, own[0], own[1], second_plane]
-        return jnp.concatenate([lax.dynamic_index_in_dim(p, y, 0, keepdims=False) for p in pieces])
-
-    first_row, second_row = swaps(
-        edge((1 - odd_y) * (cells_y - 1)), edge(odd_y * (cells_y - 1)), "py"
-    )
-    planes = (own, first_plane, second_plane)
+    planes = (first_plane, first_own, second_own, second_plane)
+    first_row, second_row = swaps(*edge_rows(planes), "py")
     rows = channels * cells_x * cells_y
     interior = convolve(interior_kernel, "convolve_interior", planes + (taps,), rows)
     edges = convolve(

time: 41.4 us -> 40.5 us (0.978)
  blocking collectives: 0 us -> 14.8 us
  starting transfers between devices: 17.3 us -> 7.07 us
  waiting for transfers between devices: 7.71 us -> 4.49 us
  local copies, waits for them, and re-layouts: 4.56 us -> 2.86 us
  Pallas kernels: 11.3 us -> 10.7 us
    all_to_all x0 -> x1, blocking collectives: none -> 14.8 us  [exchanged(): lax.all_to_all(value, ('px', 'py'), split_axis=0, concat_axis=0, tiled=True)]
    all_to_all x2 -> x1, starting transfers between devices: 9.86 us -> 2.57 us  [exchanged(): lax.all_to_all(value, ('px', 'py'), split_axis=0, concat_axis=0, tiled=True)]
    all_to_all x2 -> x1, waiting for transfers between devices: 7.7 us -> 4.48 us  [exchanged(): lax.all_to_all(value, ('px', 'py'), split_axis=0, concat_axis=0, tiled=True)]
    ppermute x2, starting transfers between devices: 6.1 us -> 3.18 us  [swaps(): lax.ppermute(first, axis, inside)]
    slice x1 -> x0, local copies, waits for them, and re-layouts: 1 us -> none  [edge(): pieces = [first_plane, own[0], own[1], second_plane]]
    squeeze x3 -> x0, local copies, waits for them, and re-layouts: 0.77 us -> none  [edge(): lax.dynamic_index_in_dim(p, y, 0, keepdims=False)]
    pallas_call x1, Pallas kernels: 2.68 us -> 2.08 us  [forward_modes(): pl.pallas_call(forward_kernel, out_shape=jax.ShapeDtypeStruct((32, 8, 128...]
  transfers between devices with their start and end apart: 6 -> 5, of which waited for: 2 -> 1; matrix products, arithmetic and copies ran while one was open for 2% -> 0% of each run, Pallas kernels for 14% -> 9%
where the time goes in v2:
time: 40.5 us; the launch traced here: 40.1 us
  blocking collectives  14.8 us (37%)
  Pallas kernels  10.7 us (26%)
  starting transfers between devices  7.07 us (17%)
  waiting for transfers between devices  4.49 us (11%)
  local copies, waits for them, and re-layouts  2.86 us (7%)
    all_to_all x1, blocking collectives, exchanged(): lax.all_to_all(value, ('px', 'py'), split_axis=0, concat_axis=0, tiled=True)  14.8 us
    all_to_all x1, waiting for transfers between devices, exchanged(): lax.all_to_all(value, ('px', 'py'), split_axis=0, concat_axis=0, tiled=True)  4.48 us
    ppermute x2, starting transfers between devices, swaps(): lax.ppermute(first, axis, inside)  3.18 us
    unnamed x18, local copies, waits for them, and re-layouts  2.86 us
    all_to_all x1, starting transfers between devices, exchanged(): lax.all_to_all(value, ('px', 'py'), split_axis=0, concat_axis=0, tiled=True)  2.57 us
    pallas_call x1, Pallas kernels, prepare(): pl.pallas_call(prepare_kernel, out_shape=(jax.ShapeDtypeStruct((2, 4, 16,...  2.48 us
    pallas_call x1, Pallas kernels, forward_modes(): pl.pallas_call(forward_kernel, out_shape=jax.ShapeDtypeStruct((32, 8, 128...  2.08 us
    pallas_call x1, Pallas kernels, finish(): pl.pallas_call(finish_kernel, out_shape=jax.ShapeDtypeStruct(convolved.sh...  2.03 us
  transfers between devices with their start and end apart: 5, of which 1 were waited for; matrix products, arithmetic and copies ran while one was open for 0% of the time, Pallas kernels for 9%

profile of v2, /device:TPU:0, one launch (start us, length us, event | category | flops | bytes accessed | tf_op | source)
XLA Modules:
  0.0 40.1 jit_solution(10594295824363836193)
XLA Ops:
  0.0 2.1 %forward_modes.1.after_ref = bf16[32,8,128]{2,1,0:T(8,128)(2,1)S(1)} custom-call(bf16[64,32,128]{2,1,0:T(8,128)(2,1)} %bitcast.5, f32[32,128]{1,0:T(8,128)} %constant.12.clone.z_hbm, f32[4,64,512]{2,1,0:T(8,128)} %constant.13.clone.y_hbm), custom_call_target="tpu_custom_call" | custom-call | flops 134217728 | bytes 2097152 | tf_op jit(solution)/shard_map/forward_modes/pallas_call | solution.py:289
  2.1 0.0 copy-start.2
  2.1 0.9 %copy-done.2 = f32[4,32,512]{2,1,0:T(8,128)S(1)} copy-done((f32[4,32,512]{2,1,0:T(8,128)S(1)}, f32[4,32,512]{2,1,0:T(8,128)}, u32[]{:S(2)}) %copy-start.2) | copy-done | bytes 262168
  3.1 0.9 %copy-done.5 = bf16[32,32,3,3,3]{1,0,4,3,2:T(8,128)(2,1)S(1)} copy-done((bf16[32,32,3,3,3]{1,0,4,3,2:T(8,128)(2,1)S(1)}, bf16[32,32,3,3,3]{1,0,4,3,2:T(8,128)(2,1)}, u32[]{:S(2)}) %copy-start.5) | copy-done | bytes 55320
  4.0 2.5 %prepare_weights.1 = (f32[2,4,16,16,128]{4,3,2,1,0:T(8,128)S(1)}, bf16[384,512]{1,0:T(8,128)(2,1)S(1)}, bf16[512,512]{1,0:T(8,128)(2,1)S(1)}) custom-call(bf16[32,8,128]{2,1,0:T(8,128)(2,1)S(1)} %forward_modes.1.after_ref, f32[2,4,4,16,16,32]{5,4,3,2,1,0:T(8,128)} %bitcast.9, bf16[3,3,3,32,32]{4,3,2,1,0:T(8,128)(2,1)S(1)} %bitcast.8, f32[4,32,512]{2,1,0:T(8,128)S(1)} %copy-done.2), custom_call_target="tpu_custom_call" | custom-call | flops 1048576 | bytes 6291456 | tf_op jit(solution)/shard_map/prepare_weights/pallas_call | solution.py:352
  6.5 0.7 %arrange_cells.1 = (bf16[32,32,128]{2,1,0:T(8,128)(2,1)S(1)}, bf16[32,32,128]{2,1,0:T(8,128)(2,1)S(1)}) custom-call(bf16[384,512]{1,0:T(8,128)(2,1)S(1)} %get-tuple-element.14.after_ref.refs_4_.refs_6_, bf16[32,2,32,128]{3,2,1,0:T(8,128)(2,1)S(1)} %copy-done), custom_call_target="tpu_custom_call" | custom-call | flops 1048576 | bytes 2097152 | tf_op jit(solution)/shard_map/arrange_cells/pallas_call | solution.py:439
  7.1 3.0 %collective-permute-start = (bf16[32,32,128]{2,1,0:T(8,128)(2,1)S(1)}, bf16[32,32,128]{2,1,0:T(8,128)(2,1)S(1)}, u32[]{:S(2)}, u32[]{:S(2)}) collective-permute-start(bf16[32,32,128]{2,1,0:T(8,128)(2,1)S(1)} %get-tuple-element.15.refs_1_), channel_id=1, source_target_pairs={{0,4},{4,0},{8,12},{12,8},{16,20},{20,16},{24,28},{28,24},{1,5},{5... | collective-permute-start | bytes 786440 | tf_op jit(solution)/shard_map/ppermute | solution.py:627
  10.2 0.7 %collective-permute-start.1 = (bf16[32,32,128]{2,1,0:T(8,128)(2,1)S(1)}, bf16[32,32,128]{2,1,0:T(8,128)(2,1)S(1)}, u32[]{:S(2)}, u32[]{:S(2)}) collective-permute-start(bf16[32,32,128]{2,1,0:T(8,128)(2,1)S(1)} %get-tuple-element.16.refs_2_), channel_id=1, source_target_pairs={{4,8},{8,4},{12,16},{16,12},{20,24},{24,20},{5,9},{9,5},{13,17},{1... | collective-permute-start | bytes 786440 | tf_op jit(solution)/shard_map/ppermute | solution.py:627
  10.8 14.8 %all_to_all.10.modes_ref = bf16[32,8,128]{2,1,0:T(8,128)(2,1)S(1)} all-to-all(bf16[32,8,128]{2,1,0:T(8,128)(2,1)S(1)} %forward_modes.1.after_ref), channel_id=1, replica_groups=mesh['px'=8,'py'=4] {'px','py'}, dimensions={0} | all-to-all | bytes 131072 | tf_op jit(solution)/shard_map/all_to_all | solution.py:620
  25.7 1.6 %mix_modes.1 = bf16[32,16,128]{2,1,0:T(8,128)(2,1)} custom-call(bf16[32,8,128]{2,1,0:T(8,128)(2,1)S(1)} %all_to_all.10.modes_ref, f32[64,256]{1,0:T(8,128)S(1)} %copy-done.7, f32[2,4,16,16,128]{4,3,2,1,0:T(8,128)S(1)} %get-tuple-element.12.weight_ref, f32[128,128]{1,0:T(8,128)S(1)} %copy-done.6), custom_call_target="tpu_custom_call" | custom-call | flops 4194304 | bytes 2097152 | tf_op jit(solution)/shard_map/mix_modes/pallas_call | solution.py:415
  27.3 2.6 %all-to-all-start.1 = ((bf16[32,16,128]{2,1,0:T(8,128)(2,1)}), bf16[32,16,128]{2,1,0:T(8,128)(2,1)S(1)}, u32[]{:S(2)}, u32[]{:S(2)}) async-start(bf16[32,16,128]{2,1,0:T(8,128)(2,1)} %mix_modes.1), calls=%async_computation.1 | async-start | bytes 262144 | tf_op jit(solution)/shard_map/all_to_all | solution.py:620
  29.9 0.0 collective-permute-done.1.refs_3_
  29.9 0.0 copy-start.3
  29.9 0.0 copy-start.1
  29.9 0.0 copy-start.8
  30.0 0.2 collective-permute-start.2
  30.1 0.7 %collective-permute-start.3 = (bf16[128,128]{1,0:T(8,128)(2,1)S(1)}, bf16[128,128]{1,0:T(8,128)(2,1)S(1)}, u32[]{:S(2)}, u32[]{:S(2)}) collective-permute-start(bf16[128,128]{1,0:T(8,128)(2,1)S(1)} %get-tuple-element.18), channel_id=1, source_target_pairs={{1,2},{2,1},{5,6},{6,5},{9,10},{10,9},{13,14},{14,13},{17,18},{18,... | collective-permute-start | bytes 98312 | tf_op jit(solution)/shard_map/ppermute | solution.py:627
  30.8 1.3 %convolve_interior.1 = f32[2048,128]{1,0:T(8,128)S(1)} custom-call(bf16[32,32,128]{2,1,0:T(8,128)(2,1)S(1)} %collective-permute-done.refs_0_, bf16[32,32,128]{2,1,0:T(8,128)(2,1)S(1)} %get-tuple-element.15.refs_1_, bf16[32,32,128]{2,1,0:T(8,128)(2,1)S(1)} %get-tuple-element.16.refs_2_, bf16[32,32,128]{2,1,0:T(8,128)(2,1)S(1)} %collective-permute-done.1.refs_3_, ...), custom_call_target="tpu_custom_call" | custom-call | flops 1073741824 | bytes 2097152 | tf_op jit(solution)/shard_map/convolve_interior/pallas_call | solution.py:527
  32.1 0.0 collective-permute-done.2.refs_4_
  32.2 0.0 copy-start.4
  32.2 0.9 %copy-done.4 = bf16[32,32,128]{2,1,0:T(8,128)(2,1)S(1)} copy-done((bf16[32,32,128]{2,1,0:T(8,128)(2,1)S(1)}, bf16[32,32,128]{2,1,0:T(8,128)(2,1)}, u32[]{:S(2)}) %copy-start.4) | copy-done | bytes 262168
  33.1 0.5 %convolve_edges.1 = f32[512,128]{1,0:T(8,128)S(1)} custom-call(bf16[32,32,128]{2,1,0:T(8,128)(2,1)S(1)} %collective-permute-done.refs_0_, bf16[32,32,128]{2,1,0:T(8,128)(2,1)S(1)} %get-tuple-element.15.refs_1_, bf16[32,32,128]{2,1,0:T(8,128)(2,1)S(1)} %get-tuple-element.16.refs_2_, bf16[32,32,128]{2,1,0:T(8,128)(2,1)S(1)} %copy-done.4, ...), custom_call_target="tpu_custom_call" | custom-call | flops 1073741824 | bytes 2097152 | tf_op jit(solution)/shard_map/convolve_edges/pallas_call | solution.py:527
  33.6 4.5 %all-to-all-done.1.values_ref = bf16[32,16,128]{2,1,0:T(8,128)(2,1)S(1)} async-done(((bf16[32,16,128]{2,1,0:T(8,128)(2,1)}), bf16[32,16,128]{2,1,0:T(8,128)(2,1)S(1)}, u32[]{:S(2)}, u32[]{:S(2)}) %all-to-all-start.1) | async-done | bytes 131104 | tf_op jit(solution)/shard_map/all_to_all | solution.py:620
  38.1 2.0 %finish_layer.1 = bf16[32,2,32,128]{3,2,1,0:T(8,128)(2,1)} custom-call(f32[32]{0:T(128)S(1)} %copy-done.8, bf16[32,16,128]{2,1,0:T(8,128)(2,1)S(1)} %all-to-all-done.1.values_ref, f32[128,512]{1,0:T(8,128)S(1)} %copy-done.1, bf16[512,512]{1,0:T(8,128)(2,1)S(1)} %get-tuple-element.13.y_ref, f32[32,2,32,128]{3,2,1,0:T(8,128)S(1)} %bitcast.6, ...), custom_call_target="tpu_custom_call" | custom-call | flops 268435456 | bytes 4194304 | tf_op jit(solution)/shard_map/finish_layer/pallas_call | solution.py:604
  (13 shorter events, 0.0 us)
Async XLA Ops:
  0.0 25.7 %copy-start.6 = (f32[128,128]{1,0:T(8,128)S(1)}, f32[128,128]{1,0:T(8,128)}, u32[]{:S(2)}) copy-start(f32[128,128]{1,0:T(8,128)} %constant.16.clone.inverse_ref) | copy-start | bytes 196612
  0.0 25.7 %copy-start.7 = (f32[64,256]{1,0:T(8,128)S(1)}, f32[64,256]{1,0:T(8,128)}, u32[]{:S(2)}) copy-start(f32[64,256]{1,0:T(8,128)} %constant.15.clone.forward_ref) | copy-start | bytes 196612
  0.0 6.5 %copy-start = (bf16[32,2,32,128]{3,2,1,0:T(8,128)(2,1)S(1)}, bf16[32,2,32,128]{3,2,1,0:T(8,128)(2,1)}, u32[]{:S(2)}) copy-start(bf16[32,2,32,128]{3,2,1,0:T(8,128)(2,1)} %state_ref.1) | copy-start | bytes 1572868
  2.1 1.0 %copy-start.2 = (f32[4,32,512]{2,1,0:T(8,128)S(1)}, f32[4,32,512]{2,1,0:T(8,128)}, u32[]{:S(2)}) copy-start(f32[4,32,512]{2,1,0:T(8,128)} %constant.14.clone.y_ref) | copy-start | bytes 786436
  3.1 0.9 %copy-start.5 = (bf16[32,32,3,3,3]{1,0,4,3,2:T(8,128)(2,1)S(1)}, bf16[32,32,3,3,3]{1,0,4,3,2:T(8,128)(2,1)}, u32[]{:S(2)}) copy-start(bf16[32,32,3,3,3]{1,0,4,3,2:T(8,128)(2,1)} %param.11) | copy-start | bytes 165892
  7.1 22.7 %collective-permute-start = (bf16[32,32,128]{2,1,0:T(8,128)(2,1)S(1)}, bf16[32,32,128]{2,1,0:T(8,128)(2,1)S(1)}, u32[]{:S(2)}, u32[]{:S(2)}) collective-permute-start(bf16[32,32,128]{2,1,0:T(8,128)(2,1)S(1)} %get-tuple-element.15.refs_1_), channel_id=1, source_target_pairs={{0,4},{4,0},{8,12},{12,8},{16,20},{20,16},{24,28},{28,24},{1,5},{5... | collective-permute-start | bytes 786440 | tf_op jit(solution)/shard_map/ppermute | solution.py:627
  10.2 19.7 %collective-permute-start.1 = (bf16[32,32,128]{2,1,0:T(8,128)(2,1)S(1)}, bf16[32,32,128]{2,1,0:T(8,128)(2,1)S(1)}, u32[]{:S(2)}, u32[]{:S(2)}) collective-permute-start(bf16[32,32,128]{2,1,0:T(8,128)(2,1)S(1)} %get-tuple-element.16.refs_2_), channel_id=1, source_target_pairs={{4,8},{8,4},{12,16},{16,12},{20,24},{24,20},{5,9},{9,5},{13,17},{1... | collective-permute-start | bytes 786440 | tf_op jit(solution)/shard_map/ppermute | solution.py:627
  27.3 10.8 %all-to-all-start.1 = ((bf16[32,16,128]{2,1,0:T(8,128)(2,1)}), bf16[32,16,128]{2,1,0:T(8,128)(2,1)S(1)}, u32[]{:S(2)}, u32[]{:S(2)}) async-start(bf16[32,16,128]{2,1,0:T(8,128)(2,1)} %mix_modes.1), calls=%async_computation.1 | async-start | bytes 262144 | tf_op jit(solution)/shard_map/all_to_all | solution.py:620
  29.9 2.3 %copy-start.3 = (bf16[32,32,128]{2,1,0:T(8,128)(2,1)}, bf16[32,32,128]{2,1,0:T(8,128)(2,1)S(1)}, u32[]{:S(2)}) copy-start(bf16[32,32,128]{2,1,0:T(8,128)(2,1)S(1)} %collective-permute-done.1.refs_3_) | copy-start | bytes 786436
  29.9 8.2 %copy-start.1 = (f32[128,512]{1,0:T(8,128)S(1)}, f32[128,512]{1,0:T(8,128)}, u32[]{:S(2)}) copy-start(f32[128,512]{1,0:T(8,128)} %constant.17.clone.z_ref) | copy-start | bytes 786436
  29.9 8.2 %copy-start.8 = (f32[32]{0:T(128)S(1)}, f32[32]{0:T(128)}, u32[]{:S(2)}) copy-start(f32[32]{0:T(128)} %bias_ref.1) | copy-start | bytes 388
  30.0 2.2 %collective-permute-start.2 = (bf16[128,128]{1,0:T(8,128)(2,1)S(1)}, bf16[128,128]{1,0:T(8,128)(2,1)S(1)}, u32[]{:S(2)}, u32[]{:S(2)}) collective-permute-start(bf16[128,128]{1,0:T(8,128)(2,1)S(1)} %get-tuple-element.17), channel_id=1, source_target_pairs={{0,1},{1,0},{2,3},{3,2},{4,5},{5,4},{6,7},{7,6},{8,9},{9,8},{10,11... | collective-permute-start | bytes 98312 | tf_op jit(solution)/shard_map/ppermute | solution.py:627
  30.1 2.0 %collective-permute-start.3 = (bf16[128,128]{1,0:T(8,128)(2,1)S(1)}, bf16[128,128]{1,0:T(8,128)(2,1)S(1)}, u32[]{:S(2)}, u32[]{:S(2)}) collective-permute-start(bf16[128,128]{1,0:T(8,128)(2,1)S(1)} %get-tuple-element.18), channel_id=1, source_target_pairs={{1,2},{2,1},{5,6},{6,5},{9,10},{10,9},{13,14},{14,13},{17,18},{18,... | collective-permute-start | bytes 98312 | tf_op jit(solution)/shard_map/ppermute | solution.py:627
  32.2 1.0 %copy-start.4 = (bf16[32,32,128]{2,1,0:T(8,128)(2,1)S(1)}, bf16[32,32,128]{2,1,0:T(8,128)(2,1)}, u32[]{:S(2)}) copy-start(bf16[32,32,128]{2,1,0:T(8,128)(2,1)} %copy-done.3) | copy-start | bytes 786436

commit v3 on v2

--- a/solution.py
+++ b/solution.py
@@ -298,15 +298,29 @@
             pltpu.VMEM((32 * state.shape[1], y_table.shape[2]), jnp.bfloat16),
             pltpu.SemaphoreType.DMA((6,)),
         ],
-        compiler_params=pltpu.CompilerParams(vmem_limit_bytes=40 * 2**20),
+        compiler_params=pltpu.CompilerParams(vmem_limit_bytes=16 * 2**20),
         cost_estimate=pl.CostEstimate(flops=2**27, bytes_accessed=2**21, transcendentals=0),
         name="forward_modes",
     )(*(pltpu.with_memory_space_constraint(v, pltpu.HBM) for v in (state, z_table, y_table)))
 
 
 def prepare_kernel(
-    after_ref, weight_hbm, conv_ref, y_ref, weight_out, conv_out, y_out, weight_ref, sems
+    after_ref,
+    weight_hbm,
+    conv_hbm,
+    y_hbm,
+    weight_out,
+    conv_out,
+    y_out,
+    weight_ref,
+    conv_ref,
+    y_ref,
+    sems,
 ):
+    conv_copy = pltpu.make_async_copy(conv_hbm, conv_ref, sems.at[8])
+    y_copy = pltpu.make_async_copy(y_hbm.at[lax.axis_index("py")], y_ref, sems.at[9])
+    conv_copy.start()
+    y_copy.start()
     copies = [
         pltpu.make_async_copy(
             weight_hbm.at[part, kz], weight_ref.at[part, kz], sems.at[part * 4 + kz]
@@ -317,6 +331,7 @@
     for copy in copies:
         copy.start()
     odd_x = lax.rem(lax.axis_index("px"), 2) == 1
+    conv_copy.wait()
     zero = jnp.zeros((32, 32), jnp.float32)
     for dz in range(3):
         taps = {
@@ -333,7 +348,8 @@
                     conv_out[row : row + 32, y_in * 128 : (y_in + 1) * 128] = jnp.concatenate(
                         blocks, axis=1
                     ).astype(jnp.bfloat16)
-    table = y_ref[lax.axis_index("py")]
+    y_copy.wait()
+    table = y_ref[...]
     lane = lax.broadcasted_iota(jnp.int32, table.shape, 1) % 16
     span = table.shape[0]
     for o in range(16):
@@ -356,25 +372,23 @@
             jax.ShapeDtypeStruct((384, 512), jnp.bfloat16),
             jax.ShapeDtypeStruct((16 * y_table.shape[1], y_table.shape[2]), jnp.bfloat16),
         ),
-        in_specs=[
-            pl.BlockSpec(memory_space=pl.ANY),
-            pl.BlockSpec(memory_space=pltpu.HBM),
-            vmem,
-            vmem,
-        ],
+        in_specs=[pl.BlockSpec(memory_space=pl.ANY)] + [pl.BlockSpec(memory_space=pltpu.HBM)] * 3,
         out_specs=(vmem,) * 3,
         scratch_shapes=[
             pltpu.VMEM(spectral_weight.shape, jnp.float32),
-            pltpu.SemaphoreType.DMA((8,)),
+            pltpu.VMEM(conv_weight.shape, jnp.bfloat16),
+            pltpu.VMEM(y_table.shape[1:], jnp.float32),
+            pltpu.SemaphoreType.DMA((10,)),
         ],
-        compiler_params=pltpu.CompilerParams(vmem_limit_bytes=40 * 2**20),
-        cost_estimate=pl.CostEstimate(flops=2**20, bytes_accessed=6 * 2**20, transcendentals=0),
+        compiler_params=pltpu.CompilerParams(vmem_limit_bytes=16 * 2**20),
+        cost_estimate=pl.CostEstimate(flops=2**10, bytes_accessed=2**10, transcendentals=0),
         name="prepare_weights",
     )(
         after,
-        pltpu.with_memory_space_constraint(spectral_weight, pltpu.HBM),
-        conv_weight,
-        y_table,
+        *(
+            pltpu.with_memory_space_constraint(v, pltpu.HBM)
+            for v in (spectral_weight, conv_weight, y_table)
+        ),
     )
 
 
@@ -417,8 +431,8 @@
         out_shape=jax.ShapeDtypeStruct((32, 16, 128), jnp.bfloat16),
         in_specs=[vmem] * 4,
         out_specs=vmem,
-        compiler_params=pltpu.CompilerParams(vmem_limit_bytes=40 * 2**20),
-        cost_estimate=pl.CostEstimate(flops=2**22, bytes_accessed=2**21, transcendentals=0),
+        compiler_params=pltpu.CompilerParams(vmem_limit_bytes=16 * 2**20),
+        cost_estimate=pl.CostEstimate(flops=2**35, bytes_accessed=2**21, transcendentals=0),
         name="mix_modes",
     )(modes, forward_table, weights, inverse_table)
 
@@ -442,8 +456,8 @@
         in_specs=[pl.BlockSpec(memory_space=pl.ANY), vmem],
         out_specs=(vmem, vmem),
         scratch_shapes=[pltpu.VMEM((32 * cells_y, 128), jnp.float32)],
-        compiler_params=pltpu.CompilerParams(vmem_limit_bytes=40 * 2**20),
-        cost_estimate=pl.CostEstimate(flops=2**20, bytes_accessed=2**21, transcendentals=0),
+        compiler_params=pltpu.CompilerParams(vmem_limit_bytes=16 * 2**20),
+        cost_estimate=pl.CostEstimate(flops=2**10, bytes_accessed=2**10, transcendentals=0),
         name="arrange_cells",
     )(after, state)
 
@@ -468,7 +482,7 @@
         out_shape=(row, row),
         in_specs=[vmem] * 4,
         out_specs=(vmem, vmem),
-        compiler_params=pltpu.CompilerParams(vmem_limit_bytes=40 * 2**20),
+        compiler_params=pltpu.CompilerParams(vmem_limit_bytes=16 * 2**20),
         cost_estimate=pl.CostEstimate(flops=2**10, bytes_accessed=2**17, transcendentals=0),
         name="edge_rows",
     )(*planes)
@@ -529,7 +543,7 @@
         out_shape=jax.ShapeDtypeStruct((rows, 128), jnp.float32),
         in_specs=[vmem] * len(operands),
         out_specs=vmem,
-        compiler_params=pltpu.CompilerParams(vmem_limit_bytes=40 * 2**20),
+        compiler_params=pltpu.CompilerParams(vmem_limit_bytes=16 * 2**20),
         cost_estimate=pl.CostEstimate(flops=2**30, bytes_accessed=2**21, transcendentals=0),
         name=name,
     )(*operands)
@@ -610,7 +624,7 @@
             pltpu.VMEM(convolved.shape, jnp.bfloat16),
             pltpu.SemaphoreType.DMA((8,)),
         ],
-        compiler_params=pltpu.CompilerParams(vmem_limit_bytes=40 * 2**20),
+        compiler_params=pltpu.CompilerParams(vmem_limit_bytes=16 * 2**20),
         cost_estimate=pl.CostEstimate(flops=2**28, bytes_accessed=2**22, transcendentals=2**18),
         name="finish_layer",
     )(bias, values, z_table, y_table, convolved, edges)

time: 40.5 us -> 37.6 us (0.928)
  blocking collectives: 14.8 us -> 0 us
  starting transfers between devices: 7.07 us -> 17.4 us
  Pallas kernels: 10.7 us -> 11.5 us
  waiting for transfers between devices: 4.49 us -> 5.11 us
    all_to_all x1 -> x0, blocking collectives: 14.8 us -> none  [exchanged(): lax.all_to_all(value, ('px', 'py'), split_axis=0, concat_axis=0, tiled=True)]
    all_to_all x1 -> x2, starting transfers between devices: 2.57 us -> 14 us  [exchanged(): lax.all_to_all(value, ('px', 'py'), split_axis=0, concat_axis=0, tiled=True)]
    ppermute x2, starting transfers between devices: 3.18 us -> 1.91 us  [swaps(): lax.ppermute(first, axis, inside)]
    pallas_call x1, Pallas kernels: 2.08 us -> 2.71 us  [forward_modes(): pl.pallas_call(forward_kernel, out_shape=jax.ShapeDtypeStruct((32, 8, 128...]
    ppermute x2, waiting for transfers between devices: 0.01 us -> 0.63 us  [swaps(): lax.ppermute(first, axis, inside)]
    all_to_all x1 -> x2, waiting for transfers between devices: 4.48 us -> 4.48 us  [exchanged(): lax.all_to_all(value, ('px', 'py'), split_axis=0, concat_axis=0, tiled=True)]
  transfers between devices with their start and end apart: 5 -> 6, of which waited for: 1 -> 3; matrix products, arithmetic and copies ran while one was open for 0% -> 0% of each run, Pallas kernels for 9% -> 18%
where the time goes in v3:
time: 37.6 us; the launch traced here: 37.3 us
  starting transfers between devices  17.4 us (46%)
  Pallas kernels  11.5 us (31%)
  waiting for transfers between devices  5.11 us (14%)
  local copies, waits for them, and re-layouts  3.17 us (8%)
    all_to_all x2, starting transfers between devices, exchanged(): lax.all_to_all(value, ('px', 'py'), split_axis=0, concat_axis=0, tiled=True)  14 us
    all_to_all x2, waiting for transfers between devices, exchanged(): lax.all_to_all(value, ('px', 'py'), split_axis=0, concat_axis=0, tiled=True)  4.48 us
    unnamed x18, local copies, waits for them, and re-layouts  3.17 us
    pallas_call x1, Pallas kernels, forward_modes(): pl.pallas_call(forward_kernel, out_shape=jax.ShapeDtypeStruct((32, 8, 128...  2.71 us
    pallas_call x1, Pallas kernels, prepare(): pl.pallas_call(prepare_kernel, out_shape=(jax.ShapeDtypeStruct((2, 4, 16,...  2.64 us
    pallas_call x1, Pallas kernels, finish(): pl.pallas_call(finish_kernel, out_shape=jax.ShapeDtypeStruct(convolved.sh...  2.04 us
    ppermute x2, starting transfers between devices, swaps(): lax.ppermute(first, axis, inside)  1.91 us
    pallas_call x2, Pallas kernels, convolve(): pl.pallas_call(kernel, out_shape=jax.ShapeDtypeStruct((rows, 128), jnp.fl...  1.82 us
  transfers between devices with their start and end apart: 6, of which 3 were waited for; matrix products, arithmetic and copies ran while one was open for 0% of the time, Pallas kernels for 18%

profile of v3, /device:TPU:0, one launch (start us, length us, event | category | flops | bytes accessed | tf_op | source)
XLA Modules:
  0.0 37.3 jit_solution(10772564051885074939)
XLA Ops:
  0.0 2.7 %forward_modes.1.after_ref = bf16[32,8,128]{2,1,0:T(8,128)(2,1)} custom-call(bf16[64,32,128]{2,1,0:T(8,128)(2,1)} %bitcast.5, f32[32,128]{1,0:T(8,128)} %constant.12.clone.z_hbm, f32[4,64,512]{2,1,0:T(8,128)} %constant.13.clone.y_hbm), custom_call_target="tpu_custom_call" | custom-call | flops 134217728 | bytes 2097152 | tf_op jit(solution)/shard_map/forward_modes/pallas_call | solution.py:289
  2.7 7.3 %all-to-all-start = ((bf16[32,8,128]{2,1,0:T(8,128)(2,1)}), bf16[32,8,128]{2,1,0:T(8,128)(2,1)S(1)}, u32[]{:S(2)}, u32[]{:S(2)}) async-start(bf16[32,8,128]{2,1,0:T(8,128)(2,1)} %forward_modes.1.after_ref), calls=%async_computation | async-start | bytes 131072 | tf_op jit(solution)/shard_map/all_to_all | solution.py:634
  10.0 2.6 %prepare_weights.1 = (f32[2,4,16,16,128]{4,3,2,1,0:T(8,128)S(1)}, bf16[384,512]{1,0:T(8,128)(2,1)S(1)}, bf16[512,512]{1,0:T(8,128)(2,1)S(1)}) custom-call(bf16[32,8,128]{2,1,0:T(8,128)(2,1)} %forward_modes.1.after_ref, f32[2,4,4,16,16,32]{5,4,3,2,1,0:T(8,128)} %bitcast.8, bf16[3,3,3,32,32]{4,3,2,1,0:T(8,128)(2,1)} %bitcast.9, f32[4,32,512]{2,1,0:T(8,128)} %constant.14.clone.y_hbm), custom_call_target="tpu_custom_call" | custom-call | flops 1024 | bytes 1024 | tf_op jit(solution)/shard_map/prepare_weights/pallas_call | solution.py:368
  12.7 1.0 %copy-done.5 = f32[2,4,16,16,128]{4,3,2,1,0:T(8,128)} copy-done((f32[2,4,16,16,128]{4,3,2,1,0:T(8,128)}, f32[2,4,16,16,128]{4,3,2,1,0:T(8,128)S(1)}, u32[]{:S(2)}) %copy-start.5) | copy-done | bytes 1048600
  13.7 0.6 %arrange_cells.1 = (bf16[32,32,128]{2,1,0:T(8,128)(2,1)S(1)}, bf16[32,32,128]{2,1,0:T(8,128)(2,1)S(1)}) custom-call(bf16[384,512]{1,0:T(8,128)(2,1)S(1)} %get-tuple-element.14.after_ref.refs_4_.refs_6_, bf16[32,2,32,128]{3,2,1,0:T(8,128)(2,1)S(1)} %copy-done), custom_call_target="tpu_custom_call" | custom-call | flops 1024 | bytes 1024 | tf_op jit(solution)/shard_map/arrange_cells/pallas_call | solution.py:453
  14.3 1.8 %collective-permute-start = (bf16[32,32,128]{2,1,0:T(8,128)(2,1)S(1)}, bf16[32,32,128]{2,1,0:T(8,128)(2,1)S(1)}, u32[]{:S(2)}, u32[]{:S(2)}) collective-permute-start(bf16[32,32,128]{2,1,0:T(8,128)(2,1)S(1)} %get-tuple-element.15.refs_1_), channel_id=1, source_target_pairs={{0,4},{4,0},{8,12},{12,8},{16,20},{20,16},{24,28},{28,24},{1,5},{5... | collective-permute-start | bytes 786440 | tf_op jit(solution)/shard_map/ppermute | solution.py:641
  16.2 0.7 %collective-permute-start.1 = (bf16[32,32,128]{2,1,0:T(8,128)(2,1)S(1)}, bf16[32,32,128]{2,1,0:T(8,128)(2,1)S(1)}, u32[]{:S(2)}, u32[]{:S(2)}) collective-permute-start(bf16[32,32,128]{2,1,0:T(8,128)(2,1)S(1)} %get-tuple-element.16.refs_2_), channel_id=1, source_target_pairs={{4,8},{8,4},{12,16},{16,12},{20,24},{24,20},{5,9},{9,5},{13,17},{1... | collective-permute-start | bytes 786440 | tf_op jit(solution)/shard_map/ppermute | solution.py:641
  16.8 0.6 %all-to-all-done.modes_ref = bf16[32,8,128]{2,1,0:T(8,128)(2,1)S(1)} async-done(((bf16[32,8,128]{2,1,0:T(8,128)(2,1)}), bf16[32,8,128]{2,1,0:T(8,128)(2,1)S(1)}, u32[]{:S(2)}, u32[]{:S(2)}) %all-to-all-start) | async-done | bytes 65568 | tf_op jit(solution)/shard_map/all_to_all | solution.py:634
  17.5 1.2 %copy-done.6 = f32[2,4,16,16,128]{4,3,2,1,0:T(8,128)S(1)} copy-done((f32[2,4,16,16,128]{4,3,2,1,0:T(8,128)S(1)}, f32[2,4,16,16,128]{4,3,2,1,0:T(8,128)}, u32[]{:S(2)}) %copy-start.6) | copy-done | bytes 1048600
  18.7 1.6 %mix_modes.1 = bf16[32,16,128]{2,1,0:T(8,128)(2,1)} custom-call(bf16[32,8,128]{2,1,0:T(8,128)(2,1)S(1)} %all-to-all-done.modes_ref, f32[64,256]{1,0:T(8,128)S(1)} %copy-done.8, f32[2,4,16,16,128]{4,3,2,1,0:T(8,128)S(1)} %copy-done.6, f32[128,128]{1,0:T(8,128)S(1)} %copy-done.7), custom_call_target="tpu_custom_call" | custom-call | flops 34359738368 | bytes 2097152 | tf_op jit(solution)/shard_map/mix_modes/pallas_call | solution.py:429
  20.3 6.7 %all-to-all-start.1 = ((bf16[32,16,128]{2,1,0:T(8,128)(2,1)}), bf16[32,16,128]{2,1,0:T(8,128)(2,1)S(1)}, u32[]{:S(2)}, u32[]{:S(2)}) async-start(bf16[32,16,128]{2,1,0:T(8,128)(2,1)} %mix_modes.1), calls=%async_computation.1 | async-start | bytes 262144 | tf_op jit(solution)/shard_map/all_to_all | solution.py:634
  27.0 0.6 %collective-permute-done.refs_0_ = bf16[32,32,128]{2,1,0:T(8,128)(2,1)S(1)} collective-permute-done((bf16[32,32,128]{2,1,0:T(8,128)(2,1)S(1)}, bf16[32,32,128]{2,1,0:T(8,128)(2,1)S(1)}, u32[]{:S(2)}, u32[]{:S(2)}) %collective-permute-start) | collective-permute-done | bytes 262176 | tf_op jit(solution)/shard_map/ppermute | solution.py:641
  27.7 0.0 collective-permute-done.1.refs_3_
  27.7 0.0 copy-start.1
  27.7 0.0 copy-start.4
  27.7 0.1 collective-permute-start.2
  27.8 0.8 %collective-permute-start.3 = (bf16[128,128]{1,0:T(8,128)(2,1)S(1)}, bf16[128,128]{1,0:T(8,128)(2,1)S(1)}, u32[]{:S(2)}, u32[]{:S(2)}) collective-permute-start(bf16[128,128]{1,0:T(8,128)(2,1)S(1)} %get-tuple-element.18), channel_id=1, source_target_pairs={{1,2},{2,1},{5,6},{6,5},{9,10},{10,9},{13,14},{14,13},{17,18},{18,... | collective-permute-start | bytes 98312 | tf_op jit(solution)/shard_map/ppermute | solution.py:641
  28.6 1.3 %convolve_interior.1 = f32[2048,128]{1,0:T(8,128)S(1)} custom-call(bf16[32,32,128]{2,1,0:T(8,128)(2,1)S(1)} %collective-permute-done.refs_0_, bf16[32,32,128]{2,1,0:T(8,128)(2,1)S(1)} %get-tuple-element.15.refs_1_, bf16[32,32,128]{2,1,0:T(8,128)(2,1)S(1)} %get-tuple-element.16.refs_2_, bf16[32,32,128]{2,1,0:T(8,128)(2,1)S(1)} %collective-permute-done.1.refs_3_, ...), custom_call_target="tpu_custom_call" | custom-call | flops 1073741824 | bytes 2097152 | tf_op jit(solution)/shard_map/convolve_interior/pallas_call | solution.py:541
  29.9 0.0 collective-permute-done.2.refs_4_
  30.0 0.0 copy-start.3
  30.0 0.9 %copy-done.3 = bf16[32,32,128]{2,1,0:T(8,128)(2,1)S(1)} copy-done((bf16[32,32,128]{2,1,0:T(8,128)(2,1)S(1)}, bf16[32,32,128]{2,1,0:T(8,128)(2,1)}, u32[]{:S(2)}) %copy-start.3) | copy-done | bytes 262168
  30.9 0.5 %convolve_edges.1 = f32[512,128]{1,0:T(8,128)S(1)} custom-call(bf16[32,32,128]{2,1,0:T(8,128)(2,1)S(1)} %collective-permute-done.refs_0_, bf16[32,32,128]{2,1,0:T(8,128)(2,1)S(1)} %get-tuple-element.15.refs_1_, bf16[32,32,128]{2,1,0:T(8,128)(2,1)S(1)} %get-tuple-element.16.refs_2_, bf16[32,32,128]{2,1,0:T(8,128)(2,1)S(1)} %copy-done.3, ...), custom_call_target="tpu_custom_call" | custom-call | flops 1073741824 | bytes 2097152 | tf_op jit(solution)/shard_map/convolve_edges/pallas_call | solution.py:541
  31.4 3.9 %all-to-all-done.1.values_ref = bf16[32,16,128]{2,1,0:T(8,128)(2,1)S(1)} async-done(((bf16[32,16,128]{2,1,0:T(8,128)(2,1)}), bf16[32,16,128]{2,1,0:T(8,128)(2,1)S(1)}, u32[]{:S(2)}, u32[]{:S(2)}) %all-to-all-start.1) | async-done | bytes 131104 | tf_op jit(solution)/shard_map/all_to_all | solution.py:634
  35.3 2.0 %finish_layer.1 = bf16[32,2,32,128]{3,2,1,0:T(8,128)(2,1)} custom-call(f32[32]{0:T(128)S(1)} %copy-done.4, bf16[32,16,128]{2,1,0:T(8,128)(2,1)S(1)} %all-to-all-done.1.values_ref, f32[128,512]{1,0:T(8,128)S(1)} %copy-done.1, bf16[512,512]{1,0:T(8,128)(2,1)S(1)} %get-tuple-element.13.y_ref, f32[32,2,32,128]{3,2,1,0:T(8,128)S(1)} %bitcast.6, ...), custom_call_target="tpu_custom_call" | custom-call | flops 268435456 | bytes 4194304 | tf_op jit(solution)/shard_map/finish_layer/pallas_call | solution.py:618
  (14 shorter events, 0.0 us)
Async XLA Ops:
  0.0 17.5 %copy-start.7 = (f32[128,128]{1,0:T(8,128)S(1)}, f32[128,128]{1,0:T(8,128)}, u32[]{:S(2)}) copy-start(f32[128,128]{1,0:T(8,128)} %constant.16.clone.inverse_ref) | copy-start | bytes 196612
  0.0 17.5 %copy-start.8 = (f32[64,256]{1,0:T(8,128)S(1)}, f32[64,256]{1,0:T(8,128)}, u32[]{:S(2)}) copy-start(f32[64,256]{1,0:T(8,128)} %constant.15.clone.forward_ref) | copy-start | bytes 196612
  0.0 13.7 %copy-start = (bf16[32,2,32,128]{3,2,1,0:T(8,128)(2,1)S(1)}, bf16[32,2,32,128]{3,2,1,0:T(8,128)(2,1)}, u32[]{:S(2)}) copy-start(bf16[32,2,32,128]{3,2,1,0:T(8,128)(2,1)} %state_ref.1) | copy-start | bytes 1572868
  2.7 14.7 %all-to-all-start = ((bf16[32,8,128]{2,1,0:T(8,128)(2,1)}), bf16[32,8,128]{2,1,0:T(8,128)(2,1)S(1)}, u32[]{:S(2)}, u32[]{:S(2)}) async-start(bf16[32,8,128]{2,1,0:T(8,128)(2,1)} %forward_modes.1.after_ref), calls=%async_computation | async-start | bytes 131072 | tf_op jit(solution)/shard_map/all_to_all | solution.py:634
  12.7 1.0 %copy-start.5 = (f32[2,4,16,16,128]{4,3,2,1,0:T(8,128)}, f32[2,4,16,16,128]{4,3,2,1,0:T(8,128)S(1)}, u32[]{:S(2)}) copy-start(f32[2,4,16,16,128]{4,3,2,1,0:T(8,128)S(1)} %get-tuple-element.12.weight_ref) | copy-start | bytes 3145732
  14.3 13.3 %collective-permute-start = (bf16[32,32,128]{2,1,0:T(8,128)(2,1)S(1)}, bf16[32,32,128]{2,1,0:T(8,128)(2,1)S(1)}, u32[]{:S(2)}, u32[]{:S(2)}) collective-permute-start(bf16[32,32,128]{2,1,0:T(8,128)(2,1)S(1)} %get-tuple-element.15.refs_1_), channel_id=1, source_target_pairs={{0,4},{4,0},{8,12},{12,8},{16,20},{20,16},{24,28},{28,24},{1,5},{5... | collective-permute-start | bytes 786440 | tf_op jit(solution)/shard_map/ppermute | solution.py:641
  16.2 11.5 %collective-permute-start.1 = (bf16[32,32,128]{2,1,0:T(8,128)(2,1)S(1)}, bf16[32,32,128]{2,1,0:T(8,128)(2,1)S(1)}, u32[]{:S(2)}, u32[]{:S(2)}) collective-permute-start(bf16[32,32,128]{2,1,0:T(8,128)(2,1)S(1)} %get-tuple-element.16.refs_2_), channel_id=1, source_target_pairs={{4,8},{8,4},{12,16},{16,12},{20,24},{24,20},{5,9},{9,5},{13,17},{1... | collective-permute-start | bytes 786440 | tf_op jit(solution)/shard_map/ppermute | solution.py:641
  17.5 1.2 %copy-start.6 = (f32[2,4,16,16,128]{4,3,2,1,0:T(8,128)S(1)}, f32[2,4,16,16,128]{4,3,2,1,0:T(8,128)}, u32[]{:S(2)}) copy-start(f32[2,4,16,16,128]{4,3,2,1,0:T(8,128)} %copy-done.5) | copy-start | bytes 3145732
  20.3 15.0 %all-to-all-start.1 = ((bf16[32,16,128]{2,1,0:T(8,128)(2,1)}), bf16[32,16,128]{2,1,0:T(8,128)(2,1)S(1)}, u32[]{:S(2)}, u32[]{:S(2)}) async-start(bf16[32,16,128]{2,1,0:T(8,128)(2,1)} %mix_modes.1), calls=%async_computation.1 | async-start | bytes 262144 | tf_op jit(solution)/shard_map/all_to_all | solution.py:634
  27.7 2.3 %copy-start.2 = (bf16[32,32,128]{2,1,0:T(8,128)(2,1)}, bf16[32,32,128]{2,1,0:T(8,128)(2,1)S(1)}, u32[]{:S(2)}) copy-start(bf16[32,32,128]{2,1,0:T(8,128)(2,1)S(1)} %collective-permute-done.1.refs_3_) | copy-start | bytes 786436
  27.7 7.6 %copy-start.1 = (f32[128,512]{1,0:T(8,128)S(1)}, f32[128,512]{1,0:T(8,128)}, u32[]{:S(2)}) copy-start(f32[128,512]{1,0:T(8,128)} %constant.17.clone.z_ref) | copy-start | bytes 786436
  27.7 7.6 %copy-start.4 = (f32[32]{0:T(128)S(1)}, f32[32]{0:T(128)}, u32[]{:S(2)}) copy-start(f32[32]{0:T(128)} %bias_ref.1) | copy-start | bytes 388
  27.7 2.2 %collective-permute-start.2 = (bf16[128,128]{1,0:T(8,128)(2,1)S(1)}, bf16[128,128]{1,0:T(8,128)(2,1)S(1)}, u32[]{:S(2)}, u32[]{:S(2)}) collective-permute-start(bf16[128,128]{1,0:T(8,128)(2,1)S(1)} %get-tuple-element.17), channel_id=1, source_target_pairs={{0,1},{1,0},{2,3},{3,2},{4,5},{5,4},{6,7},{7,6},{8,9},{9,8},{10,11... | collective-permute-start | bytes 98312 | tf_op jit(solution)/shard_map/ppermute | solution.py:641
  27.8 2.2 %collective-permute-start.3 = (bf16[128,128]{1,0:T(8,128)(2,1)S(1)}, bf16[128,128]{1,0:T(8,128)(2,1)S(1)}, u32[]{:S(2)}, u32[]{:S(2)}) collective-permute-start(bf16[128,128]{1,0:T(8,128)(2,1)S(1)} %get-tuple-element.18), channel_id=1, source_target_pairs={{1,2},{2,1},{5,6},{6,5},{9,10},{10,9},{13,14},{14,13},{17,18},{18,... | collective-permute-start | bytes 98312 | tf_op jit(solution)/shard_map/ppermute | solution.py:641
  30.0 1.0 %copy-start.3 = (bf16[32,32,128]{2,1,0:T(8,128)(2,1)S(1)}, bf16[32,32,128]{2,1,0:T(8,128)(2,1)}, u32[]{:S(2)}) copy-start(bf16[32,32,128]{2,1,0:T(8,128)(2,1)} %copy-done.2) | copy-start | bytes 786436

commit v4 on v3

--- a/solution.py
+++ b/solution.py
@@ -306,21 +306,21 @@
 
 def prepare_kernel(
     after_ref,
+    state_hbm,
     weight_hbm,
     conv_hbm,
-    y_hbm,
+    first_ref,
+    second_ref,
+    conv_out,
     weight_out,
-    conv_out,
-    y_out,
+    state_ref,
     weight_ref,
     conv_ref,
-    y_ref,
+    wide,
     sems,
 ):
-    conv_copy = pltpu.make_async_copy(conv_hbm, conv_ref, sems.at[8])
-    y_copy = pltpu.make_async_copy(y_hbm.at[lax.axis_index("py")], y_ref, sems.at[9])
-    conv_copy.start()
-    y_copy.start()
+    state_copy = pltpu.make_async_copy(state_hbm, state_ref, sems.at[8])
+    conv_copy = pltpu.make_async_copy(conv_hbm, conv_ref, sems.at[9])
     copies = [
         pltpu.make_async_copy(
             weight_hbm.at[part, kz], weight_ref.at[part, kz], sems.at[part * 4 + kz]
@@ -328,9 +328,15 @@
         for part in range(2)
         for kz in range(4)
     ]
-    for copy in copies:
+    for copy in [state_copy, conv_copy] + copies:
         copy.start()
-    odd_x = lax.rem(lax.axis_index("px"), 2) == 1
+    odd_x = lax.rem(lax.axis_index("px"), 2)
+    state_copy.wait()
+    cells_y = state_ref.shape[2]
+    for slot, (out_ref, x) in enumerate(((first_ref, 1 - odd_x), (second_ref, odd_x))):
+        wide[slot] = state_ref[:, x].astype(jnp.float32).reshape(32 * cells_y, 128)
+        for y in range(cells_y):
+            out_ref[y] = wide[slot, pl.ds(y, 32, stride=cells_y), :].astype(jnp.bfloat16)
     conv_copy.wait()
     zero = jnp.zeros((32, 32), jnp.float32)
     for dz in range(3):
@@ -344,16 +350,10 @@
                 row = ((dz * 2 + y_at) * 2 + x_at) * 32
                 for y_in in range(4):
                     blocks = [taps.get((x_in - x_at, y_in - y_at), zero) for x_in in range(4)]
-                    blocks = [jnp.where(odd_x, blocks[i], blocks[3 - i]) for i in range(4)]
+                    blocks = [jnp.where(odd_x == 1, blocks[i], blocks[3 - i]) for i in range(4)]
                     conv_out[row : row + 32, y_in * 128 : (y_in + 1) * 128] = jnp.concatenate(
                         blocks, axis=1
                     ).astype(jnp.bfloat16)
-    y_copy.wait()
-    table = y_ref[...]
-    lane = lax.broadcasted_iota(jnp.int32, table.shape, 1) % 16
-    span = table.shape[0]
-    for o in range(16):
-        y_out[o * span : (o + 1) * span] = jnp.where(lane == o, table, 0.0).astype(jnp.bfloat16)
     for part in range(2):
         for kz in range(4):
             copies[part * 4 + kz].wait()
@@ -363,31 +363,35 @@
                 )
 
 
-def prepare(after, spectral_weight, conv_weight, y_table):
+def prepare(after, state, spectral_weight, conv_weight):
     vmem = pl.BlockSpec(memory_space=pltpu.VMEM)
+    cells_y = state.shape[2]
+    plane = jax.ShapeDtypeStruct((cells_y, 32, 128), jnp.bfloat16)
     return pl.pallas_call(
         prepare_kernel,
         out_shape=(
+            plane,
+            plane,
+            jax.ShapeDtypeStruct((384, 512), jnp.bfloat16),
             jax.ShapeDtypeStruct((2, 4, 16, KX, 128), jnp.float32),
-            jax.ShapeDtypeStruct((384, 512), jnp.bfloat16),
-            jax.ShapeDtypeStruct((16 * y_table.shape[1], y_table.shape[2]), jnp.bfloat16),
         ),
         in_specs=[pl.BlockSpec(memory_space=pl.ANY)] + [pl.BlockSpec(memory_space=pltpu.HBM)] * 3,
-        out_specs=(vmem,) * 3,
+        out_specs=(vmem,) * 4,
         scratch_shapes=[
+            pltpu.VMEM(state.shape, jnp.bfloat16),
             pltpu.VMEM(spectral_weight.shape, jnp.float32),
             pltpu.VMEM(conv_weight.shape, jnp.bfloat16),
-            pltpu.VMEM(y_table.shape[1:], jnp.float32),
+            pltpu.VMEM((2, 32 * cells_y, 128), jnp.float32),
             pltpu.SemaphoreType.DMA((10,)),
         ],
         compiler_params=pltpu.CompilerParams(vmem_limit_bytes=16 * 2**20),
         cost_estimate=pl.CostEstimate(flops=2**10, bytes_accessed=2**10, transcendentals=0),
-        name="prepare_weights",
+        name="prepare_operands",
     )(
         after,
         *(
             pltpu.with_memory_space_constraint(v, pltpu.HBM)
-            for v in (spectral_weight, conv_weight, y_table)
+            for v in (state, spectral_weight, conv_weight)
         ),
     )
 
@@ -437,31 +441,6 @@
     )(modes, forward_table, weights, inverse_table)
 
 
-def arrange_kernel(after_ref, state_ref, first_ref, second_ref, wide):
-    cells_y = state_ref.shape[2]
-    odd_x = lax.rem(lax.axis_index("px"), 2)
-    for out_ref, x in ((first_ref, 1 - odd_x), (second_ref, odd_x)):
-        wide[...] = state_ref[:, x].astype(jnp.float32).reshape(32 * cells_y, 128)
-        for y in range(cells_y):
-            out_ref[y] = wide[pl.ds(y, 32, stride=cells_y), :].astype(jnp.bfloat16)
-
-
-def arrange(after, state):
-    vmem = pl.BlockSpec(memory_space=pltpu.VMEM)
-    cells_y = state.shape[2]
-    plane = jax.ShapeDtypeStruct((cells_y, 32, 128), jnp.bfloat16)
-    return pl.pallas_call(
-        arrange_kernel,
-        out_shape=(plane, plane),
-        in_specs=[pl.BlockSpec(memory_space=pl.ANY), vmem],
-        out_specs=(vmem, vmem),
-        scratch_shapes=[pltpu.VMEM((32 * cells_y, 128), jnp.float32)],
-        compiler_params=pltpu.CompilerParams(vmem_limit_bytes=16 * 2**20),
-        cost_estimate=pl.CostEstimate(flops=2**10, bytes_accessed=2**10, transcendentals=0),
-        name="arrange_cells",
-    )(after, state)
-
-
 def cell_row(planes, y):
     return jnp.concatenate([plane[y] for plane in planes], axis=0)
 
@@ -510,8 +489,14 @@
 
 
 def interior_kernel(*refs):
-    *planes, weight_ref, out_ref = refs
+    *planes, weight_ref, y_ref, out_ref, y_out = refs
     cells_y = planes[0].shape[0]
+    table = y_ref[lax.axis_index("py")]
+    lane = lax.broadcasted_iota(jnp.int32, table.shape, 1) % 16
+    for o in range(16):
+        y_out[o * cells_y : (o + 1) * cells_y] = jnp.where(lane == o, table, 0.0).astype(
+            jnp.bfloat16
+        )
     weight = weight_ref[...]
     for quad in range(1, cells_y // 4 - 1):
         convolve_quad(
@@ -536,13 +521,13 @@
         convolve_quad(quad, row, weight, lambda y: (y % 8, 8), out_ref)
 
 
-def convolve(kernel, name, operands, rows):
+def convolve(kernel, name, operands, out_shape):
     vmem = pl.BlockSpec(memory_space=pltpu.VMEM)
     return pl.pallas_call(
         kernel,
-        out_shape=jax.ShapeDtypeStruct((rows, 128), jnp.float32),
+        out_shape=out_shape,
         in_specs=[vmem] * len(operands),
-        out_specs=vmem,
+        out_specs=(vmem,) * len(out_shape),
         compiler_params=pltpu.CompilerParams(vmem_limit_bytes=16 * 2**20),
         cost_estimate=pl.CostEstimate(flops=2**30, bytes_accessed=2**21, transcendentals=0),
         name=name,
@@ -651,18 +636,28 @@
         state_field.reshape(channels * cells_x, cells_y, depth), z_forward, y_forward
     )
     modes = exchanged(sent)
-    weights, taps, y_expanded = prepare(
-        sent, spectral_weight.swapaxes(4, 5), conv_weight.transpose(2, 3, 4, 0, 1), y_inverse
-    )
-    first_own, second_own = arrange(taps, state_field)
+    first_own, second_own, taps, weights = prepare(
+        sent, state_field, spectral_weight.swapaxes(4, 5), conv_weight.transpose(2, 3, 4, 0, 1)
+    )
     first_plane, second_plane = swaps(first_own, second_own, "px")
     values = exchanged(mix_modes(modes, x_forward, weights, x_inverse))
     planes = (first_plane, first_own, second_own, second_plane)
     first_row, second_row = swaps(*edge_rows(planes), "py")
-    rows = channels * cells_x * cells_y
-    interior = convolve(interior_kernel, "convolve_interior", planes + (taps,), rows)
-    edges = convolve(
-        edge_kernel, "convolve_edges", planes + (first_row, second_row, taps), rows // cells_y * 8
+    rows = channels * cells_x
+    interior, y_expanded = convolve(
+        interior_kernel,
+        "convolve_interior",
+        planes + (taps, y_inverse),
+        (
+            jax.ShapeDtypeStruct((rows * cells_y, depth), jnp.float32),
+            jax.ShapeDtypeStruct((16 * cells_y, y_inverse.shape[2]), jnp.bfloat16),
+        ),
+    )
+    (edges,) = convolve(
+        edge_kernel,
+        "convolve_edges",
+        planes + (first_row, second_row, taps),
+        (jax.ShapeDtypeStruct((rows * 8, depth), jnp.float32),),
     )
     return finish(
         conv_bias,

time: 37.6 us -> 35.7 us (0.949)
  local copies, waits for them, and re-layouts: 3.17 us -> 1.02 us
  starting transfers between devices: 17.4 us -> 16.2 us
  waiting for transfers between devices: 5.11 us -> 6.21 us
    unnamed x18 -> x14, local copies, waits for them, and re-layouts: 3.17 us -> 1.02 us
    ppermute x2, waiting for transfers between devices: 0.63 us -> 2.06 us  [swaps(): lax.ppermute(first, axis, inside)]
    all_to_all x2, starting transfers between devices: 14 us -> 13 us  [exchanged(): lax.all_to_all(value, ('px', 'py'), split_axis=0, concat_axis=0, tiled=True)]
    pallas_call x4 -> x3, Pallas kernels: 5.1 us -> 5.17 us  [the longest x1 3.33 us: prepare(): pl.pallas_call(prepare_kernel, out_shape=(plane, plane, jax.ShapeDtypeStr...]
  transfers between devices with their start and end apart: 6 -> 6, of which waited for: 3 -> 3; matrix products, arithmetic and copies ran while one was open for 0% -> 0% of each run, Pallas kernels for 18% -> 19%
where the time goes in v4:
time: 35.7 us; the launch traced here: 35.1 us
  starting transfers between devices  16.2 us (45%)
  Pallas kernels  11.5 us (32%)
  waiting for transfers between devices  6.21 us (17%)
  local copies, waits for them, and re-layouts  1.02 us (3%)
    all_to_all x2, starting transfers between devices, exchanged(): lax.all_to_all(value, ('px', 'py'), split_axis=0, concat_axis=0, tiled=True)  13 us
    all_to_all x2, waiting for transfers between devices, exchanged(): lax.all_to_all(value, ('px', 'py'), split_axis=0, concat_axis=0, tiled=True)  4.15 us
    pallas_call x1, Pallas kernels, prepare(): pl.pallas_call(prepare_kernel, out_shape=(plane, plane, jax.ShapeDtypeStr...  3.33 us
    pallas_call x1, Pallas kernels, forward_modes(): pl.pallas_call(forward_kernel, out_shape=jax.ShapeDtypeStruct((32, 8, 128...  2.68 us
    ppermute x2, waiting for transfers between devices, swaps(): lax.ppermute(first, axis, inside)  2.06 us
    pallas_call x1, Pallas kernels, finish(): pl.pallas_call(finish_kernel, out_shape=jax.ShapeDtypeStruct(convolved.sh...  2.03 us
    ppermute x2, starting transfers between devices, swaps(): lax.ppermute(first, axis, inside)  1.9 us
    pallas_call x2, Pallas kernels, convolve(): pl.pallas_call(kernel, out_shape=out_shape, in_specs=[vmem] * len(operand...  1.84 us
  transfers between devices with their start and end apart: 6, of which 3 were waited for; matrix products, arithmetic and copies ran while one was open for 0% of the time, Pallas kernels for 19%

profile of v4, /device:TPU:0, one launch (start us, length us, event | category | flops | bytes accessed | tf_op | source)
XLA Modules:
  0.0 35.1 jit_solution(3551796317694949847)
XLA Ops:
  0.0 2.7 %forward_modes.1.after_ref = bf16[32,8,128]{2,1,0:T(8,128)(2,1)} custom-call(bf16[64,32,128]{2,1,0:T(8,128)(2,1)} %bitcast.8, f32[32,128]{1,0:T(8,128)} %constant.12.clone.z_hbm, f32[4,64,512]{2,1,0:T(8,128)} %constant.13.clone.y_hbm), custom_call_target="tpu_custom_call" | custom-call | flops 134217728 | bytes 2097152 | tf_op jit(solution)/shard_map/forward_modes/pallas_call | solution.py:289
  2.7 7.3 %all-to-all-start = ((bf16[32,8,128]{2,1,0:T(8,128)(2,1)}), bf16[32,8,128]{2,1,0:T(8,128)(2,1)S(1)}, u32[]{:S(2)}, u32[]{:S(2)}) async-start(bf16[32,8,128]{2,1,0:T(8,128)(2,1)} %forward_modes.1.after_ref), calls=%async_computation | async-start | bytes 131072 | tf_op jit(solution)/shard_map/all_to_all | solution.py:619
  10.0 3.3 %prepare_operands.1 = (bf16[32,32,128]{2,1,0:T(8,128)(2,1)S(1)}, bf16[32,32,128]{2,1,0:T(8,128)(2,1)S(1)}, bf16[384,512]{1,0:T(8,128)(2,1)S(1)}, f32[2,4,16,16,128]{4,3,2,1,0:T(8,128)S(1)}) custom-call(bf16[32,8,128]{2,1,0:T(8,128)(2,1)} %forward_modes.1.after_ref, bf16[32,2,32,128]{3,2,1,0:T(8,128)(2,1)} %state_hbm.1, f32[2,4,4,16,16,32]{5,4,3,2,1,0:T(8,128)} %bitcast.7, ...), custom_call_target="tpu_custom_call" | custom-call | flops 1024 | bytes 1024 | tf_op jit(solution)/shard_map/prepare_operands/pallas_call | solution.py:370
  13.3 0.0 copy-start.2
  13.4 1.8 %collective-permute-start = (bf16[32,32,128]{2,1,0:T(8,128)(2,1)S(1)}, bf16[32,32,128]{2,1,0:T(8,128)(2,1)S(1)}, u32[]{:S(2)}, u32[]{:S(2)}) collective-permute-start(bf16[32,32,128]{2,1,0:T(8,128)(2,1)S(1)} %get-tuple-element.14.refs_1_), channel_id=1, source_target_pairs={{0,4},{4,0},{8,12},{12,8},{16,20},{20,16},{24,28},{28,24},{1,5},{5... | collective-permute-start | bytes 786440 | tf_op jit(solution)/shard_map/ppermute | solution.py:626
  15.2 0.7 %collective-permute-start.1 = (bf16[32,32,128]{2,1,0:T(8,128)(2,1)S(1)}, bf16[32,32,128]{2,1,0:T(8,128)(2,1)S(1)}, u32[]{:S(2)}, u32[]{:S(2)}) collective-permute-start(bf16[32,32,128]{2,1,0:T(8,128)(2,1)S(1)} %get-tuple-element.15.refs_2_), channel_id=1, source_target_pairs={{4,8},{8,4},{12,16},{16,12},{20,24},{24,20},{5,9},{9,5},{13,17},{1... | collective-permute-start | bytes 786440 | tf_op jit(solution)/shard_map/ppermute | solution.py:626
  15.9 1.7 %all-to-all-done.modes_ref = bf16[32,8,128]{2,1,0:T(8,128)(2,1)S(1)} async-done(((bf16[32,8,128]{2,1,0:T(8,128)(2,1)}), bf16[32,8,128]{2,1,0:T(8,128)(2,1)S(1)}, u32[]{:S(2)}, u32[]{:S(2)}) %all-to-all-start) | async-done | bytes 65568 | tf_op jit(solution)/shard_map/all_to_all | solution.py:619
  17.5 1.6 %mix_modes.1 = bf16[32,16,128]{2,1,0:T(8,128)(2,1)} custom-call(bf16[32,8,128]{2,1,0:T(8,128)(2,1)S(1)} %all-to-all-done.modes_ref, f32[64,256]{1,0:T(8,128)S(1)} %copy-done.6, f32[2,4,16,16,128]{4,3,2,1,0:T(8,128)S(1)} %get-tuple-element.13.weight_ref, f32[128,128]{1,0:T(8,128)S(1)} %copy-done.5), custom_call_target="tpu_custom_call" | custom-call | flops 34359738368 | bytes 2097152 | tf_op jit(solution)/shard_map/mix_modes/pallas_call | solution.py:433
  19.1 5.7 %all-to-all-start.1 = ((bf16[32,16,128]{2,1,0:T(8,128)(2,1)}), bf16[32,16,128]{2,1,0:T(8,128)(2,1)S(1)}, u32[]{:S(2)}, u32[]{:S(2)}) async-start(bf16[32,16,128]{2,1,0:T(8,128)(2,1)} %mix_modes.1), calls=%async_computation.1 | async-start | bytes 262144 | tf_op jit(solution)/shard_map/all_to_all | solution.py:619
  24.8 2.1 %collective-permute-done.refs_0_ = bf16[32,32,128]{2,1,0:T(8,128)(2,1)S(1)} collective-permute-done((bf16[32,32,128]{2,1,0:T(8,128)(2,1)S(1)}, bf16[32,32,128]{2,1,0:T(8,128)(2,1)S(1)}, u32[]{:S(2)}, u32[]{:S(2)}) %collective-permute-start) | collective-permute-done | bytes 262176 | tf_op jit(solution)/shard_map/ppermute | solution.py:626
  26.9 0.0 collective-permute-done.1.refs_3_
  26.9 0.0 copy-start
  26.9 0.0 copy-start.1
  27.0 0.1 collective-permute-start.2
  27.0 0.7 %collective-permute-start.3 = (bf16[128,128]{1,0:T(8,128)(2,1)S(1)}, bf16[128,128]{1,0:T(8,128)(2,1)S(1)}, u32[]{:S(2)}, u32[]{:S(2)}) collective-permute-start(bf16[128,128]{1,0:T(8,128)(2,1)S(1)} %get-tuple-element.20), channel_id=1, source_target_pairs={{1,2},{2,1},{5,6},{6,5},{9,10},{10,9},{13,14},{14,13},{17,18},{18,... | collective-permute-start | bytes 98312 | tf_op jit(solution)/shard_map/ppermute | solution.py:626
  27.7 0.0 copy-start.3
  27.7 1.0 %copy-done.3 = bf16[384,512]{1,0:T(8,128)(2,1)S(1)} copy-done((bf16[384,512]{1,0:T(8,128)(2,1)S(1)}, bf16[384,512]{1,0:T(8,128)(2,1)}, u32[]{:S(2)}) %copy-start.3) | copy-done | bytes 393240
  28.7 1.3 %convolve_interior.1 = (f32[2048,128]{1,0:T(8,128)S(1)}, bf16[512,512]{1,0:T(8,128)(2,1)S(1)}) custom-call(bf16[32,32,128]{2,1,0:T(8,128)(2,1)S(1)} %collective-permute-done.refs_0_, bf16[32,32,128]{2,1,0:T(8,128)(2,1)S(1)} %get-tuple-element.14.refs_1_, bf16[32,32,128]{2,1,0:T(8,128)(2,1)S(1)} %get-tuple-element.15.refs_2_, ...), custom_call_target="tpu_custom_call" | custom-call | flops 1073741824 | bytes 2097152 | tf_op jit(solution)/shard_map/convolve_interior/pallas_call | solution.py:526
  30.1 0.0 collective-permute-done.2.refs_4_
  30.1 0.0 collective-permute-done.3.refs_5_
  30.1 0.5 %convolve_edges.1 = f32[512,128]{1,0:T(8,128)S(1)} custom-call(bf16[32,32,128]{2,1,0:T(8,128)(2,1)S(1)} %collective-permute-done.refs_0_, bf16[32,32,128]{2,1,0:T(8,128)(2,1)S(1)} %get-tuple-element.14.refs_1_, bf16[32,32,128]{2,1,0:T(8,128)(2,1)S(1)} %get-tuple-element.15.refs_2_, bf16[32,32,128]{2,1,0:T(8,128)(2,1)S(1)} %collective-permute-done.1.refs_3_, ...), custom_call_target="tpu_custom_call" | custom-call | flops 1073741824 | bytes 2097152 | tf_op jit(solution)/shard_map/convolve_edges/pallas_call | solution.py:526
  30.6 2.5 %all-to-all-done.1.values_ref = bf16[32,16,128]{2,1,0:T(8,128)(2,1)S(1)} async-done(((bf16[32,16,128]{2,1,0:T(8,128)(2,1)}), bf16[32,16,128]{2,1,0:T(8,128)(2,1)S(1)}, u32[]{:S(2)}, u32[]{:S(2)}) %all-to-all-start.1) | async-done | bytes 131104 | tf_op jit(solution)/shard_map/all_to_all | solution.py:619
  33.1 0.0 copy-done
  33.1 2.0 %finish_layer.1 = bf16[32,2,32,128]{3,2,1,0:T(8,128)(2,1)} custom-call(f32[32]{0:T(128)S(1)} %copy-done.1, bf16[32,16,128]{2,1,0:T(8,128)(2,1)S(1)} %all-to-all-done.1.values_ref, f32[128,512]{1,0:T(8,128)S(1)} %copy-done, bf16[512,512]{1,0:T(8,128)(2,1)S(1)} %get-tuple-element.17.y_ref, f32[32,2,32,128]{3,2,1,0:T(8,128)S(1)} %bitcast.5, ...), custom_call_target="tpu_custom_call" | custom-call | flops 268435456 | bytes 4194304 | tf_op jit(solution)/shard_map/finish_layer/pallas_call | solution.py:603
  (9 shorter events, 0.0 us)
Async XLA Ops:
  0.0 17.5 %copy-start.5 = (f32[128,128]{1,0:T(8,128)S(1)}, f32[128,128]{1,0:T(8,128)}, u32[]{:S(2)}) copy-start(f32[128,128]{1,0:T(8,128)} %constant.15.clone.inverse_ref) | copy-start | bytes 196612
  0.0 17.5 %copy-start.6 = (f32[64,256]{1,0:T(8,128)S(1)}, f32[64,256]{1,0:T(8,128)}, u32[]{:S(2)}) copy-start(f32[64,256]{1,0:T(8,128)} %constant.14.clone.forward_ref) | copy-start | bytes 196612
  2.7 14.8 %all-to-all-start = ((bf16[32,8,128]{2,1,0:T(8,128)(2,1)}), bf16[32,8,128]{2,1,0:T(8,128)(2,1)S(1)}, u32[]{:S(2)}, u32[]{:S(2)}) async-start(bf16[32,8,128]{2,1,0:T(8,128)(2,1)} %forward_modes.1.after_ref), calls=%async_computation | async-start | bytes 131072 | tf_op jit(solution)/shard_map/all_to_all | solution.py:619
  13.3 5.8 %copy-start.2 = (bf16[384,512]{1,0:T(8,128)(2,1)}, bf16[384,512]{1,0:T(8,128)(2,1)S(1)}, u32[]{:S(2)}) copy-start(bf16[384,512]{1,0:T(8,128)(2,1)S(1)} %get-tuple-element.16.refs_4_.refs_6_) | copy-start | bytes 1179652
  13.4 13.6 %collective-permute-start = (bf16[32,32,128]{2,1,0:T(8,128)(2,1)S(1)}, bf16[32,32,128]{2,1,0:T(8,128)(2,1)S(1)}, u32[]{:S(2)}, u32[]{:S(2)}) collective-permute-start(bf16[32,32,128]{2,1,0:T(8,128)(2,1)S(1)} %get-tuple-element.14.refs_1_), channel_id=1, source_target_pairs={{0,4},{4,0},{8,12},{12,8},{16,20},{20,16},{24,28},{28,24},{1,5},{5... | collective-permute-start | bytes 786440 | tf_op jit(solution)/shard_map/ppermute | solution.py:626
  15.2 11.7 %collective-permute-start.1 = (bf16[32,32,128]{2,1,0:T(8,128)(2,1)S(1)}, bf16[32,32,128]{2,1,0:T(8,128)(2,1)S(1)}, u32[]{:S(2)}, u32[]{:S(2)}) collective-permute-start(bf16[32,32,128]{2,1,0:T(8,128)(2,1)S(1)} %get-tuple-element.15.refs_2_), channel_id=1, source_target_pairs={{4,8},{8,4},{12,16},{16,12},{20,24},{24,20},{5,9},{9,5},{13,17},{1... | collective-permute-start | bytes 786440 | tf_op jit(solution)/shard_map/ppermute | solution.py:626
  17.5 10.2 %copy-start.4 = (f32[4,32,512]{2,1,0:T(8,128)S(1)}, f32[4,32,512]{2,1,0:T(8,128)}, u32[]{:S(2)}) copy-start(f32[4,32,512]{2,1,0:T(8,128)} %constant.16.clone.refs_5_) | copy-start | bytes 786436
  19.1 13.9 %all-to-all-start.1 = ((bf16[32,16,128]{2,1,0:T(8,128)(2,1)}), bf16[32,16,128]{2,1,0:T(8,128)(2,1)S(1)}, u32[]{:S(2)}, u32[]{:S(2)}) async-start(bf16[32,16,128]{2,1,0:T(8,128)(2,1)} %mix_modes.1), calls=%async_computation.1 | async-start | bytes 262144 | tf_op jit(solution)/shard_map/all_to_all | solution.py:619
  26.9 6.2 %copy-start = (f32[128,512]{1,0:T(8,128)S(1)}, f32[128,512]{1,0:T(8,128)}, u32[]{:S(2)}) copy-start(f32[128,512]{1,0:T(8,128)} %constant.17.clone.z_ref) | copy-start | bytes 786436
  26.9 6.1 %copy-start.1 = (f32[32]{0:T(128)S(1)}, f32[32]{0:T(128)}, u32[]{:S(2)}) copy-start(f32[32]{0:T(128)} %bias_ref.1) | copy-start | bytes 388
  27.0 3.1 %collective-permute-start.2 = (bf16[128,128]{1,0:T(8,128)(2,1)S(1)}, bf16[128,128]{1,0:T(8,128)(2,1)S(1)}, u32[]{:S(2)}, u32[]{:S(2)}) collective-permute-start(bf16[128,128]{1,0:T(8,128)(2,1)S(1)} %get-tuple-element.19), channel_id=1, source_target_pairs={{0,1},{1,0},{2,3},{3,2},{4,5},{5,4},{6,7},{7,6},{8,9},{9,8},{10,11... | collective-permute-start | bytes 98312 | tf_op jit(solution)/shard_map/ppermute | solution.py:626
  27.0 3.0 %collective-permute-start.3 = (bf16[128,128]{1,0:T(8,128)(2,1)S(1)}, bf16[128,128]{1,0:T(8,128)(2,1)S(1)}, u32[]{:S(2)}, u32[]{:S(2)}) collective-permute-start(bf16[128,128]{1,0:T(8,128)(2,1)S(1)} %get-tuple-element.20), channel_id=1, source_target_pairs={{1,2},{2,1},{5,6},{6,5},{9,10},{10,9},{13,14},{14,13},{17,18},{18,... | collective-permute-start | bytes 98312 | tf_op jit(solution)/shard_map/ppermute | solution.py:626
  27.7 1.0 %copy-start.3 = (bf16[384,512]{1,0:T(8,128)(2,1)S(1)}, bf16[384,512]{1,0:T(8,128)(2,1)}, u32[]{:S(2)}) copy-start(bf16[384,512]{1,0:T(8,128)(2,1)} %copy-done.2) | copy-start | bytes 1179652

commit v5 on v4

--- a/solution.py
+++ b/solution.py
@@ -304,40 +304,13 @@
     )(*(pltpu.with_memory_space_constraint(v, pltpu.HBM) for v in (state, z_table, y_table)))
 
 
-def prepare_kernel(
-    after_ref,
-    state_hbm,
-    weight_hbm,
-    conv_hbm,
-    first_ref,
-    second_ref,
-    conv_out,
-    weight_out,
-    state_ref,
-    weight_ref,
-    conv_ref,
-    wide,
-    sems,
-):
-    state_copy = pltpu.make_async_copy(state_hbm, state_ref, sems.at[8])
-    conv_copy = pltpu.make_async_copy(conv_hbm, conv_ref, sems.at[9])
-    copies = [
-        pltpu.make_async_copy(
-            weight_hbm.at[part, kz], weight_ref.at[part, kz], sems.at[part * 4 + kz]
-        )
-        for part in range(2)
-        for kz in range(4)
-    ]
-    for copy in [state_copy, conv_copy] + copies:
-        copy.start()
+def arrange_kernel(after_ref, state_ref, conv_ref, first_ref, second_ref, conv_out, wide):
     odd_x = lax.rem(lax.axis_index("px"), 2)
-    state_copy.wait()
     cells_y = state_ref.shape[2]
-    for slot, (out_ref, x) in enumerate(((first_ref, 1 - odd_x), (second_ref, odd_x))):
+    for slot, (out_ref, x) in enumerate(((first_ref, odd_x), (second_ref, 1 - odd_x))):
         wide[slot] = state_ref[:, x].astype(jnp.float32).reshape(32 * cells_y, 128)
         for y in range(cells_y):
             out_ref[y] = wide[slot, pl.ds(y, 32, stride=cells_y), :].astype(jnp.bfloat16)
-    conv_copy.wait()
     zero = jnp.zeros((32, 32), jnp.float32)
     for dz in range(3):
         taps = {
@@ -350,50 +323,48 @@
                 row = ((dz * 2 + y_at) * 2 + x_at) * 32
                 for y_in in range(4):
                     blocks = [taps.get((x_in - x_at, y_in - y_at), zero) for x_in in range(4)]
-                    blocks = [jnp.where(odd_x == 1, blocks[i], blocks[3 - i]) for i in range(4)]
+                    blocks = [jnp.where(odd_x == 1, blocks[3 - i], blocks[i]) for i in range(4)]
                     conv_out[row : row + 32, y_in * 128 : (y_in + 1) * 128] = jnp.concatenate(
                         blocks, axis=1
                     ).astype(jnp.bfloat16)
+
+
+def arrange(after, state, conv_weight):
+    vmem = pl.BlockSpec(memory_space=pltpu.VMEM)
+    cells_y = state.shape[2]
+    plane = jax.ShapeDtypeStruct((cells_y, 32, 128), jnp.bfloat16)
+    return pl.pallas_call(
+        arrange_kernel,
+        out_shape=(plane, plane, jax.ShapeDtypeStruct((384, 512), jnp.bfloat16)),
+        in_specs=[pl.BlockSpec(memory_space=pl.ANY), vmem, vmem],
+        out_specs=(vmem,) * 3,
+        scratch_shapes=[pltpu.VMEM((2, 32 * cells_y, 128), jnp.float32)],
+        compiler_params=pltpu.CompilerParams(vmem_limit_bytes=16 * 2**20),
+        cost_estimate=pl.CostEstimate(flops=2**10, bytes_accessed=2**10, transcendentals=0),
+        name="arrange_cells",
+    )(after, state, conv_weight)
+
+
+def pack_kernel(after_ref, weight_ref, weight_out):
     for part in range(2):
         for kz in range(4):
-            copies[part * 4 + kz].wait()
             for c in range(16):
                 weight_out[part, kz, c] = jnp.concatenate(
                     [weight_ref[part, kz, u, c] for u in range(4)], axis=1
                 )
 
 
-def prepare(after, state, spectral_weight, conv_weight):
+def pack(after, spectral_weight):
     vmem = pl.BlockSpec(memory_space=pltpu.VMEM)
-    cells_y = state.shape[2]
-    plane = jax.ShapeDtypeStruct((cells_y, 32, 128), jnp.bfloat16)
     return pl.pallas_call(
-        prepare_kernel,
-        out_shape=(
-            plane,
-            plane,
-            jax.ShapeDtypeStruct((384, 512), jnp.bfloat16),
-            jax.ShapeDtypeStruct((2, 4, 16, KX, 128), jnp.float32),
-        ),
-        in_specs=[pl.BlockSpec(memory_space=pl.ANY)] + [pl.BlockSpec(memory_space=pltpu.HBM)] * 3,
-        out_specs=(vmem,) * 4,
-        scratch_shapes=[
-            pltpu.VMEM(state.shape, jnp.bfloat16),
-            pltpu.VMEM(spectral_weight.shape, jnp.float32),
-            pltpu.VMEM(conv_weight.shape, jnp.bfloat16),
-            pltpu.VMEM((2, 32 * cells_y, 128), jnp.float32),
-            pltpu.SemaphoreType.DMA((10,)),
-        ],
+        pack_kernel,
+        out_shape=jax.ShapeDtypeStruct((2, 4, 16, KX, 128), jnp.float32),
+        in_specs=[pl.BlockSpec(memory_space=pl.ANY), vmem],
+        out_specs=vmem,
         compiler_params=pltpu.CompilerParams(vmem_limit_bytes=16 * 2**20),
         cost_estimate=pl.CostEstimate(flops=2**10, bytes_accessed=2**10, transcendentals=0),
-        name="prepare_operands",
-    )(
-        after,
-        *(
-            pltpu.with_memory_space_constraint(v, pltpu.HBM)
-            for v in (state, spectral_weight, conv_weight)
-        ),
-    )
+        name="pack_weights",
+    )(after, spectral_weight)
 
 
 def mix_kernel(modes_ref, forward_ref, weight_ref, inverse_ref, out_ref):
@@ -449,8 +420,8 @@
     *planes, first_ref, second_ref = refs
     end = planes[0].shape[0] - 1
     odd_y = lax.rem(lax.axis_index("py"), 2)
-    first_ref[...] = cell_row(planes, (1 - odd_y) * end)
-    second_ref[...] = cell_row(planes, odd_y * end)
+    first_ref[...] = cell_row(planes, odd_y * end)
+    second_ref[...] = cell_row(planes, (1 - odd_y) * end)
 
 
 def edge_rows(planes):
@@ -489,19 +460,22 @@
 
 
 def interior_kernel(*refs):
-    *planes, weight_ref, y_ref, out_ref, y_out = refs
+    *planes, weight_ref, y_hbm, out_ref, y_out, y_ref, y_sem = refs
     cells_y = planes[0].shape[0]
-    table = y_ref[lax.axis_index("py")]
+    y_copy = pltpu.make_async_copy(y_hbm.at[lax.axis_index("py")], y_ref, y_sem)
+    y_copy.start()
+    weight = weight_ref[...]
+    for quad in range(1, cells_y // 4 - 1):
+        convolve_quad(
+            quad, lambda y: cell_row(planes, y), weight, lambda y: (y, cells_y), out_ref
+        )
+    y_copy.wait()
+    table = y_ref[...]
     lane = lax.broadcasted_iota(jnp.int32, table.shape, 1) % 16
     for o in range(16):
         y_out[o * cells_y : (o + 1) * cells_y] = jnp.where(lane == o, table, 0.0).astype(
             jnp.bfloat16
         )
-    weight = weight_ref[...]
-    for quad in range(1, cells_y // 4 - 1):
-        convolve_quad(
-            quad, lambda y: cell_row(planes, y), weight, lambda y: (y, cells_y), out_ref
-        )
 
 
 def edge_kernel(*refs):
@@ -511,9 +485,9 @@
 
     def row(y):
         if y < 0:
+            return jnp.where(odd_y, second_row[...], first_row[...])
+        if y >= cells_y:
             return jnp.where(odd_y, first_row[...], second_row[...])
-        if y >= cells_y:
-            return jnp.where(odd_y, second_row[...], first_row[...])
         return cell_row(planes, y)
 
     weight = weight_ref[...]
@@ -521,17 +495,18 @@
         convolve_quad(quad, row, weight, lambda y: (y % 8, 8), out_ref)
 
 
-def convolve(kernel, name, operands, out_shape):
+def convolve(kernel, name, operands, out_shape, fetched=(), scratch=()):
     vmem = pl.BlockSpec(memory_space=pltpu.VMEM)
     return pl.pallas_call(
         kernel,
         out_shape=out_shape,
-        in_specs=[vmem] * len(operands),
+        in_specs=[vmem] * len(operands) + [pl.BlockSpec(memory_space=pltpu.HBM)] * len(fetched),
         out_specs=(vmem,) * len(out_shape),
+        scratch_shapes=scratch,
         compiler_params=pltpu.CompilerParams(vmem_limit_bytes=16 * 2**20),
         cost_estimate=pl.CostEstimate(flops=2**30, bytes_accessed=2**21, transcendentals=0),
         name=name,
-    )(*operands)
+    )(*operands, *(pltpu.with_memory_space_constraint(v, pltpu.HBM) for v in fetched))
 
 
 def gelu(value):
@@ -623,7 +598,7 @@
     count = lax.axis_size(axis)
     inside = [(i, i ^ 1) for i in range(count)]
     across = [(i, i + 1 if i % 2 else i - 1) for i in range(1, count - 1)]
-    return lax.ppermute(first, axis, inside), lax.ppermute(second, axis, across)
+    return lax.ppermute(first, axis, across), lax.ppermute(second, axis, inside)
 
 
 def body(state_field, conv_weight, conv_bias, spectral_weight):
@@ -636,9 +611,8 @@
         state_field.reshape(channels * cells_x, cells_y, depth), z_forward, y_forward
     )
     modes = exchanged(sent)
-    first_own, second_own, taps, weights = prepare(
-        sent, state_field, spectral_weight.swapaxes(4, 5), conv_weight.transpose(2, 3, 4, 0, 1)
-    )
+    first_own, second_own, taps = arrange(sent, state_field, conv_weight.transpose(2, 3, 4, 0, 1))
+    weights = pack(taps, spectral_weight.swapaxes(4, 5))
     first_plane, second_plane = swaps(first_own, second_own, "px")
     values = exchanged(mix_modes(modes, x_forward, weights, x_inverse))
     planes = (first_plane, first_own, second_own, second_plane)
@@ -647,11 +621,13 @@
     interior, y_expanded = convolve(
         interior_kernel,
         "convolve_interior",
-        planes + (taps, y_inverse),
+        planes + (taps,),
         (
             jax.ShapeDtypeStruct((rows * cells_y, depth), jnp.float32),
             jax.ShapeDtypeStruct((16 * cells_y, y_inverse.shape[2]), jnp.bfloat16),
         ),
+        (y_inverse,),
+        (pltpu.VMEM(y_inverse.shape[1:], jnp.float32), pltpu.SemaphoreType.DMA),
     )
     (edges,) = convolve(
         edge_kernel,

time: 35.7 us -> 38.7 us (1.084)
  waiting for transfers between devices: 6.21 us -> 1.66 us
  starting transfers between devices: 16.2 us -> 20.7 us
  local copies, waits for them, and re-layouts: 1.02 us -> 5.13 us
  Pallas kernels: 11.5 us -> 10.5 us
    ppermute x4, starting transfers between devices: 3.23 us -> 8.89 us  [the longest x2 7.42 us: swaps(): lax.ppermute(second, axis, inside)]
    all_to_all x2, waiting for transfers between devices: 4.15 us -> 0.01 us  [exchanged(): lax.all_to_all(value, ('px', 'py'), split_axis=0, concat_axis=0, tiled=True)]
    unnamed x14 -> x18, local copies, waits for them, and re-layouts: 1.02 us -> 5.13 us
    pallas_call x1 -> x2, Pallas kernels: 3.33 us -> 1.7 us  [the longest x1 0.87 us: pack(): pl.pallas_call(pack_kernel, out_shape=jax.ShapeDtypeStruct((2, 4, 16, KX,...]
    all_to_all x2, starting transfers between devices: 13 us -> 11.9 us  [exchanged(): lax.all_to_all(value, ('px', 'py'), split_axis=0, concat_axis=0, tiled=True)]
    pallas_call x2, Pallas kernels: 1.84 us -> 2.5 us  [convolve(): pl.pallas_call(kernel, out_shape=out_shape, in_specs=[vmem] * len(operand...]
    ppermute x4, waiting for transfers between devices: 2.06 us -> 1.65 us  [the longest x2 1.65 us: swaps(): lax.ppermute(second, axis, inside)]
  transfers between devices with their start and end apart: 6 -> 6, of which waited for: 3 -> 1; matrix products, arithmetic and copies ran while one was open for 0% -> 0% of each run, Pallas kernels for 19% -> 15%
where the time goes in v5:
time: 38.7 us; the launch traced here: 38.3 us
  starting transfers between devices  20.7 us (53%)
  Pallas kernels  10.5 us (27%)
  local copies, waits for them, and re-layouts  5.13 us (13%)
  waiting for transfers between devices  1.66 us (4%)
    all_to_all x2, starting transfers between devices, exchanged(): lax.all_to_all(value, ('px', 'py'), split_axis=0, concat_axis=0, tiled=True)  11.9 us
    ppermute x2, starting transfers between devices, swaps(): lax.ppermute(second, axis, inside)  7.42 us
    unnamed x18, local copies, waits for them, and re-layouts  5.13 us
    pallas_call x1, Pallas kernels, forward_modes(): pl.pallas_call(forward_kernel, out_shape=jax.ShapeDtypeStruct((32, 8, 128...  2.68 us
    pallas_call x2, Pallas kernels, convolve(): pl.pallas_call(kernel, out_shape=out_shape, in_specs=[vmem] * len(operand...  2.5 us
    pallas_call x1, Pallas kernels, finish(): pl.pallas_call(finish_kernel, out_shape=jax.ShapeDtypeStruct(convolved.sh...  2.03 us
    ppermute x2, waiting for transfers between devices, swaps(): lax.ppermute(second, axis, inside)  1.65 us
    pallas_call x1, Pallas kernels, mix_modes(): pl.pallas_call(mix_kernel, out_shape=jax.ShapeDtypeStruct((32, 16, 128),...  1.62 us
  transfers between devices with their start and end apart: 6, of which 1 were waited for; matrix products, arithmetic and copies ran while one was open for 0% of the time, Pallas kernels for 15%

profile of v5, /device:TPU:0, one launch (start us, length us, event | category | flops | bytes accessed | tf_op | source)
XLA Modules:
  0.0 38.3 jit_solution(6923794745889375025)
XLA Ops:
  0.0 2.7 %forward_modes.1.after_ref = bf16[32,8,128]{2,1,0:T(8,128)(2,1)} custom-call(bf16[64,32,128]{2,1,0:T(8,128)(2,1)} %bitcast.6, f32[32,128]{1,0:T(8,128)} %constant.12.clone.z_hbm, f32[4,64,512]{2,1,0:T(8,128)} %constant.13.clone.y_hbm), custom_call_target="tpu_custom_call" | custom-call | flops 134217728 | bytes 2097152 | tf_op jit(solution)/shard_map/forward_modes/pallas_call | solution.py:289
  2.7 7.3 %all-to-all-start = ((bf16[32,8,128]{2,1,0:T(8,128)(2,1)}), bf16[32,8,128]{2,1,0:T(8,128)(2,1)S(1)}, u32[]{:S(2)}, u32[]{:S(2)}) async-start(bf16[32,8,128]{2,1,0:T(8,128)(2,1)} %forward_modes.1.after_ref), calls=%async_computation | async-start | bytes 131072 | tf_op jit(solution)/shard_map/all_to_all | solution.py:594
  10.0 0.0 copy-start.1
  10.0 1.0 %copy-done.1 = bf16[32,2,32,128]{3,2,1,0:T(8,128)(2,1)S(1)} copy-done((bf16[32,2,32,128]{3,2,1,0:T(8,128)(2,1)S(1)}, bf16[32,2,32,128]{3,2,1,0:T(8,128)(2,1)}, u32[]{:S(2)}) %copy-start.1) | copy-done | bytes 524312
  11.1 0.9 %copy-done.5 = bf16[32,32,3,3,3]{1,0,4,3,2:T(8,128)(2,1)S(1)} copy-done((bf16[32,32,3,3,3]{1,0,4,3,2:T(8,128)(2,1)S(1)}, bf16[32,32,3,3,3]{1,0,4,3,2:T(8,128)(2,1)}, u32[]{:S(2)}) %copy-start.5) | copy-done | bytes 55320
  12.0 0.8 %arrange_cells.1 = (bf16[32,32,128]{2,1,0:T(8,128)(2,1)S(1)}, bf16[32,32,128]{2,1,0:T(8,128)(2,1)S(1)}, bf16[384,512]{1,0:T(8,128)(2,1)S(1)}) custom-call(bf16[32,8,128]{2,1,0:T(8,128)(2,1)} %forward_modes.1.after_ref, bf16[32,2,32,128]{3,2,1,0:T(8,128)(2,1)S(1)} %copy-done.1, bf16[3,3,3,32,32]{4,3,2,1,0:T(8,128)(2,1)S(1)} %bitcast.9), custom_call_target="tpu_custom_call" | custom-call | flops 1024 | bytes 1024 | tf_op jit(solution)/shard_map/arrange_cells/pallas_call | solution.py:336
  12.8 0.7 %collective-permute-start = (bf16[32,32,128]{2,1,0:T(8,128)(2,1)S(1)}, bf16[32,32,128]{2,1,0:T(8,128)(2,1)S(1)}, u32[]{:S(2)}, u32[]{:S(2)}) collective-permute-start(bf16[32,32,128]{2,1,0:T(8,128)(2,1)S(1)} %get-tuple-element.13.refs_1_), channel_id=1, source_target_pairs={{4,8},{8,4},{12,16},{16,12},{20,24},{24,20},{5,9},{9,5},{13,17},{1... | collective-permute-start | bytes 786440 | tf_op jit(solution)/shard_map/ppermute | solution.py:601
  13.5 4.5 %collective-permute-start.1 = (bf16[32,32,128]{2,1,0:T(8,128)(2,1)S(1)}, bf16[32,32,128]{2,1,0:T(8,128)(2,1)S(1)}, u32[]{:S(2)}, u32[]{:S(2)}) collective-permute-start(bf16[32,32,128]{2,1,0:T(8,128)(2,1)S(1)} %get-tuple-element.14.refs_2_), channel_id=1, source_target_pairs={{0,4},{4,0},{8,12},{12,8},{16,20},{20,16},{24,28},{28,24},{1,5},{5... | collective-permute-start | bytes 786440 | tf_op jit(solution)/shard_map/ppermute | solution.py:601
  18.0 2.2 %copy-done = f32[2,4,4,16,32,16]{4,5,3,2,1,0:T(8,128)S(1)} copy-done((f32[2,4,4,16,32,16]{4,5,3,2,1,0:T(8,128)S(1)}, f32[2,4,4,16,32,16]{4,5,3,2,1,0:T(8,128)}, u32[]{:S(2)}) %copy-start) | copy-done | bytes 1048600
  20.2 0.9 %pack_weights.1.weight_ref = f32[2,4,16,16,128]{4,3,2,1,0:T(8,128)S(1)} custom-call(bf16[384,512]{1,0:T(8,128)(2,1)S(1)} %get-tuple-element.12.after_ref.refs_4_.refs_6_, f32[2,4,4,16,16,32]{5,4,3,2,1,0:T(8,128)S(1)} %bitcast.5), custom_call_target="tpu_custom_call" | custom-call | flops 1024 | bytes 1024 | tf_op jit(solution)/shard_map/pack_weights/pallas_call | solution.py:359
  21.1 1.6 %mix_modes.1 = bf16[32,16,128]{2,1,0:T(8,128)(2,1)} custom-call(bf16[32,8,128]{2,1,0:T(8,128)(2,1)S(1)} %all-to-all-done.modes_ref, f32[64,256]{1,0:T(8,128)S(1)} %copy-done.8, f32[2,4,16,16,128]{4,3,2,1,0:T(8,128)S(1)} %pack_weights.1.weight_ref, f32[128,128]{1,0:T(8,128)S(1)} %copy-done.7), custom_call_target="tpu_custom_call" | custom-call | flops 34359738368 | bytes 2097152 | tf_op jit(solution)/shard_map/mix_modes/pallas_call | solution.py:404
  22.8 4.5 %all-to-all-start.1 = ((bf16[32,16,128]{2,1,0:T(8,128)(2,1)}), bf16[32,16,128]{2,1,0:T(8,128)(2,1)S(1)}, u32[]{:S(2)}, u32[]{:S(2)}) async-start(bf16[32,16,128]{2,1,0:T(8,128)(2,1)} %mix_modes.1), calls=%async_computation.1 | async-start | bytes 262144 | tf_op jit(solution)/shard_map/all_to_all | solution.py:594
  27.3 0.0 collective-permute-done.refs_0_
  27.3 1.6 %collective-permute-done.1.refs_3_ = bf16[32,32,128]{2,1,0:T(8,128)(2,1)S(1)} collective-permute-done((bf16[32,32,128]{2,1,0:T(8,128)(2,1)S(1)}, bf16[32,32,128]{2,1,0:T(8,128)(2,1)S(1)}, u32[]{:S(2)}, u32[]{:S(2)}) %collective-permute-start.1) | collective-permute-done | bytes 262176 | tf_op jit(solution)/shard_map/ppermute | solution.py:601
  29.0 0.0 copy-start.2
  29.0 0.0 copy-start.6
  29.0 0.8 %collective-permute-start.2 = (bf16[128,128]{1,0:T(8,128)(2,1)S(1)}, bf16[128,128]{1,0:T(8,128)(2,1)S(1)}, u32[]{:S(2)}, u32[]{:S(2)}) collective-permute-start(bf16[128,128]{1,0:T(8,128)(2,1)S(1)} %get-tuple-element.17), channel_id=1, source_target_pairs={{1,2},{2,1},{5,6},{6,5},{9,10},{10,9},{13,14},{14,13},{17,18},{18,... | collective-permute-start | bytes 98312 | tf_op jit(solution)/shard_map/ppermute | solution.py:601
  29.8 2.9 %collective-permute-start.3 = (bf16[128,128]{1,0:T(8,128)(2,1)S(1)}, bf16[128,128]{1,0:T(8,128)(2,1)S(1)}, u32[]{:S(2)}, u32[]{:S(2)}) collective-permute-start(bf16[128,128]{1,0:T(8,128)(2,1)S(1)} %get-tuple-element.18), channel_id=1, source_target_pairs={{0,1},{1,0},{2,3},{3,2},{4,5},{5,4},{6,7},{7,6},{8,9},{9,8},{10,11... | collective-permute-start | bytes 98312 | tf_op jit(solution)/shard_map/ppermute | solution.py:601
  32.7 2.0 %convolve_interior.1 = (f32[2048,128]{1,0:T(8,128)S(1)}, bf16[512,512]{1,0:T(8,128)(2,1)S(1)}) custom-call(bf16[32,32,128]{2,1,0:T(8,128)(2,1)S(1)} %collective-permute-done.refs_0_, bf16[32,32,128]{2,1,0:T(8,128)(2,1)S(1)} %get-tuple-element.13.refs_1_, bf16[32,32,128]{2,1,0:T(8,128)(2,1)S(1)} %get-tuple-element.14.refs_2_, ...), custom_call_target="tpu_custom_call" | custom-call | flops 1073741824 | bytes 2097152 | tf_op jit(solution)/shard_map/convolve_interior/pallas_call | solution.py:500
  34.7 0.0 collective-permute-done.2.refs_4_
  34.7 0.0 copy-start.4
  34.8 0.9 %copy-done.4 = bf16[32,32,128]{2,1,0:T(8,128)(2,1)S(1)} copy-done((bf16[32,32,128]{2,1,0:T(8,128)(2,1)S(1)}, bf16[32,32,128]{2,1,0:T(8,128)(2,1)}, u32[]{:S(2)}) %copy-start.4) | copy-done | bytes 262168
  35.7 0.5 %convolve_edges.1 = f32[512,128]{1,0:T(8,128)S(1)} custom-call(bf16[32,32,128]{2,1,0:T(8,128)(2,1)S(1)} %collective-permute-done.refs_0_, bf16[32,32,128]{2,1,0:T(8,128)(2,1)S(1)} %get-tuple-element.13.refs_1_, bf16[32,32,128]{2,1,0:T(8,128)(2,1)S(1)} %get-tuple-element.14.refs_2_, bf16[32,32,128]{2,1,0:T(8,128)(2,1)S(1)} %copy-done.4, ...), custom_call_target="tpu_custom_call" | custom-call | flops 1073741824 | bytes 2097152 | tf_op jit(solution)/shard_map/convolve_edges/pallas_call | solution.py:500
  36.2 2.0 %finish_layer.1 = bf16[32,2,32,128]{3,2,1,0:T(8,128)(2,1)} custom-call(f32[32]{0:T(128)S(1)} %copy-done.6, bf16[32,16,128]{2,1,0:T(8,128)(2,1)S(1)} %all-to-all-done.1.values_ref, f32[128,512]{1,0:T(8,128)S(1)} %copy-done.2, bf16[512,512]{1,0:T(8,128)(2,1)S(1)} %get-tuple-element.15.y_ref, f32[32,2,32,128]{3,2,1,0:T(8,128)S(1)} %bitcast.7, ...), custom_call_target="tpu_custom_call" | custom-call | flops 268435456 | bytes 4194304 | tf_op jit(solution)/shard_map/finish_layer/pallas_call | solution.py:578
  (14 shorter events, 0.0 us)
Async XLA Ops:
  0.0 21.1 %copy-start.7 = (f32[128,128]{1,0:T(8,128)S(1)}, f32[128,128]{1,0:T(8,128)}, u32[]{:S(2)}) copy-start(f32[128,128]{1,0:T(8,128)} %constant.15.clone.inverse_ref) | copy-start | bytes 196612
  0.0 21.1 %copy-start.8 = (f32[64,256]{1,0:T(8,128)S(1)}, f32[64,256]{1,0:T(8,128)}, u32[]{:S(2)}) copy-start(f32[64,256]{1,0:T(8,128)} %constant.14.clone.forward_ref) | copy-start | bytes 196612
  2.7 18.4 %all-to-all-start = ((bf16[32,8,128]{2,1,0:T(8,128)(2,1)}), bf16[32,8,128]{2,1,0:T(8,128)(2,1)S(1)}, u32[]{:S(2)}, u32[]{:S(2)}) async-start(bf16[32,8,128]{2,1,0:T(8,128)(2,1)} %forward_modes.1.after_ref), calls=%async_computation | async-start | bytes 131072 | tf_op jit(solution)/shard_map/all_to_all | solution.py:594
  10.0 1.0 %copy-start.1 = (bf16[32,2,32,128]{3,2,1,0:T(8,128)(2,1)S(1)}, bf16[32,2,32,128]{3,2,1,0:T(8,128)(2,1)}, u32[]{:S(2)}) copy-start(bf16[32,2,32,128]{3,2,1,0:T(8,128)(2,1)} %state_ref.1) | copy-start | bytes 1572868
  11.0 0.9 %copy-start.5 = (bf16[32,32,3,3,3]{1,0,4,3,2:T(8,128)(2,1)S(1)}, bf16[32,32,3,3,3]{1,0,4,3,2:T(8,128)(2,1)}, u32[]{:S(2)}) copy-start(bf16[32,32,3,3,3]{1,0,4,3,2:T(8,128)(2,1)} %param.11) | copy-start | bytes 165892
  12.8 14.5 %collective-permute-start = (bf16[32,32,128]{2,1,0:T(8,128)(2,1)S(1)}, bf16[32,32,128]{2,1,0:T(8,128)(2,1)S(1)}, u32[]{:S(2)}, u32[]{:S(2)}) collective-permute-start(bf16[32,32,128]{2,1,0:T(8,128)(2,1)S(1)} %get-tuple-element.13.refs_1_), channel_id=1, source_target_pairs={{4,8},{8,4},{12,16},{16,12},{20,24},{24,20},{5,9},{9,5},{13,17},{1... | collective-permute-start | bytes 786440 | tf_op jit(solution)/shard_map/ppermute | solution.py:601
  13.5 15.5 %collective-permute-start.1 = (bf16[32,32,128]{2,1,0:T(8,128)(2,1)S(1)}, bf16[32,32,128]{2,1,0:T(8,128)(2,1)S(1)}, u32[]{:S(2)}, u32[]{:S(2)}) collective-permute-start(bf16[32,32,128]{2,1,0:T(8,128)(2,1)S(1)} %get-tuple-element.14.refs_2_), channel_id=1, source_target_pairs={{0,4},{4,0},{8,12},{12,8},{16,20},{20,16},{24,28},{28,24},{1,5},{5... | collective-permute-start | bytes 786440 | tf_op jit(solution)/shard_map/ppermute | solution.py:601
  18.0 2.2 %copy-start = (f32[2,4,4,16,32,16]{4,5,3,2,1,0:T(8,128)S(1)}, f32[2,4,4,16,32,16]{4,5,3,2,1,0:T(8,128)}, u32[]{:S(2)}) copy-start(f32[2,4,4,16,32,16]{4,5,3,2,1,0:T(8,128)} %param.13) | copy-start | bytes 3145732
  22.8 13.4 %all-to-all-start.1 = ((bf16[32,16,128]{2,1,0:T(8,128)(2,1)}), bf16[32,16,128]{2,1,0:T(8,128)(2,1)S(1)}, u32[]{:S(2)}, u32[]{:S(2)}) async-start(bf16[32,16,128]{2,1,0:T(8,128)(2,1)} %mix_modes.1), calls=%async_computation.1 | async-start | bytes 262144 | tf_op jit(solution)/shard_map/all_to_all | solution.py:594
  29.0 5.8 %copy-start.3 = (bf16[32,32,128]{2,1,0:T(8,128)(2,1)}, bf16[32,32,128]{2,1,0:T(8,128)(2,1)S(1)}, u32[]{:S(2)}) copy-start(bf16[32,32,128]{2,1,0:T(8,128)(2,1)S(1)} %collective-permute-done.1.refs_3_) | copy-start | bytes 786436
  29.0 7.2 %copy-start.2 = (f32[128,512]{1,0:T(8,128)S(1)}, f32[128,512]{1,0:T(8,128)}, u32[]{:S(2)}) copy-start(f32[128,512]{1,0:T(8,128)} %constant.17.clone.z_ref) | copy-start | bytes 786436
  29.0 7.2 %copy-start.6 = (f32[32]{0:T(128)S(1)}, f32[32]{0:T(128)}, u32[]{:S(2)}) copy-start(f32[32]{0:T(128)} %bias_ref.1) | copy-start | bytes 388
  29.0 5.7 %collective-permute-start.2 = (bf16[128,128]{1,0:T(8,128)(2,1)S(1)}, bf16[128,128]{1,0:T(8,128)(2,1)S(1)}, u32[]{:S(2)}, u32[]{:S(2)}) collective-permute-start(bf16[128,128]{1,0:T(8,128)(2,1)S(1)} %get-tuple-element.17), channel_id=1, source_target_pairs={{1,2},{2,1},{5,6},{6,5},{9,10},{10,9},{13,14},{14,13},{17,18},{18,... | collective-permute-start | bytes 98312 | tf_op jit(solution)/shard_map/ppermute | solution.py:601
  29.8 4.9 %collective-permute-start.3 = (bf16[128,128]{1,0:T(8,128)(2,1)S(1)}, bf16[128,128]{1,0:T(8,128)(2,1)S(1)}, u32[]{:S(2)}, u32[]{:S(2)}) collective-permute-start(bf16[128,128]{1,0:T(8,128)(2,1)S(1)} %get-tuple-element.18), channel_id=1, source_target_pairs={{0,1},{1,0},{2,3},{3,2},{4,5},{5,4},{6,7},{7,6},{8,9},{9,8},{10,11... | collective-permute-start | bytes 98312 | tf_op jit(solution)/shard_map/ppermute | solution.py:601
  34.7 1.0 %copy-start.4 = (bf16[32,32,128]{2,1,0:T(8,128)(2,1)S(1)}, bf16[32,32,128]{2,1,0:T(8,128)(2,1)}, u32[]{:S(2)}) copy-start(bf16[32,32,128]{2,1,0:T(8,128)(2,1)} %copy-done.3) | copy-start | bytes 786436

commit v6 on v3

--- a/solution.py
+++ b/solution.py
@@ -288,11 +288,13 @@
 def forward_modes(state, z_table, y_table):
     return pl.pallas_call(
         forward_kernel,
-        out_shape=jax.ShapeDtypeStruct((32, 8, 128), jnp.bfloat16),
+        out_shape=(
+            jax.ShapeDtypeStruct((32, 8, 128), jnp.bfloat16),
+            jax.ShapeDtypeStruct(state.shape, jnp.bfloat16),
+        ),
         in_specs=[pl.BlockSpec(memory_space=pltpu.HBM)] * 3,
-        out_specs=pl.BlockSpec(memory_space=pltpu.VMEM),
+        out_specs=(pl.BlockSpec(memory_space=pltpu.VMEM),) * 2,
         scratch_shapes=[
-            pltpu.VMEM(state.shape, jnp.bfloat16),
             pltpu.VMEM(z_table.shape, jnp.float32),
             pltpu.VMEM(y_table.shape[1:], jnp.float32),
             pltpu.VMEM((32 * state.shape[1], y_table.shape[2]), jnp.bfloat16),
@@ -304,23 +306,35 @@
     )(*(pltpu.with_memory_space_constraint(v, pltpu.HBM) for v in (state, z_table, y_table)))
 
 
-def prepare_kernel(
-    after_ref,
-    weight_hbm,
-    conv_hbm,
-    y_hbm,
-    weight_out,
-    conv_out,
-    y_out,
-    weight_ref,
-    conv_ref,
-    y_ref,
-    sems,
+def arrange_kernel(state_ref, first_ref, second_ref, wide):
+    odd_x = lax.rem(lax.axis_index("px"), 2)
+    cells_y = state_ref.shape[2]
+    for slot, (out_ref, x) in enumerate(((first_ref, odd_x), (second_ref, 1 - odd_x))):
+        wide[slot] = state_ref[:, x].astype(jnp.float32).reshape(32 * cells_y, 128)
+        for y in range(cells_y):
+            out_ref[y] = wide[slot, pl.ds(y, 32, stride=cells_y), :].astype(jnp.bfloat16)
+
+
+def arrange(state):
+    vmem = pl.BlockSpec(memory_space=pltpu.VMEM)
+    cells_y = state.shape[2]
+    plane = jax.ShapeDtypeStruct((cells_y, 32, 128), jnp.bfloat16)
+    return pl.pallas_call(
+        arrange_kernel,
+        out_shape=(plane, plane),
+        in_specs=[vmem],
+        out_specs=(vmem, vmem),
+        scratch_shapes=[pltpu.VMEM((2, 32 * cells_y, 128), jnp.float32)],
+        compiler_params=pltpu.CompilerParams(vmem_limit_bytes=16 * 2**20),
+        cost_estimate=pl.CostEstimate(flops=2**10, bytes_accessed=2**10, transcendentals=0),
+        name="arrange_cells",
+    )(state)
+
+
+def pack_kernel(
+    after_ref, weight_hbm, conv_hbm, weight_out, conv_out, weight_ref, conv_ref, sems
 ):
     conv_copy = pltpu.make_async_copy(conv_hbm, conv_ref, sems.at[8])
-    y_copy = pltpu.make_async_copy(y_hbm.at[lax.axis_index("py")], y_ref, sems.at[9])
-    conv_copy.start()
-    y_copy.start()
     copies = [
         pltpu.make_async_copy(
             weight_hbm.at[part, kz], weight_ref.at[part, kz], sems.at[part * 4 + kz]
@@ -328,9 +342,9 @@
         for part in range(2)
         for kz in range(4)
     ]
-    for copy in copies:
+    for copy in [conv_copy] + copies:
         copy.start()
-    odd_x = lax.rem(lax.axis_index("px"), 2) == 1
+    odd_x = lax.rem(lax.axis_index("px"), 2)
     conv_copy.wait()
     zero = jnp.zeros((32, 32), jnp.float32)
     for dz in range(3):
@@ -344,16 +358,10 @@
                 row = ((dz * 2 + y_at) * 2 + x_at) * 32
                 for y_in in range(4):
                     blocks = [taps.get((x_in - x_at, y_in - y_at), zero) for x_in in range(4)]
-                    blocks = [jnp.where(odd_x, blocks[i], blocks[3 - i]) for i in range(4)]
+                    blocks = [jnp.where(odd_x == 1, blocks[3 - i], blocks[i]) for i in range(4)]
                     conv_out[row : row + 32, y_in * 128 : (y_in + 1) * 128] = jnp.concatenate(
                         blocks, axis=1
                     ).astype(jnp.bfloat16)
-    y_copy.wait()
-    table = y_ref[...]
-    lane = lax.broadcasted_iota(jnp.int32, table.shape, 1) % 16
-    span = table.shape[0]
-    for o in range(16):
-        y_out[o * span : (o + 1) * span] = jnp.where(lane == o, table, 0.0).astype(jnp.bfloat16)
     for part in range(2):
         for kz in range(4):
             copies[part * 4 + kz].wait()
@@ -363,32 +371,27 @@
                 )
 
 
-def prepare(after, spectral_weight, conv_weight, y_table):
+def pack(after, spectral_weight, conv_weight):
     vmem = pl.BlockSpec(memory_space=pltpu.VMEM)
     return pl.pallas_call(
-        prepare_kernel,
+        pack_kernel,
         out_shape=(
             jax.ShapeDtypeStruct((2, 4, 16, KX, 128), jnp.float32),
             jax.ShapeDtypeStruct((384, 512), jnp.bfloat16),
-            jax.ShapeDtypeStruct((16 * y_table.shape[1], y_table.shape[2]), jnp.bfloat16),
         ),
-        in_specs=[pl.BlockSpec(memory_space=pl.ANY)] + [pl.BlockSpec(memory_space=pltpu.HBM)] * 3,
-        out_specs=(vmem,) * 3,
+        in_specs=[pl.BlockSpec(memory_space=pl.ANY)] + [pl.BlockSpec(memory_space=pltpu.HBM)] * 2,
+        out_specs=(vmem, vmem),
         scratch_shapes=[
             pltpu.VMEM(spectral_weight.shape, jnp.float32),
             pltpu.VMEM(conv_weight.shape, jnp.bfloat16),
-            pltpu.VMEM(y_table.shape[1:], jnp.float32),
-            pltpu.SemaphoreType.DMA((10,)),
+            pltpu.SemaphoreType.DMA((9,)),
         ],
         compiler_params=pltpu.CompilerParams(vmem_limit_bytes=16 * 2**20),
         cost_estimate=pl.CostEstimate(flops=2**10, bytes_accessed=2**10, transcendentals=0),
-        name="prepare_weights",
+        name="pack_weights",
     )(
         after,
-        *(
-            pltpu.with_memory_space_constraint(v, pltpu.HBM)
-            for v in (spectral_weight, conv_weight, y_table)
-        ),
+        *(pltpu.with_memory_space_constraint(v, pltpu.HBM) for v in (spectral_weight, conv_weight)),
     )
 
 
@@ -437,31 +440,6 @@
     )(modes, forward_table, weights, inverse_table)
 
 
-def arrange_kernel(after_ref, state_ref, first_ref, second_ref, wide):
-    cells_y = state_ref.shape[2]
-    odd_x = lax.rem(lax.axis_index("px"), 2)
-    for out_ref, x in ((first_ref, 1 - odd_x), (second_ref, odd_x)):
-        wide[...] = state_ref[:, x].astype(jnp.float32).reshape(32 * cells_y, 128)
-        for y in range(cells_y):
-            out_ref[y] = wide[pl.ds(y, 32, stride=cells_y), :].astype(jnp.bfloat16)
-
-
-def arrange(after, state):
-    vmem = pl.BlockSpec(memory_space=pltpu.VMEM)
-    cells_y = state.shape[2]
-    plane = jax.ShapeDtypeStruct((cells_y, 32, 128), jnp.bfloat16)
-    return pl.pallas_call(
-        arrange_kernel,
-        out_shape=(plane, plane),
-        in_specs=[pl.BlockSpec(memory_space=pl.ANY), vmem],
-        out_specs=(vmem, vmem),
-        scratch_shapes=[pltpu.VMEM((32 * cells_y, 128), jnp.float32)],
-        compiler_params=pltpu.CompilerParams(vmem_limit_bytes=16 * 2**20),
-        cost_estimate=pl.CostEstimate(flops=2**10, bytes_accessed=2**10, transcendentals=0),
-        name="arrange_cells",
-    )(after, state)
-
-
 def cell_row(planes, y):
     return jnp.concatenate([plane[y] for plane in planes], axis=0)
 
@@ -470,8 +448,8 @@
     *planes, first_ref, second_ref = refs
     end = planes[0].shape[0] - 1
     odd_y = lax.rem(lax.axis_index("py"), 2)
-    first_ref[...] = cell_row(planes, (1 - odd_y) * end)
-    second_ref[...] = cell_row(planes, odd_y * end)
+    first_ref[...] = cell_row(planes, odd_y * end)
+    second_ref[...] = cell_row(planes, (1 - odd_y) * end)
 
 
 def edge_rows(planes):
@@ -526,9 +504,9 @@
 
     def row(y):
         if y < 0:
+            return jnp.where(odd_y, second_row[...], first_row[...])
+        if y >= cells_y:
             return jnp.where(odd_y, first_row[...], second_row[...])
-        if y >= cells_y:
-            return jnp.where(odd_y, second_row[...], first_row[...])
         return cell_row(planes, y)
 
     weight = weight_ref[...]
@@ -557,6 +535,9 @@
     bias_ref, values_ref, z_ref, y_ref, conv_ref, edge_ref, out_hbm, out_ref, sems
 ):
     upper = lax.broadcasted_iota(jnp.int32, (8, 128), 0) < 4
+    table = y_ref[lax.axis_index("py")]
+    lane = lax.broadcasted_iota(jnp.int32, table.shape, 1) % 16
+    expanded = [jnp.where(lane == o, table, 0.0).astype(jnp.bfloat16) for o in range(16)]
     columns = []
     for group in range(4):
         columns.append(
@@ -586,7 +567,9 @@
         right = jnp.concatenate(sides, axis=1)
         for block in range(4):
             spectral = jnp.dot(
-                y_ref[block * 128 : (block + 1) * 128], right, preferred_element_type=jnp.float32
+                jnp.concatenate(expanded[block * 4 : block * 4 + 4], axis=0),
+                right,
+                preferred_element_type=jnp.float32,
             )
             for o4 in range(4):
                 o = half * 16 + block * 4 + o4
@@ -638,7 +621,7 @@
     count = lax.axis_size(axis)
     inside = [(i, i ^ 1) for i in range(count)]
     across = [(i, i + 1 if i % 2 else i - 1) for i in range(1, count - 1)]
-    return lax.ppermute(first, axis, inside), lax.ppermute(second, axis, across)
+    return lax.ppermute(first, axis, across), lax.ppermute(second, axis, inside)
 
 
 def body(state_field, conv_weight, conv_bias, spectral_weight):
@@ -647,28 +630,28 @@
     if sizes != (8, 4, 2, 32, 128):
         return general_body(state_field, conv_weight, conv_bias, spectral_weight)
     z_forward, y_forward, x_forward, x_inverse, z_inverse, y_inverse = tables(*sizes)
-    sent = forward_modes(
+    sent, held = forward_modes(
         state_field.reshape(channels * cells_x, cells_y, depth), z_forward, y_forward
     )
     modes = exchanged(sent)
-    weights, taps, y_expanded = prepare(
-        sent, spectral_weight.swapaxes(4, 5), conv_weight.transpose(2, 3, 4, 0, 1), y_inverse
-    )
-    first_own, second_own = arrange(taps, state_field)
+    first_own, second_own = arrange(held.reshape(state_field.shape))
+    weights, taps = pack(
+        first_own, spectral_weight.swapaxes(4, 5), conv_weight.transpose(2, 3, 4, 0, 1)
+    )
     first_plane, second_plane = swaps(first_own, second_own, "px")
     values = exchanged(mix_modes(modes, x_forward, weights, x_inverse))
     planes = (first_plane, first_own, second_own, second_plane)
     first_row, second_row = swaps(*edge_rows(planes), "py")
-    rows = channels * cells_x * cells_y
-    interior = convolve(interior_kernel, "convolve_interior", planes + (taps,), rows)
+    rows = channels * cells_x
+    interior = convolve(interior_kernel, "convolve_interior", planes + (taps,), rows * cells_y)
     edges = convolve(
-        edge_kernel, "convolve_edges", planes + (first_row, second_row, taps), rows // cells_y * 8
+        edge_kernel, "convolve_edges", planes + (first_row, second_row, taps), rows * 8
     )
     return finish(
         conv_bias,
         values,
         z_inverse,
-        y_expanded,
+        y_inverse,
         interior.reshape(channels, cells_x, cells_y, depth),
         edges.reshape(channels, cells_x, 8, depth),
     )

time: 37.6 us -> 35.3 us (0.939)
  local copies, waits for them, and re-layouts: 3.17 us -> 0.03 us
  starting transfers between devices: 17.4 us -> 19.5 us
  waiting for transfers between devices: 5.11 us -> 3.93 us
    unnamed x18 -> x10, local copies, waits for them, and re-layouts: 3.17 us -> 0.03 us
    ppermute x4, starting transfers between devices: 3.37 us -> 6.48 us  [the longest x2 5.02 us: swaps(): lax.ppermute(second, axis, inside)]
    all_to_all x2, starting transfers between devices: 14 us -> 13 us  [exchanged(): lax.all_to_all(value, ('px', 'py'), split_axis=0, concat_axis=0, tiled=True)]
    ppermute x4, waiting for transfers between devices: 0.63 us -> 0.01 us  [the longest x2 0.01 us: swaps(): lax.ppermute(second, axis, inside)]
    all_to_all x2, waiting for transfers between devices: 4.48 us -> 3.91 us  [exchanged(): lax.all_to_all(value, ('px', 'py'), split_axis=0, concat_axis=0, tiled=True)]
  transfers between devices with their start and end apart: 6 -> 6, of which waited for: 3 -> 2; matrix products, arithmetic and copies ran while one was open for 0% -> 0% of each run, Pallas kernels for 18% -> 19%
where the time goes in v6:
time: 35.3 us; the launch traced here: 35 us
  starting transfers between devices  19.5 us (55%)
  Pallas kernels  11.5 us (33%)
  waiting for transfers between devices  3.93 us (11%)
    all_to_all x2, starting transfers between devices, exchanged(): lax.all_to_all(value, ('px', 'py'), split_axis=0, concat_axis=0, tiled=True)  13 us
    ppermute x2, starting transfers between devices, swaps(): lax.ppermute(second, axis, inside)  5.02 us
    all_to_all x2, waiting for transfers between devices, exchanged(): lax.all_to_all(value, ('px', 'py'), split_axis=0, concat_axis=0, tiled=True)  3.91 us
    pallas_call x1, Pallas kernels, forward_modes(): pl.pallas_call(forward_kernel, out_shape=(jax.ShapeDtypeStruct((32, 8, 12...  2.68 us
    pallas_call x1, Pallas kernels, pack(): pl.pallas_call(pack_kernel, out_shape=(jax.ShapeDtypeStruct((2, 4, 16, KX...  2.6 us
    pallas_call x1, Pallas kernels, finish(): pl.pallas_call(finish_kernel, out_shape=jax.ShapeDtypeStruct(convolved.sh...  2.04 us
    pallas_call x2, Pallas kernels, convolve(): pl.pallas_call(kernel, out_shape=jax.ShapeDtypeStruct((rows, 128), jnp.fl...  1.83 us
    pallas_call x1, Pallas kernels, mix_modes(): pl.pallas_call(mix_kernel, out_shape=jax.ShapeDtypeStruct((32, 16, 128),...  1.62 us
  transfers between devices with their start and end apart: 6, of which 2 were waited for; matrix products, arithmetic and copies ran while one was open for 0% of the time, Pallas kernels for 19%

profile of v6, /device:TPU:0, one launch (start us, length us, event | category | flops | bytes accessed | tf_op | source)
XLA Modules:
  0.0 35.0 jit_solution(4261928694459235742)
XLA Ops:
  0.0 2.7 %forward_modes.1 = (bf16[32,8,128]{2,1,0:T(8,128)(2,1)}, bf16[64,32,128]{2,1,0:T(8,128)(2,1)S(1)}) custom-call(bf16[64,32,128]{2,1,0:T(8,128)(2,1)} %bitcast.10, f32[32,128]{1,0:T(8,128)} %constant.12.clone.z_hbm, f32[4,64,512]{2,1,0:T(8,128)} %constant.13.clone.y_hbm), custom_call_target="tpu_custom_call" | custom-call | flops 134217728 | bytes 2097152 | tf_op jit(solution)/shard_map/forward_modes/pallas_call | solution.py:289
  2.7 7.3 %all-to-all-start = ((bf16[32,8,128]{2,1,0:T(8,128)(2,1)}), bf16[32,8,128]{2,1,0:T(8,128)(2,1)S(1)}, u32[]{:S(2)}, u32[]{:S(2)}) async-start(bf16[32,8,128]{2,1,0:T(8,128)(2,1)} %get-tuple-element.13), calls=%async_computation | async-start | bytes 131072 | tf_op jit(solution)/shard_map/all_to_all | solution.py:617
  10.0 0.7 %arrange_cells.1 = (bf16[32,32,128]{2,1,0:T(8,128)(2,1)S(1)}, bf16[32,32,128]{2,1,0:T(8,128)(2,1)S(1)}) custom-call(bf16[32,2,32,128]{3,2,1,0:T(8,128)(2,1)S(1)} %bitcast.7), custom_call_target="tpu_custom_call" | custom-call | flops 1024 | bytes 1024 | tf_op jit(solution)/shard_map/arrange_cells/pallas_call | solution.py:322
  10.7 1.8 %collective-permute-start.1 = (bf16[32,32,128]{2,1,0:T(8,128)(2,1)S(1)}, bf16[32,32,128]{2,1,0:T(8,128)(2,1)S(1)}, u32[]{:S(2)}, u32[]{:S(2)}) collective-permute-start(bf16[32,32,128]{2,1,0:T(8,128)(2,1)S(1)} %get-tuple-element.17.refs_2_), channel_id=1, source_target_pairs={{0,4},{4,0},{8,12},{12,8},{16,20},{20,16},{24,28},{28,24},{1,5},{5... | collective-permute-start | bytes 786440 | tf_op jit(solution)/shard_map/ppermute | solution.py:624
  12.5 0.7 %collective-permute-start = (bf16[32,32,128]{2,1,0:T(8,128)(2,1)S(1)}, bf16[32,32,128]{2,1,0:T(8,128)(2,1)S(1)}, u32[]{:S(2)}, u32[]{:S(2)}) collective-permute-start(bf16[32,32,128]{2,1,0:T(8,128)(2,1)S(1)} %get-tuple-element.15.after_ref.refs_1_), channel_id=1, source_target_pairs={{4,8},{8,4},{12,16},{16,12},{20,24},{24,20},{5,9},{9,5},{13,17},{1... | collective-permute-start | bytes 786440 | tf_op jit(solution)/shard_map/ppermute | solution.py:624
  13.2 2.6 %pack_weights.1 = (f32[2,4,16,16,128]{4,3,2,1,0:T(8,128)S(1)}, bf16[384,512]{1,0:T(8,128)(2,1)S(1)}) custom-call(bf16[32,32,128]{2,1,0:T(8,128)(2,1)S(1)} %get-tuple-element.15.after_ref.refs_1_, f32[2,4,4,16,16,32]{5,4,3,2,1,0:T(8,128)} %bitcast.9, bf16[3,3,3,32,32]{4,3,2,1,0:T(8,128)(2,1)} %bitcast.11), custom_call_target="tpu_custom_call" | custom-call | flops 1024 | bytes 1024 | tf_op jit(solution)/shard_map/pack_weights/pallas_call | solution.py:376
  15.8 1.6 %all-to-all-done.modes_ref = bf16[32,8,128]{2,1,0:T(8,128)(2,1)S(1)} async-done(((bf16[32,8,128]{2,1,0:T(8,128)(2,1)}), bf16[32,8,128]{2,1,0:T(8,128)(2,1)S(1)}, u32[]{:S(2)}, u32[]{:S(2)}) %all-to-all-start) | async-done | bytes 65568 | tf_op jit(solution)/shard_map/all_to_all | solution.py:617
  17.4 0.0 copy-done.3
  17.4 1.6 %mix_modes.1 = bf16[32,16,128]{2,1,0:T(8,128)(2,1)} custom-call(bf16[32,8,128]{2,1,0:T(8,128)(2,1)S(1)} %all-to-all-done.modes_ref, f32[64,256]{1,0:T(8,128)S(1)} %copy-done.4, f32[2,4,16,16,128]{4,3,2,1,0:T(8,128)S(1)} %get-tuple-element.16.weight_ref, f32[128,128]{1,0:T(8,128)S(1)} %copy-done.3), custom_call_target="tpu_custom_call" | custom-call | flops 34359738368 | bytes 2097152 | tf_op jit(solution)/shard_map/mix_modes/pallas_call | solution.py:432
  19.0 5.7 %all-to-all-start.1 = ((bf16[32,16,128]{2,1,0:T(8,128)(2,1)}), bf16[32,16,128]{2,1,0:T(8,128)(2,1)S(1)}, u32[]{:S(2)}, u32[]{:S(2)}) async-start(bf16[32,16,128]{2,1,0:T(8,128)(2,1)} %mix_modes.1), calls=%async_computation.1 | async-start | bytes 262144 | tf_op jit(solution)/shard_map/all_to_all | solution.py:617
  24.7 0.0 collective-permute-done.1.refs_3_
  24.8 0.0 collective-permute-done.refs_0_
  24.8 0.0 copy-start
  24.8 0.0 copy-start.1
  24.8 0.0 copy-start.2
  24.8 0.8 %collective-permute-start.2 = (bf16[128,128]{1,0:T(8,128)(2,1)S(1)}, bf16[128,128]{1,0:T(8,128)(2,1)S(1)}, u32[]{:S(2)}, u32[]{:S(2)}) collective-permute-start(bf16[128,128]{1,0:T(8,128)(2,1)S(1)} %get-tuple-element.19), channel_id=1, source_target_pairs={{1,2},{2,1},{5,6},{6,5},{9,10},{10,9},{13,14},{14,13},{17,18},{18,... | collective-permute-start | bytes 98312 | tf_op jit(solution)/shard_map/ppermute | solution.py:624
  25.6 3.2 %collective-permute-start.3 = (bf16[128,128]{1,0:T(8,128)(2,1)S(1)}, bf16[128,128]{1,0:T(8,128)(2,1)S(1)}, u32[]{:S(2)}, u32[]{:S(2)}) collective-permute-start(bf16[128,128]{1,0:T(8,128)(2,1)S(1)} %get-tuple-element.20), channel_id=1, source_target_pairs={{0,1},{1,0},{2,3},{3,2},{4,5},{5,4},{6,7},{7,6},{8,9},{9,8},{10,11... | collective-permute-start | bytes 98312 | tf_op jit(solution)/shard_map/ppermute | solution.py:624
  28.8 1.3 %convolve_interior.1 = f32[2048,128]{1,0:T(8,128)S(1)} custom-call(bf16[32,32,128]{2,1,0:T(8,128)(2,1)S(1)} %collective-permute-done.refs_0_, bf16[32,32,128]{2,1,0:T(8,128)(2,1)S(1)} %get-tuple-element.15.after_ref.refs_1_, bf16[32,32,128]{2,1,0:T(8,128)(2,1)S(1)} %get-tuple-element.17.refs_2_, bf16[32,32,128]{2,1,0:T(8,128)(2,1)S(1)} %collective-permute-done.1.refs_3_, ...), custom_call_target="tpu_custom_call" | custom-call | flops 1073741824 | bytes 2097152 | tf_op jit(solution)/shard_map/convolve_interior/pallas_call | solution.py:519
  30.2 0.0 collective-permute-done.2.refs_4_
  30.2 0.0 collective-permute-done.3.refs_5_
  30.2 0.5 %convolve_edges.1 = f32[512,128]{1,0:T(8,128)S(1)} custom-call(bf16[32,32,128]{2,1,0:T(8,128)(2,1)S(1)} %collective-permute-done.refs_0_, bf16[32,32,128]{2,1,0:T(8,128)(2,1)S(1)} %get-tuple-element.15.after_ref.refs_1_, bf16[32,32,128]{2,1,0:T(8,128)(2,1)S(1)} %get-tuple-element.17.refs_2_, bf16[32,32,128]{2,1,0:T(8,128)(2,1)S(1)} %collective-permute-done.1.refs_3_, ...), custom_call_target="tpu_custom_call" | custom-call | flops 1073741824 | bytes 2097152 | tf_op jit(solution)/shard_map/convolve_edges/pallas_call | solution.py:519
  30.7 2.3 %all-to-all-done.1.values_ref = bf16[32,16,128]{2,1,0:T(8,128)(2,1)S(1)} async-done(((bf16[32,16,128]{2,1,0:T(8,128)(2,1)}), bf16[32,16,128]{2,1,0:T(8,128)(2,1)S(1)}, u32[]{:S(2)}, u32[]{:S(2)}) %all-to-all-start.1) | async-done | bytes 131104 | tf_op jit(solution)/shard_map/all_to_all | solution.py:617
  33.0 0.0 copy-done.1
  33.0 2.0 %finish_layer.1 = bf16[32,2,32,128]{3,2,1,0:T(8,128)(2,1)} custom-call(f32[32]{0:T(128)S(1)} %copy-done.2, bf16[32,16,128]{2,1,0:T(8,128)(2,1)S(1)} %all-to-all-done.1.values_ref, f32[128,512]{1,0:T(8,128)S(1)} %copy-done.1, f32[4,32,512]{2,1,0:T(8,128)S(1)} %copy-done, f32[32,2,32,128]{3,2,1,0:T(8,128)S(1)} %bitcast.6, f32[32,2,8,128]{3,2,1,0:T(8,128)S(1)} %bitcast.8), custom_call_target="tpu_custom_call" | custom-call | flops 268435456 | bytes 4194304 | tf_op jit(solution)/shard_map/finish_layer/pallas_call | solution.py:601
  (6 shorter events, 0.0 us)
Async XLA Ops:
  0.0 17.4 %copy-start.3 = (f32[128,128]{1,0:T(8,128)S(1)}, f32[128,128]{1,0:T(8,128)}, u32[]{:S(2)}) copy-start(f32[128,128]{1,0:T(8,128)} %constant.15.clone.inverse_ref) | copy-start | bytes 196612
  0.0 17.4 %copy-start.4 = (f32[64,256]{1,0:T(8,128)S(1)}, f32[64,256]{1,0:T(8,128)}, u32[]{:S(2)}) copy-start(f32[64,256]{1,0:T(8,128)} %constant.14.clone.forward_ref) | copy-start | bytes 196612
  2.7 14.7 %all-to-all-start = ((bf16[32,8,128]{2,1,0:T(8,128)(2,1)}), bf16[32,8,128]{2,1,0:T(8,128)(2,1)S(1)}, u32[]{:S(2)}, u32[]{:S(2)}) async-start(bf16[32,8,128]{2,1,0:T(8,128)(2,1)} %get-tuple-element.13), calls=%async_computation | async-start | bytes 131072 | tf_op jit(solution)/shard_map/all_to_all | solution.py:617
  10.7 14.1 %collective-permute-start.1 = (bf16[32,32,128]{2,1,0:T(8,128)(2,1)S(1)}, bf16[32,32,128]{2,1,0:T(8,128)(2,1)S(1)}, u32[]{:S(2)}, u32[]{:S(2)}) collective-permute-start(bf16[32,32,128]{2,1,0:T(8,128)(2,1)S(1)} %get-tuple-element.17.refs_2_), channel_id=1, source_target_pairs={{0,4},{4,0},{8,12},{12,8},{16,20},{20,16},{24,28},{28,24},{1,5},{5... | collective-permute-start | bytes 786440 | tf_op jit(solution)/shard_map/ppermute | solution.py:624
  12.5 12.3 %collective-permute-start = (bf16[32,32,128]{2,1,0:T(8,128)(2,1)S(1)}, bf16[32,32,128]{2,1,0:T(8,128)(2,1)S(1)}, u32[]{:S(2)}, u32[]{:S(2)}) collective-permute-start(bf16[32,32,128]{2,1,0:T(8,128)(2,1)S(1)} %get-tuple-element.15.after_ref.refs_1_), channel_id=1, source_target_pairs={{4,8},{8,4},{12,16},{16,12},{20,24},{24,20},{5,9},{9,5},{13,17},{1... | collective-permute-start | bytes 786440 | tf_op jit(solution)/shard_map/ppermute | solution.py:624
  19.0 13.9 %all-to-all-start.1 = ((bf16[32,16,128]{2,1,0:T(8,128)(2,1)}), bf16[32,16,128]{2,1,0:T(8,128)(2,1)S(1)}, u32[]{:S(2)}, u32[]{:S(2)}) async-start(bf16[32,16,128]{2,1,0:T(8,128)(2,1)} %mix_modes.1), calls=%async_computation.1 | async-start | bytes 262144 | tf_op jit(solution)/shard_map/all_to_all | solution.py:617
  24.8 8.2 %copy-start = (f32[4,32,512]{2,1,0:T(8,128)S(1)}, f32[4,32,512]{2,1,0:T(8,128)}, u32[]{:S(2)}) copy-start(f32[4,32,512]{2,1,0:T(8,128)} %constant.17.clone.y_ref) | copy-start | bytes 786436
  24.8 8.2 %copy-start.1 = (f32[128,512]{1,0:T(8,128)S(1)}, f32[128,512]{1,0:T(8,128)}, u32[]{:S(2)}) copy-start(f32[128,512]{1,0:T(8,128)} %constant.16.clone.z_ref) | copy-start | bytes 786436
  24.8 8.2 %copy-start.2 = (f32[32]{0:T(128)S(1)}, f32[32]{0:T(128)}, u32[]{:S(2)}) copy-start(f32[32]{0:T(128)} %bias_ref.1) | copy-start | bytes 388
  24.8 5.3 %collective-permute-start.2 = (bf16[128,128]{1,0:T(8,128)(2,1)S(1)}, bf16[128,128]{1,0:T(8,128)(2,1)S(1)}, u32[]{:S(2)}, u32[]{:S(2)}) collective-permute-start(bf16[128,128]{1,0:T(8,128)(2,1)S(1)} %get-tuple-element.19), channel_id=1, source_target_pairs={{1,2},{2,1},{5,6},{6,5},{9,10},{10,9},{13,14},{14,13},{17,18},{18,... | collective-permute-start | bytes 98312 | tf_op jit(solution)/shard_map/ppermute | solution.py:624
  25.6 4.6 %collective-permute-start.3 = (bf16[128,128]{1,0:T(8,128)(2,1)S(1)}, bf16[128,128]{1,0:T(8,128)(2,1)S(1)}, u32[]{:S(2)}, u32[]{:S(2)}) collective-permute-start(bf16[128,128]{1,0:T(8,128)(2,1)S(1)} %get-tuple-element.20), channel_id=1, source_target_pairs={{0,1},{1,0},{2,3},{3,2},{4,5},{5,4},{6,7},{7,6},{8,9},{9,8},{10,11... | collective-permute-start | bytes 98312 | tf_op jit(solution)/shard_map/ppermute | solution.py:624

commit v7 on v6

--- a/solution.py
+++ b/solution.py
@@ -215,7 +215,9 @@
         narrow(z_forward),
         narrow(y_forward),
         narrow(x_forward),
-        x_inverse.astype(np.float32),
+        np.concatenate(
+            [narrow(x_inverse), narrow(x_inverse), narrow(x_inverse - narrow(x_inverse))], axis=1
+        ),
         narrow(z_inverse),
         narrow(y_inverse),
     )
@@ -236,7 +238,9 @@
     return result
 
 
-def forward_kernel(state_hbm, z_hbm, y_hbm, out_ref, state_ref, z_ref, y_ref, table_ref, sems):
+def forward_kernel(
+    state_hbm, z_hbm, y_hbm, weight_hbm, out_ref, state_ref, weight_ref, z_ref, y_ref, table_ref, sems
+):
     count = state_ref.shape[0] // 4
     span = state_ref.shape[1]
     y_copy = pltpu.make_async_copy(y_hbm.at[lax.axis_index("py")], y_ref, sems.at[0])
@@ -249,7 +253,8 @@
         )
         for g in range(4)
     ]
-    for copy in [y_copy, z_copy] + copies:
+    weight_copy = pltpu.make_async_copy(weight_hbm.at[0], weight_ref, sems.at[6])
+    for copy in [y_copy, z_copy] + copies + [weight_copy]:
         copy.start()
     y_copy.wait()
     table = y_ref[...]
@@ -283,36 +288,44 @@
                     rows4 = slice(4 * side, 4 * side + 4)
                     chunk = jnp.concatenate([first[rows4], second[rows4]], axis=0)
                     out_ref[(half * 4 + group) * 4 + 2 * pair + side] = chunk.astype(jnp.bfloat16)
-
-
-def forward_modes(state, z_table, y_table):
+    weight_copy.wait()
+
+
+def forward_modes(state, z_table, y_table, spectral_weight):
     return pl.pallas_call(
         forward_kernel,
         out_shape=(
             jax.ShapeDtypeStruct((32, 8, 128), jnp.bfloat16),
             jax.ShapeDtypeStruct(state.shape, jnp.bfloat16),
+            jax.ShapeDtypeStruct(spectral_weight.shape[1:], jnp.float32),
         ),
-        in_specs=[pl.BlockSpec(memory_space=pltpu.HBM)] * 3,
-        out_specs=(pl.BlockSpec(memory_space=pltpu.VMEM),) * 2,
+        in_specs=[pl.BlockSpec(memory_space=pltpu.HBM)] * 4,
+        out_specs=(pl.BlockSpec(memory_space=pltpu.VMEM),) * 3,
         scratch_shapes=[
             pltpu.VMEM(z_table.shape, jnp.float32),
             pltpu.VMEM(y_table.shape[1:], jnp.float32),
             pltpu.VMEM((32 * state.shape[1], y_table.shape[2]), jnp.bfloat16),
-            pltpu.SemaphoreType.DMA((6,)),
+            pltpu.SemaphoreType.DMA((7,)),
         ],
         compiler_params=pltpu.CompilerParams(vmem_limit_bytes=16 * 2**20),
         cost_estimate=pl.CostEstimate(flops=2**27, bytes_accessed=2**21, transcendentals=0),
         name="forward_modes",
-    )(*(pltpu.with_memory_space_constraint(v, pltpu.HBM) for v in (state, z_table, y_table)))
-
-
-def arrange_kernel(state_ref, first_ref, second_ref, wide):
+    )(
+        *(
+            pltpu.with_memory_space_constraint(v, pltpu.HBM)
+            for v in (state, z_table, y_table, spectral_weight)
+        )
+    )
+
+
+def arrange_kernel(state_ref, first_ref, second_ref, token_ref, wide):
     odd_x = lax.rem(lax.axis_index("px"), 2)
     cells_y = state_ref.shape[2]
     for slot, (out_ref, x) in enumerate(((first_ref, odd_x), (second_ref, 1 - odd_x))):
         wide[slot] = state_ref[:, x].astype(jnp.float32).reshape(32 * cells_y, 128)
         for y in range(cells_y):
             out_ref[y] = wide[slot, pl.ds(y, 32, stride=cells_y), :].astype(jnp.bfloat16)
+    token_ref[...] = jnp.zeros_like(token_ref)
 
 
 def arrange(state):
@@ -321,9 +334,9 @@
     plane = jax.ShapeDtypeStruct((cells_y, 32, 128), jnp.bfloat16)
     return pl.pallas_call(
         arrange_kernel,
-        out_shape=(plane, plane),
+        out_shape=(plane, plane, jax.ShapeDtypeStruct((8, 128), jnp.float32)),
         in_specs=[vmem],
-        out_specs=(vmem, vmem),
+        out_specs=(vmem,) * 3,
         scratch_shapes=[pltpu.VMEM((2, 32 * cells_y, 128), jnp.float32)],
         compiler_params=pltpu.CompilerParams(vmem_limit_bytes=16 * 2**20),
         cost_estimate=pl.CostEstimate(flops=2**10, bytes_accessed=2**10, transcendentals=0),
@@ -332,15 +345,11 @@
 
 
 def pack_kernel(
-    after_ref, weight_hbm, conv_hbm, weight_out, conv_out, weight_ref, conv_ref, sems
+    after_ref, real_ref, weight_hbm, conv_hbm, weight_out, conv_out, imag_ref, conv_ref, sems
 ):
-    conv_copy = pltpu.make_async_copy(conv_hbm, conv_ref, sems.at[8])
+    conv_copy = pltpu.make_async_copy(conv_hbm, conv_ref, sems.at[4])
     copies = [
-        pltpu.make_async_copy(
-            weight_hbm.at[part, kz], weight_ref.at[part, kz], sems.at[part * 4 + kz]
-        )
-        for part in range(2)
-        for kz in range(4)
+        pltpu.make_async_copy(weight_hbm.at[1, kz], imag_ref.at[kz], sems.at[kz]) for kz in range(4)
     ]
     for copy in [conv_copy] + copies:
         copy.start()
@@ -362,16 +371,17 @@
                     conv_out[row : row + 32, y_in * 128 : (y_in + 1) * 128] = jnp.concatenate(
                         blocks, axis=1
                     ).astype(jnp.bfloat16)
-    for part in range(2):
+    for part, part_ref in enumerate((real_ref, imag_ref)):
         for kz in range(4):
-            copies[part * 4 + kz].wait()
+            if part == 1:
+                copies[kz].wait()
             for c in range(16):
                 weight_out[part, kz, c] = jnp.concatenate(
-                    [weight_ref[part, kz, u, c] for u in range(4)], axis=1
+                    [part_ref[kz, u, c] for u in range(4)], axis=1
                 )
 
 
-def pack(after, spectral_weight, conv_weight):
+def pack(after, real_weight, spectral_weight, conv_weight):
     vmem = pl.BlockSpec(memory_space=pltpu.VMEM)
     return pl.pallas_call(
         pack_kernel,
@@ -379,18 +389,20 @@
             jax.ShapeDtypeStruct((2, 4, 16, KX, 128), jnp.float32),
             jax.ShapeDtypeStruct((384, 512), jnp.bfloat16),
         ),
-        in_specs=[pl.BlockSpec(memory_space=pl.ANY)] + [pl.BlockSpec(memory_space=pltpu.HBM)] * 2,
+        in_specs=[pl.BlockSpec(memory_space=pl.ANY), vmem]
+        + [pl.BlockSpec(memory_space=pltpu.HBM)] * 2,
         out_specs=(vmem, vmem),
         scratch_shapes=[
-            pltpu.VMEM(spectral_weight.shape, jnp.float32),
+            pltpu.VMEM(spectral_weight.shape[1:], jnp.float32),
             pltpu.VMEM(conv_weight.shape, jnp.bfloat16),
-            pltpu.SemaphoreType.DMA((9,)),
+            pltpu.SemaphoreType.DMA((5,)),
         ],
         compiler_params=pltpu.CompilerParams(vmem_limit_bytes=16 * 2**20),
         cost_estimate=pl.CostEstimate(flops=2**10, bytes_accessed=2**10, transcendentals=0),
         name="pack_weights",
     )(
         after,
+        real_weight,
         *(pltpu.with_memory_space_constraint(v, pltpu.HBM) for v in (spectral_weight, conv_weight)),
     )
 
@@ -416,11 +428,13 @@
             real_sum = real_term if real_sum is None else real_sum + real_term
             imag_sum = imag_term if imag_sum is None else imag_sum + imag_term
         mixed += [real_sum, imag_sum]
+    mixed = jnp.concatenate(mixed, axis=0)
+    high = mixed.astype(jnp.bfloat16)
+    low = (mixed - high.astype(jnp.float32)).astype(jnp.bfloat16)
     values = jnp.dot(
-        inverse_ref[...],
-        jnp.concatenate(mixed, axis=0),
+        inverse_ref[...].astype(jnp.bfloat16),
+        jnp.concatenate([high, low, high], axis=0),
         preferred_element_type=jnp.float32,
-        precision=lax.Precision.HIGHEST,
     ).astype(jnp.bfloat16)
     for x in range(8):
         for y in range(4):
@@ -630,13 +644,17 @@
     if sizes != (8, 4, 2, 32, 128):
         return general_body(state_field, conv_weight, conv_bias, spectral_weight)
     z_forward, y_forward, x_forward, x_inverse, z_inverse, y_inverse = tables(*sizes)
-    sent, held = forward_modes(
-        state_field.reshape(channels * cells_x, cells_y, depth), z_forward, y_forward
+    spectral_weight = spectral_weight.swapaxes(4, 5)
+    sent, held, real_weight = forward_modes(
+        state_field.reshape(channels * cells_x, cells_y, depth),
+        z_forward,
+        y_forward,
+        spectral_weight,
     )
     modes = exchanged(sent)
-    first_own, second_own = arrange(held.reshape(state_field.shape))
+    first_own, second_own, token = arrange(held.reshape(state_field.shape))
     weights, taps = pack(
-        first_own, spectral_weight.swapaxes(4, 5), conv_weight.transpose(2, 3, 4, 0, 1)
+        token, real_weight, spectral_weight, conv_weight.transpose(2, 3, 4, 0, 1)
     )
     first_plane, second_plane = swaps(first_own, second_own, "px")
     values = exchanged(mix_modes(modes, x_forward, weights, x_inverse))

time: 35.3 us -> 37.9 us (1.074)
  local copies, waits for them, and re-layouts: 0.03 us -> 3.98 us
  waiting for transfers between devices: 3.93 us -> 1.28 us
  starting transfers between devices: 19.5 us -> 21 us
  Pallas kernels: 11.5 us -> 11 us
    unnamed x10 -> x18, local copies, waits for them, and re-layouts: 0.03 us -> 3.98 us
    ppermute x2, starting transfers between devices: 5.02 us -> 7.72 us  [swaps(): lax.ppermute(second, axis, inside)]
    all_to_all x2, waiting for transfers between devices: 3.91 us -> 1.27 us  [exchanged(): lax.all_to_all(value, ('px', 'py'), split_axis=0, concat_axis=0, tiled=True)]
    all_to_all x2, starting transfers between devices: 13 us -> 11.9 us  [exchanged(): lax.all_to_all(value, ('px', 'py'), split_axis=0, concat_axis=0, tiled=True)]
  transfers between devices with their start and end apart: 6 -> 6, of which waited for: 2 -> 1; matrix products, arithmetic and copies ran while one was open for 0% -> 0% of each run, Pallas kernels for 19% -> 17%
where the time goes in v7:
time: 37.9 us; the launch traced here: 37.5 us
  starting transfers between devices  21 us (55%)
  Pallas kernels  11 us (29%)
  local copies, waits for them, and re-layouts  3.98 us (11%)
  waiting for transfers between devices  1.28 us (3%)
    all_to_all x2, starting transfers between devices, exchanged(): lax.all_to_all(value, ('px', 'py'), split_axis=0, concat_axis=0, tiled=True)  11.9 us
    ppermute x2, starting transfers between devices, swaps(): lax.ppermute(second, axis, inside)  7.72 us
    unnamed x18, local copies, waits for them, and re-layouts  3.98 us
    pallas_call x1, Pallas kernels, forward_modes(): pl.pallas_call(forward_kernel, out_shape=(jax.ShapeDtypeStruct((32, 8, 12...  2.64 us
    pallas_call x1, Pallas kernels, pack(): pl.pallas_call(pack_kernel, out_shape=(jax.ShapeDtypeStruct((2, 4, 16, KX...  2.25 us
    pallas_call x1, Pallas kernels, finish(): pl.pallas_call(finish_kernel, out_shape=jax.ShapeDtypeStruct(convolved.sh...  2.04 us
    pallas_call x2, Pallas kernels, convolve(): pl.pallas_call(kernel, out_shape=jax.ShapeDtypeStruct((rows, 128), jnp.fl...  1.84 us
    pallas_call x1, Pallas kernels, mix_modes(): pl.pallas_call(mix_kernel, out_shape=jax.ShapeDtypeStruct((32, 16, 128),...  1.58 us
  transfers between devices with their start and end apart: 6, of which 1 were waited for; matrix products, arithmetic and copies ran while one was open for 0% of the time, Pallas kernels for 17%

profile of v7, /device:TPU:0, one launch (start us, length us, event | category | flops | bytes accessed | tf_op | source)
XLA Modules:
  0.0 37.5 jit_solution(11975610528007714956)
XLA Ops:
  0.0 2.6 %forward_modes.1 = (bf16[32,8,128]{2,1,0:T(8,128)(2,1)}, bf16[64,32,128]{2,1,0:T(8,128)(2,1)S(1)}, f32[4,4,16,16,32]{4,3,2,1,0:T(8,128)S(1)}) custom-call(bf16[64,32,128]{2,1,0:T(8,128)(2,1)} %bitcast.11, f32[32,128]{1,0:T(8,128)} %constant.12.clone.z_hbm, f32[4,64,512]{2,1,0:T(8,128)} %constant.13.clone.y_hbm, f32[2,4,4,16,16,32]{5,4,3,2,1,0:T(8,128)} %bitcast.9), custom_call_target="tpu_custom_call" | custom-call | flops 134217728 | bytes 2097152 | tf_op jit(solution)/shard_map/forward_modes/pallas_call | solution.py:295
  2.7 0.0 copy-start.7
  2.7 0.0 copy-start.8
  2.7 7.3 %all-to-all-start = ((bf16[32,8,128]{2,1,0:T(8,128)(2,1)}), bf16[32,8,128]{2,1,0:T(8,128)(2,1)S(1)}, u32[]{:S(2)}, u32[]{:S(2)}) async-start(bf16[32,8,128]{2,1,0:T(8,128)(2,1)} %get-tuple-element.15), calls=%async_computation | async-start | bytes 131072 | tf_op jit(solution)/shard_map/all_to_all | solution.py:631
  10.0 0.7 %arrange_cells.1 = (bf16[32,32,128]{2,1,0:T(8,128)(2,1)S(1)}, bf16[32,32,128]{2,1,0:T(8,128)(2,1)S(1)}, f32[8,128]{1,0:T(8,128)S(1)}) custom-call(bf16[32,2,32,128]{3,2,1,0:T(8,128)(2,1)S(1)} %bitcast.7), custom_call_target="tpu_custom_call" | custom-call | flops 1024 | bytes 1024 | tf_op jit(solution)/shard_map/arrange_cells/pallas_call | solution.py:335
  10.7 0.7 %collective-permute-start = (bf16[32,32,128]{2,1,0:T(8,128)(2,1)S(1)}, bf16[32,32,128]{2,1,0:T(8,128)(2,1)S(1)}, u32[]{:S(2)}, u32[]{:S(2)}) collective-permute-start(bf16[32,32,128]{2,1,0:T(8,128)(2,1)S(1)} %get-tuple-element.20.refs_1_), channel_id=1, source_target_pairs={{4,8},{8,4},{12,16},{16,12},{20,24},{24,20},{5,9},{9,5},{13,17},{1... | collective-permute-start | bytes 786440 | tf_op jit(solution)/shard_map/ppermute | solution.py:638
  11.3 4.5 %collective-permute-start.1 = (bf16[32,32,128]{2,1,0:T(8,128)(2,1)S(1)}, bf16[32,32,128]{2,1,0:T(8,128)(2,1)S(1)}, u32[]{:S(2)}, u32[]{:S(2)}) collective-permute-start(bf16[32,32,128]{2,1,0:T(8,128)(2,1)S(1)} %get-tuple-element.21.refs_2_), channel_id=1, source_target_pairs={{0,4},{4,0},{8,12},{12,8},{16,20},{20,16},{24,28},{28,24},{1,5},{5... | collective-permute-start | bytes 786440 | tf_op jit(solution)/shard_map/ppermute | solution.py:638
  15.9 2.2 %pack_weights.1 = (f32[2,4,16,16,128]{4,3,2,1,0:T(8,128)S(1)}, bf16[384,512]{1,0:T(8,128)(2,1)S(1)}) custom-call(f32[8,128]{1,0:T(8,128)S(1)} %get-tuple-element.17.after_ref, f32[4,4,16,16,32]{4,3,2,1,0:T(8,128)S(1)} %get-tuple-element.18.real_ref, f32[2,4,4,16,16,32]{5,4,3,2,1,0:T(8,128)} %bitcast.10, bf16[3,3,3,32,32]{4,3,2,1,0:T(8,128)(2,1)} %bitcast.12), custom_call_target="tpu_custom_call" | custom-call | flops 1024 | bytes 1024 | tf_op jit(solution)/shard_map/pack_weights/pallas_call | solution.py:386
  18.1 1.0 %copy-done.3 = f32[2,4,16,16,128]{4,3,2,1,0:T(8,128)} copy-done((f32[2,4,16,16,128]{4,3,2,1,0:T(8,128)}, f32[2,4,16,16,128]{4,3,2,1,0:T(8,128)S(1)}, u32[]{:S(2)}) %copy-start.3) | copy-done | bytes 1048600
  19.1 0.7 %copy-done.5 = bf16[384,512]{1,0:T(8,128)(2,1)} copy-done((bf16[384,512]{1,0:T(8,128)(2,1)}, bf16[384,512]{1,0:T(8,128)(2,1)S(1)}, u32[]{:S(2)}) %copy-start.5) | copy-done | bytes 393240
  19.9 1.2 %copy-done.4 = f32[2,4,16,16,128]{4,3,2,1,0:T(8,128)S(1)} copy-done((f32[2,4,16,16,128]{4,3,2,1,0:T(8,128)S(1)}, f32[2,4,16,16,128]{4,3,2,1,0:T(8,128)}, u32[]{:S(2)}) %copy-start.4) | copy-done | bytes 1048600
  21.1 1.6 %mix_modes.1 = bf16[32,16,128]{2,1,0:T(8,128)(2,1)} custom-call(bf16[32,8,128]{2,1,0:T(8,128)(2,1)S(1)} %all-to-all-done.modes_ref, f32[64,256]{1,0:T(8,128)S(1)} %copy-done.8, f32[2,4,16,16,128]{4,3,2,1,0:T(8,128)S(1)} %copy-done.4, f32[128,384]{1,0:T(8,128)S(1)} %copy-done.7), custom_call_target="tpu_custom_call" | custom-call | flops 34359738368 | bytes 2097152 | tf_op jit(solution)/shard_map/mix_modes/pallas_call | solution.py:446
  22.7 4.5 %all-to-all-start.1 = ((bf16[32,16,128]{2,1,0:T(8,128)(2,1)}), bf16[32,16,128]{2,1,0:T(8,128)(2,1)S(1)}, u32[]{:S(2)}, u32[]{:S(2)}) async-start(bf16[32,16,128]{2,1,0:T(8,128)(2,1)} %mix_modes.1), calls=%async_computation.1 | async-start | bytes 262144 | tf_op jit(solution)/shard_map/all_to_all | solution.py:631
  27.2 0.0 collective-permute-done.refs_0_
  27.3 0.0 copy-start
  27.3 0.0 copy-start.1
  27.3 0.0 copy-start.2
  27.3 0.8 %collective-permute-start.2 = (bf16[128,128]{1,0:T(8,128)(2,1)S(1)}, bf16[128,128]{1,0:T(8,128)(2,1)S(1)}, u32[]{:S(2)}, u32[]{:S(2)}) collective-permute-start(bf16[128,128]{1,0:T(8,128)(2,1)S(1)} %get-tuple-element.23), channel_id=1, source_target_pairs={{1,2},{2,1},{5,6},{6,5},{9,10},{10,9},{13,14},{14,13},{17,18},{18,... | collective-permute-start | bytes 98312 | tf_op jit(solution)/shard_map/ppermute | solution.py:638
  28.1 3.2 %collective-permute-start.3 = (bf16[128,128]{1,0:T(8,128)(2,1)S(1)}, bf16[128,128]{1,0:T(8,128)(2,1)S(1)}, u32[]{:S(2)}, u32[]{:S(2)}) collective-permute-start(bf16[128,128]{1,0:T(8,128)(2,1)S(1)} %get-tuple-element.24), channel_id=1, source_target_pairs={{0,1},{1,0},{2,3},{3,2},{4,5},{5,4},{6,7},{7,6},{8,9},{9,8},{10,11... | collective-permute-start | bytes 98312 | tf_op jit(solution)/shard_map/ppermute | solution.py:638
  31.3 1.0 %copy-done.6 = bf16[384,512]{1,0:T(8,128)(2,1)S(1)} copy-done((bf16[384,512]{1,0:T(8,128)(2,1)S(1)}, bf16[384,512]{1,0:T(8,128)(2,1)}, u32[]{:S(2)}) %copy-start.6) | copy-done | bytes 393240
  32.3 1.3 %convolve_interior.1 = f32[2048,128]{1,0:T(8,128)S(1)} custom-call(bf16[32,32,128]{2,1,0:T(8,128)(2,1)S(1)} %collective-permute-done.refs_0_, bf16[32,32,128]{2,1,0:T(8,128)(2,1)S(1)} %get-tuple-element.20.refs_1_, bf16[32,32,128]{2,1,0:T(8,128)(2,1)S(1)} %get-tuple-element.21.refs_2_, bf16[32,32,128]{2,1,0:T(8,128)(2,1)S(1)} %collective-permute-done.1.refs_3_, ...), custom_call_target="tpu_custom_call" | custom-call | flops 1073741824 | bytes 2097152 | tf_op jit(solution)/shard_map/convolve_interior/pallas_call | solution.py:533
  33.7 0.5 %convolve_edges.1 = f32[512,128]{1,0:T(8,128)S(1)} custom-call(bf16[32,32,128]{2,1,0:T(8,128)(2,1)S(1)} %collective-permute-done.refs_0_, bf16[32,32,128]{2,1,0:T(8,128)(2,1)S(1)} %get-tuple-element.20.refs_1_, bf16[32,32,128]{2,1,0:T(8,128)(2,1)S(1)} %get-tuple-element.21.refs_2_, bf16[32,32,128]{2,1,0:T(8,128)(2,1)S(1)} %collective-permute-done.1.refs_3_, ...), custom_call_target="tpu_custom_call" | custom-call | flops 1073741824 | bytes 2097152 | tf_op jit(solution)/shard_map/convolve_edges/pallas_call | solution.py:533
  34.2 1.3 %all-to-all-done.1.values_ref = bf16[32,16,128]{2,1,0:T(8,128)(2,1)S(1)} async-done(((bf16[32,16,128]{2,1,0:T(8,128)(2,1)}), bf16[32,16,128]{2,1,0:T(8,128)(2,1)S(1)}, u32[]{:S(2)}, u32[]{:S(2)}) %all-to-all-start.1) | async-done | bytes 131104 | tf_op jit(solution)/shard_map/all_to_all | solution.py:631
  35.5 2.0 %finish_layer.1 = bf16[32,2,32,128]{3,2,1,0:T(8,128)(2,1)} custom-call(f32[32]{0:T(128)S(1)} %copy-done.2, bf16[32,16,128]{2,1,0:T(8,128)(2,1)S(1)} %all-to-all-done.1.values_ref, f32[128,512]{1,0:T(8,128)S(1)} %copy-done.1, f32[4,32,512]{2,1,0:T(8,128)S(1)} %copy-done, f32[32,2,32,128]{3,2,1,0:T(8,128)S(1)} %bitcast.6, f32[32,2,8,128]{3,2,1,0:T(8,128)S(1)} %bitcast.8), custom_call_target="tpu_custom_call" | custom-call | flops 268435456 | bytes 4194304 | tf_op jit(solution)/shard_map/finish_layer/pallas_call | solution.py:615
  (14 shorter events, 0.1 us)
Async XLA Ops:
  2.7 17.2 %copy-start.7 = (f32[128,384]{1,0:T(8,128)S(1)}, f32[128,384]{1,0:T(8,128)}, u32[]{:S(2)}) copy-start(f32[128,384]{1,0:T(8,128)} %constant.15.clone.inverse_ref) | copy-start | bytes 589828
  2.7 17.2 %copy-start.8 = (f32[64,256]{1,0:T(8,128)S(1)}, f32[64,256]{1,0:T(8,128)}, u32[]{:S(2)}) copy-start(f32[64,256]{1,0:T(8,128)} %constant.14.clone.forward_ref) | copy-start | bytes 196612
  2.7 17.2 %all-to-all-start = ((bf16[32,8,128]{2,1,0:T(8,128)(2,1)}), bf16[32,8,128]{2,1,0:T(8,128)(2,1)S(1)}, u32[]{:S(2)}, u32[]{:S(2)}) async-start(bf16[32,8,128]{2,1,0:T(8,128)(2,1)} %get-tuple-element.15), calls=%async_computation | async-start | bytes 131072 | tf_op jit(solution)/shard_map/all_to_all | solution.py:631
  10.7 16.6 %collective-permute-start = (bf16[32,32,128]{2,1,0:T(8,128)(2,1)S(1)}, bf16[32,32,128]{2,1,0:T(8,128)(2,1)S(1)}, u32[]{:S(2)}, u32[]{:S(2)}) collective-permute-start(bf16[32,32,128]{2,1,0:T(8,128)(2,1)S(1)} %get-tuple-element.20.refs_1_), channel_id=1, source_target_pairs={{4,8},{8,4},{12,16},{16,12},{20,24},{24,20},{5,9},{9,5},{13,17},{1... | collective-permute-start | bytes 786440 | tf_op jit(solution)/shard_map/ppermute | solution.py:638
  11.3 15.9 %collective-permute-start.1 = (bf16[32,32,128]{2,1,0:T(8,128)(2,1)S(1)}, bf16[32,32,128]{2,1,0:T(8,128)(2,1)S(1)}, u32[]{:S(2)}, u32[]{:S(2)}) collective-permute-start(bf16[32,32,128]{2,1,0:T(8,128)(2,1)S(1)} %get-tuple-element.21.refs_2_), channel_id=1, source_target_pairs={{0,4},{4,0},{8,12},{12,8},{16,20},{20,16},{24,28},{28,24},{1,5},{5... | collective-permute-start | bytes 786440 | tf_op jit(solution)/shard_map/ppermute | solution.py:638
  18.1 1.0 %copy-start.3 = (f32[2,4,16,16,128]{4,3,2,1,0:T(8,128)}, f32[2,4,16,16,128]{4,3,2,1,0:T(8,128)S(1)}, u32[]{:S(2)}) copy-start(f32[2,4,16,16,128]{4,3,2,1,0:T(8,128)S(1)} %get-tuple-element.19.weight_ref) | copy-start | bytes 3145732
  19.1 0.7 %copy-start.5 = (bf16[384,512]{1,0:T(8,128)(2,1)}, bf16[384,512]{1,0:T(8,128)(2,1)S(1)}, u32[]{:S(2)}) copy-start(bf16[384,512]{1,0:T(8,128)(2,1)S(1)} %get-tuple-element.22.refs_4_.refs_6_) | copy-start | bytes 1179652
  19.9 1.2 %copy-start.4 = (f32[2,4,16,16,128]{4,3,2,1,0:T(8,128)S(1)}, f32[2,4,16,16,128]{4,3,2,1,0:T(8,128)}, u32[]{:S(2)}) copy-start(f32[2,4,16,16,128]{4,3,2,1,0:T(8,128)} %copy-done.3) | copy-start | bytes 3145732
  22.7 12.8 %all-to-all-start.1 = ((bf16[32,16,128]{2,1,0:T(8,128)(2,1)}), bf16[32,16,128]{2,1,0:T(8,128)(2,1)S(1)}, u32[]{:S(2)}, u32[]{:S(2)}) async-start(bf16[32,16,128]{2,1,0:T(8,128)(2,1)} %mix_modes.1), calls=%async_computation.1 | async-start | bytes 262144 | tf_op jit(solution)/shard_map/all_to_all | solution.py:631
  27.3 8.2 %copy-start = (f32[4,32,512]{2,1,0:T(8,128)S(1)}, f32[4,32,512]{2,1,0:T(8,128)}, u32[]{:S(2)}) copy-start(f32[4,32,512]{2,1,0:T(8,128)} %constant.17.clone.y_ref) | copy-start | bytes 786436
  27.3 8.2 %copy-start.1 = (f32[128,512]{1,0:T(8,128)S(1)}, f32[128,512]{1,0:T(8,128)}, u32[]{:S(2)}) copy-start(f32[128,512]{1,0:T(8,128)} %constant.16.clone.z_ref) | copy-start | bytes 786436
  27.3 8.2 %copy-start.2 = (f32[32]{0:T(128)S(1)}, f32[32]{0:T(128)}, u32[]{:S(2)}) copy-start(f32[32]{0:T(128)} %bias_ref.1) | copy-start | bytes 388
  27.3 6.3 %collective-permute-start.2 = (bf16[128,128]{1,0:T(8,128)(2,1)S(1)}, bf16[128,128]{1,0:T(8,128)(2,1)S(1)}, u32[]{:S(2)}, u32[]{:S(2)}) collective-permute-start(bf16[128,128]{1,0:T(8,128)(2,1)S(1)} %get-tuple-element.23), channel_id=1, source_target_pairs={{1,2},{2,1},{5,6},{6,5},{9,10},{10,9},{13,14},{14,13},{17,18},{18,... | collective-permute-start | bytes 98312 | tf_op jit(solution)/shard_map/ppermute | solution.py:638
  28.1 5.5 %collective-permute-start.3 = (bf16[128,128]{1,0:T(8,128)(2,1)S(1)}, bf16[128,128]{1,0:T(8,128)(2,1)S(1)}, u32[]{:S(2)}, u32[]{:S(2)}) collective-permute-start(bf16[128,128]{1,0:T(8,128)(2,1)S(1)} %get-tuple-element.24), channel_id=1, source_target_pairs={{0,1},{1,0},{2,3},{3,2},{4,5},{5,4},{6,7},{7,6},{8,9},{9,8},{10,11... | collective-permute-start | bytes 98312 | tf_op jit(solution)/shard_map/ppermute | solution.py:638
  31.3 1.0 %copy-start.6 = (bf16[384,512]{1,0:T(8,128)(2,1)S(1)}, bf16[384,512]{1,0:T(8,128)(2,1)}, u32[]{:S(2)}) copy-start(bf16[384,512]{1,0:T(8,128)(2,1)} %copy-done.5) | copy-start | bytes 1179652

commit v8 on v6

--- a/solution.py
+++ b/solution.py
@@ -215,7 +215,9 @@
         narrow(z_forward),
         narrow(y_forward),
         narrow(x_forward),
-        x_inverse.astype(np.float32),
+        np.concatenate(
+            [narrow(x_inverse), narrow(x_inverse - narrow(x_inverse))], axis=1
+        ),
         narrow(z_inverse),
         narrow(y_inverse),
     )
@@ -306,13 +308,18 @@
     )(*(pltpu.with_memory_space_constraint(v, pltpu.HBM) for v in (state, z_table, y_table)))
 
 
-def arrange_kernel(state_ref, first_ref, second_ref, wide):
+def arrange_kernel(state_ref, first_ref, second_ref, sent_hbm, token_ref, wide, sem):
     odd_x = lax.rem(lax.axis_index("px"), 2)
     cells_y = state_ref.shape[2]
+    copy = pltpu.make_async_copy(first_ref, sent_hbm, sem)
     for slot, (out_ref, x) in enumerate(((first_ref, odd_x), (second_ref, 1 - odd_x))):
         wide[slot] = state_ref[:, x].astype(jnp.float32).reshape(32 * cells_y, 128)
         for y in range(cells_y):
             out_ref[y] = wide[slot, pl.ds(y, 32, stride=cells_y), :].astype(jnp.bfloat16)
+        if slot == 0:
+            copy.start()
+    token_ref[...] = jnp.zeros_like(token_ref)
+    copy.wait()
 
 
 def arrange(state):
@@ -321,10 +328,13 @@
     plane = jax.ShapeDtypeStruct((cells_y, 32, 128), jnp.bfloat16)
     return pl.pallas_call(
         arrange_kernel,
-        out_shape=(plane, plane),
+        out_shape=(plane, plane, plane, jax.ShapeDtypeStruct((8, 128), jnp.float32)),
         in_specs=[vmem],
-        out_specs=(vmem, vmem),
-        scratch_shapes=[pltpu.VMEM((2, 32 * cells_y, 128), jnp.float32)],
+        out_specs=(vmem, vmem, pl.BlockSpec(memory_space=pltpu.HBM), vmem),
+        scratch_shapes=[
+            pltpu.VMEM((2, 32 * cells_y, 128), jnp.float32),
+            pltpu.SemaphoreType.DMA,
+        ],
         compiler_params=pltpu.CompilerParams(vmem_limit_bytes=16 * 2**20),
         cost_estimate=pl.CostEstimate(flops=2**10, bytes_accessed=2**10, transcendentals=0),
         name="arrange_cells",
@@ -344,7 +354,9 @@
     ]
     for copy in [conv_copy] + copies:
         copy.start()
-    odd_x = lax.rem(lax.axis_index("px"), 2)
+    index_x = lax.axis_index("px")
+    odd_x = lax.rem(index_x, 2) == 1
+    outer = (index_x == 0) | (index_x == lax.axis_size("px") - 1)
     conv_copy.wait()
     zero = jnp.zeros((32, 32), jnp.float32)
     for dz in range(3):
@@ -358,7 +370,8 @@
                 row = ((dz * 2 + y_at) * 2 + x_at) * 32
                 for y_in in range(4):
                     blocks = [taps.get((x_in - x_at, y_in - y_at), zero) for x_in in range(4)]
-                    blocks = [jnp.where(odd_x == 1, blocks[3 - i], blocks[i]) for i in range(4)]
+                    blocks = [jnp.where(odd_x, blocks[3 - i], blocks[i]) for i in range(4)]
+                    blocks[0] = jnp.where(outer, zero, blocks[0])
                     conv_out[row : row + 32, y_in * 128 : (y_in + 1) * 128] = jnp.concatenate(
                         blocks, axis=1
                     ).astype(jnp.bfloat16)
@@ -416,11 +429,14 @@
             real_sum = real_term if real_sum is None else real_sum + real_term
             imag_sum = imag_term if imag_sum is None else imag_sum + imag_term
         mixed += [real_sum, imag_sum]
+    mixed = jnp.concatenate(mixed, axis=0)
+    inverse = inverse_ref[...].astype(jnp.bfloat16)
+    high = mixed.astype(jnp.bfloat16)
+    low = (mixed - high.astype(jnp.float32)).astype(jnp.bfloat16)
     values = jnp.dot(
-        inverse_ref[...],
-        jnp.concatenate(mixed, axis=0),
+        jnp.concatenate([inverse[:, :128], inverse], axis=1),
+        jnp.concatenate([high, low, high], axis=0),
         preferred_element_type=jnp.float32,
-        precision=lax.Precision.HIGHEST,
     ).astype(jnp.bfloat16)
     for x in range(8):
         for y in range(4):
@@ -444,26 +460,34 @@
     return jnp.concatenate([plane[y] for plane in planes], axis=0)
 
 
-def edge_rows_kernel(*refs):
-    *planes, first_ref, second_ref = refs
-    end = planes[0].shape[0] - 1
+def edge_rows_kernel(
+    gathered_ref, own_ref, other_ref, inside_ref, plane_ref, first_ref, second_ref, sem
+):
+    copy = pltpu.make_async_copy(
+        gathered_ref.at[lax.rem(lax.axis_index("px"), 2)], plane_ref, sem
+    )
+    copy.start()
+    copy.wait()
+    planes = (plane_ref, own_ref, other_ref, inside_ref)
+    end = plane_ref.shape[0] - 1
     odd_y = lax.rem(lax.axis_index("py"), 2)
     first_ref[...] = cell_row(planes, odd_y * end)
     second_ref[...] = cell_row(planes, (1 - odd_y) * end)
 
 
-def edge_rows(planes):
+def edge_rows(gathered, own, other, inside):
     vmem = pl.BlockSpec(memory_space=pltpu.VMEM)
     row = jax.ShapeDtypeStruct((128, 128), jnp.bfloat16)
     return pl.pallas_call(
         edge_rows_kernel,
-        out_shape=(row, row),
-        in_specs=[vmem] * 4,
-        out_specs=(vmem, vmem),
+        out_shape=(jax.ShapeDtypeStruct(own.shape, jnp.bfloat16), row, row),
+        in_specs=[pl.BlockSpec(memory_space=pltpu.HBM)] + [vmem] * 3,
+        out_specs=(vmem,) * 3,
+        scratch_shapes=[pltpu.SemaphoreType.DMA],
         compiler_params=pltpu.CompilerParams(vmem_limit_bytes=16 * 2**20),
         cost_estimate=pl.CostEstimate(flops=2**10, bytes_accessed=2**17, transcendentals=0),
         name="edge_rows",
-    )(*planes)
+    )(pltpu.with_memory_space_constraint(gathered, pltpu.HBM), own, other, inside)
 
 
 def convolve_quad(quad, row, weight, place, out_ref):
@@ -617,11 +641,18 @@
     return lax.all_to_all(value, ("px", "py"), split_axis=0, concat_axis=0, tiled=True)
 
 
-def swaps(first, second, axis):
+def pairs_inside(count):
+    return [(i, i ^ 1) for i in range(count)]
+
+
+def pairs_across(count):
+    return [(i, i + 1 if i % 2 else i - 1) for i in range(1, count - 1)]
+
+
+def gathered_across(value, axis):
     count = lax.axis_size(axis)
-    inside = [(i, i ^ 1) for i in range(count)]
-    across = [(i, i + 1 if i % 2 else i - 1) for i in range(1, count - 1)]
-    return lax.ppermute(first, axis, across), lax.ppermute(second, axis, inside)
+    groups = [[i, (i + 1) % count] for i in range(1, count, 2)]
+    return lax.all_gather(value, axis, axis_index_groups=groups)
 
 
 def body(state_field, conv_weight, conv_bias, spectral_weight):
@@ -634,14 +665,17 @@
         state_field.reshape(channels * cells_x, cells_y, depth), z_forward, y_forward
     )
     modes = exchanged(sent)
-    first_own, second_own = arrange(held.reshape(state_field.shape))
+    first_own, second_own, leaving, token = arrange(held.reshape(state_field.shape))
     weights, taps = pack(
-        first_own, spectral_weight.swapaxes(4, 5), conv_weight.transpose(2, 3, 4, 0, 1)
-    )
-    first_plane, second_plane = swaps(first_own, second_own, "px")
+        token, spectral_weight.swapaxes(4, 5), conv_weight.transpose(2, 3, 4, 0, 1)
+    )
+    gathered = gathered_across(leaving, "px")
+    inside = lax.ppermute(second_own, "px", pairs_inside(sizes[0]))
     values = exchanged(mix_modes(modes, x_forward, weights, x_inverse))
-    planes = (first_plane, first_own, second_own, second_plane)
-    first_row, second_row = swaps(*edge_rows(planes), "py")
+    across, *edges = edge_rows(gathered, first_own, second_own, inside)
+    planes = (across, first_own, second_own, inside)
+    first_row = lax.ppermute(edges[0], "py", pairs_across(sizes[1]))
+    second_row = lax.ppermute(edges[1], "py", pairs_inside(sizes[1]))
     rows = channels * cells_x
     interior = convolve(interior_kernel, "convolve_interior", planes + (taps,), rows * cells_y)
     edges = convolve(

time: 35.3 us -> 44 us (1.25)
  blocking collectives: 0 us -> 13.5 us
  starting transfers between devices: 19.5 us -> 15.4 us
  waiting for transfers between devices: 3.93 us -> 2.28 us
  Pallas kernels: 11.5 us -> 12.4 us
    all_gather x0 -> x1, blocking collectives: none -> 13.5 us  [gathered_across(): return lax.all_gather(value, axis, axis_index_groups=groups)]
    all_to_all x2, starting transfers between devices: 13 us -> 9.88 us  [exchanged(): lax.all_to_all(value, ('px', 'py'), split_axis=0, concat_axis=0, tiled=True)]
    all_to_all x2, waiting for transfers between devices: 3.91 us -> 2.27 us  [exchanged(): lax.all_to_all(value, ('px', 'py'), split_axis=0, concat_axis=0, tiled=True)]
    pallas_call x2, Pallas kernels: 0.68 us -> 1.67 us  [the longest x1 0.97 us: edge_rows(): pl.pallas_call(edge_rows_kernel, out_shape=(jax.ShapeDtypeStruct(own.shap...]
    ppermute x4 -> x3, starting transfers between devices: 6.48 us -> 5.55 us  [the longest x1 2.92 us: body(): second_row = lax.ppermute(edges[1], 'py', pairs_inside(sizes[1]))]
  transfers between devices with their start and end apart: 6 -> 5, of which waited for: 2 -> 1; matrix products, arithmetic and copies ran while one was open for 0% -> 0% of each run, Pallas kernels for 19% -> 18%
where the time goes in v8:
time: 44 us; the launch traced here: 43.7 us
  starting transfers between devices  15.4 us (35%)
  blocking collectives  13.5 us (31%)
  Pallas kernels  12.4 us (28%)
  waiting for transfers between devices  2.28 us (5%)
    all_gather x1, blocking collectives, gathered_across(): return lax.all_gather(value, axis, axis_index_groups=groups)  13.5 us
    all_to_all x2, starting transfers between devices, exchanged(): lax.all_to_all(value, ('px', 'py'), split_axis=0, concat_axis=0, tiled=True)  9.88 us
    ppermute x1, starting transfers between devices, body(): second_row = lax.ppermute(edges[1], 'py', pairs_inside(sizes[1]))  2.92 us
    pallas_call x1, Pallas kernels, forward_modes(): pl.pallas_call(forward_kernel, out_shape=(jax.ShapeDtypeStruct((32, 8, 12...  2.68 us
    pallas_call x1, Pallas kernels, pack(): pl.pallas_call(pack_kernel, out_shape=(jax.ShapeDtypeStruct((2, 4, 16, KX...  2.59 us
    all_to_all x2, waiting for transfers between devices, exchanged(): lax.all_to_all(value, ('px', 'py'), split_axis=0, concat_axis=0, tiled=True)  2.27 us
    pallas_call x1, Pallas kernels, finish(): pl.pallas_call(finish_kernel, out_shape=jax.ShapeDtypeStruct(convolved.sh...  2.04 us
    ppermute x1, starting transfers between devices, body(): inside = lax.ppermute(second_own, 'px', pairs_inside(sizes[0]))  1.83 us
  transfers between devices with their start and end apart: 5, of which 1 were waited for; matrix products, arithmetic and copies ran while one was open for 0% of the time, Pallas kernels for 18%

profile of v8, /device:TPU:0, one launch (start us, length us, event | category | flops | bytes accessed | tf_op | source)
XLA Modules:
  0.0 43.7 jit_solution(12978771073736406010)
XLA Ops:
  0.0 2.7 %forward_modes.1 = (bf16[32,8,128]{2,1,0:T(8,128)(2,1)}, bf16[64,32,128]{2,1,0:T(8,128)(2,1)S(1)}) custom-call(bf16[64,32,128]{2,1,0:T(8,128)(2,1)} %bitcast.12, f32[32,128]{1,0:T(8,128)} %constant.12.clone.z_hbm, f32[4,64,512]{2,1,0:T(8,128)} %constant.13.clone.y_hbm), custom_call_target="tpu_custom_call" | custom-call | flops 134217728 | bytes 2097152 | tf_op jit(solution)/shard_map/forward_modes/pallas_call | solution.py:291
  2.7 7.3 %all-to-all-start = ((bf16[32,8,128]{2,1,0:T(8,128)(2,1)}), bf16[32,8,128]{2,1,0:T(8,128)(2,1)S(1)}, u32[]{:S(2)}, u32[]{:S(2)}) async-start(bf16[32,8,128]{2,1,0:T(8,128)(2,1)} %get-tuple-element.16), calls=%async_computation | async-start | bytes 131072 | tf_op jit(solution)/shard_map/all_to_all | solution.py:641
  10.0 0.7 %arrange_cells.1 = (bf16[32,32,128]{2,1,0:T(8,128)(2,1)S(1)}, bf16[32,32,128]{2,1,0:T(8,128)(2,1)S(1)}, bf16[32,32,128]{2,1,0:T(8,128)(2,1)S(1)}, f32[8,128]{1,0:T(8,128)S(1)}) custom-call(bf16[32,2,32,128]{3,2,1,0:T(8,128)(2,1)S(1)} %bitcast.8), custom_call_target="tpu_custom_call" | custom-call | flops 1024 | bytes 1024 | tf_op jit(solution)/shard_map/arrange_cells/pallas_call | solution.py:329
  10.7 1.8 %collective-permute-start = (bf16[32,32,128]{2,1,0:T(8,128)(2,1)S(1)}, bf16[32,32,128]{2,1,0:T(8,128)(2,1)S(1)}, u32[]{:S(2)}, u32[]{:S(2)}) collective-permute-start(bf16[32,32,128]{2,1,0:T(8,128)(2,1)S(1)} %get-tuple-element.22.other_ref.refs_2_), channel_id=1, source_target_pairs={{0,4},{4,0},{8,12},{12,8},{16,20},{20,16},{24,28},{28,24},{1,5},{5... | collective-permute-start | bytes 786440 | tf_op jit(solution)/shard_map/ppermute | solution.py:673
  12.5 2.6 %pack_weights.1 = (f32[2,4,16,16,128]{4,3,2,1,0:T(8,128)S(1)}, bf16[384,512]{1,0:T(8,128)(2,1)S(1)}) custom-call(f32[8,128]{1,0:T(8,128)S(1)} %get-tuple-element.18.after_ref, f32[2,4,4,16,16,32]{5,4,3,2,1,0:T(8,128)} %bitcast.10, bf16[3,3,3,32,32]{4,3,2,1,0:T(8,128)(2,1)} %bitcast.13), custom_call_target="tpu_custom_call" | custom-call | flops 1024 | bytes 1024 | tf_op jit(solution)/shard_map/pack_weights/pallas_call | solution.py:389
  15.1 2.3 %all-to-all-done.modes_ref = bf16[32,8,128]{2,1,0:T(8,128)(2,1)S(1)} async-done(((bf16[32,8,128]{2,1,0:T(8,128)(2,1)}), bf16[32,8,128]{2,1,0:T(8,128)(2,1)S(1)}, u32[]{:S(2)}, u32[]{:S(2)}) %all-to-all-start) | async-done | bytes 65568 | tf_op jit(solution)/shard_map/all_to_all | solution.py:641
  17.4 0.0 copy-done.3
  17.4 0.0 copy-done.4
  17.4 1.6 %mix_modes.1 = bf16[32,16,128]{2,1,0:T(8,128)(2,1)} custom-call(bf16[32,8,128]{2,1,0:T(8,128)(2,1)S(1)} %all-to-all-done.modes_ref, f32[64,256]{1,0:T(8,128)S(1)} %copy-done.4, f32[2,4,16,16,128]{4,3,2,1,0:T(8,128)S(1)} %get-tuple-element.19.weight_ref, f32[128,256]{1,0:T(8,128)S(1)} %copy-done.3), custom_call_target="tpu_custom_call" | custom-call | flops 34359738368 | bytes 2097152 | tf_op jit(solution)/shard_map/mix_modes/pallas_call | solution.py:448
  19.0 2.6 %all-to-all-start.1 = ((bf16[32,16,128]{2,1,0:T(8,128)(2,1)}), bf16[32,16,128]{2,1,0:T(8,128)(2,1)S(1)}, u32[]{:S(2)}, u32[]{:S(2)}) async-start(bf16[32,16,128]{2,1,0:T(8,128)(2,1)} %mix_modes.1), calls=%async_computation.1 | async-start | bytes 262144 | tf_op jit(solution)/shard_map/all_to_all | solution.py:641
  21.6 13.5 %all-gather = bf16[64,32,128]{2,1,0:T(8,128)(2,1)} all-gather(bf16[32,32,128]{2,1,0:T(8,128)(2,1)S(1)} %get-tuple-element.20), channel_id=2, replica_groups={{4,8},{12,16},{20,24},{28,0},{5,9},{13,17},{21,25},{29,1},{6,10},{14,18..., dimensions={0}, use_global_device_ids=true | all-gather | bytes 786432 | tf_op jit(solution)/shard_map/all_gather | solution.py:655
  35.0 0.0 collective-permute-done.inside_ref.refs_3_
  35.1 1.0 %edge_rows.1 = (bf16[32,32,128]{2,1,0:T(8,128)(2,1)S(1)}, bf16[128,128]{1,0:T(8,128)(2,1)S(1)}, bf16[128,128]{1,0:T(8,128)(2,1)S(1)}) custom-call(bf16[2,32,32,128]{3,2,1,0:T(8,128)(2,1)} %bitcast.11, bf16[32,32,128]{2,1,0:T(8,128)(2,1)S(1)} %get-tuple-element.21.own_ref.refs_1_, bf16[32,32,128]{2,1,0:T(8,128)(2,1)S(1)} %get-tuple-element.22.other_ref.refs_2_, ...), custom_call_target="tpu_custom_call" | custom-call | flops 1024 | bytes 131072 | tf_op jit(solution)/shard_map/edge_rows/pallas_call | solution.py:481
  36.0 0.0 copy-start
  36.0 0.0 copy-start.1
  36.1 0.0 copy-start.2
  36.1 0.8 %collective-permute-start.1 = (bf16[128,128]{1,0:T(8,128)(2,1)S(1)}, bf16[128,128]{1,0:T(8,128)(2,1)S(1)}, u32[]{:S(2)}, u32[]{:S(2)}) collective-permute-start(bf16[128,128]{1,0:T(8,128)(2,1)S(1)} %get-tuple-element.25), channel_id=1, source_target_pairs={{1,2},{2,1},{5,6},{6,5},{9,10},{10,9},{13,14},{14,13},{17,18},{18,... | collective-permute-start | bytes 98312 | tf_op jit(solution)/shard_map/ppermute | solution.py:677
  36.9 2.9 %collective-permute-start.2 = (bf16[128,128]{1,0:T(8,128)(2,1)S(1)}, bf16[128,128]{1,0:T(8,128)(2,1)S(1)}, u32[]{:S(2)}, u32[]{:S(2)}) collective-permute-start(bf16[128,128]{1,0:T(8,128)(2,1)S(1)} %get-tuple-element.26), channel_id=1, source_target_pairs={{0,1},{1,0},{2,3},{3,2},{4,5},{5,4},{6,7},{7,6},{8,9},{9,8},{10,11... | collective-permute-start | bytes 98312 | tf_op jit(solution)/shard_map/ppermute | solution.py:678
  39.8 1.3 %convolve_interior.1 = f32[2048,128]{1,0:T(8,128)S(1)} custom-call(bf16[32,32,128]{2,1,0:T(8,128)(2,1)S(1)} %get-tuple-element.23.refs_0_, bf16[32,32,128]{2,1,0:T(8,128)(2,1)S(1)} %get-tuple-element.21.own_ref.refs_1_, bf16[32,32,128]{2,1,0:T(8,128)(2,1)S(1)} %get-tuple-element.22.other_ref.refs_2_, ...), custom_call_target="tpu_custom_call" | custom-call | flops 1073741824 | bytes 2097152 | tf_op jit(solution)/shard_map/convolve_interior/pallas_call | solution.py:543
  41.1 0.0 collective-permute-done.1.refs_4_
  41.1 0.0 collective-permute-done.2.refs_5_
  41.2 0.5 %convolve_edges.1 = f32[512,128]{1,0:T(8,128)S(1)} custom-call(bf16[32,32,128]{2,1,0:T(8,128)(2,1)S(1)} %get-tuple-element.23.refs_0_, bf16[32,32,128]{2,1,0:T(8,128)(2,1)S(1)} %get-tuple-element.21.own_ref.refs_1_, bf16[32,32,128]{2,1,0:T(8,128)(2,1)S(1)} %get-tuple-element.22.other_ref.refs_2_, ...), custom_call_target="tpu_custom_call" | custom-call | flops 1073741824 | bytes 2097152 | tf_op jit(solution)/shard_map/convolve_edges/pallas_call | solution.py:543
  41.7 0.0 all-to-all-done.1.values_ref
  41.7 2.0 %finish_layer.1 = bf16[32,2,32,128]{3,2,1,0:T(8,128)(2,1)} custom-call(f32[32]{0:T(128)S(1)} %copy-done.2, bf16[32,16,128]{2,1,0:T(8,128)(2,1)S(1)} %all-to-all-done.1.values_ref, f32[128,512]{1,0:T(8,128)S(1)} %copy-done.1, f32[4,32,512]{2,1,0:T(8,128)S(1)} %copy-done, f32[32,2,32,128]{3,2,1,0:T(8,128)S(1)} %bitcast.7, f32[32,2,8,128]{3,2,1,0:T(8,128)S(1)} %bitcast.9), custom_call_target="tpu_custom_call" | custom-call | flops 268435456 | bytes 4194304 | tf_op jit(solution)/shard_map/finish_layer/pallas_call | solution.py:625
  (5 shorter events, 0.0 us)
Async XLA Ops:
  0.0 17.4 %copy-start.3 = (f32[128,256]{1,0:T(8,128)S(1)}, f32[128,256]{1,0:T(8,128)}, u32[]{:S(2)}) copy-start(f32[128,256]{1,0:T(8,128)} %constant.15.clone.inverse_ref) | copy-start | bytes 393220
  0.0 17.4 %copy-start.4 = (f32[64,256]{1,0:T(8,128)S(1)}, f32[64,256]{1,0:T(8,128)}, u32[]{:S(2)}) copy-start(f32[64,256]{1,0:T(8,128)} %constant.14.clone.forward_ref) | copy-start | bytes 196612
  2.7 14.7 %all-to-all-start = ((bf16[32,8,128]{2,1,0:T(8,128)(2,1)}), bf16[32,8,128]{2,1,0:T(8,128)(2,1)S(1)}, u32[]{:S(2)}, u32[]{:S(2)}) async-start(bf16[32,8,128]{2,1,0:T(8,128)(2,1)} %get-tuple-element.16), calls=%async_computation | async-start | bytes 131072 | tf_op jit(solution)/shard_map/all_to_all | solution.py:641
  10.7 24.3 %collective-permute-start = (bf16[32,32,128]{2,1,0:T(8,128)(2,1)S(1)}, bf16[32,32,128]{2,1,0:T(8,128)(2,1)S(1)}, u32[]{:S(2)}, u32[]{:S(2)}) collective-permute-start(bf16[32,32,128]{2,1,0:T(8,128)(2,1)S(1)} %get-tuple-element.22.other_ref.refs_2_), channel_id=1, source_target_pairs={{0,4},{4,0},{8,12},{12,8},{16,20},{20,16},{24,28},{28,24},{1,5},{5... | collective-permute-start | bytes 786440 | tf_op jit(solution)/shard_map/ppermute | solution.py:673
  19.0 22.7 %all-to-all-start.1 = ((bf16[32,16,128]{2,1,0:T(8,128)(2,1)}), bf16[32,16,128]{2,1,0:T(8,128)(2,1)S(1)}, u32[]{:S(2)}, u32[]{:S(2)}) async-start(bf16[32,16,128]{2,1,0:T(8,128)(2,1)} %mix_modes.1), calls=%async_computation.1 | async-start | bytes 262144 | tf_op jit(solution)/shard_map/all_to_all | solution.py:641
  36.0 5.6 %copy-start = (f32[4,32,512]{2,1,0:T(8,128)S(1)}, f32[4,32,512]{2,1,0:T(8,128)}, u32[]{:S(2)}) copy-start(f32[4,32,512]{2,1,0:T(8,128)} %constant.17.clone.y_ref) | copy-start | bytes 786436
  36.0 5.6 %copy-start.1 = (f32[128,512]{1,0:T(8,128)S(1)}, f32[128,512]{1,0:T(8,128)}, u32[]{:S(2)}) copy-start(f32[128,512]{1,0:T(8,128)} %constant.16.clone.z_ref) | copy-start | bytes 786436
  36.1 5.6 %copy-start.2 = (f32[32]{0:T(128)S(1)}, f32[32]{0:T(128)}, u32[]{:S(2)}) copy-start(f32[32]{0:T(128)} %bias_ref.1) | copy-start | bytes 388
  36.1 5.1 %collective-permute-start.1 = (bf16[128,128]{1,0:T(8,128)(2,1)S(1)}, bf16[128,128]{1,0:T(8,128)(2,1)S(1)}, u32[]{:S(2)}, u32[]{:S(2)}) collective-permute-start(bf16[128,128]{1,0:T(8,128)(2,1)S(1)} %get-tuple-element.25), channel_id=1, source_target_pairs={{1,2},{2,1},{5,6},{6,5},{9,10},{10,9},{13,14},{14,13},{17,18},{18,... | collective-permute-start | bytes 98312 | tf_op jit(solution)/shard_map/ppermute | solution.py:677
  36.9 4.3 %collective-permute-start.2 = (bf16[128,128]{1,0:T(8,128)(2,1)S(1)}, bf16[128,128]{1,0:T(8,128)(2,1)S(1)}, u32[]{:S(2)}, u32[]{:S(2)}) collective-permute-start(bf16[128,128]{1,0:T(8,128)(2,1)S(1)} %get-tuple-element.26), channel_id=1, source_target_pairs={{0,1},{1,0},{2,3},{3,2},{4,5},{5,4},{6,7},{7,6},{8,9},{9,8},{10,11... | collective-permute-start | bytes 98312 | tf_op jit(solution)/shard_map/ppermute | solution.py:678

commit v9 on v7

--- a/solution.py
+++ b/solution.py
@@ -216,7 +216,7 @@
         narrow(y_forward),
         narrow(x_forward),
         np.concatenate(
-            [narrow(x_inverse), narrow(x_inverse), narrow(x_inverse - narrow(x_inverse))], axis=1
+            [narrow(x_inverse), narrow(x_inverse - narrow(x_inverse))], axis=1
         ),
         narrow(z_inverse),
         narrow(y_inverse),
@@ -239,7 +239,21 @@
 
 
 def forward_kernel(
-    state_hbm, z_hbm, y_hbm, weight_hbm, out_ref, state_ref, weight_ref, z_ref, y_ref, table_ref, sems
+    state_hbm,
+    z_hbm,
+    y_hbm,
+    weight_hbm,
+    conv_hbm,
+    out_hbm,
+    state_ref,
+    packed_ref,
+    conv_ref,
+    out_ref,
+    z_ref,
+    y_ref,
+    table_ref,
+    weight_ref,
+    sems,
 ):
     count = state_ref.shape[0] // 4
     span = state_ref.shape[1]
@@ -253,8 +267,15 @@
         )
         for g in range(4)
     ]
-    weight_copy = pltpu.make_async_copy(weight_hbm.at[0], weight_ref, sems.at[6])
-    for copy in [y_copy, z_copy] + copies + [weight_copy]:
+    conv_copy = pltpu.make_async_copy(conv_hbm, conv_ref, sems.at[6])
+    weight_copies = [
+        pltpu.make_async_copy(
+            weight_hbm.at[part, kz], weight_ref.at[part, kz], sems.at[7 + part * 4 + kz]
+        )
+        for part in range(2)
+        for kz in range(4)
+    ]
+    for copy in [y_copy, z_copy] + copies + weight_copies + [conv_copy]:
         copy.start()
     y_copy.wait()
     table = y_ref[...]
@@ -288,24 +309,39 @@
                     rows4 = slice(4 * side, 4 * side + 4)
                     chunk = jnp.concatenate([first[rows4], second[rows4]], axis=0)
                     out_ref[(half * 4 + group) * 4 + 2 * pair + side] = chunk.astype(jnp.bfloat16)
-    weight_copy.wait()
-
-
-def forward_modes(state, z_table, y_table, spectral_weight):
+    out_copy = pltpu.make_async_copy(out_ref, out_hbm, sems.at[15])
+    out_copy.start()
+    for part in range(2):
+        for kz in range(4):
+            weight_copies[part * 4 + kz].wait()
+            for c in range(16):
+                packed_ref[part, kz, c] = jnp.concatenate(
+                    [weight_ref[part, kz, u, c] for u in range(4)], axis=1
+                )
+    conv_copy.wait()
+    out_copy.wait()
+
+
+def forward_modes(state, z_table, y_table, spectral_weight, conv_weight):
+    vmem, hbm = (pl.BlockSpec(memory_space=space) for space in (pltpu.VMEM, pltpu.HBM))
+    sent = (32, 8, 128)
     return pl.pallas_call(
         forward_kernel,
         out_shape=(
-            jax.ShapeDtypeStruct((32, 8, 128), jnp.bfloat16),
+            jax.ShapeDtypeStruct(sent, jnp.bfloat16),
             jax.ShapeDtypeStruct(state.shape, jnp.bfloat16),
-            jax.ShapeDtypeStruct(spectral_weight.shape[1:], jnp.float32),
+            jax.ShapeDtypeStruct((2, 4, 16, KX, 128), jnp.float32),
+            jax.ShapeDtypeStruct(conv_weight.shape, jnp.bfloat16),
         ),
-        in_specs=[pl.BlockSpec(memory_space=pltpu.HBM)] * 4,
-        out_specs=(pl.BlockSpec(memory_space=pltpu.VMEM),) * 3,
+        in_specs=[hbm] * 5,
+        out_specs=(hbm, vmem, vmem, vmem),
         scratch_shapes=[
+            pltpu.VMEM(sent, jnp.bfloat16),
             pltpu.VMEM(z_table.shape, jnp.float32),
             pltpu.VMEM(y_table.shape[1:], jnp.float32),
             pltpu.VMEM((32 * state.shape[1], y_table.shape[2]), jnp.bfloat16),
-            pltpu.SemaphoreType.DMA((7,)),
+            pltpu.VMEM(spectral_weight.shape, jnp.float32),
+            pltpu.SemaphoreType.DMA((16,)),
         ],
         compiler_params=pltpu.CompilerParams(vmem_limit_bytes=16 * 2**20),
         cost_estimate=pl.CostEstimate(flops=2**27, bytes_accessed=2**21, transcendentals=0),
@@ -313,48 +349,18 @@
     )(
         *(
             pltpu.with_memory_space_constraint(v, pltpu.HBM)
-            for v in (state, z_table, y_table, spectral_weight)
+            for v in (state, z_table, y_table, spectral_weight, conv_weight)
         )
     )
 
 
-def arrange_kernel(state_ref, first_ref, second_ref, token_ref, wide):
+def arrange_kernel(state_ref, conv_ref, first_ref, second_ref, conv_out, wide):
     odd_x = lax.rem(lax.axis_index("px"), 2)
     cells_y = state_ref.shape[2]
     for slot, (out_ref, x) in enumerate(((first_ref, odd_x), (second_ref, 1 - odd_x))):
         wide[slot] = state_ref[:, x].astype(jnp.float32).reshape(32 * cells_y, 128)
         for y in range(cells_y):
             out_ref[y] = wide[slot, pl.ds(y, 32, stride=cells_y), :].astype(jnp.bfloat16)
-    token_ref[...] = jnp.zeros_like(token_ref)
-
-
-def arrange(state):
-    vmem = pl.BlockSpec(memory_space=pltpu.VMEM)
-    cells_y = state.shape[2]
-    plane = jax.ShapeDtypeStruct((cells_y, 32, 128), jnp.bfloat16)
-    return pl.pallas_call(
-        arrange_kernel,
-        out_shape=(plane, plane, jax.ShapeDtypeStruct((8, 128), jnp.float32)),
-        in_specs=[vmem],
-        out_specs=(vmem,) * 3,
-        scratch_shapes=[pltpu.VMEM((2, 32 * cells_y, 128), jnp.float32)],
-        compiler_params=pltpu.CompilerParams(vmem_limit_bytes=16 * 2**20),
-        cost_estimate=pl.CostEstimate(flops=2**10, bytes_accessed=2**10, transcendentals=0),
-        name="arrange_cells",
-    )(state)
-
-
-def pack_kernel(
-    after_ref, real_ref, weight_hbm, conv_hbm, weight_out, conv_out, imag_ref, conv_ref, sems
-):
-    conv_copy = pltpu.make_async_copy(conv_hbm, conv_ref, sems.at[4])
-    copies = [
-        pltpu.make_async_copy(weight_hbm.at[1, kz], imag_ref.at[kz], sems.at[kz]) for kz in range(4)
-    ]
-    for copy in [conv_copy] + copies:
-        copy.start()
-    odd_x = lax.rem(lax.axis_index("px"), 2)
-    conv_copy.wait()
     zero = jnp.zeros((32, 32), jnp.float32)
     for dz in range(3):
         taps = {
@@ -371,40 +377,22 @@
                     conv_out[row : row + 32, y_in * 128 : (y_in + 1) * 128] = jnp.concatenate(
                         blocks, axis=1
                     ).astype(jnp.bfloat16)
-    for part, part_ref in enumerate((real_ref, imag_ref)):
-        for kz in range(4):
-            if part == 1:
-                copies[kz].wait()
-            for c in range(16):
-                weight_out[part, kz, c] = jnp.concatenate(
-                    [part_ref[kz, u, c] for u in range(4)], axis=1
-                )
-
-
-def pack(after, real_weight, spectral_weight, conv_weight):
+
+
+def arrange(state, conv_weight):
     vmem = pl.BlockSpec(memory_space=pltpu.VMEM)
+    cells_y = state.shape[2]
+    plane = jax.ShapeDtypeStruct((cells_y, 32, 128), jnp.bfloat16)
     return pl.pallas_call(
-        pack_kernel,
-        out_shape=(
-            jax.ShapeDtypeStruct((2, 4, 16, KX, 128), jnp.float32),
-            jax.ShapeDtypeStruct((384, 512), jnp.bfloat16),
-        ),
-        in_specs=[pl.BlockSpec(memory_space=pl.ANY), vmem]
-        + [pl.BlockSpec(memory_space=pltpu.HBM)] * 2,
-        out_specs=(vmem, vmem),
-        scratch_shapes=[
-            pltpu.VMEM(spectral_weight.shape[1:], jnp.float32),
-            pltpu.VMEM(conv_weight.shape, jnp.bfloat16),
-            pltpu.SemaphoreType.DMA((5,)),
-        ],
+        arrange_kernel,
+        out_shape=(plane, plane, jax.ShapeDtypeStruct((384, 512), jnp.bfloat16)),
+        in_specs=[vmem] * 2,
+        out_specs=(vmem,) * 3,
+        scratch_shapes=[pltpu.VMEM((2, 32 * cells_y, 128), jnp.float32)],
         compiler_params=pltpu.CompilerParams(vmem_limit_bytes=16 * 2**20),
         cost_estimate=pl.CostEstimate(flops=2**10, bytes_accessed=2**10, transcendentals=0),
-        name="pack_weights",
-    )(
-        after,
-        real_weight,
-        *(pltpu.with_memory_space_constraint(v, pltpu.HBM) for v in (spectral_weight, conv_weight)),
-    )
+        name="arrange_cells",
+    )(state, conv_weight)
 
 
 def mix_kernel(modes_ref, forward_ref, weight_ref, inverse_ref, out_ref):
@@ -429,10 +417,11 @@
             imag_sum = imag_term if imag_sum is None else imag_sum + imag_term
         mixed += [real_sum, imag_sum]
     mixed = jnp.concatenate(mixed, axis=0)
+    inverse = inverse_ref[...].astype(jnp.bfloat16)
     high = mixed.astype(jnp.bfloat16)
     low = (mixed - high.astype(jnp.float32)).astype(jnp.bfloat16)
     values = jnp.dot(
-        inverse_ref[...].astype(jnp.bfloat16),
+        jnp.concatenate([inverse[:, :128], inverse], axis=1),
         jnp.concatenate([high, low, high], axis=0),
         preferred_element_type=jnp.float32,
     ).astype(jnp.bfloat16)
@@ -644,18 +633,15 @@
     if sizes != (8, 4, 2, 32, 128):
         return general_body(state_field, conv_weight, conv_bias, spectral_weight)
     z_forward, y_forward, x_forward, x_inverse, z_inverse, y_inverse = tables(*sizes)
-    spectral_weight = spectral_weight.swapaxes(4, 5)
-    sent, held, real_weight = forward_modes(
+    sent, held, weights, conv_held = forward_modes(
         state_field.reshape(channels * cells_x, cells_y, depth),
         z_forward,
         y_forward,
-        spectral_weight,
+        spectral_weight.swapaxes(4, 5),
+        conv_weight.transpose(2, 3, 4, 0, 1),
     )
     modes = exchanged(sent)
-    first_own, second_own, token = arrange(held.reshape(state_field.shape))
-    weights, taps = pack(
-        token, real_weight, spectral_weight, conv_weight.transpose(2, 3, 4, 0, 1)
-    )
+    first_own, second_own, taps = arrange(held.reshape(state_field.shape), conv_held)
     first_plane, second_plane = swaps(first_own, second_own, "px")
     values = exchanged(mix_modes(modes, x_forward, weights, x_inverse))
     planes = (first_plane, first_own, second_own, second_plane)

time: 37.9 us -> 38.4 us (1.013)
  waiting for transfers between devices: 1.28 us -> 6.33 us
  local copies, waits for them, and re-layouts: 3.98 us -> 1.76 us
  Pallas kernels: 11 us -> 9.79 us
  starting transfers between devices: 21 us -> 20.1 us
    ppermute x2, waiting for transfers between devices: 0.01 us -> 5.72 us  [swaps(): lax.ppermute(second, axis, inside)]
    unnamed x18 -> x14, local copies, waits for them, and re-layouts: 3.98 us -> 1.76 us
    pallas_call x2 -> x1, Pallas kernels: 4.89 us -> 3.5 us  [forward_modes(): pl.pallas_call(forward_kernel, out_shape=(jax.ShapeDtypeStruct(sent, jnp....]
    all_to_all x2, waiting for transfers between devices: 1.27 us -> 0.61 us  [exchanged(): lax.all_to_all(value, ('px', 'py'), split_axis=0, concat_axis=0, tiled=True)]
    all_to_all x2, starting transfers between devices: 11.9 us -> 11.3 us  [exchanged(): lax.all_to_all(value, ('px', 'py'), split_axis=0, concat_axis=0, tiled=True)]
  transfers between devices with their start and end apart: 6 -> 6, of which waited for: 1 -> 2; matrix products, arithmetic and copies ran while one was open for 0% -> 0% of each run, Pallas kernels for 17% -> 11%
where the time goes in v9:
time: 38.4 us; the launch traced here: 38.1 us
  starting transfers between devices  20.1 us (52%)
  Pallas kernels  9.79 us (25%)
  waiting for transfers between devices  6.33 us (16%)
  local copies, waits for them, and re-layouts  1.76 us (5%)
    all_to_all x2, starting transfers between devices, exchanged(): lax.all_to_all(value, ('px', 'py'), split_axis=0, concat_axis=0, tiled=True)  11.3 us
    ppermute x2, starting transfers between devices, swaps(): lax.ppermute(second, axis, inside)  7.38 us
    ppermute x2, waiting for transfers between devices, swaps(): lax.ppermute(second, axis, inside)  5.72 us
    pallas_call x1, Pallas kernels, forward_modes(): pl.pallas_call(forward_kernel, out_shape=(jax.ShapeDtypeStruct(sent, jnp....  3.5 us
    pallas_call x1, Pallas kernels, finish(): pl.pallas_call(finish_kernel, out_shape=jax.ShapeDtypeStruct(convolved.sh...  2.04 us
    pallas_call x2, Pallas kernels, convolve(): pl.pallas_call(kernel, out_shape=jax.ShapeDtypeStruct((rows, 128), jnp.fl...  1.82 us
    unnamed x14, local copies, waits for them, and re-layouts  1.76 us
    pallas_call x1, Pallas kernels, mix_modes(): pl.pallas_call(mix_kernel, out_shape=jax.ShapeDtypeStruct((32, 16, 128),...  1.58 us
  transfers between devices with their start and end apart: 6, of which 2 were waited for; matrix products, arithmetic and copies ran while one was open for 0% of the time, Pallas kernels for 11%

profile of v9, /device:TPU:0, one launch (start us, length us, event | category | flops | bytes accessed | tf_op | source)
XLA Modules:
  0.0 38.1 jit_solution(3120235764540312510)
XLA Ops:
  0.0 3.5 %forward_modes.1 = (bf16[32,8,128]{2,1,0:T(8,128)(2,1)}, bf16[64,32,128]{2,1,0:T(8,128)(2,1)S(1)}, f32[2,4,16,16,128]{4,3,2,1,0:T(8,128)S(1)}, bf16[3,3,3,32,32]{4,3,2,1,0:T(8,128)(2,1)S(1)}) custom-call(bf16[64,32,128]{2,1,0:T(8,128)(2,1)} %bitcast.10, f32[32,128]{1,0:T(8,128)} %constant.12.clone.z_hbm, f32[4,64,512]{2,1,0:T(8,128)} %constant.13.clone.y_hbm, ...), custom_call_target="tpu_custom_call" | custom-call | flops 134217728 | bytes 2097152 | tf_op jit(solution)/shard_map/forward_modes/pallas_call | solution.py:328
  3.5 7.3 %all-to-all-start = ((bf16[32,8,128]{2,1,0:T(8,128)(2,1)}), bf16[32,8,128]{2,1,0:T(8,128)(2,1)S(1)}, u32[]{:S(2)}, u32[]{:S(2)}) async-start(bf16[32,8,128]{2,1,0:T(8,128)(2,1)} %get-tuple-element.14), calls=%async_computation | async-start | bytes 131072 | tf_op jit(solution)/shard_map/all_to_all | solution.py:620
  10.8 0.8 %arrange_cells.1 = (bf16[32,32,128]{2,1,0:T(8,128)(2,1)S(1)}, bf16[32,32,128]{2,1,0:T(8,128)(2,1)S(1)}, bf16[384,512]{1,0:T(8,128)(2,1)S(1)}) custom-call(bf16[32,2,32,128]{3,2,1,0:T(8,128)(2,1)S(1)} %bitcast.7, bf16[3,3,3,32,32]{4,3,2,1,0:T(8,128)(2,1)S(1)} %get-tuple-element.17.conv_ref), custom_call_target="tpu_custom_call" | custom-call | flops 1024 | bytes 1024 | tf_op jit(solution)/shard_map/arrange_cells/pallas_call | solution.py:386
  11.7 0.0 copy-start.3
  11.7 0.7 %copy-done.3 = bf16[384,512]{1,0:T(8,128)(2,1)} copy-done((bf16[384,512]{1,0:T(8,128)(2,1)}, bf16[384,512]{1,0:T(8,128)(2,1)S(1)}, u32[]{:S(2)}) %copy-start.3) | copy-done | bytes 393240
  12.4 0.7 %collective-permute-start = (bf16[32,32,128]{2,1,0:T(8,128)(2,1)S(1)}, bf16[32,32,128]{2,1,0:T(8,128)(2,1)S(1)}, u32[]{:S(2)}, u32[]{:S(2)}) collective-permute-start(bf16[32,32,128]{2,1,0:T(8,128)(2,1)S(1)} %get-tuple-element.18.refs_1_), channel_id=1, source_target_pairs={{4,8},{8,4},{12,16},{16,12},{20,24},{24,20},{5,9},{9,5},{13,17},{1... | collective-permute-start | bytes 786440 | tf_op jit(solution)/shard_map/ppermute | solution.py:627
  13.1 4.5 %collective-permute-start.1 = (bf16[32,32,128]{2,1,0:T(8,128)(2,1)S(1)}, bf16[32,32,128]{2,1,0:T(8,128)(2,1)S(1)}, u32[]{:S(2)}, u32[]{:S(2)}) collective-permute-start(bf16[32,32,128]{2,1,0:T(8,128)(2,1)S(1)} %get-tuple-element.19.refs_2_), channel_id=1, source_target_pairs={{0,4},{4,0},{8,12},{12,8},{16,20},{20,16},{24,28},{28,24},{1,5},{5... | collective-permute-start | bytes 786440 | tf_op jit(solution)/shard_map/ppermute | solution.py:627
  17.6 0.6 %all-to-all-done.modes_ref = bf16[32,8,128]{2,1,0:T(8,128)(2,1)S(1)} async-done(((bf16[32,8,128]{2,1,0:T(8,128)(2,1)}), bf16[32,8,128]{2,1,0:T(8,128)(2,1)S(1)}, u32[]{:S(2)}, u32[]{:S(2)}) %all-to-all-start) | async-done | bytes 65568 | tf_op jit(solution)/shard_map/all_to_all | solution.py:620
  18.2 1.6 %mix_modes.1 = bf16[32,16,128]{2,1,0:T(8,128)(2,1)} custom-call(bf16[32,8,128]{2,1,0:T(8,128)(2,1)S(1)} %all-to-all-done.modes_ref, f32[64,256]{1,0:T(8,128)S(1)} %copy-done.6, f32[2,4,16,16,128]{4,3,2,1,0:T(8,128)S(1)} %get-tuple-element.15.weight_ref, f32[128,256]{1,0:T(8,128)S(1)} %copy-done.5), custom_call_target="tpu_custom_call" | custom-call | flops 34359738368 | bytes 2097152 | tf_op jit(solution)/shard_map/mix_modes/pallas_call | solution.py:435
  19.8 3.9 %all-to-all-start.1 = ((bf16[32,16,128]{2,1,0:T(8,128)(2,1)}), bf16[32,16,128]{2,1,0:T(8,128)(2,1)S(1)}, u32[]{:S(2)}, u32[]{:S(2)}) async-start(bf16[32,16,128]{2,1,0:T(8,128)(2,1)} %mix_modes.1), calls=%async_computation.1 | async-start | bytes 262144 | tf_op jit(solution)/shard_map/all_to_all | solution.py:620
  23.8 0.0 collective-permute-done.refs_0_
  23.8 5.7 %collective-permute-done.1.refs_3_ = bf16[32,32,128]{2,1,0:T(8,128)(2,1)S(1)} collective-permute-done((bf16[32,32,128]{2,1,0:T(8,128)(2,1)S(1)}, bf16[32,32,128]{2,1,0:T(8,128)(2,1)S(1)}, u32[]{:S(2)}, u32[]{:S(2)}) %collective-permute-start.1) | collective-permute-done | bytes 262176 | tf_op jit(solution)/shard_map/ppermute | solution.py:627
  29.5 0.0 copy-start
  29.5 0.0 copy-start.1
  29.5 0.0 copy-start.2
  29.6 0.8 %collective-permute-start.2 = (bf16[128,128]{1,0:T(8,128)(2,1)S(1)}, bf16[128,128]{1,0:T(8,128)(2,1)S(1)}, u32[]{:S(2)}, u32[]{:S(2)}) collective-permute-start(bf16[128,128]{1,0:T(8,128)(2,1)S(1)} %get-tuple-element.21), channel_id=1, source_target_pairs={{1,2},{2,1},{5,6},{6,5},{9,10},{10,9},{13,14},{14,13},{17,18},{18,... | collective-permute-start | bytes 98312 | tf_op jit(solution)/shard_map/ppermute | solution.py:627
  30.4 2.8 %collective-permute-start.3 = (bf16[128,128]{1,0:T(8,128)(2,1)S(1)}, bf16[128,128]{1,0:T(8,128)(2,1)S(1)}, u32[]{:S(2)}, u32[]{:S(2)}) collective-permute-start(bf16[128,128]{1,0:T(8,128)(2,1)S(1)} %get-tuple-element.22), channel_id=1, source_target_pairs={{0,1},{1,0},{2,3},{3,2},{4,5},{5,4},{6,7},{7,6},{8,9},{9,8},{10,11... | collective-permute-start | bytes 98312 | tf_op jit(solution)/shard_map/ppermute | solution.py:627
  33.2 1.0 %copy-done.4 = bf16[384,512]{1,0:T(8,128)(2,1)S(1)} copy-done((bf16[384,512]{1,0:T(8,128)(2,1)S(1)}, bf16[384,512]{1,0:T(8,128)(2,1)}, u32[]{:S(2)}) %copy-start.4) | copy-done | bytes 393240
  34.2 1.3 %convolve_interior.1 = f32[2048,128]{1,0:T(8,128)S(1)} custom-call(bf16[32,32,128]{2,1,0:T(8,128)(2,1)S(1)} %collective-permute-done.refs_0_, bf16[32,32,128]{2,1,0:T(8,128)(2,1)S(1)} %get-tuple-element.18.refs_1_, bf16[32,32,128]{2,1,0:T(8,128)(2,1)S(1)} %get-tuple-element.19.refs_2_, bf16[32,32,128]{2,1,0:T(8,128)(2,1)S(1)} %collective-permute-done.1.refs_3_, ...), custom_call_target="tpu_custom_call" | custom-call | flops 1073741824 | bytes 2097152 | tf_op jit(solution)/shard_map/convolve_interior/pallas_call | solution.py:522
  35.5 0.0 collective-permute-done.2.refs_4_
  35.5 0.0 collective-permute-done.3.refs_5_
  35.6 0.5 %convolve_edges.1 = f32[512,128]{1,0:T(8,128)S(1)} custom-call(bf16[32,32,128]{2,1,0:T(8,128)(2,1)S(1)} %collective-permute-done.refs_0_, bf16[32,32,128]{2,1,0:T(8,128)(2,1)S(1)} %get-tuple-element.18.refs_1_, bf16[32,32,128]{2,1,0:T(8,128)(2,1)S(1)} %get-tuple-element.19.refs_2_, bf16[32,32,128]{2,1,0:T(8,128)(2,1)S(1)} %collective-permute-done.1.refs_3_, ...), custom_call_target="tpu_custom_call" | custom-call | flops 1073741824 | bytes 2097152 | tf_op jit(solution)/shard_map/convolve_edges/pallas_call | solution.py:522
  36.1 0.0 all-to-all-done.1.values_ref
  36.1 2.0 %finish_layer.1 = bf16[32,2,32,128]{3,2,1,0:T(8,128)(2,1)} custom-call(f32[32]{0:T(128)S(1)} %copy-done.2, bf16[32,16,128]{2,1,0:T(8,128)(2,1)S(1)} %all-to-all-done.1.values_ref, f32[128,512]{1,0:T(8,128)S(1)} %copy-done.1, f32[4,32,512]{2,1,0:T(8,128)S(1)} %copy-done, f32[32,2,32,128]{3,2,1,0:T(8,128)S(1)} %bitcast.6, f32[32,2,8,128]{3,2,1,0:T(8,128)S(1)} %bitcast.8), custom_call_target="tpu_custom_call" | custom-call | flops 268435456 | bytes 4194304 | tf_op jit(solution)/shard_map/finish_layer/pallas_call | solution.py:604
  (9 shorter events, 0.0 us)
Async XLA Ops:
  0.0 18.2 %copy-start.5 = (f32[128,256]{1,0:T(8,128)S(1)}, f32[128,256]{1,0:T(8,128)}, u32[]{:S(2)}) copy-start(f32[128,256]{1,0:T(8,128)} %constant.15.clone.inverse_ref) | copy-start | bytes 393220
  0.0 18.2 %copy-start.6 = (f32[64,256]{1,0:T(8,128)S(1)}, f32[64,256]{1,0:T(8,128)}, u32[]{:S(2)}) copy-start(f32[64,256]{1,0:T(8,128)} %constant.14.clone.forward_ref) | copy-start | bytes 196612
  3.5 14.7 %all-to-all-start = ((bf16[32,8,128]{2,1,0:T(8,128)(2,1)}), bf16[32,8,128]{2,1,0:T(8,128)(2,1)S(1)}, u32[]{:S(2)}, u32[]{:S(2)}) async-start(bf16[32,8,128]{2,1,0:T(8,128)(2,1)} %get-tuple-element.14), calls=%async_computation | async-start | bytes 131072 | tf_op jit(solution)/shard_map/all_to_all | solution.py:620
  11.7 0.7 %copy-start.3 = (bf16[384,512]{1,0:T(8,128)(2,1)}, bf16[384,512]{1,0:T(8,128)(2,1)S(1)}, u32[]{:S(2)}) copy-start(bf16[384,512]{1,0:T(8,128)(2,1)S(1)} %get-tuple-element.20.refs_4_.refs_6_) | copy-start | bytes 1179652
  12.4 11.4 %collective-permute-start = (bf16[32,32,128]{2,1,0:T(8,128)(2,1)S(1)}, bf16[32,32,128]{2,1,0:T(8,128)(2,1)S(1)}, u32[]{:S(2)}, u32[]{:S(2)}) collective-permute-start(bf16[32,32,128]{2,1,0:T(8,128)(2,1)S(1)} %get-tuple-element.18.refs_1_), channel_id=1, source_target_pairs={{4,8},{8,4},{12,16},{16,12},{20,24},{24,20},{5,9},{9,5},{13,17},{1... | collective-permute-start | bytes 786440 | tf_op jit(solution)/shard_map/ppermute | solution.py:627
  13.1 16.4 %collective-permute-start.1 = (bf16[32,32,128]{2,1,0:T(8,128)(2,1)S(1)}, bf16[32,32,128]{2,1,0:T(8,128)(2,1)S(1)}, u32[]{:S(2)}, u32[]{:S(2)}) collective-permute-start(bf16[32,32,128]{2,1,0:T(8,128)(2,1)S(1)} %get-tuple-element.19.refs_2_), channel_id=1, source_target_pairs={{0,4},{4,0},{8,12},{12,8},{16,20},{20,16},{24,28},{28,24},{1,5},{5... | collective-permute-start | bytes 786440 | tf_op jit(solution)/shard_map/ppermute | solution.py:627
  19.8 16.2 %all-to-all-start.1 = ((bf16[32,16,128]{2,1,0:T(8,128)(2,1)}), bf16[32,16,128]{2,1,0:T(8,128)(2,1)S(1)}, u32[]{:S(2)}, u32[]{:S(2)}) async-start(bf16[32,16,128]{2,1,0:T(8,128)(2,1)} %mix_modes.1), calls=%async_computation.1 | async-start | bytes 262144 | tf_op jit(solution)/shard_map/all_to_all | solution.py:620
  29.5 6.6 %copy-start = (f32[4,32,512]{2,1,0:T(8,128)S(1)}, f32[4,32,512]{2,1,0:T(8,128)}, u32[]{:S(2)}) copy-start(f32[4,32,512]{2,1,0:T(8,128)} %constant.17.clone.y_ref) | copy-start | bytes 786436
  29.5 6.6 %copy-start.1 = (f32[128,512]{1,0:T(8,128)S(1)}, f32[128,512]{1,0:T(8,128)}, u32[]{:S(2)}) copy-start(f32[128,512]{1,0:T(8,128)} %constant.16.clone.z_ref) | copy-start | bytes 786436
  29.5 6.5 %copy-start.2 = (f32[32]{0:T(128)S(1)}, f32[32]{0:T(128)}, u32[]{:S(2)}) copy-start(f32[32]{0:T(128)} %bias_ref.1) | copy-start | bytes 388
  29.6 6.0 %collective-permute-start.2 = (bf16[128,128]{1,0:T(8,128)(2,1)S(1)}, bf16[128,128]{1,0:T(8,128)(2,1)S(1)}, u32[]{:S(2)}, u32[]{:S(2)}) collective-permute-start(bf16[128,128]{1,0:T(8,128)(2,1)S(1)} %get-tuple-element.21), channel_id=1, source_target_pairs={{1,2},{2,1},{5,6},{6,5},{9,10},{10,9},{13,14},{14,13},{17,18},{18,... | collective-permute-start | bytes 98312 | tf_op jit(solution)/shard_map/ppermute | solution.py:627
  30.4 5.2 %collective-permute-start.3 = (bf16[128,128]{1,0:T(8,128)(2,1)S(1)}, bf16[128,128]{1,0:T(8,128)(2,1)S(1)}, u32[]{:S(2)}, u32[]{:S(2)}) collective-permute-start(bf16[128,128]{1,0:T(8,128)(2,1)S(1)} %get-tuple-element.22), channel_id=1, source_target_pairs={{0,1},{1,0},{2,3},{3,2},{4,5},{5,4},{6,7},{7,6},{8,9},{9,8},{10,11... | collective-permute-start | bytes 98312 | tf_op jit(solution)/shard_map/ppermute | solution.py:627
  33.2 1.0 %copy-start.4 = (bf16[384,512]{1,0:T(8,128)(2,1)S(1)}, bf16[384,512]{1,0:T(8,128)(2,1)}, u32[]{:S(2)}) copy-start(bf16[384,512]{1,0:T(8,128)(2,1)} %copy-done.3) | copy-start | bytes 1179652

commit v10 on v9

--- a/solution.py
+++ b/solution.py
@@ -363,20 +363,14 @@
             out_ref[y] = wide[slot, pl.ds(y, 32, stride=cells_y), :].astype(jnp.bfloat16)
     zero = jnp.zeros((32, 32), jnp.float32)
     for dz in range(3):
-        taps = {
-            (dx, dy): conv_ref[dx, dy, dz].astype(jnp.float32)
-            for dx in range(3)
-            for dy in range(3)
-        }
-        for y_at in range(2):
+        for dy in range(3):
+            taps = [conv_ref[dx, dy, dz].astype(jnp.float32) for dx in range(3)]
             for x_at in range(2):
-                row = ((dz * 2 + y_at) * 2 + x_at) * 32
-                for y_in in range(4):
-                    blocks = [taps.get((x_in - x_at, y_in - y_at), zero) for x_in in range(4)]
-                    blocks = [jnp.where(odd_x == 1, blocks[3 - i], blocks[i]) for i in range(4)]
-                    conv_out[row : row + 32, y_in * 128 : (y_in + 1) * 128] = jnp.concatenate(
-                        blocks, axis=1
-                    ).astype(jnp.bfloat16)
+                blocks = [zero] * x_at + taps + [zero] * (1 - x_at)
+                blocks = [jnp.where(odd_x == 1, blocks[i], blocks[3 - i]) for i in range(4)]
+                conv_out[dz, 32 * x_at : 32 * x_at + 32, 128 * dy : 128 * dy + 128] = (
+                    jnp.concatenate(blocks, axis=1).astype(jnp.bfloat16)
+                )
 
 
 def arrange(state, conv_weight):
@@ -385,7 +379,7 @@
     plane = jax.ShapeDtypeStruct((cells_y, 32, 128), jnp.bfloat16)
     return pl.pallas_call(
         arrange_kernel,
-        out_shape=(plane, plane, jax.ShapeDtypeStruct((384, 512), jnp.bfloat16)),
+        out_shape=(plane, plane, jax.ShapeDtypeStruct((3, 64, 384), jnp.bfloat16)),
         in_specs=[vmem] * 2,
         out_specs=(vmem,) * 3,
         scratch_shapes=[pltpu.VMEM((2, 32 * cells_y, 128), jnp.float32)],
@@ -469,6 +463,15 @@
     )(*planes)
 
 
+def window_matrix(taps_ref):
+    gap = jnp.zeros((64, 128), jnp.bfloat16)
+    rows = []
+    for dz in range(3):
+        rows.append(jnp.concatenate([taps_ref[dz], gap], axis=1))
+        rows.append(jnp.concatenate([gap, taps_ref[dz]], axis=1))
+    return jnp.concatenate(rows, axis=0)
+
+
 def convolve_quad(quad, row, weight, place, out_ref):
     lane = lax.broadcasted_iota(jnp.int32, (128, 256), 1) % 128
     windows = []
@@ -493,7 +496,7 @@
 def interior_kernel(*refs):
     *planes, weight_ref, out_ref = refs
     cells_y = planes[0].shape[0]
-    weight = weight_ref[...]
+    weight = window_matrix(weight_ref)
     for quad in range(1, cells_y // 4 - 1):
         convolve_quad(
             quad, lambda y: cell_row(planes, y), weight, lambda y: (y, cells_y), out_ref
@@ -512,7 +515,7 @@
             return jnp.where(odd_y, first_row[...], second_row[...])
         return cell_row(planes, y)
 
-    weight = weight_ref[...]
+    weight = window_matrix(weight_ref)
     for quad in (0, cells_y // 4 - 1):
         convolve_quad(quad, row, weight, lambda y: (y % 8, 8), out_ref)
 
@@ -624,7 +627,8 @@
     count = lax.axis_size(axis)
     inside = [(i, i ^ 1) for i in range(count)]
     across = [(i, i + 1 if i % 2 else i - 1) for i in range(1, count - 1)]
-    return lax.ppermute(first, axis, across), lax.ppermute(second, axis, inside)
+    second = lax.ppermute(second, axis, inside)
+    return lax.ppermute(first, axis, across), second
 
 
 def body(state_field, conv_weight, conv_bias, spectral_weight):
@@ -644,7 +648,7 @@
     first_own, second_own, taps = arrange(held.reshape(state_field.shape), conv_held)
     first_plane, second_plane = swaps(first_own, second_own, "px")
     values = exchanged(mix_modes(modes, x_forward, weights, x_inverse))
-    planes = (first_plane, first_own, second_own, second_plane)
+    planes = (second_plane, second_own, first_own, first_plane)
     first_row, second_row = swaps(*edge_rows(planes), "py")
     rows = channels * cells_x
     interior = convolve(interior_kernel, "convolve_interior", planes + (taps,), rows * cells_y)

time: 38.4 us -> 33.6 us (0.88)
  starting transfers between devices: 20.1 us -> 16.7 us
  local copies, waits for them, and re-layouts: 1.76 us -> 0.03 us
    all_to_all x2, waiting for transfers between devices: 0.61 us -> 4.14 us  [exchanged(): lax.all_to_all(value, ('px', 'py'), split_axis=0, concat_axis=0, tiled=True)]
    ppermute x4, waiting for transfers between devices: 5.72 us -> 2.57 us  [the longest x2 2.56 us: swaps(): second = lax.ppermute(second, axis, inside)]
    ppermute x4, starting transfers between devices: 8.84 us -> 6.17 us  [the longest x2 4.71 us: swaps(): second = lax.ppermute(second, axis, inside)]
    unnamed x14 -> x10, local copies, waits for them, and re-layouts: 1.76 us -> 0.03 us
    all_to_all x2, starting transfers between devices: 11.3 us -> 10.6 us  [exchanged(): lax.all_to_all(value, ('px', 'py'), split_axis=0, concat_axis=0, tiled=True)]
  transfers between devices with their start and end apart: 6 -> 6, of which waited for: 2 -> 3; matrix products, arithmetic and copies ran while one was open for 0% -> 0% of each run, Pallas kernels for 11% -> 13%
where the time goes in v10:
time: 33.6 us; the launch traced here: 33.4 us
  starting transfers between devices  16.7 us (50%)
  Pallas kernels  9.8 us (29%)
  waiting for transfers between devices  6.71 us (20%)
    all_to_all x2, starting transfers between devices, exchanged(): lax.all_to_all(value, ('px', 'py'), split_axis=0, concat_axis=0, tiled=True)  10.6 us
    ppermute x2, starting transfers between devices, swaps(): second = lax.ppermute(second, axis, inside)  4.71 us
    all_to_all x2, waiting for transfers between devices, exchanged(): lax.all_to_all(value, ('px', 'py'), split_axis=0, concat_axis=0, tiled=True)  4.14 us
    pallas_call x1, Pallas kernels, forward_modes(): pl.pallas_call(forward_kernel, out_shape=(jax.ShapeDtypeStruct(sent, jnp....  3.5 us
    ppermute x2, waiting for transfers between devices, swaps(): second = lax.ppermute(second, axis, inside)  2.56 us
    pallas_call x1, Pallas kernels, finish(): pl.pallas_call(finish_kernel, out_shape=jax.ShapeDtypeStruct(convolved.sh...  2.04 us
    pallas_call x2, Pallas kernels, convolve(): pl.pallas_call(kernel, out_shape=jax.ShapeDtypeStruct((rows, 128), jnp.fl...  1.82 us
    pallas_call x1, Pallas kernels, mix_modes(): pl.pallas_call(mix_kernel, out_shape=jax.ShapeDtypeStruct((32, 16, 128),...  1.59 us
  transfers between devices with their start and end apart: 6, of which 3 were waited for; matrix products, arithmetic and copies ran while one was open for 0% of the time, Pallas kernels for 13%

profile of v10, /device:TPU:0, one launch (start us, length us, event | category | flops | bytes accessed | tf_op | source)
XLA Modules:
  0.0 33.4 jit_solution(3912356640146434562)
XLA Ops:
  0.0 3.5 %forward_modes.1 = (bf16[32,8,128]{2,1,0:T(8,128)(2,1)}, bf16[64,32,128]{2,1,0:T(8,128)(2,1)S(1)}, f32[2,4,16,16,128]{4,3,2,1,0:T(8,128)S(1)}, bf16[3,3,3,32,32]{4,3,2,1,0:T(8,128)(2,1)S(1)}) custom-call(bf16[64,32,128]{2,1,0:T(8,128)(2,1)} %bitcast.10, f32[32,128]{1,0:T(8,128)} %constant.12.clone.z_hbm, f32[4,64,512]{2,1,0:T(8,128)} %constant.13.clone.y_hbm, ...), custom_call_target="tpu_custom_call" | custom-call | flops 134217728 | bytes 2097152 | tf_op jit(solution)/shard_map/forward_modes/pallas_call | solution.py:328
  3.5 7.3 %all-to-all-start = ((bf16[32,8,128]{2,1,0:T(8,128)(2,1)}), bf16[32,8,128]{2,1,0:T(8,128)(2,1)S(1)}, u32[]{:S(2)}, u32[]{:S(2)}) async-start(bf16[32,8,128]{2,1,0:T(8,128)(2,1)} %get-tuple-element.14), calls=%async_computation | async-start | bytes 131072 | tf_op jit(solution)/shard_map/all_to_all | solution.py:623
  10.8 0.8 %arrange_cells.1 = (bf16[32,32,128]{2,1,0:T(8,128)(2,1)S(1)}, bf16[32,32,128]{2,1,0:T(8,128)(2,1)S(1)}, bf16[3,64,384]{2,1,0:T(8,128)(2,1)S(1)}) custom-call(bf16[32,2,32,128]{3,2,1,0:T(8,128)(2,1)S(1)} %bitcast.7, bf16[3,3,3,32,32]{4,3,2,1,0:T(8,128)(2,1)S(1)} %get-tuple-element.17.conv_ref), custom_call_target="tpu_custom_call" | custom-call | flops 1024 | bytes 1024 | tf_op jit(solution)/shard_map/arrange_cells/pallas_call | solution.py:380
  11.7 1.8 %collective-permute-start = (bf16[32,32,128]{2,1,0:T(8,128)(2,1)S(1)}, bf16[32,32,128]{2,1,0:T(8,128)(2,1)S(1)}, u32[]{:S(2)}, u32[]{:S(2)}) collective-permute-start(bf16[32,32,128]{2,1,0:T(8,128)(2,1)S(1)} %get-tuple-element.18.refs_1_), channel_id=1, source_target_pairs={{0,4},{4,0},{8,12},{12,8},{16,20},{20,16},{24,28},{28,24},{1,5},{5... | collective-permute-start | bytes 786440 | tf_op jit(solution)/shard_map/ppermute | solution.py:630
  13.5 0.7 %collective-permute-start.1 = (bf16[32,32,128]{2,1,0:T(8,128)(2,1)S(1)}, bf16[32,32,128]{2,1,0:T(8,128)(2,1)S(1)}, u32[]{:S(2)}, u32[]{:S(2)}) collective-permute-start(bf16[32,32,128]{2,1,0:T(8,128)(2,1)S(1)} %get-tuple-element.19.refs_2_), channel_id=1, source_target_pairs={{4,8},{8,4},{12,16},{16,12},{20,24},{24,20},{5,9},{9,5},{13,17},{1... | collective-permute-start | bytes 786440 | tf_op jit(solution)/shard_map/ppermute | solution.py:631
  14.2 4.1 %all-to-all-done.modes_ref = bf16[32,8,128]{2,1,0:T(8,128)(2,1)S(1)} async-done(((bf16[32,8,128]{2,1,0:T(8,128)(2,1)}), bf16[32,8,128]{2,1,0:T(8,128)(2,1)S(1)}, u32[]{:S(2)}, u32[]{:S(2)}) %all-to-all-start) | async-done | bytes 65568 | tf_op jit(solution)/shard_map/all_to_all | solution.py:623
  18.2 0.0 copy-done.3
  18.2 0.0 copy-done.4
  18.2 1.6 %mix_modes.1 = bf16[32,16,128]{2,1,0:T(8,128)(2,1)} custom-call(bf16[32,8,128]{2,1,0:T(8,128)(2,1)S(1)} %all-to-all-done.modes_ref, f32[64,256]{1,0:T(8,128)S(1)} %copy-done.4, f32[2,4,16,16,128]{4,3,2,1,0:T(8,128)S(1)} %get-tuple-element.15.weight_ref, f32[128,256]{1,0:T(8,128)S(1)} %copy-done.3), custom_call_target="tpu_custom_call" | custom-call | flops 34359738368 | bytes 2097152 | tf_op jit(solution)/shard_map/mix_modes/pallas_call | solution.py:429
  19.8 3.3 %all-to-all-start.1 = ((bf16[32,16,128]{2,1,0:T(8,128)(2,1)}), bf16[32,16,128]{2,1,0:T(8,128)(2,1)S(1)}, u32[]{:S(2)}, u32[]{:S(2)}) async-start(bf16[32,16,128]{2,1,0:T(8,128)(2,1)} %mix_modes.1), calls=%async_computation.1 | async-start | bytes 262144 | tf_op jit(solution)/shard_map/all_to_all | solution.py:623
  23.1 2.6 %collective-permute-done.refs_0_ = bf16[32,32,128]{2,1,0:T(8,128)(2,1)S(1)} collective-permute-done((bf16[32,32,128]{2,1,0:T(8,128)(2,1)S(1)}, bf16[32,32,128]{2,1,0:T(8,128)(2,1)S(1)}, u32[]{:S(2)}, u32[]{:S(2)}) %collective-permute-start) | collective-permute-done | bytes 262176 | tf_op jit(solution)/shard_map/ppermute | solution.py:630
  25.7 0.0 collective-permute-done.1.refs_3_
  25.7 0.0 copy-start
  25.7 0.0 copy-start.1
  25.7 0.0 copy-start.2
  25.7 0.8 %collective-permute-start.2 = (bf16[128,128]{1,0:T(8,128)(2,1)S(1)}, bf16[128,128]{1,0:T(8,128)(2,1)S(1)}, u32[]{:S(2)}, u32[]{:S(2)}) collective-permute-start(bf16[128,128]{1,0:T(8,128)(2,1)S(1)} %get-tuple-element.21), channel_id=1, source_target_pairs={{1,2},{2,1},{5,6},{6,5},{9,10},{10,9},{13,14},{14,13},{17,18},{18,... | collective-permute-start | bytes 98312 | tf_op jit(solution)/shard_map/ppermute | solution.py:631
  26.5 2.9 %collective-permute-start.3 = (bf16[128,128]{1,0:T(8,128)(2,1)S(1)}, bf16[128,128]{1,0:T(8,128)(2,1)S(1)}, u32[]{:S(2)}, u32[]{:S(2)}) collective-permute-start(bf16[128,128]{1,0:T(8,128)(2,1)S(1)} %get-tuple-element.22), channel_id=1, source_target_pairs={{0,1},{1,0},{2,3},{3,2},{4,5},{5,4},{6,7},{7,6},{8,9},{9,8},{10,11... | collective-permute-start | bytes 98312 | tf_op jit(solution)/shard_map/ppermute | solution.py:630
  29.4 1.3 %convolve_interior.1 = f32[2048,128]{1,0:T(8,128)S(1)} custom-call(bf16[32,32,128]{2,1,0:T(8,128)(2,1)S(1)} %collective-permute-done.refs_0_, bf16[32,32,128]{2,1,0:T(8,128)(2,1)S(1)} %get-tuple-element.18.refs_1_, bf16[32,32,128]{2,1,0:T(8,128)(2,1)S(1)} %get-tuple-element.19.refs_2_, bf16[32,32,128]{2,1,0:T(8,128)(2,1)S(1)} %collective-permute-done.1.refs_3_, ...), custom_call_target="tpu_custom_call" | custom-call | flops 1073741824 | bytes 2097152 | tf_op jit(solution)/shard_map/convolve_interior/pallas_call | solution.py:525
  30.7 0.0 collective-permute-done.2.refs_4_
  30.8 0.0 collective-permute-done.3.refs_5_
  30.8 0.5 %convolve_edges.1 = f32[512,128]{1,0:T(8,128)S(1)} custom-call(bf16[32,32,128]{2,1,0:T(8,128)(2,1)S(1)} %collective-permute-done.refs_0_, bf16[32,32,128]{2,1,0:T(8,128)(2,1)S(1)} %get-tuple-element.18.refs_1_, bf16[32,32,128]{2,1,0:T(8,128)(2,1)S(1)} %get-tuple-element.19.refs_2_, bf16[32,32,128]{2,1,0:T(8,128)(2,1)S(1)} %collective-permute-done.1.refs_3_, ...), custom_call_target="tpu_custom_call" | custom-call | flops 1073741824 | bytes 2097152 | tf_op jit(solution)/shard_map/convolve_edges/pallas_call | solution.py:525
  31.3 0.1 all-to-all-done.1.values_ref
  31.3 0.0 copy-done.1
  31.4 2.0 %finish_layer.1 = bf16[32,2,32,128]{3,2,1,0:T(8,128)(2,1)} custom-call(f32[32]{0:T(128)S(1)} %copy-done.2, bf16[32,16,128]{2,1,0:T(8,128)(2,1)S(1)} %all-to-all-done.1.values_ref, f32[128,512]{1,0:T(8,128)S(1)} %copy-done.1, f32[4,32,512]{2,1,0:T(8,128)S(1)} %copy-done, f32[32,2,32,128]{3,2,1,0:T(8,128)S(1)} %bitcast.6, f32[32,2,8,128]{3,2,1,0:T(8,128)S(1)} %bitcast.8), custom_call_target="tpu_custom_call" | custom-call | flops 268435456 | bytes 4194304 | tf_op jit(solution)/shard_map/finish_layer/pallas_call | solution.py:607
  (5 shorter events, 0.0 us)
Async XLA Ops:
  0.0 18.2 %copy-start.3 = (f32[128,256]{1,0:T(8,128)S(1)}, f32[128,256]{1,0:T(8,128)}, u32[]{:S(2)}) copy-start(f32[128,256]{1,0:T(8,128)} %constant.15.clone.inverse_ref) | copy-start | bytes 393220
  0.0 18.2 %copy-start.4 = (f32[64,256]{1,0:T(8,128)S(1)}, f32[64,256]{1,0:T(8,128)}, u32[]{:S(2)}) copy-start(f32[64,256]{1,0:T(8,128)} %constant.14.clone.forward_ref) | copy-start | bytes 196612
  3.5 14.7 %all-to-all-start = ((bf16[32,8,128]{2,1,0:T(8,128)(2,1)}), bf16[32,8,128]{2,1,0:T(8,128)(2,1)S(1)}, u32[]{:S(2)}, u32[]{:S(2)}) async-start(bf16[32,8,128]{2,1,0:T(8,128)(2,1)} %get-tuple-element.14), calls=%async_computation | async-start | bytes 131072 | tf_op jit(solution)/shard_map/all_to_all | solution.py:623
  11.7 14.0 %collective-permute-start = (bf16[32,32,128]{2,1,0:T(8,128)(2,1)S(1)}, bf16[32,32,128]{2,1,0:T(8,128)(2,1)S(1)}, u32[]{:S(2)}, u32[]{:S(2)}) collective-permute-start(bf16[32,32,128]{2,1,0:T(8,128)(2,1)S(1)} %get-tuple-element.18.refs_1_), channel_id=1, source_target_pairs={{0,4},{4,0},{8,12},{12,8},{16,20},{20,16},{24,28},{28,24},{1,5},{5... | collective-permute-start | bytes 786440 | tf_op jit(solution)/shard_map/ppermute | solution.py:630
  13.5 12.2 %collective-permute-start.1 = (bf16[32,32,128]{2,1,0:T(8,128)(2,1)S(1)}, bf16[32,32,128]{2,1,0:T(8,128)(2,1)S(1)}, u32[]{:S(2)}, u32[]{:S(2)}) collective-permute-start(bf16[32,32,128]{2,1,0:T(8,128)(2,1)S(1)} %get-tuple-element.19.refs_2_), channel_id=1, source_target_pairs={{4,8},{8,4},{12,16},{16,12},{20,24},{24,20},{5,9},{9,5},{13,17},{1... | collective-permute-start | bytes 786440 | tf_op jit(solution)/shard_map/ppermute | solution.py:631
  19.8 11.5 %all-to-all-start.1 = ((bf16[32,16,128]{2,1,0:T(8,128)(2,1)}), bf16[32,16,128]{2,1,0:T(8,128)(2,1)S(1)}, u32[]{:S(2)}, u32[]{:S(2)}) async-start(bf16[32,16,128]{2,1,0:T(8,128)(2,1)} %mix_modes.1), calls=%async_computation.1 | async-start | bytes 262144 | tf_op jit(solution)/shard_map/all_to_all | solution.py:623
  25.7 5.7 %copy-start = (f32[4,32,512]{2,1,0:T(8,128)S(1)}, f32[4,32,512]{2,1,0:T(8,128)}, u32[]{:S(2)}) copy-start(f32[4,32,512]{2,1,0:T(8,128)} %constant.17.clone.y_ref) | copy-start | bytes 786436
  25.7 5.6 %copy-start.1 = (f32[128,512]{1,0:T(8,128)S(1)}, f32[128,512]{1,0:T(8,128)}, u32[]{:S(2)}) copy-start(f32[128,512]{1,0:T(8,128)} %constant.16.clone.z_ref) | copy-start | bytes 786436
  25.7 5.6 %copy-start.2 = (f32[32]{0:T(128)S(1)}, f32[32]{0:T(128)}, u32[]{:S(2)}) copy-start(f32[32]{0:T(128)} %bias_ref.1) | copy-start | bytes 388
  25.7 5.0 %collective-permute-start.2 = (bf16[128,128]{1,0:T(8,128)(2,1)S(1)}, bf16[128,128]{1,0:T(8,128)(2,1)S(1)}, u32[]{:S(2)}, u32[]{:S(2)}) collective-permute-start(bf16[128,128]{1,0:T(8,128)(2,1)S(1)} %get-tuple-element.21), channel_id=1, source_target_pairs={{1,2},{2,1},{5,6},{6,5},{9,10},{10,9},{13,14},{14,13},{17,18},{18,... | collective-permute-start | bytes 98312 | tf_op jit(solution)/shard_map/ppermute | solution.py:631
  26.5 4.2 %collective-permute-start.3 = (bf16[128,128]{1,0:T(8,128)(2,1)S(1)}, bf16[128,128]{1,0:T(8,128)(2,1)S(1)}, u32[]{:S(2)}, u32[]{:S(2)}) collective-permute-start(bf16[128,128]{1,0:T(8,128)(2,1)S(1)} %get-tuple-element.22), channel_id=1, source_target_pairs={{0,1},{1,0},{2,3},{3,2},{4,5},{5,4},{6,7},{7,6},{8,9},{9,8},{10,11... | collective-permute-start | bytes 98312 | tf_op jit(solution)/shard_map/ppermute | solution.py:630

commit v11 on v10

--- a/solution.py
+++ b/solution.py
@@ -245,18 +245,22 @@
     weight_hbm,
     conv_hbm,
     out_hbm,
+    first_ref,
+    second_ref,
+    taps_ref,
+    packed_ref,
+    out_ref,
     state_ref,
-    packed_ref,
-    conv_ref,
-    out_ref,
     z_ref,
     y_ref,
     table_ref,
     weight_ref,
+    conv_ref,
+    wide,
     sems,
 ):
     count = state_ref.shape[0] // 4
-    span = state_ref.shape[1]
+    span = state_ref.shape[2]
     y_copy = pltpu.make_async_copy(y_hbm.at[lax.axis_index("py")], y_ref, sems.at[0])
     z_copy = pltpu.make_async_copy(z_hbm, z_ref, sems.at[1])
     copies = [
@@ -292,7 +296,7 @@
     pieces = []
     for g in range(4):
         copies[g].wait()
-        cells = state_ref[g * count : (g + 1) * count].reshape(count * span, state_ref.shape[2])
+        cells = state_ref[g * count : (g + 1) * count].reshape(2 * count * span, 128)
         z_modes = lax.dot_general(
             z_table, cells, (((1,), (1,)), ((), ())), preferred_element_type=jnp.float32
         ).astype(jnp.bfloat16)
@@ -311,6 +315,22 @@
                     out_ref[(half * 4 + group) * 4 + 2 * pair + side] = chunk.astype(jnp.bfloat16)
     out_copy = pltpu.make_async_copy(out_ref, out_hbm, sems.at[15])
     out_copy.start()
+    odd_x = lax.rem(lax.axis_index("px"), 2)
+    for slot, (plane_ref, x) in enumerate(((first_ref, odd_x), (second_ref, 1 - odd_x))):
+        wide[slot] = state_ref[:, x].astype(jnp.float32).reshape(32 * span, 128)
+        for y in range(span):
+            plane_ref[y] = wide[slot, pl.ds(y, 32, stride=span), :].astype(jnp.bfloat16)
+    conv_copy.wait()
+    zero = jnp.zeros((32, 32), jnp.float32)
+    for dz in range(3):
+        for dy in range(3):
+            taps = [conv_ref[dx, dy, dz].astype(jnp.float32) for dx in range(3)]
+            for x_at in range(2):
+                blocks = [zero] * x_at + taps + [zero] * (1 - x_at)
+                blocks = [jnp.where(odd_x == 1, blocks[i], blocks[3 - i]) for i in range(4)]
+                taps_ref[dz, 32 * x_at : 32 * x_at + 32, 128 * dy : 128 * dy + 128] = (
+                    jnp.concatenate(blocks, axis=1).astype(jnp.bfloat16)
+                )
     for part in range(2):
         for kz in range(4):
             weight_copies[part * 4 + kz].wait()
@@ -318,29 +338,33 @@
                 packed_ref[part, kz, c] = jnp.concatenate(
                     [weight_ref[part, kz, u, c] for u in range(4)], axis=1
                 )
-    conv_copy.wait()
     out_copy.wait()
 
 
 def forward_modes(state, z_table, y_table, spectral_weight, conv_weight):
     vmem, hbm = (pl.BlockSpec(memory_space=space) for space in (pltpu.VMEM, pltpu.HBM))
     sent = (32, 8, 128)
+    plane = jax.ShapeDtypeStruct((state.shape[2], 32, 128), jnp.bfloat16)
     return pl.pallas_call(
         forward_kernel,
         out_shape=(
             jax.ShapeDtypeStruct(sent, jnp.bfloat16),
-            jax.ShapeDtypeStruct(state.shape, jnp.bfloat16),
+            plane,
+            plane,
+            jax.ShapeDtypeStruct((3, 64, 384), jnp.bfloat16),
             jax.ShapeDtypeStruct((2, 4, 16, KX, 128), jnp.float32),
-            jax.ShapeDtypeStruct(conv_weight.shape, jnp.bfloat16),
         ),
         in_specs=[hbm] * 5,
-        out_specs=(hbm, vmem, vmem, vmem),
+        out_specs=(hbm, vmem, vmem, vmem, vmem),
         scratch_shapes=[
             pltpu.VMEM(sent, jnp.bfloat16),
+            pltpu.VMEM(state.shape, jnp.bfloat16),
             pltpu.VMEM(z_table.shape, jnp.float32),
             pltpu.VMEM(y_table.shape[1:], jnp.float32),
-            pltpu.VMEM((32 * state.shape[1], y_table.shape[2]), jnp.bfloat16),
+            pltpu.VMEM((32 * state.shape[2], y_table.shape[2]), jnp.bfloat16),
             pltpu.VMEM(spectral_weight.shape, jnp.float32),
+            pltpu.VMEM(conv_weight.shape, jnp.bfloat16),
+            pltpu.VMEM((2, 32 * state.shape[2], 128), jnp.float32),
             pltpu.SemaphoreType.DMA((16,)),
         ],
         compiler_params=pltpu.CompilerParams(vmem_limit_bytes=16 * 2**20),
@@ -352,41 +376,6 @@
             for v in (state, z_table, y_table, spectral_weight, conv_weight)
         )
     )
-
-
-def arrange_kernel(state_ref, conv_ref, first_ref, second_ref, conv_out, wide):
-    odd_x = lax.rem(lax.axis_index("px"), 2)
-    cells_y = state_ref.shape[2]
-    for slot, (out_ref, x) in enumerate(((first_ref, odd_x), (second_ref, 1 - odd_x))):
-        wide[slot] = state_ref[:, x].astype(jnp.float32).reshape(32 * cells_y, 128)
-        for y in range(cells_y):
-            out_ref[y] = wide[slot, pl.ds(y, 32, stride=cells_y), :].astype(jnp.bfloat16)
-    zero = jnp.zeros((32, 32), jnp.float32)
-    for dz in range(3):
-        for dy in range(3):
-            taps = [conv_ref[dx, dy, dz].astype(jnp.float32) for dx in range(3)]
-            for x_at in range(2):
-                blocks = [zero] * x_at + taps + [zero] * (1 - x_at)
-                blocks = [jnp.where(odd_x == 1, blocks[i], blocks[3 - i]) for i in range(4)]
-                conv_out[dz, 32 * x_at : 32 * x_at + 32, 128 * dy : 128 * dy + 128] = (
-                    jnp.concatenate(blocks, axis=1).astype(jnp.bfloat16)
-                )
-
-
-def arrange(state, conv_weight):
-    vmem = pl.BlockSpec(memory_space=pltpu.VMEM)
-    cells_y = state.shape[2]
-    plane = jax.ShapeDtypeStruct((cells_y, 32, 128), jnp.bfloat16)
-    return pl.pallas_call(
-        arrange_kernel,
-        out_shape=(plane, plane, jax.ShapeDtypeStruct((3, 64, 384), jnp.bfloat16)),
-        in_specs=[vmem] * 2,
-        out_specs=(vmem,) * 3,
-        scratch_shapes=[pltpu.VMEM((2, 32 * cells_y, 128), jnp.float32)],
-        compiler_params=pltpu.CompilerParams(vmem_limit_bytes=16 * 2**20),
-        cost_estimate=pl.CostEstimate(flops=2**10, bytes_accessed=2**10, transcendentals=0),
-        name="arrange_cells",
-    )(state, conv_weight)
 
 
 def mix_kernel(modes_ref, forward_ref, weight_ref, inverse_ref, out_ref):
@@ -637,15 +626,14 @@
     if sizes != (8, 4, 2, 32, 128):
         return general_body(state_field, conv_weight, conv_bias, spectral_weight)
     z_forward, y_forward, x_forward, x_inverse, z_inverse, y_inverse = tables(*sizes)
-    sent, held, weights, conv_held = forward_modes(
-        state_field.reshape(channels * cells_x, cells_y, depth),
+    sent, first_own, second_own, taps, weights = forward_modes(
+        state_field,
         z_forward,
         y_forward,
         spectral_weight.swapaxes(4, 5),
         conv_weight.transpose(2, 3, 4, 0, 1),
     )
     modes = exchanged(sent)
-    first_own, second_own, taps = arrange(held.reshape(state_field.shape), conv_held)
     first_plane, second_plane = swaps(first_own, second_own, "px")
     values = exchanged(mix_modes(modes, x_forward, weights, x_inverse))
     planes = (second_plane, second_own, first_own, first_plane)

time: 33.6 us -> 33.9 us (level)
  waiting for transfers between devices: 6.71 us -> 7.53 us
  starting transfers between devices: 16.7 us -> 16.1 us
    pallas_call x1 -> x0, Pallas kernels: 0.84 us -> none  [arrange(): pl.pallas_call(arrange_kernel, out_shape=(plane, plane, jax.ShapeDtypeStr...]
    pallas_call x1, Pallas kernels: 3.5 us -> 4.32 us  [forward_modes(): pl.pallas_call(forward_kernel, out_shape=(jax.ShapeDtypeStruct(sent, jnp....]
    all_to_all x2, waiting for transfers between devices: 4.14 us -> 4.91 us  [exchanged(): lax.all_to_all(value, ('px', 'py'), split_axis=0, concat_axis=0, tiled=True)]
    all_to_all x2, starting transfers between devices: 10.6 us -> 9.88 us  [exchanged(): lax.all_to_all(value, ('px', 'py'), split_axis=0, concat_axis=0, tiled=True)]
  transfers between devices with their start and end apart: 6 -> 6, of which waited for: 3 -> 2; matrix products, arithmetic and copies ran while one was open for 0% -> 0% of each run, Pallas kernels for 13% -> 10%
where the time goes in v11:
time: 33.9 us; the launch traced here: 33.5 us
  starting transfers between devices  16.1 us (47%)
  Pallas kernels  9.78 us (29%)
  waiting for transfers between devices  7.53 us (22%)
    all_to_all x2, starting transfers between devices, exchanged(): lax.all_to_all(value, ('px', 'py'), split_axis=0, concat_axis=0, tiled=True)  9.88 us
    all_to_all x2, waiting for transfers between devices, exchanged(): lax.all_to_all(value, ('px', 'py'), split_axis=0, concat_axis=0, tiled=True)  4.91 us
    ppermute x2, starting transfers between devices, swaps(): second = lax.ppermute(second, axis, inside)  4.72 us
    pallas_call x1, Pallas kernels, forward_modes(): pl.pallas_call(forward_kernel, out_shape=(jax.ShapeDtypeStruct(sent, jnp....  4.32 us
    ppermute x2, waiting for transfers between devices, swaps(): second = lax.ppermute(second, axis, inside)  2.61 us
    pallas_call x1, Pallas kernels, finish(): pl.pallas_call(finish_kernel, out_shape=jax.ShapeDtypeStruct(convolved.sh...  2.04 us
    pallas_call x2, Pallas kernels, convolve(): pl.pallas_call(kernel, out_shape=jax.ShapeDtypeStruct((rows, 128), jnp.fl...  1.83 us
    pallas_call x1, Pallas kernels, mix_modes(): pl.pallas_call(mix_kernel, out_shape=jax.ShapeDtypeStruct((32, 16, 128),...  1.59 us
  transfers between devices with their start and end apart: 6, of which 2 were waited for; matrix products, arithmetic and copies ran while one was open for 0% of the time, Pallas kernels for 10%

profile of v11, /device:TPU:0, one launch (start us, length us, event | category | flops | bytes accessed | tf_op | source)
XLA Modules:
  0.0 33.5 jit_solution(16312853577487766468)
XLA Ops:
  0.0 4.3 %forward_modes.1 = (bf16[32,8,128]{2,1,0:T(8,128)(2,1)}, bf16[32,32,128]{2,1,0:T(8,128)(2,1)S(1)}, bf16[32,32,128]{2,1,0:T(8,128)(2,1)S(1)}, bf16[3,64,384]{2,1,0:T(8,128)(2,1)S(1)}, f32[2,4,16,16,128]{4,3,2,1,0:T(8,128)S(1)}) custom-call(bf16[32,2,32,128]{3,2,1,0:T(8,128)(2,1)} %state_hbm.1, f32[32,128]{1,0:T(8,128)} %constant.12.clone.z_hbm, ...), custom_call_target="tpu_custom_call" | custom-call | flops 134217728 | bytes 2097152 | tf_op jit(solution)/shard_map/forward_modes/pallas_call | solution.py:348
  4.3 7.3 %all-to-all-start = ((bf16[32,8,128]{2,1,0:T(8,128)(2,1)}), bf16[32,8,128]{2,1,0:T(8,128)(2,1)S(1)}, u32[]{:S(2)}, u32[]{:S(2)}) async-start(bf16[32,8,128]{2,1,0:T(8,128)(2,1)} %get-tuple-element.12), calls=%async_computation | async-start | bytes 131072 | tf_op jit(solution)/shard_map/all_to_all | solution.py:612
  11.6 1.8 %collective-permute-start = (bf16[32,32,128]{2,1,0:T(8,128)(2,1)S(1)}, bf16[32,32,128]{2,1,0:T(8,128)(2,1)S(1)}, u32[]{:S(2)}, u32[]{:S(2)}) collective-permute-start(bf16[32,32,128]{2,1,0:T(8,128)(2,1)S(1)} %get-tuple-element.14.refs_1_), channel_id=1, source_target_pairs={{0,4},{4,0},{8,12},{12,8},{16,20},{20,16},{24,28},{28,24},{1,5},{5... | collective-permute-start | bytes 786440 | tf_op jit(solution)/shard_map/ppermute | solution.py:619
  13.5 0.7 %collective-permute-start.1 = (bf16[32,32,128]{2,1,0:T(8,128)(2,1)S(1)}, bf16[32,32,128]{2,1,0:T(8,128)(2,1)S(1)}, u32[]{:S(2)}, u32[]{:S(2)}) collective-permute-start(bf16[32,32,128]{2,1,0:T(8,128)(2,1)S(1)} %get-tuple-element.15.refs_2_), channel_id=1, source_target_pairs={{4,8},{8,4},{12,16},{16,12},{20,24},{24,20},{5,9},{9,5},{13,17},{1... | collective-permute-start | bytes 786440 | tf_op jit(solution)/shard_map/ppermute | solution.py:620
  14.1 4.9 %all-to-all-done.modes_ref = bf16[32,8,128]{2,1,0:T(8,128)(2,1)S(1)} async-done(((bf16[32,8,128]{2,1,0:T(8,128)(2,1)}), bf16[32,8,128]{2,1,0:T(8,128)(2,1)S(1)}, u32[]{:S(2)}, u32[]{:S(2)}) %all-to-all-start) | async-done | bytes 65568 | tf_op jit(solution)/shard_map/all_to_all | solution.py:612
  19.1 0.0 copy-done.4
  19.1 1.6 %mix_modes.1 = bf16[32,16,128]{2,1,0:T(8,128)(2,1)} custom-call(bf16[32,8,128]{2,1,0:T(8,128)(2,1)S(1)} %all-to-all-done.modes_ref, f32[64,256]{1,0:T(8,128)S(1)} %copy-done.4, f32[2,4,16,16,128]{4,3,2,1,0:T(8,128)S(1)} %get-tuple-element.13.weight_ref, f32[128,256]{1,0:T(8,128)S(1)} %copy-done.3), custom_call_target="tpu_custom_call" | custom-call | flops 34359738368 | bytes 2097152 | tf_op jit(solution)/shard_map/mix_modes/pallas_call | solution.py:418
  20.6 2.6 %all-to-all-start.1 = ((bf16[32,16,128]{2,1,0:T(8,128)(2,1)}), bf16[32,16,128]{2,1,0:T(8,128)(2,1)S(1)}, u32[]{:S(2)}, u32[]{:S(2)}) async-start(bf16[32,16,128]{2,1,0:T(8,128)(2,1)} %mix_modes.1), calls=%async_computation.1 | async-start | bytes 262144 | tf_op jit(solution)/shard_map/all_to_all | solution.py:612
  23.2 2.6 %collective-permute-done.refs_0_ = bf16[32,32,128]{2,1,0:T(8,128)(2,1)S(1)} collective-permute-done((bf16[32,32,128]{2,1,0:T(8,128)(2,1)S(1)}, bf16[32,32,128]{2,1,0:T(8,128)(2,1)S(1)}, u32[]{:S(2)}, u32[]{:S(2)}) %collective-permute-start) | collective-permute-done | bytes 262176 | tf_op jit(solution)/shard_map/ppermute | solution.py:619
  25.8 0.0 collective-permute-done.1.refs_3_
  25.9 0.0 copy-start
  25.9 0.0 copy-start.1
  25.9 0.0 copy-start.2
  25.9 0.8 %collective-permute-start.2 = (bf16[128,128]{1,0:T(8,128)(2,1)S(1)}, bf16[128,128]{1,0:T(8,128)(2,1)S(1)}, u32[]{:S(2)}, u32[]{:S(2)}) collective-permute-start(bf16[128,128]{1,0:T(8,128)(2,1)S(1)} %get-tuple-element.17), channel_id=1, source_target_pairs={{1,2},{2,1},{5,6},{6,5},{9,10},{10,9},{13,14},{14,13},{17,18},{18,... | collective-permute-start | bytes 98312 | tf_op jit(solution)/shard_map/ppermute | solution.py:620
  26.7 2.9 %collective-permute-start.3 = (bf16[128,128]{1,0:T(8,128)(2,1)S(1)}, bf16[128,128]{1,0:T(8,128)(2,1)S(1)}, u32[]{:S(2)}, u32[]{:S(2)}) collective-permute-start(bf16[128,128]{1,0:T(8,128)(2,1)S(1)} %get-tuple-element.18), channel_id=1, source_target_pairs={{0,1},{1,0},{2,3},{3,2},{4,5},{5,4},{6,7},{7,6},{8,9},{9,8},{10,11... | collective-permute-start | bytes 98312 | tf_op jit(solution)/shard_map/ppermute | solution.py:619
  29.6 1.3 %convolve_interior.1 = f32[2048,128]{1,0:T(8,128)S(1)} custom-call(bf16[32,32,128]{2,1,0:T(8,128)(2,1)S(1)} %collective-permute-done.refs_0_, bf16[32,32,128]{2,1,0:T(8,128)(2,1)S(1)} %get-tuple-element.14.refs_1_, bf16[32,32,128]{2,1,0:T(8,128)(2,1)S(1)} %get-tuple-element.15.refs_2_, bf16[32,32,128]{2,1,0:T(8,128)(2,1)S(1)} %collective-permute-done.1.refs_3_, ...), custom_call_target="tpu_custom_call" | custom-call | flops 1073741824 | bytes 2097152 | tf_op jit(solution)/shard_map/convolve_interior/pallas_call | solution.py:514
  30.9 0.0 collective-permute-done.2.refs_4_
  30.9 0.0 collective-permute-done.3.refs_5_
  31.0 0.5 %convolve_edges.1 = f32[512,128]{1,0:T(8,128)S(1)} custom-call(bf16[32,32,128]{2,1,0:T(8,128)(2,1)S(1)} %collective-permute-done.refs_0_, bf16[32,32,128]{2,1,0:T(8,128)(2,1)S(1)} %get-tuple-element.14.refs_1_, bf16[32,32,128]{2,1,0:T(8,128)(2,1)S(1)} %get-tuple-element.15.refs_2_, bf16[32,32,128]{2,1,0:T(8,128)(2,1)S(1)} %collective-permute-done.1.refs_3_, ...), custom_call_target="tpu_custom_call" | custom-call | flops 1073741824 | bytes 2097152 | tf_op jit(solution)/shard_map/convolve_edges/pallas_call | solution.py:514
  31.5 0.0 all-to-all-done.1.values_ref
  31.5 0.0 copy-done
  31.5 0.0 copy-done.1
  31.5 0.0 copy-done.2
  31.5 2.0 %finish_layer.1 = bf16[32,2,32,128]{3,2,1,0:T(8,128)(2,1)} custom-call(f32[32]{0:T(128)S(1)} %copy-done.2, bf16[32,16,128]{2,1,0:T(8,128)(2,1)S(1)} %all-to-all-done.1.values_ref, f32[128,512]{1,0:T(8,128)S(1)} %copy-done.1, f32[4,32,512]{2,1,0:T(8,128)S(1)} %copy-done, f32[32,2,32,128]{3,2,1,0:T(8,128)S(1)} %bitcast.4, f32[32,2,8,128]{3,2,1,0:T(8,128)S(1)} %bitcast.5), custom_call_target="tpu_custom_call" | custom-call | flops 268435456 | bytes 4194304 | tf_op jit(solution)/shard_map/finish_layer/pallas_call | solution.py:596
  (4 shorter events, 0.0 us)
Async XLA Ops:
  0.0 19.1 %copy-start.3 = (f32[128,256]{1,0:T(8,128)S(1)}, f32[128,256]{1,0:T(8,128)}, u32[]{:S(2)}) copy-start(f32[128,256]{1,0:T(8,128)} %constant.15.clone.inverse_ref) | copy-start | bytes 393220
  0.0 19.1 %copy-start.4 = (f32[64,256]{1,0:T(8,128)S(1)}, f32[64,256]{1,0:T(8,128)}, u32[]{:S(2)}) copy-start(f32[64,256]{1,0:T(8,128)} %constant.14.clone.forward_ref) | copy-start | bytes 196612
  4.3 14.7 %all-to-all-start = ((bf16[32,8,128]{2,1,0:T(8,128)(2,1)}), bf16[32,8,128]{2,1,0:T(8,128)(2,1)S(1)}, u32[]{:S(2)}, u32[]{:S(2)}) async-start(bf16[32,8,128]{2,1,0:T(8,128)(2,1)} %get-tuple-element.12), calls=%async_computation | async-start | bytes 131072 | tf_op jit(solution)/shard_map/all_to_all | solution.py:612
  11.6 14.2 %collective-permute-start = (bf16[32,32,128]{2,1,0:T(8,128)(2,1)S(1)}, bf16[32,32,128]{2,1,0:T(8,128)(2,1)S(1)}, u32[]{:S(2)}, u32[]{:S(2)}) collective-permute-start(bf16[32,32,128]{2,1,0:T(8,128)(2,1)S(1)} %get-tuple-element.14.refs_1_), channel_id=1, source_target_pairs={{0,4},{4,0},{8,12},{12,8},{16,20},{20,16},{24,28},{28,24},{1,5},{5... | collective-permute-start | bytes 786440 | tf_op jit(solution)/shard_map/ppermute | solution.py:619
  13.5 12.4 %collective-permute-start.1 = (bf16[32,32,128]{2,1,0:T(8,128)(2,1)S(1)}, bf16[32,32,128]{2,1,0:T(8,128)(2,1)S(1)}, u32[]{:S(2)}, u32[]{:S(2)}) collective-permute-start(bf16[32,32,128]{2,1,0:T(8,128)(2,1)S(1)} %get-tuple-element.15.refs_2_), channel_id=1, source_target_pairs={{4,8},{8,4},{12,16},{16,12},{20,24},{24,20},{5,9},{9,5},{13,17},{1... | collective-permute-start | bytes 786440 | tf_op jit(solution)/shard_map/ppermute | solution.py:620
  20.6 10.8 %all-to-all-start.1 = ((bf16[32,16,128]{2,1,0:T(8,128)(2,1)}), bf16[32,16,128]{2,1,0:T(8,128)(2,1)S(1)}, u32[]{:S(2)}, u32[]{:S(2)}) async-start(bf16[32,16,128]{2,1,0:T(8,128)(2,1)} %mix_modes.1), calls=%async_computation.1 | async-start | bytes 262144 | tf_op jit(solution)/shard_map/all_to_all | solution.py:612
  25.9 5.6 %copy-start = (f32[4,32,512]{2,1,0:T(8,128)S(1)}, f32[4,32,512]{2,1,0:T(8,128)}, u32[]{:S(2)}) copy-start(f32[4,32,512]{2,1,0:T(8,128)} %constant.17.clone.y_ref) | copy-start | bytes 786436
  25.9 5.6 %copy-start.1 = (f32[128,512]{1,0:T(8,128)S(1)}, f32[128,512]{1,0:T(8,128)}, u32[]{:S(2)}) copy-start(f32[128,512]{1,0:T(8,128)} %constant.16.clone.z_ref) | copy-start | bytes 786436
  25.9 5.6 %copy-start.2 = (f32[32]{0:T(128)S(1)}, f32[32]{0:T(128)}, u32[]{:S(2)}) copy-start(f32[32]{0:T(128)} %bias_ref.1) | copy-start | bytes 388
  25.9 5.0 %collective-permute-start.2 = (bf16[128,128]{1,0:T(8,128)(2,1)S(1)}, bf16[128,128]{1,0:T(8,128)(2,1)S(1)}, u32[]{:S(2)}, u32[]{:S(2)}) collective-permute-start(bf16[128,128]{1,0:T(8,128)(2,1)S(1)} %get-tuple-element.17), channel_id=1, source_target_pairs={{1,2},{2,1},{5,6},{6,5},{9,10},{10,9},{13,14},{14,13},{17,18},{18,... | collective-permute-start | bytes 98312 | tf_op jit(solution)/shard_map/ppermute | solution.py:620
  26.7 4.2 %collective-permute-start.3 = (bf16[128,128]{1,0:T(8,128)(2,1)S(1)}, bf16[128,128]{1,0:T(8,128)(2,1)S(1)}, u32[]{:S(2)}, u32[]{:S(2)}) collective-permute-start(bf16[128,128]{1,0:T(8,128)(2,1)S(1)} %get-tuple-element.18), channel_id=1, source_target_pairs={{0,1},{1,0},{2,3},{3,2},{4,5},{5,4},{6,7},{7,6},{8,9},{9,8},{10,11... | collective-permute-start | bytes 98312 | tf_op jit(solution)/shard_map/ppermute | solution.py:619

commit v12 on v11

--- a/solution.py
+++ b/solution.py
@@ -279,7 +279,7 @@
         for part in range(2)
         for kz in range(4)
     ]
-    for copy in [y_copy, z_copy] + copies + weight_copies + [conv_copy]:
+    for copy in [y_copy, z_copy] + copies:
         copy.start()
     y_copy.wait()
     table = y_ref[...]
@@ -296,6 +296,9 @@
     pieces = []
     for g in range(4):
         copies[g].wait()
+        if g == 3:
+            for copy in [conv_copy] + weight_copies:
+                copy.start()
         cells = state_ref[g * count : (g + 1) * count].reshape(2 * count * span, 128)
         z_modes = lax.dot_general(
             z_table, cells, (((1,), (1,)), ((), ())), preferred_element_type=jnp.float32
@@ -336,7 +339,7 @@
             weight_copies[part * 4 + kz].wait()
             for c in range(16):
                 packed_ref[part, kz, c] = jnp.concatenate(
-                    [weight_ref[part, kz, u, c] for u in range(4)], axis=1
+                    [weight_ref[part, kz, u, c].astype(jnp.bfloat16) for u in range(4)], axis=1
                 )
     out_copy.wait()
 
@@ -352,7 +355,7 @@
             plane,
             plane,
             jax.ShapeDtypeStruct((3, 64, 384), jnp.bfloat16),
-            jax.ShapeDtypeStruct((2, 4, 16, KX, 128), jnp.float32),
+            jax.ShapeDtypeStruct((2, 4, 16, KX, 128), jnp.bfloat16),
         ),
         in_specs=[hbm] * 5,
         out_specs=(hbm, vmem, vmem, vmem, vmem),
@@ -392,8 +395,8 @@
             index = base + (kz * 32 + c8)
             real_in = jnp.take_along_axis(x_modes[half * 32 : half * 32 + 16], index, axis=1)
             imag_in = jnp.take_along_axis(x_modes[half * 32 + 16 : half * 32 + 32], index, axis=1)
-            real_weight = weight_ref[0, kz, c]
-            imag_weight = weight_ref[1, kz, c]
+            real_weight = weight_ref[0, kz, c].astype(jnp.float32)
+            imag_weight = weight_ref[1, kz, c].astype(jnp.float32)
             real_term = real_weight * real_in - imag_weight * imag_in
             imag_term = real_weight * imag_in + imag_weight * real_in
             real_sum = real_term if real_sum is None else real_sum + real_term

time: 33.9 us -> 33.9 us (level)
  no operation moved by 1% of the time
where the time goes in v12:
time: 33.9 us; the launch traced here: 33.6 us
  starting transfers between devices  16.1 us (47%)
  Pallas kernels  9.86 us (29%)
  waiting for transfers between devices  7.53 us (22%)
    all_to_all x2, starting transfers between devices, exchanged(): lax.all_to_all(value, ('px', 'py'), split_axis=0, concat_axis=0, tiled=True)  9.88 us
    all_to_all x2, waiting for transfers between devices, exchanged(): lax.all_to_all(value, ('px', 'py'), split_axis=0, concat_axis=0, tiled=True)  4.93 us
    ppermute x2, starting transfers between devices, swaps(): second = lax.ppermute(second, axis, inside)  4.72 us
    pallas_call x1, Pallas kernels, forward_modes(): pl.pallas_call(forward_kernel, out_shape=(jax.ShapeDtypeStruct(sent, jnp....  4.39 us
    ppermute x2, waiting for transfers between devices, swaps(): second = lax.ppermute(second, axis, inside)  2.6 us
    pallas_call x1, Pallas kernels, finish(): pl.pallas_call(finish_kernel, out_shape=jax.ShapeDtypeStruct(convolved.sh...  2.04 us
    pallas_call x2, Pallas kernels, convolve(): pl.pallas_call(kernel, out_shape=jax.ShapeDtypeStruct((rows, 128), jnp.fl...  1.83 us
    pallas_call x1, Pallas kernels, mix_modes(): pl.pallas_call(mix_kernel, out_shape=jax.ShapeDtypeStruct((32, 16, 128),...  1.6 us
  transfers between devices with their start and end apart: 6, of which 2 were waited for; matrix products, arithmetic and copies ran while one was open for 0% of the time, Pallas kernels for 10%

profile of v12, /device:TPU:0, one launch (start us, length us, event | category | flops | bytes accessed | tf_op | source)
XLA Modules:
  0.0 33.6 jit_solution(6697120123338146727)
XLA Ops:
  0.0 4.4 %forward_modes.1 = (bf16[32,8,128]{2,1,0:T(8,128)(2,1)}, bf16[32,32,128]{2,1,0:T(8,128)(2,1)S(1)}, bf16[32,32,128]{2,1,0:T(8,128)(2,1)S(1)}, bf16[3,64,384]{2,1,...) custom-call(bf16[32,2,32,128]{3,2,1,0:T(8,128)(2,1)} %state_hbm.1, f32[32,128]{1,0:T(8,128)} %constant.12.clone.z_hbm, ...), custom_call_target="tpu_custom_call" | custom-call | flops 134217728 | bytes 2097152 | tf_op jit(solution)/shard_map/forward_modes/pallas_call | solution.py:351
  4.4 7.3 %all-to-all-start = ((bf16[32,8,128]{2,1,0:T(8,128)(2,1)}), bf16[32,8,128]{2,1,0:T(8,128)(2,1)S(1)}, u32[]{:S(2)}, u32[]{:S(2)}) async-start(bf16[32,8,128]{2,1,0:T(8,128)(2,1)} %get-tuple-element.12), calls=%async_computation | async-start | bytes 131072 | tf_op jit(solution)/shard_map/all_to_all | solution.py:615
  11.7 1.8 %collective-permute-start = (bf16[32,32,128]{2,1,0:T(8,128)(2,1)S(1)}, bf16[32,32,128]{2,1,0:T(8,128)(2,1)S(1)}, u32[]{:S(2)}, u32[]{:S(2)}) collective-permute-start(bf16[32,32,128]{2,1,0:T(8,128)(2,1)S(1)} %get-tuple-element.14.refs_1_), channel_id=1, source_target_pairs={{0,4},{4,0},{8,12},{12,8},{16,20},{20,16},{24,28},{28,24},{1,5},{5... | collective-permute-start | bytes 786440 | tf_op jit(solution)/shard_map/ppermute | solution.py:622
  13.5 0.7 %collective-permute-start.1 = (bf16[32,32,128]{2,1,0:T(8,128)(2,1)S(1)}, bf16[32,32,128]{2,1,0:T(8,128)(2,1)S(1)}, u32[]{:S(2)}, u32[]{:S(2)}) collective-permute-start(bf16[32,32,128]{2,1,0:T(8,128)(2,1)S(1)} %get-tuple-element.15.refs_2_), channel_id=1, source_target_pairs={{4,8},{8,4},{12,16},{16,12},{20,24},{24,20},{5,9},{9,5},{13,17},{1... | collective-permute-start | bytes 786440 | tf_op jit(solution)/shard_map/ppermute | solution.py:623
  14.2 4.9 %all-to-all-done.modes_ref = bf16[32,8,128]{2,1,0:T(8,128)(2,1)S(1)} async-done(((bf16[32,8,128]{2,1,0:T(8,128)(2,1)}), bf16[32,8,128]{2,1,0:T(8,128)(2,1)S(1)}, u32[]{:S(2)}, u32[]{:S(2)}) %all-to-all-start) | async-done | bytes 65568 | tf_op jit(solution)/shard_map/all_to_all | solution.py:615
  19.1 0.0 copy-done.3
  19.1 0.0 copy-done.4
  19.1 1.6 %mix_modes.1 = bf16[32,16,128]{2,1,0:T(8,128)(2,1)} custom-call(bf16[32,8,128]{2,1,0:T(8,128)(2,1)S(1)} %all-to-all-done.modes_ref, f32[64,256]{1,0:T(8,128)S(1)} %copy-done.4, bf16[2,4,16,16,128]{4,3,2,1,0:T(8,128)(2,1)S(1)} %get-tuple-element.13.weight_ref, f32[128,256]{1,0:T(8,128)S(1)} %copy-done.3), custom_call_target="tpu_custom_call" | custom-call | flops 34359738368 | bytes 2097152 | tf_op jit(solution)/shard_map/mix_modes/pallas_call | solution.py:421
  20.7 2.6 %all-to-all-start.1 = ((bf16[32,16,128]{2,1,0:T(8,128)(2,1)}), bf16[32,16,128]{2,1,0:T(8,128)(2,1)S(1)}, u32[]{:S(2)}, u32[]{:S(2)}) async-start(bf16[32,16,128]{2,1,0:T(8,128)(2,1)} %mix_modes.1), calls=%async_computation.1 | async-start | bytes 262144 | tf_op jit(solution)/shard_map/all_to_all | solution.py:615
  23.3 2.6 %collective-permute-done.refs_0_ = bf16[32,32,128]{2,1,0:T(8,128)(2,1)S(1)} collective-permute-done((bf16[32,32,128]{2,1,0:T(8,128)(2,1)S(1)}, bf16[32,32,128]{2,1,0:T(8,128)(2,1)S(1)}, u32[]{:S(2)}, u32[]{:S(2)}) %collective-permute-start) | collective-permute-done | bytes 262176 | tf_op jit(solution)/shard_map/ppermute | solution.py:622
  25.9 0.0 collective-permute-done.1.refs_3_
  25.9 0.0 copy-start
  25.9 0.0 copy-start.1
  26.0 0.0 copy-start.2
  26.0 0.8 %collective-permute-start.2 = (bf16[128,128]{1,0:T(8,128)(2,1)S(1)}, bf16[128,128]{1,0:T(8,128)(2,1)S(1)}, u32[]{:S(2)}, u32[]{:S(2)}) collective-permute-start(bf16[128,128]{1,0:T(8,128)(2,1)S(1)} %get-tuple-element.17), channel_id=1, source_target_pairs={{1,2},{2,1},{5,6},{6,5},{9,10},{10,9},{13,14},{14,13},{17,18},{18,... | collective-permute-start | bytes 98312 | tf_op jit(solution)/shard_map/ppermute | solution.py:623
  26.8 2.9 %collective-permute-start.3 = (bf16[128,128]{1,0:T(8,128)(2,1)S(1)}, bf16[128,128]{1,0:T(8,128)(2,1)S(1)}, u32[]{:S(2)}, u32[]{:S(2)}) collective-permute-start(bf16[128,128]{1,0:T(8,128)(2,1)S(1)} %get-tuple-element.18), channel_id=1, source_target_pairs={{0,1},{1,0},{2,3},{3,2},{4,5},{5,4},{6,7},{7,6},{8,9},{9,8},{10,11... | collective-permute-start | bytes 98312 | tf_op jit(solution)/shard_map/ppermute | solution.py:622
  29.7 1.3 %convolve_interior.1 = f32[2048,128]{1,0:T(8,128)S(1)} custom-call(bf16[32,32,128]{2,1,0:T(8,128)(2,1)S(1)} %collective-permute-done.refs_0_, bf16[32,32,128]{2,1,0:T(8,128)(2,1)S(1)} %get-tuple-element.14.refs_1_, bf16[32,32,128]{2,1,0:T(8,128)(2,1)S(1)} %get-tuple-element.15.refs_2_, bf16[32,32,128]{2,1,0:T(8,128)(2,1)S(1)} %collective-permute-done.1.refs_3_, ...), custom_call_target="tpu_custom_call" | custom-call | flops 1073741824 | bytes 2097152 | tf_op jit(solution)/shard_map/convolve_interior/pallas_call | solution.py:517
  31.0 0.0 collective-permute-done.2.refs_4_
  31.0 0.0 collective-permute-done.3.refs_5_
  31.0 0.5 %convolve_edges.1 = f32[512,128]{1,0:T(8,128)S(1)} custom-call(bf16[32,32,128]{2,1,0:T(8,128)(2,1)S(1)} %collective-permute-done.refs_0_, bf16[32,32,128]{2,1,0:T(8,128)(2,1)S(1)} %get-tuple-element.14.refs_1_, bf16[32,32,128]{2,1,0:T(8,128)(2,1)S(1)} %get-tuple-element.15.refs_2_, bf16[32,32,128]{2,1,0:T(8,128)(2,1)S(1)} %collective-permute-done.1.refs_3_, ...), custom_call_target="tpu_custom_call" | custom-call | flops 1073741824 | bytes 2097152 | tf_op jit(solution)/shard_map/convolve_edges/pallas_call | solution.py:517
  31.5 0.0 all-to-all-done.1.values_ref
  31.5 0.0 copy-done
  31.5 0.0 copy-done.1
  31.6 2.0 %finish_layer.1 = bf16[32,2,32,128]{3,2,1,0:T(8,128)(2,1)} custom-call(f32[32]{0:T(128)S(1)} %copy-done.2, bf16[32,16,128]{2,1,0:T(8,128)(2,1)S(1)} %all-to-all-done.1.values_ref, f32[128,512]{1,0:T(8,128)S(1)} %copy-done.1, f32[4,32,512]{2,1,0:T(8,128)S(1)} %copy-done, f32[32,2,32,128]{3,2,1,0:T(8,128)S(1)} %bitcast.4, f32[32,2,8,128]{3,2,1,0:T(8,128)S(1)} %bitcast.5), custom_call_target="tpu_custom_call" | custom-call | flops 268435456 | bytes 4194304 | tf_op jit(solution)/shard_map/finish_layer/pallas_call | solution.py:599
  (4 shorter events, 0.0 us)
Async XLA Ops:
  0.0 19.1 %copy-start.3 = (f32[128,256]{1,0:T(8,128)S(1)}, f32[128,256]{1,0:T(8,128)}, u32[]{:S(2)}) copy-start(f32[128,256]{1,0:T(8,128)} %constant.15.clone.inverse_ref) | copy-start | bytes 393220
  0.0 19.1 %copy-start.4 = (f32[64,256]{1,0:T(8,128)S(1)}, f32[64,256]{1,0:T(8,128)}, u32[]{:S(2)}) copy-start(f32[64,256]{1,0:T(8,128)} %constant.14.clone.forward_ref) | copy-start | bytes 196612
  4.4 14.7 %all-to-all-start = ((bf16[32,8,128]{2,1,0:T(8,128)(2,1)}), bf16[32,8,128]{2,1,0:T(8,128)(2,1)S(1)}, u32[]{:S(2)}, u32[]{:S(2)}) async-start(bf16[32,8,128]{2,1,0:T(8,128)(2,1)} %get-tuple-element.12), calls=%async_computation | async-start | bytes 131072 | tf_op jit(solution)/shard_map/all_to_all | solution.py:615
  11.7 14.2 %collective-permute-start = (bf16[32,32,128]{2,1,0:T(8,128)(2,1)S(1)}, bf16[32,32,128]{2,1,0:T(8,128)(2,1)S(1)}, u32[]{:S(2)}, u32[]{:S(2)}) collective-permute-start(bf16[32,32,128]{2,1,0:T(8,128)(2,1)S(1)} %get-tuple-element.14.refs_1_), channel_id=1, source_target_pairs={{0,4},{4,0},{8,12},{12,8},{16,20},{20,16},{24,28},{28,24},{1,5},{5... | collective-permute-start | bytes 786440 | tf_op jit(solution)/shard_map/ppermute | solution.py:622
  13.5 12.4 %collective-permute-start.1 = (bf16[32,32,128]{2,1,0:T(8,128)(2,1)S(1)}, bf16[32,32,128]{2,1,0:T(8,128)(2,1)S(1)}, u32[]{:S(2)}, u32[]{:S(2)}) collective-permute-start(bf16[32,32,128]{2,1,0:T(8,128)(2,1)S(1)} %get-tuple-element.15.refs_2_), channel_id=1, source_target_pairs={{4,8},{8,4},{12,16},{16,12},{20,24},{24,20},{5,9},{9,5},{13,17},{1... | collective-permute-start | bytes 786440 | tf_op jit(solution)/shard_map/ppermute | solution.py:623
  20.7 10.8 %all-to-all-start.1 = ((bf16[32,16,128]{2,1,0:T(8,128)(2,1)}), bf16[32,16,128]{2,1,0:T(8,128)(2,1)S(1)}, u32[]{:S(2)}, u32[]{:S(2)}) async-start(bf16[32,16,128]{2,1,0:T(8,128)(2,1)} %mix_modes.1), calls=%async_computation.1 | async-start | bytes 262144 | tf_op jit(solution)/shard_map/all_to_all | solution.py:615
  25.9 5.6 %copy-start = (f32[4,32,512]{2,1,0:T(8,128)S(1)}, f32[4,32,512]{2,1,0:T(8,128)}, u32[]{:S(2)}) copy-start(f32[4,32,512]{2,1,0:T(8,128)} %constant.17.clone.y_ref) | copy-start | bytes 786436
  25.9 5.6 %copy-start.1 = (f32[128,512]{1,0:T(8,128)S(1)}, f32[128,512]{1,0:T(8,128)}, u32[]{:S(2)}) copy-start(f32[128,512]{1,0:T(8,128)} %constant.16.clone.z_ref) | copy-start | bytes 786436
  26.0 5.6 %copy-start.2 = (f32[32]{0:T(128)S(1)}, f32[32]{0:T(128)}, u32[]{:S(2)}) copy-start(f32[32]{0:T(128)} %bias_ref.1) | copy-start | bytes 388
  26.0 5.0 %collective-permute-start.2 = (bf16[128,128]{1,0:T(8,128)(2,1)S(1)}, bf16[128,128]{1,0:T(8,128)(2,1)S(1)}, u32[]{:S(2)}, u32[]{:S(2)}) collective-permute-start(bf16[128,128]{1,0:T(8,128)(2,1)S(1)} %get-tuple-element.17), channel_id=1, source_target_pairs={{1,2},{2,1},{5,6},{6,5},{9,10},{10,9},{13,14},{14,13},{17,18},{18,... | collective-permute-start | bytes 98312 | tf_op jit(solution)/shard_map/ppermute | solution.py:623
  26.8 4.2 %collective-permute-start.3 = (bf16[128,128]{1,0:T(8,128)(2,1)S(1)}, bf16[128,128]{1,0:T(8,128)(2,1)S(1)}, u32[]{:S(2)}, u32[]{:S(2)}) collective-permute-start(bf16[128,128]{1,0:T(8,128)(2,1)S(1)} %get-tuple-element.18), channel_id=1, source_target_pairs={{0,1},{1,0},{2,3},{3,2},{4,5},{5,4},{6,7},{7,6},{8,9},{9,8},{10,11... | collective-permute-start | bytes 98312 | tf_op jit(solution)/shard_map/ppermute | solution.py:622

commit v13 on v10

--- a/solution.py
+++ b/solution.py
@@ -316,7 +316,7 @@
             weight_copies[part * 4 + kz].wait()
             for c in range(16):
                 packed_ref[part, kz, c] = jnp.concatenate(
-                    [weight_ref[part, kz, u, c] for u in range(4)], axis=1
+                    [weight_ref[part, kz, u, c].astype(jnp.bfloat16) for u in range(4)], axis=1
                 )
     conv_copy.wait()
     out_copy.wait()
@@ -330,7 +330,7 @@
         out_shape=(
             jax.ShapeDtypeStruct(sent, jnp.bfloat16),
             jax.ShapeDtypeStruct(state.shape, jnp.bfloat16),
-            jax.ShapeDtypeStruct((2, 4, 16, KX, 128), jnp.float32),
+            jax.ShapeDtypeStruct((2, 4, 16, KX, 128), jnp.bfloat16),
             jax.ShapeDtypeStruct(conv_weight.shape, jnp.bfloat16),
         ),
         in_specs=[hbm] * 5,
@@ -403,8 +403,8 @@
             index = base + (kz * 32 + c8)
             real_in = jnp.take_along_axis(x_modes[half * 32 : half * 32 + 16], index, axis=1)
             imag_in = jnp.take_along_axis(x_modes[half * 32 + 16 : half * 32 + 32], index, axis=1)
-            real_weight = weight_ref[0, kz, c]
-            imag_weight = weight_ref[1, kz, c]
+            real_weight = weight_ref[0, kz, c].astype(jnp.float32)
+            imag_weight = weight_ref[1, kz, c].astype(jnp.float32)
             real_term = real_weight * real_in - imag_weight * imag_in
             imag_term = real_weight * imag_in + imag_weight * real_in
             real_sum = real_term if real_sum is None else real_sum + real_term

time: 33.6 us -> 33.3 us (level)
  Pallas kernels: 9.8 us -> 9.43 us
    pallas_call x1, Pallas kernels: 3.5 us -> 3.11 us  [forward_modes(): pl.pallas_call(forward_kernel, out_shape=(jax.ShapeDtypeStruct(sent, jnp....]
where the time goes in v13:
time: 33.3 us; the launch traced here: 33 us
  starting transfers between devices  16.7 us (50%)
  Pallas kernels  9.43 us (28%)
  waiting for transfers between devices  6.7 us (20%)
    all_to_all x2, starting transfers between devices, exchanged(): lax.all_to_all(value, ('px', 'py'), split_axis=0, concat_axis=0, tiled=True)  10.6 us
    ppermute x2, starting transfers between devices, swaps(): second = lax.ppermute(second, axis, inside)  4.71 us
    all_to_all x2, waiting for transfers between devices, exchanged(): lax.all_to_all(value, ('px', 'py'), split_axis=0, concat_axis=0, tiled=True)  4.15 us
    pallas_call x1, Pallas kernels, forward_modes(): pl.pallas_call(forward_kernel, out_shape=(jax.ShapeDtypeStruct(sent, jnp....  3.11 us
    ppermute x2, waiting for transfers between devices, swaps(): second = lax.ppermute(second, axis, inside)  2.54 us
    pallas_call x1, Pallas kernels, finish(): pl.pallas_call(finish_kernel, out_shape=jax.ShapeDtypeStruct(convolved.sh...  2.04 us
    pallas_call x2, Pallas kernels, convolve(): pl.pallas_call(kernel, out_shape=jax.ShapeDtypeStruct((rows, 128), jnp.fl...  1.83 us
    pallas_call x1, Pallas kernels, mix_modes(): pl.pallas_call(mix_kernel, out_shape=jax.ShapeDtypeStruct((32, 16, 128),...  1.6 us
  transfers between devices with their start and end apart: 6, of which 3 were waited for; matrix products, arithmetic and copies ran while one was open for 0% of the time, Pallas kernels for 13%

profile of v13, /device:TPU:0, one launch (start us, length us, event | category | flops | bytes accessed | tf_op | source)
XLA Modules:
  0.0 33.0 jit_solution(111973264193309161)
XLA Ops:
  0.0 3.1 %forward_modes.1 = (bf16[32,8,128]{2,1,0:T(8,128)(2,1)}, bf16[64,32,128]{2,1,0:T(8,128)(2,1)S(1)}, bf16[2,4,16,16,128]{4,3,2,1,0:T(8,128)(2,1)S(1)}, bf16[3,3,3,32,32]{4,3,2,1,0:T(8,128)(2,1)S(1)}) custom-call(bf16[64,32,128]{2,1,0:T(8,128)(2,1)} %bitcast.10, f32[32,128]{1,0:T(8,128)} %constant.12.clone.z_hbm, f32[4,64,512]{2,1,0:T(8,128)} %constant.13.clone.y_hbm, ...), custom_call_target="tpu_custom_call" | custom-call | flops 134217728 | bytes 2097152 | tf_op jit(solution)/shard_map/forward_modes/pallas_call | solution.py:328
  3.1 7.3 %all-to-all-start = ((bf16[32,8,128]{2,1,0:T(8,128)(2,1)}), bf16[32,8,128]{2,1,0:T(8,128)(2,1)S(1)}, u32[]{:S(2)}, u32[]{:S(2)}) async-start(bf16[32,8,128]{2,1,0:T(8,128)(2,1)} %get-tuple-element.14), calls=%async_computation | async-start | bytes 131072 | tf_op jit(solution)/shard_map/all_to_all | solution.py:623
  10.4 0.8 %arrange_cells.1 = (bf16[32,32,128]{2,1,0:T(8,128)(2,1)S(1)}, bf16[32,32,128]{2,1,0:T(8,128)(2,1)S(1)}, bf16[3,64,384]{2,1,0:T(8,128)(2,1)S(1)}) custom-call(bf16[32,2,32,128]{3,2,1,0:T(8,128)(2,1)S(1)} %bitcast.7, bf16[3,3,3,32,32]{4,3,2,1,0:T(8,128)(2,1)S(1)} %get-tuple-element.17.conv_ref), custom_call_target="tpu_custom_call" | custom-call | flops 1024 | bytes 1024 | tf_op jit(solution)/shard_map/arrange_cells/pallas_call | solution.py:380
  11.3 1.8 %collective-permute-start = (bf16[32,32,128]{2,1,0:T(8,128)(2,1)S(1)}, bf16[32,32,128]{2,1,0:T(8,128)(2,1)S(1)}, u32[]{:S(2)}, u32[]{:S(2)}) collective-permute-start(bf16[32,32,128]{2,1,0:T(8,128)(2,1)S(1)} %get-tuple-element.18.refs_1_), channel_id=1, source_target_pairs={{0,4},{4,0},{8,12},{12,8},{16,20},{20,16},{24,28},{28,24},{1,5},{5... | collective-permute-start | bytes 786440 | tf_op jit(solution)/shard_map/ppermute | solution.py:630
  13.1 0.7 %collective-permute-start.1 = (bf16[32,32,128]{2,1,0:T(8,128)(2,1)S(1)}, bf16[32,32,128]{2,1,0:T(8,128)(2,1)S(1)}, u32[]{:S(2)}, u32[]{:S(2)}) collective-permute-start(bf16[32,32,128]{2,1,0:T(8,128)(2,1)S(1)} %get-tuple-element.19.refs_2_), channel_id=1, source_target_pairs={{4,8},{8,4},{12,16},{16,12},{20,24},{24,20},{5,9},{9,5},{13,17},{1... | collective-permute-start | bytes 786440 | tf_op jit(solution)/shard_map/ppermute | solution.py:631
  13.8 4.1 %all-to-all-done.modes_ref = bf16[32,8,128]{2,1,0:T(8,128)(2,1)S(1)} async-done(((bf16[32,8,128]{2,1,0:T(8,128)(2,1)}), bf16[32,8,128]{2,1,0:T(8,128)(2,1)S(1)}, u32[]{:S(2)}, u32[]{:S(2)}) %all-to-all-start) | async-done | bytes 65568 | tf_op jit(solution)/shard_map/all_to_all | solution.py:623
  17.9 0.0 copy-done.3
  17.9 0.0 copy-done.4
  17.9 1.6 %mix_modes.1 = bf16[32,16,128]{2,1,0:T(8,128)(2,1)} custom-call(bf16[32,8,128]{2,1,0:T(8,128)(2,1)S(1)} %all-to-all-done.modes_ref, f32[64,256]{1,0:T(8,128)S(1)} %copy-done.4, bf16[2,4,16,16,128]{4,3,2,1,0:T(8,128)(2,1)S(1)} %get-tuple-element.15.weight_ref, f32[128,256]{1,0:T(8,128)S(1)} %copy-done.3), custom_call_target="tpu_custom_call" | custom-call | flops 34359738368 | bytes 2097152 | tf_op jit(solution)/shard_map/mix_modes/pallas_call | solution.py:429
  19.5 3.3 %all-to-all-start.1 = ((bf16[32,16,128]{2,1,0:T(8,128)(2,1)}), bf16[32,16,128]{2,1,0:T(8,128)(2,1)S(1)}, u32[]{:S(2)}, u32[]{:S(2)}) async-start(bf16[32,16,128]{2,1,0:T(8,128)(2,1)} %mix_modes.1), calls=%async_computation.1 | async-start | bytes 262144 | tf_op jit(solution)/shard_map/all_to_all | solution.py:623
  22.7 2.5 %collective-permute-done.refs_0_ = bf16[32,32,128]{2,1,0:T(8,128)(2,1)S(1)} collective-permute-done((bf16[32,32,128]{2,1,0:T(8,128)(2,1)S(1)}, bf16[32,32,128]{2,1,0:T(8,128)(2,1)S(1)}, u32[]{:S(2)}, u32[]{:S(2)}) %collective-permute-start) | collective-permute-done | bytes 262176 | tf_op jit(solution)/shard_map/ppermute | solution.py:630
  25.3 0.0 collective-permute-done.1.refs_3_
  25.3 0.0 copy-start
  25.3 0.0 copy-start.1
  25.3 0.0 copy-start.2
  25.3 0.8 %collective-permute-start.2 = (bf16[128,128]{1,0:T(8,128)(2,1)S(1)}, bf16[128,128]{1,0:T(8,128)(2,1)S(1)}, u32[]{:S(2)}, u32[]{:S(2)}) collective-permute-start(bf16[128,128]{1,0:T(8,128)(2,1)S(1)} %get-tuple-element.21), channel_id=1, source_target_pairs={{1,2},{2,1},{5,6},{6,5},{9,10},{10,9},{13,14},{14,13},{17,18},{18,... | collective-permute-start | bytes 98312 | tf_op jit(solution)/shard_map/ppermute | solution.py:631
  26.1 2.9 %collective-permute-start.3 = (bf16[128,128]{1,0:T(8,128)(2,1)S(1)}, bf16[128,128]{1,0:T(8,128)(2,1)S(1)}, u32[]{:S(2)}, u32[]{:S(2)}) collective-permute-start(bf16[128,128]{1,0:T(8,128)(2,1)S(1)} %get-tuple-element.22), channel_id=1, source_target_pairs={{0,1},{1,0},{2,3},{3,2},{4,5},{5,4},{6,7},{7,6},{8,9},{9,8},{10,11... | collective-permute-start | bytes 98312 | tf_op jit(solution)/shard_map/ppermute | solution.py:630
  29.0 1.3 %convolve_interior.1 = f32[2048,128]{1,0:T(8,128)S(1)} custom-call(bf16[32,32,128]{2,1,0:T(8,128)(2,1)S(1)} %collective-permute-done.refs_0_, bf16[32,32,128]{2,1,0:T(8,128)(2,1)S(1)} %get-tuple-element.18.refs_1_, bf16[32,32,128]{2,1,0:T(8,128)(2,1)S(1)} %get-tuple-element.19.refs_2_, bf16[32,32,128]{2,1,0:T(8,128)(2,1)S(1)} %collective-permute-done.1.refs_3_, ...), custom_call_target="tpu_custom_call" | custom-call | flops 1073741824 | bytes 2097152 | tf_op jit(solution)/shard_map/convolve_interior/pallas_call | solution.py:525
  30.4 0.0 collective-permute-done.2.refs_4_
  30.4 0.0 collective-permute-done.3.refs_5_
  30.4 0.5 %convolve_edges.1 = f32[512,128]{1,0:T(8,128)S(1)} custom-call(bf16[32,32,128]{2,1,0:T(8,128)(2,1)S(1)} %collective-permute-done.refs_0_, bf16[32,32,128]{2,1,0:T(8,128)(2,1)S(1)} %get-tuple-element.18.refs_1_, bf16[32,32,128]{2,1,0:T(8,128)(2,1)S(1)} %get-tuple-element.19.refs_2_, bf16[32,32,128]{2,1,0:T(8,128)(2,1)S(1)} %collective-permute-done.1.refs_3_, ...), custom_call_target="tpu_custom_call" | custom-call | flops 1073741824 | bytes 2097152 | tf_op jit(solution)/shard_map/convolve_edges/pallas_call | solution.py:525
  30.9 0.1 all-to-all-done.1.values_ref
  31.0 0.0 copy-done.2
  31.0 2.0 %finish_layer.1 = bf16[32,2,32,128]{3,2,1,0:T(8,128)(2,1)} custom-call(f32[32]{0:T(128)S(1)} %copy-done.2, bf16[32,16,128]{2,1,0:T(8,128)(2,1)S(1)} %all-to-all-done.1.values_ref, f32[128,512]{1,0:T(8,128)S(1)} %copy-done.1, f32[4,32,512]{2,1,0:T(8,128)S(1)} %copy-done, f32[32,2,32,128]{3,2,1,0:T(8,128)S(1)} %bitcast.6, f32[32,2,8,128]{3,2,1,0:T(8,128)S(1)} %bitcast.8), custom_call_target="tpu_custom_call" | custom-call | flops 268435456 | bytes 4194304 | tf_op jit(solution)/shard_map/finish_layer/pallas_call | solution.py:607
  (5 shorter events, 0.0 us)
Async XLA Ops:
  0.0 17.9 %copy-start.3 = (f32[128,256]{1,0:T(8,128)S(1)}, f32[128,256]{1,0:T(8,128)}, u32[]{:S(2)}) copy-start(f32[128,256]{1,0:T(8,128)} %constant.15.clone.inverse_ref) | copy-start | bytes 393220
  0.0 17.9 %copy-start.4 = (f32[64,256]{1,0:T(8,128)S(1)}, f32[64,256]{1,0:T(8,128)}, u32[]{:S(2)}) copy-start(f32[64,256]{1,0:T(8,128)} %constant.14.clone.forward_ref) | copy-start | bytes 196612
  3.1 14.7 %all-to-all-start = ((bf16[32,8,128]{2,1,0:T(8,128)(2,1)}), bf16[32,8,128]{2,1,0:T(8,128)(2,1)S(1)}, u32[]{:S(2)}, u32[]{:S(2)}) async-start(bf16[32,8,128]{2,1,0:T(8,128)(2,1)} %get-tuple-element.14), calls=%async_computation | async-start | bytes 131072 | tf_op jit(solution)/shard_map/all_to_all | solution.py:623
  11.3 14.0 %collective-permute-start = (bf16[32,32,128]{2,1,0:T(8,128)(2,1)S(1)}, bf16[32,32,128]{2,1,0:T(8,128)(2,1)S(1)}, u32[]{:S(2)}, u32[]{:S(2)}) collective-permute-start(bf16[32,32,128]{2,1,0:T(8,128)(2,1)S(1)} %get-tuple-element.18.refs_1_), channel_id=1, source_target_pairs={{0,4},{4,0},{8,12},{12,8},{16,20},{20,16},{24,28},{28,24},{1,5},{5... | collective-permute-start | bytes 786440 | tf_op jit(solution)/shard_map/ppermute | solution.py:630
  13.1 12.2 %collective-permute-start.1 = (bf16[32,32,128]{2,1,0:T(8,128)(2,1)S(1)}, bf16[32,32,128]{2,1,0:T(8,128)(2,1)S(1)}, u32[]{:S(2)}, u32[]{:S(2)}) collective-permute-start(bf16[32,32,128]{2,1,0:T(8,128)(2,1)S(1)} %get-tuple-element.19.refs_2_), channel_id=1, source_target_pairs={{4,8},{8,4},{12,16},{16,12},{20,24},{24,20},{5,9},{9,5},{13,17},{1... | collective-permute-start | bytes 786440 | tf_op jit(solution)/shard_map/ppermute | solution.py:631
  19.5 11.5 %all-to-all-start.1 = ((bf16[32,16,128]{2,1,0:T(8,128)(2,1)}), bf16[32,16,128]{2,1,0:T(8,128)(2,1)S(1)}, u32[]{:S(2)}, u32[]{:S(2)}) async-start(bf16[32,16,128]{2,1,0:T(8,128)(2,1)} %mix_modes.1), calls=%async_computation.1 | async-start | bytes 262144 | tf_op jit(solution)/shard_map/all_to_all | solution.py:623
  25.3 5.7 %copy-start = (f32[4,32,512]{2,1,0:T(8,128)S(1)}, f32[4,32,512]{2,1,0:T(8,128)}, u32[]{:S(2)}) copy-start(f32[4,32,512]{2,1,0:T(8,128)} %constant.17.clone.y_ref) | copy-start | bytes 786436
  25.3 5.7 %copy-start.1 = (f32[128,512]{1,0:T(8,128)S(1)}, f32[128,512]{1,0:T(8,128)}, u32[]{:S(2)}) copy-start(f32[128,512]{1,0:T(8,128)} %constant.16.clone.z_ref) | copy-start | bytes 786436
  25.3 5.6 %copy-start.2 = (f32[32]{0:T(128)S(1)}, f32[32]{0:T(128)}, u32[]{:S(2)}) copy-start(f32[32]{0:T(128)} %bias_ref.1) | copy-start | bytes 388
  25.3 5.0 %collective-permute-start.2 = (bf16[128,128]{1,0:T(8,128)(2,1)S(1)}, bf16[128,128]{1,0:T(8,128)(2,1)S(1)}, u32[]{:S(2)}, u32[]{:S(2)}) collective-permute-start(bf16[128,128]{1,0:T(8,128)(2,1)S(1)} %get-tuple-element.21), channel_id=1, source_target_pairs={{1,2},{2,1},{5,6},{6,5},{9,10},{10,9},{13,14},{14,13},{17,18},{18,... | collective-permute-start | bytes 98312 | tf_op jit(solution)/shard_map/ppermute | solution.py:631
  26.1 4.2 %collective-permute-start.3 = (bf16[128,128]{1,0:T(8,128)(2,1)S(1)}, bf16[128,128]{1,0:T(8,128)(2,1)S(1)}, u32[]{:S(2)}, u32[]{:S(2)}) collective-permute-start(bf16[128,128]{1,0:T(8,128)(2,1)S(1)} %get-tuple-element.22), channel_id=1, source_target_pairs={{0,1},{1,0},{2,3},{3,2},{4,5},{5,4},{6,7},{7,6},{8,9},{9,8},{10,11... | collective-permute-start | bytes 98312 | tf_op jit(solution)/shard_map/ppermute | solution.py:630

commit v14 on v13

--- a/solution.py
+++ b/solution.py
@@ -226,8 +226,8 @@
 def block_moves(value):
     rows = value.shape[0]
     tiles = value.reshape(rows // 8, 8, 128)
-    row = lax.broadcasted_iota(jnp.int32, tiles.shape, 1) % 4
-    block = lax.broadcasted_iota(jnp.int32, tiles.shape, 2) // 32
+    row = lax.broadcasted_iota(jnp.int32, (1, 8, 128), 1) % 4
+    block = lax.broadcasted_iota(jnp.int32, (1, 8, 128), 2) // 32
     result = tiles
     for lane_step in (1, 2, 3):
         moved = pltpu.roll(tiles, 128 - 32 * lane_step, 2)
@@ -279,13 +279,14 @@
         copy.start()
     y_copy.wait()
     table = y_ref[...]
-    lane = lax.broadcasted_iota(jnp.int32, (span, table.shape[1]), 1)
+    lane = lax.broadcasted_iota(jnp.int32, (1, 8, table.shape[1]), 2)
+    halves = table.reshape(2, span // 8, 8, table.shape[1])
     for x in range(2):
         for c in range(8):
             own = (lane % 8 == c) & (lane // 64 % 2 == x)
             for part in range(2):
                 first = part * 16 * span + (c * 2 + x) * span
-                block = jnp.where(own, table[part * span : (part + 1) * span], 0.0)
+                block = jnp.where(own, halves[part], 0.0).reshape(span, table.shape[1])
                 table_ref[first : first + span] = block.astype(jnp.bfloat16)
     z_copy.wait()
     z_table = z_ref[...].astype(jnp.bfloat16)
@@ -542,8 +543,12 @@
 ):
     upper = lax.broadcasted_iota(jnp.int32, (8, 128), 0) < 4
     table = y_ref[lax.axis_index("py")]
-    lane = lax.broadcasted_iota(jnp.int32, table.shape, 1) % 16
-    expanded = [jnp.where(lane == o, table, 0.0).astype(jnp.bfloat16) for o in range(16)]
+    lane = lax.broadcasted_iota(jnp.int32, (1, 8, table.shape[1]), 2) % 16
+    tiles = table.reshape(-1, 8, table.shape[1])
+    expanded = [
+        jnp.where(lane == o, tiles, 0.0).reshape(table.shape).astype(jnp.bfloat16)
+        for o in range(16)
+    ]
     columns = []
     for group in range(4):
         columns.append(

time: 33.3 us -> 33.3 us (level)
  no operation moved by 1% of the time
where the time goes in v14:
time: 33.3 us; the launch traced here: 33 us
  starting transfers between devices  16.7 us (50%)
  Pallas kernels  9.43 us (28%)
  waiting for transfers between devices  6.7 us (20%)
    all_to_all x2, starting transfers between devices, exchanged(): lax.all_to_all(value, ('px', 'py'), split_axis=0, concat_axis=0, tiled=True)  10.6 us
    ppermute x2, starting transfers between devices, swaps(): second = lax.ppermute(second, axis, inside)  4.71 us
    all_to_all x2, waiting for transfers between devices, exchanged(): lax.all_to_all(value, ('px', 'py'), split_axis=0, concat_axis=0, tiled=True)  4.15 us
    pallas_call x1, Pallas kernels, forward_modes(): pl.pallas_call(forward_kernel, out_shape=(jax.ShapeDtypeStruct(sent, jnp....  3.11 us
    ppermute x2, waiting for transfers between devices, swaps(): second = lax.ppermute(second, axis, inside)  2.54 us
    pallas_call x1, Pallas kernels, finish(): pl.pallas_call(finish_kernel, out_shape=jax.ShapeDtypeStruct(convolved.sh...  2.04 us
    pallas_call x2, Pallas kernels, convolve(): pl.pallas_call(kernel, out_shape=jax.ShapeDtypeStruct((rows, 128), jnp.fl...  1.83 us
    pallas_call x1, Pallas kernels, mix_modes(): pl.pallas_call(mix_kernel, out_shape=jax.ShapeDtypeStruct((32, 16, 128),...  1.6 us
  transfers between devices with their start and end apart: 6, of which 3 were waited for; matrix products, arithmetic and copies ran while one was open for 0% of the time, Pallas kernels for 13%

profile of v14, /device:TPU:0, one launch (start us, length us, event | category | flops | bytes accessed | tf_op | source)
XLA Modules:
  0.0 33.0 jit_solution(2683687197915096987)
XLA Ops:
  0.0 3.1 %forward_modes.1 = (bf16[32,8,128]{2,1,0:T(8,128)(2,1)}, bf16[64,32,128]{2,1,0:T(8,128)(2,1)S(1)}, bf16[2,4,16,16,128]{4,3,2,1,0:T(8,128)(2,1)S(1)}, bf16[3,3,3,32,32]{4,3,2,1,0:T(8,128)(2,1)S(1)}) custom-call(bf16[64,32,128]{2,1,0:T(8,128)(2,1)} %bitcast.10, f32[32,128]{1,0:T(8,128)} %constant.12.clone.z_hbm, f32[4,64,512]{2,1,0:T(8,128)} %constant.13.clone.y_hbm, ...), custom_call_target="tpu_custom_call" | custom-call | flops 134217728 | bytes 2097152 | tf_op jit(solution)/shard_map/forward_modes/pallas_call | solution.py:329
  3.1 7.3 %all-to-all-start = ((bf16[32,8,128]{2,1,0:T(8,128)(2,1)}), bf16[32,8,128]{2,1,0:T(8,128)(2,1)S(1)}, u32[]{:S(2)}, u32[]{:S(2)}) async-start(bf16[32,8,128]{2,1,0:T(8,128)(2,1)} %get-tuple-element.14), calls=%async_computation | async-start | bytes 131072 | tf_op jit(solution)/shard_map/all_to_all | solution.py:628
  10.4 0.8 %arrange_cells.1 = (bf16[32,32,128]{2,1,0:T(8,128)(2,1)S(1)}, bf16[32,32,128]{2,1,0:T(8,128)(2,1)S(1)}, bf16[3,64,384]{2,1,0:T(8,128)(2,1)S(1)}) custom-call(bf16[32,2,32,128]{3,2,1,0:T(8,128)(2,1)S(1)} %bitcast.7, bf16[3,3,3,32,32]{4,3,2,1,0:T(8,128)(2,1)S(1)} %get-tuple-element.17.conv_ref), custom_call_target="tpu_custom_call" | custom-call | flops 1024 | bytes 1024 | tf_op jit(solution)/shard_map/arrange_cells/pallas_call | solution.py:381
  11.3 1.8 %collective-permute-start = (bf16[32,32,128]{2,1,0:T(8,128)(2,1)S(1)}, bf16[32,32,128]{2,1,0:T(8,128)(2,1)S(1)}, u32[]{:S(2)}, u32[]{:S(2)}) collective-permute-start(bf16[32,32,128]{2,1,0:T(8,128)(2,1)S(1)} %get-tuple-element.18.refs_1_), channel_id=1, source_target_pairs={{0,4},{4,0},{8,12},{12,8},{16,20},{20,16},{24,28},{28,24},{1,5},{5... | collective-permute-start | bytes 786440 | tf_op jit(solution)/shard_map/ppermute | solution.py:635
  13.1 0.7 %collective-permute-start.1 = (bf16[32,32,128]{2,1,0:T(8,128)(2,1)S(1)}, bf16[32,32,128]{2,1,0:T(8,128)(2,1)S(1)}, u32[]{:S(2)}, u32[]{:S(2)}) collective-permute-start(bf16[32,32,128]{2,1,0:T(8,128)(2,1)S(1)} %get-tuple-element.19.refs_2_), channel_id=1, source_target_pairs={{4,8},{8,4},{12,16},{16,12},{20,24},{24,20},{5,9},{9,5},{13,17},{1... | collective-permute-start | bytes 786440 | tf_op jit(solution)/shard_map/ppermute | solution.py:636
  13.8 4.1 %all-to-all-done.modes_ref = bf16[32,8,128]{2,1,0:T(8,128)(2,1)S(1)} async-done(((bf16[32,8,128]{2,1,0:T(8,128)(2,1)}), bf16[32,8,128]{2,1,0:T(8,128)(2,1)S(1)}, u32[]{:S(2)}, u32[]{:S(2)}) %all-to-all-start) | async-done | bytes 65568 | tf_op jit(solution)/shard_map/all_to_all | solution.py:628
  17.9 0.0 copy-done.3
  17.9 0.0 copy-done.4
  17.9 1.6 %mix_modes.1 = bf16[32,16,128]{2,1,0:T(8,128)(2,1)} custom-call(bf16[32,8,128]{2,1,0:T(8,128)(2,1)S(1)} %all-to-all-done.modes_ref, f32[64,256]{1,0:T(8,128)S(1)} %copy-done.4, bf16[2,4,16,16,128]{4,3,2,1,0:T(8,128)(2,1)S(1)} %get-tuple-element.15.weight_ref, f32[128,256]{1,0:T(8,128)S(1)} %copy-done.3), custom_call_target="tpu_custom_call" | custom-call | flops 34359738368 | bytes 2097152 | tf_op jit(solution)/shard_map/mix_modes/pallas_call | solution.py:430
  19.5 3.3 %all-to-all-start.1 = ((bf16[32,16,128]{2,1,0:T(8,128)(2,1)}), bf16[32,16,128]{2,1,0:T(8,128)(2,1)S(1)}, u32[]{:S(2)}, u32[]{:S(2)}) async-start(bf16[32,16,128]{2,1,0:T(8,128)(2,1)} %mix_modes.1), calls=%async_computation.1 | async-start | bytes 262144 | tf_op jit(solution)/shard_map/all_to_all | solution.py:628
  22.7 2.5 %collective-permute-done.refs_0_ = bf16[32,32,128]{2,1,0:T(8,128)(2,1)S(1)} collective-permute-done((bf16[32,32,128]{2,1,0:T(8,128)(2,1)S(1)}, bf16[32,32,128]{2,1,0:T(8,128)(2,1)S(1)}, u32[]{:S(2)}, u32[]{:S(2)}) %collective-permute-start) | collective-permute-done | bytes 262176 | tf_op jit(solution)/shard_map/ppermute | solution.py:635
  25.3 0.0 collective-permute-done.1.refs_3_
  25.3 0.0 copy-start
  25.3 0.0 copy-start.1
  25.3 0.0 copy-start.2
  25.3 0.8 %collective-permute-start.2 = (bf16[128,128]{1,0:T(8,128)(2,1)S(1)}, bf16[128,128]{1,0:T(8,128)(2,1)S(1)}, u32[]{:S(2)}, u32[]{:S(2)}) collective-permute-start(bf16[128,128]{1,0:T(8,128)(2,1)S(1)} %get-tuple-element.21), channel_id=1, source_target_pairs={{1,2},{2,1},{5,6},{6,5},{9,10},{10,9},{13,14},{14,13},{17,18},{18,... | collective-permute-start | bytes 98312 | tf_op jit(solution)/shard_map/ppermute | solution.py:636
  26.1 2.9 %collective-permute-start.3 = (bf16[128,128]{1,0:T(8,128)(2,1)S(1)}, bf16[128,128]{1,0:T(8,128)(2,1)S(1)}, u32[]{:S(2)}, u32[]{:S(2)}) collective-permute-start(bf16[128,128]{1,0:T(8,128)(2,1)S(1)} %get-tuple-element.22), channel_id=1, source_target_pairs={{0,1},{1,0},{2,3},{3,2},{4,5},{5,4},{6,7},{7,6},{8,9},{9,8},{10,11... | collective-permute-start | bytes 98312 | tf_op jit(solution)/shard_map/ppermute | solution.py:635
  29.0 1.3 %convolve_interior.1 = f32[2048,128]{1,0:T(8,128)S(1)} custom-call(bf16[32,32,128]{2,1,0:T(8,128)(2,1)S(1)} %collective-permute-done.refs_0_, bf16[32,32,128]{2,1,0:T(8,128)(2,1)S(1)} %get-tuple-element.18.refs_1_, bf16[32,32,128]{2,1,0:T(8,128)(2,1)S(1)} %get-tuple-element.19.refs_2_, bf16[32,32,128]{2,1,0:T(8,128)(2,1)S(1)} %collective-permute-done.1.refs_3_, ...), custom_call_target="tpu_custom_call" | custom-call | flops 1073741824 | bytes 2097152 | tf_op jit(solution)/shard_map/convolve_interior/pallas_call | solution.py:526
  30.4 0.0 collective-permute-done.2.refs_4_
  30.4 0.0 collective-permute-done.3.refs_5_
  30.4 0.5 %convolve_edges.1 = f32[512,128]{1,0:T(8,128)S(1)} custom-call(bf16[32,32,128]{2,1,0:T(8,128)(2,1)S(1)} %collective-permute-done.refs_0_, bf16[32,32,128]{2,1,0:T(8,128)(2,1)S(1)} %get-tuple-element.18.refs_1_, bf16[32,32,128]{2,1,0:T(8,128)(2,1)S(1)} %get-tuple-element.19.refs_2_, bf16[32,32,128]{2,1,0:T(8,128)(2,1)S(1)} %collective-permute-done.1.refs_3_, ...), custom_call_target="tpu_custom_call" | custom-call | flops 1073741824 | bytes 2097152 | tf_op jit(solution)/shard_map/convolve_edges/pallas_call | solution.py:526
  30.9 0.1 all-to-all-done.1.values_ref
  31.0 0.0 copy-done.2
  31.0 2.0 %finish_layer.1 = bf16[32,2,32,128]{3,2,1,0:T(8,128)(2,1)} custom-call(f32[32]{0:T(128)S(1)} %copy-done.2, bf16[32,16,128]{2,1,0:T(8,128)(2,1)S(1)} %all-to-all-done.1.values_ref, f32[128,512]{1,0:T(8,128)S(1)} %copy-done.1, f32[4,32,512]{2,1,0:T(8,128)S(1)} %copy-done, f32[32,2,32,128]{3,2,1,0:T(8,128)S(1)} %bitcast.6, f32[32,2,8,128]{3,2,1,0:T(8,128)S(1)} %bitcast.8), custom_call_target="tpu_custom_call" | custom-call | flops 268435456 | bytes 4194304 | tf_op jit(solution)/shard_map/finish_layer/pallas_call | solution.py:612
  (5 shorter events, 0.0 us)
Async XLA Ops:
  0.0 17.9 %copy-start.3 = (f32[128,256]{1,0:T(8,128)S(1)}, f32[128,256]{1,0:T(8,128)}, u32[]{:S(2)}) copy-start(f32[128,256]{1,0:T(8,128)} %constant.15.clone.inverse_ref) | copy-start | bytes 393220
  0.0 17.9 %copy-start.4 = (f32[64,256]{1,0:T(8,128)S(1)}, f32[64,256]{1,0:T(8,128)}, u32[]{:S(2)}) copy-start(f32[64,256]{1,0:T(8,128)} %constant.14.clone.forward_ref) | copy-start | bytes 196612
  3.1 14.7 %all-to-all-start = ((bf16[32,8,128]{2,1,0:T(8,128)(2,1)}), bf16[32,8,128]{2,1,0:T(8,128)(2,1)S(1)}, u32[]{:S(2)}, u32[]{:S(2)}) async-start(bf16[32,8,128]{2,1,0:T(8,128)(2,1)} %get-tuple-element.14), calls=%async_computation | async-start | bytes 131072 | tf_op jit(solution)/shard_map/all_to_all | solution.py:628
  11.3 14.0 %collective-permute-start = (bf16[32,32,128]{2,1,0:T(8,128)(2,1)S(1)}, bf16[32,32,128]{2,1,0:T(8,128)(2,1)S(1)}, u32[]{:S(2)}, u32[]{:S(2)}) collective-permute-start(bf16[32,32,128]{2,1,0:T(8,128)(2,1)S(1)} %get-tuple-element.18.refs_1_), channel_id=1, source_target_pairs={{0,4},{4,0},{8,12},{12,8},{16,20},{20,16},{24,28},{28,24},{1,5},{5... | collective-permute-start | bytes 786440 | tf_op jit(solution)/shard_map/ppermute | solution.py:635
  13.1 12.2 %collective-permute-start.1 = (bf16[32,32,128]{2,1,0:T(8,128)(2,1)S(1)}, bf16[32,32,128]{2,1,0:T(8,128)(2,1)S(1)}, u32[]{:S(2)}, u32[]{:S(2)}) collective-permute-start(bf16[32,32,128]{2,1,0:T(8,128)(2,1)S(1)} %get-tuple-element.19.refs_2_), channel_id=1, source_target_pairs={{4,8},{8,4},{12,16},{16,12},{20,24},{24,20},{5,9},{9,5},{13,17},{1... | collective-permute-start | bytes 786440 | tf_op jit(solution)/shard_map/ppermute | solution.py:636
  19.5 11.5 %all-to-all-start.1 = ((bf16[32,16,128]{2,1,0:T(8,128)(2,1)}), bf16[32,16,128]{2,1,0:T(8,128)(2,1)S(1)}, u32[]{:S(2)}, u32[]{:S(2)}) async-start(bf16[32,16,128]{2,1,0:T(8,128)(2,1)} %mix_modes.1), calls=%async_computation.1 | async-start | bytes 262144 | tf_op jit(solution)/shard_map/all_to_all | solution.py:628
  25.3 5.7 %copy-start = (f32[4,32,512]{2,1,0:T(8,128)S(1)}, f32[4,32,512]{2,1,0:T(8,128)}, u32[]{:S(2)}) copy-start(f32[4,32,512]{2,1,0:T(8,128)} %constant.17.clone.y_ref) | copy-start | bytes 786436
  25.3 5.7 %copy-start.1 = (f32[128,512]{1,0:T(8,128)S(1)}, f32[128,512]{1,0:T(8,128)}, u32[]{:S(2)}) copy-start(f32[128,512]{1,0:T(8,128)} %constant.16.clone.z_ref) | copy-start | bytes 786436
  25.3 5.6 %copy-start.2 = (f32[32]{0:T(128)S(1)}, f32[32]{0:T(128)}, u32[]{:S(2)}) copy-start(f32[32]{0:T(128)} %bias_ref.1) | copy-start | bytes 388
  25.3 5.0 %collective-permute-start.2 = (bf16[128,128]{1,0:T(8,128)(2,1)S(1)}, bf16[128,128]{1,0:T(8,128)(2,1)S(1)}, u32[]{:S(2)}, u32[]{:S(2)}) collective-permute-start(bf16[128,128]{1,0:T(8,128)(2,1)S(1)} %get-tuple-element.21), channel_id=1, source_target_pairs={{1,2},{2,1},{5,6},{6,5},{9,10},{10,9},{13,14},{14,13},{17,18},{18,... | collective-permute-start | bytes 98312 | tf_op jit(solution)/shard_map/ppermute | solution.py:636
  26.1 4.2 %collective-permute-start.3 = (bf16[128,128]{1,0:T(8,128)(2,1)S(1)}, bf16[128,128]{1,0:T(8,128)(2,1)S(1)}, u32[]{:S(2)}, u32[]{:S(2)}) collective-permute-start(bf16[128,128]{1,0:T(8,128)(2,1)S(1)} %get-tuple-element.22), channel_id=1, source_target_pairs={{0,1},{1,0},{2,3},{3,2},{4,5},{5,4},{6,7},{7,6},{8,9},{9,8},{10,11... | collective-permute-start | bytes 98312 | tf_op jit(solution)/shard_map/ppermute | solution.py:635
